TPU v7x, 32 devices: a whole 2x2x4 slice. The times are simulated.
32 devices in a mesh: group: 1, pre: 4 (over z), dec: 4 (over y, x), tp: 2 (over core).
Axes of the slice: x: 2, y: 2, z: 4, core: 2. Of those that a mesh axis runs over, the one named last changes fastest.
Arguments:
- hidden: bfloat16 [1536, 8192], P(('group', 'pre')), may hold values from -6 to 6
- queries: bfloat16 [1536, 8192], P(('group', 'pre'), ('dec', 'tp')), may hold values from -60 to 60
- key_weight: bfloat16 [8192, 1024], P('pre', ('dec', 'tp')), may hold values from -0.0625 to 0.0625
- value_weight: bfloat16 [8192, 1024], P('pre', ('dec', 'tp')), may hold values from -0.0625 to 0.0625
- key_bias: bfloat16 [1024], P(('dec', 'tp')), may hold values from -3 to 3
- value_bias: bfloat16 [1024], P(('dec', 'tp')), may hold values from -3 to 3
- segment_ids: int32 [1536], P('group'), may hold values from 0 to 3, never falling along the last dimension, each value on 1 to 1152 neighbouring positions
- page_owner: int32 [96, 1], P(('group', 'pre')), may hold values from 0 to 3; in each aligned block of 24 rows (0 to 23, 24 to 47, ...) at most 12 rows name the same one
Outputs:
- attention: bfloat16 [1536, 8192], P(('group', 'pre'), ('dec', 'tp'))
- kv_cache: bfloat16 [4, 4, 192, 2048], P(('group', 'pre'), None, None, ('dec', 'tp'))
Inputs may be any that keep to these rules, and one draw needn't show every extreme that they name: `segment_ids`: prompts are contiguous runs of tokens; ids never fall; every prompt has 1 to 1152 tokens and one has exactly 1152. `page_owner`: among the 24 pages of one device no owner is named more than 12 times, and on at least one device on at least one device that many is reached.
All inputs are finite; a program needn't handle non-finite values.
Results may differ from a plain program's by a relative error of at most 0.0074.
Values may be sent and summed in bfloat16 or wider, within the bound.
No kernel may reach another device: no remote copies, remote signals or barrier semaphores. Data moves between devices by JAX's collectives and lax.ppermute only.
A program may use at most 192 MiB of HBM per device.

v0:
```python
import jax
import jax.numpy as jnp
from jax import lax
from jax.sharding import PartitionSpec as P

HD = 128
PAGE = 16


def attend(carry, query_block, key_piece, value_piece, allowed, scale):
    running_max, running_total, running_sum = carry
    count = key_piece.shape[0]
    kv_local = query_block.shape[1]
    key_block = key_piece.reshape(count, kv_local, -1)
    value_block = value_piece.reshape(count, kv_local, -1)
    scores = (
        jnp.einsum("ilgd,jld->lgij", query_block, key_block, preferred_element_type=jnp.float32)
        * scale
    )
    scores = jnp.where(allowed[None, None], scores, -1e30)
    new_max = jnp.maximum(running_max, jnp.max(scores, axis=-1))
    weights = jnp.where(allowed[None, None], jnp.exp(scores - new_max[..., None]), 0.0)
    new_total = jnp.sum(weights, axis=-1)
    mixed = jnp.einsum(
        "lgij,jld->lgid",
        weights.astype(jnp.bfloat16),
        value_block,
        preferred_element_type=jnp.float32,
    )
    return (new_max, new_total, mixed)


def body(hidden, queries, key_weight, value_weight, key_bias, value_bias, segment_ids, page_owner):
    n_pre = lax.axis_size("pre")
    index = lax.axis_index("pre")
    span = hidden.shape[0]
    head_cols = key_weight.shape[1]
    kv_local = head_cols // HD
    q_local = queries.shape[1] // HD
    group_size = q_local // kv_local
    scale = float(HD) ** (-0.5)
    pieces = (
        lax.all_gather(key_weight, "pre", axis=0, tiled=True),
        lax.all_gather(value_weight, "pre", axis=0, tiled=True),
    )
    joined = jnp.concatenate([pieces[0], pieces[1]], axis=1)
    projected = jnp.dot(hidden, joined, preferred_element_type=jnp.float32)
    key_local = (projected[:, :head_cols] + key_bias.astype(jnp.float32)).astype(jnp.bfloat16)
    value_local = (projected[:, head_cols:] + value_bias.astype(jnp.float32)).astype(jnp.bfloat16)
    query_block = queries.reshape(span, kv_local, group_size, HD)
    base = index * span
    query_pos = base + jnp.arange(span, dtype=jnp.int32)
    query_seg = lax.dynamic_slice_in_dim(segment_ids, base, span)
    start_carry = (
        jnp.full((kv_local, group_size, span), -1e30, jnp.float32),
        jnp.zeros((kv_local, group_size, span), jnp.float32),
        jnp.zeros((kv_local, group_size, span, HD), jnp.float32),
    )
    pieces = (
        lax.all_gather(key_local, "pre", axis=0, tiled=True),
        lax.all_gather(value_local, "pre", axis=0, tiled=True),
    )
    key_pos = jnp.arange(pieces[0].shape[0], dtype=jnp.int32)
    allowed = (query_seg[:, None] == segment_ids[None, :]) & (
        key_pos[None, :] <= query_pos[:, None]
    )
    result = attend(start_carry, query_block, pieces[0], pieces[1], allowed, scale)
    normed = result[2] / result[1][..., None]
    attention = normed.transpose(2, 0, 1, 3).reshape(span, q_local * HD).astype(jnp.bfloat16)
    pages_dev = span // PAGE
    capacity = 2 * pages_dev // n_pre
    width = kv_local * 2 * HD
    paired = jnp.stack(
        [key_local.reshape(span, kv_local, HD), value_local.reshape(span, kv_local, HD)], axis=2
    )
    pages = paired.reshape(pages_dev, PAGE * width)
    owners = page_owner[:, 0]
    onehot = (owners[:, None] == jnp.arange(n_pre, dtype=jnp.int32)[None, :]).astype(jnp.int32)
    rank = jnp.sum((jnp.cumsum(onehot, axis=0) - onehot) * onehot, axis=1)
    slot_ids = jnp.arange(capacity, dtype=jnp.int32)
    select = (onehot.T[:, None, :] == 1) & (rank[None, None, :] == slot_ids[None, :, None])
    outgoing = jnp.einsum(
        "orp,pf->orf", select.astype(jnp.bfloat16), pages, preferred_element_type=jnp.float32
    ).astype(jnp.bfloat16)
    outgoing = outgoing.reshape(n_pre, capacity * PAGE, width)
    received = lax.all_to_all(outgoing, "pre", split_axis=0, concat_axis=0, tiled=True)
    return (attention, received[None])


def solution(mesh):
    return jax.shard_map(
        body,
        mesh=mesh,
        in_specs=(
            P(("group", "pre"), None),
            P(("group", "pre"), ("dec", "tp")),
            P("pre", ("dec", "tp")),
            P("pre", ("dec", "tp")),
            P(("dec", "tp")),
            P(("dec", "tp")),
            P("group"),
            P(("group", "pre"), None),
        ),
        out_specs=(
            P(("group", "pre"), ("dec", "tp")),
            P(("group", "pre"), None, None, ("dec", "tp")),
        ),
        check_vma=False,
    )
```

profile of v0, /device:TPU:16, one launch (start us, length us, event | category | flops | bytes accessed | tf_op | source)
XLA Modules:
  0.0 182.1 jit_solution(7682921028498926576)
XLA Ops:
  7.2 0.0 copy-start
  7.2 0.0 all-gather.3.cloned.1.call-start
  7.2 0.7 all-gather.3.cloned.1.call-update
  7.9 0.0 all-gather.5.cloned.1.call-start
  8.0 0.7 all-gather.5.cloned.1.call-update
  8.7 0.7 convert_element_type.41
  9.3 0.7 convert_element_type.44
  10.0 0.7 fusion.27
  10.8 0.8 dynamic_slice.3
  11.5 0.8 select_reduce_fusion
  12.4 0.7 convert_compare_fusion
  13.0 1.2 fusion.11
  14.3 41.0 %all-gather.3.cloned.1.call-done = bf16[8192,128]{1,0:T(8,128)(2,1)} async-done(((bf16[2048,128]{1,0:T(8,128)(2,1)}), bf16[8192,128]{1,0:T(8,128)(2,1)}) %all-gather.3.cloned.1.call-update) | async-done | bytes 2097168 | tf_op jit(solution)/shard_map/all_gather | solution.py:43
  55.3 46.3 %all-gather.5.cloned.1.call-done = bf16[8192,128]{1,0:T(8,128)(2,1)} async-done(((bf16[2048,128]{1,0:T(8,128)(2,1)}), bf16[8192,128]{1,0:T(8,128)(2,1)}) %all-gather.5.cloned.1.call-update) | async-done | bytes 2097168 | tf_op jit(solution)/shard_map/all_gather | solution.py:44
  101.5 6.4 %fusion.12 = f32[384,256]{0,1:T(8,128)S(1)} fusion(bf16[384,8192]{1,0:T(8,128)(2,1)} %param.8, bf16[8192,128]{1,0:T(8,128)(2,1)} %all-gather.5.cloned.1.call-done, bf16[8192,128]{1,0:T(8,128)(2,1)} %all-gather.3.cloned.1.call-done), kind=kOutput, calls=%fused_computation.16 | convolution fusion | flops 1619001344 | bytes 10878976 | tf_op jit(solution)/shard_map/dot_general | solution.py:47
  108.0 0.1 fusion.23
  108.1 14.8 %all_gather.14 = bf16[1536,128]{0,1:T(8,128)(2,1)S(1)} all-gather(bf16[384,128]{0,1:T(8,128)(2,1)S(1)} %get-tuple-element.7), channel_id=1, replica_groups=mesh['group'=1,'pre'=4,'dec'=4,'tp'=2] {'pre'}, dimensions={0}, use_global_device_ids=true | all-gather | bytes 491520 | tf_op jit(solution)/shard_map/all_gather | solution.py:60
  122.9 0.0 copy-done
  122.9 8.3 %fusion = (f32[8,384]{1,0:T(8,128)S(1)}, f32[1536,384,8]{1,0,2:T(8,128)}) fusion(pred[384,1536]{0,1:T(8,128)(4,1)S(1)} %fusion.11, bf16[1536,128]{0,1:T(8,128)(2,1)S(1)} %all_gather.14, bf16[384,1024]{1,0:T(8,128)(2,1)S(1)} %copy-done), kind=kOutput, calls=%fused_computation.2 | convolution fusion | flops 1222112256 | bytes 20656128 | tf_op jit(solution)/shard_map/ilgd,jld->lgij/dot_general | solution.py:17
  131.1 14.6 %all_gather.15 = bf16[1536,128]{0,1:T(8,128)(2,1)S(1)} all-gather(bf16[384,128]{0,1:T(8,128)(2,1)S(1)} %get-tuple-element.6), channel_id=1, replica_groups=mesh['group'=1,'pre'=4,'dec'=4,'tp'=2] {'pre'}, dimensions={0}, use_global_device_ids=true | all-gather | bytes 491520 | tf_op jit(solution)/shard_map/all_gather | solution.py:61
  145.7 0.2 copy.17
  145.9 0.1 reshape.154
  146.0 0.3 convolution_convert_fusion
  146.3 1.0 reshape.151
  147.4 5.7 %all-to-all-start = ((bf16[4,192,256]{2,1,0:T(8,128)(2,1)}), bf16[4,192,256]{2,1,0:T(8,128)(2,1)S(1)}, u32[]{:S(2)}, u32[]{:S(2)}) async-start(bf16[4,192,256]{2,1,0:T(8,128)(2,1)} %reshape.151), calls=%async_computation | async-start | bytes 786432 | tf_op jit(solution)/shard_map/all_to_all | solution.py:86
  153.1 10.9 %fusion.1 = f32[8,384]{1,0:T(8,128)S(1)} fusion(f32[1536,384,8]{1,0,2:T(8,128)} %get-tuple-element.9, f32[8,384]{1,0:T(8,128)S(1)} %broadcast_maximum_fusion, pred[384,1536]{0,1:T(8,128)(4,1)S(1)} %fusion.11), kind=kLoop, calls=%fused_computation.3 | loop fusion | flops 23589888 | bytes 19488768 | tf_op jit(solution)/shard_map/reduce_sum | solution.py:23
  164.0 9.3 %divide_convert_fusion = bf16[8,384,128]{1,2,0:T(8,128)(2,1)S(1)} fusion(f32[1536,384,8]{1,0,2:T(8,128)} %get-tuple-element.9, f32[8,384]{1,0:T(8,128)S(1)} %broadcast_maximum_fusion, pred[384,1536]{0,1:T(8,128)(4,1)S(1)} %fusion.11, f32[8,384]{1,0:T(8,128)S(1)} %fusion.1, bf16[1536,128]{0,1:T(8,128)(2,1)S(1)} %all_gather.15), kind=kOutput, calls=%fused_computation.15 | convolution fusion | flops 1232338944 | bytes 20668416 | tf_op jit(solution)/shard_map/lgij,jld->lgid/dot_general | solution.py:24
  173.3 1.2 copy.18
  174.5 0.0 all-to-all-done
  174.5 0.7 copy.30
  (5 shorter events, 0.1 us)
Async XLA Ops:
  7.2 115.7 %copy-start = (bf16[384,1024]{1,0:T(8,128)(2,1)S(1)}, bf16[384,1024]{1,0:T(8,128)(2,1)}, u32[]{:S(2)}) copy-start(bf16[384,1024]{1,0:T(8,128)(2,1)} %param.9) | copy-start | bytes 2359300
  7.2 48.1 %all-gather.3.cloned.1.call-start = ((), (), s32[]{:S(2)}) async-start(), calls=%async_computation.1 | async-start | bytes 2621440 | tf_op jit(solution)/shard_map/all_gather | solution.py:43
  7.9 93.6 %all-gather.5.cloned.1.call-start = ((), (), s32[]{:S(2)}) async-start(), calls=%async_computation.2 | async-start | bytes 2621440 | tf_op jit(solution)/shard_map/all_gather | solution.py:44
  147.4 27.2 %all-to-all-start = ((bf16[4,192,256]{2,1,0:T(8,128)(2,1)}), bf16[4,192,256]{2,1,0:T(8,128)(2,1)S(1)}, u32[]{:S(2)}, u32[]{:S(2)}) async-start(bf16[4,192,256]{2,1,0:T(8,128)(2,1)} %reshape.151), calls=%async_computation | async-start | bytes 786432 | tf_op jit(solution)/shard_map/all_to_all | solution.py:86
Sparse Core Ops, SparseCore 0:
  9.6 45.6 all-gather.2
  56.8 44.6 all-gather.4
where the time goes:
time: 184 us; the launch traced here: 182 us
  waiting for transfers between devices  88.6 us (48%)
  blocking collectives  29.4 us (16%)
  matrix products  24.3 us (13%)
  other arithmetic  15.9 us (9%)
  between operations  14.1 us (8%)
  starting transfers between devices  5.78 us (3%)
  local copies, waits for them, and re-layouts  4.04 us (2%)
    all_gather x1, waiting for transfers between devices, body(): lax.all_gather(value_weight, 'pre', axis=0, tiled=True)  46.3 us
    all_gather x1, waiting for transfers between devices, body(): lax.all_gather(key_weight, 'pre', axis=0, tiled=True)  41 us
    all_gather x1, blocking collectives, body(): lax.all_gather(key_local, 'pre', axis=0, tiled=True)  14.8 us
    all_gather x1, blocking collectives, body(): lax.all_gather(value_local, 'pre', axis=0, tiled=True)  14.6 us
    reduce_sum x1, other arithmetic, attend(): new_total = jnp.sum(weights, axis=-1)  10.9 us
    dot_general x1, matrix products, attend(): jnp.einsum('lgij,jld->lgid', weights.astype(jnp.bfloat16), value_block, p...  9.33 us
    dot_general x1, matrix products, attend(): jnp.einsum('ilgd,jld->lgij', query_block, key_block, preferred_element_ty...  8.27 us
    dot_general x1, matrix products, body(): projected = jnp.dot(hidden, joined, preferred_element_type=jnp.float32)  6.43 us
  transfers between devices with their start and end apart: 3, of which 2 were waited for; matrix products, arithmetic and copies ran while one was open for 15% of the time, Pallas kernels for 0%

commit v1 on v0

v1 whole, which is shorter than its diff:
```python
import functools
import math

import jax
import jax.numpy as jnp
from jax import lax
from jax.experimental import pallas as pl
from jax.experimental.pallas import tpu as pltpu
from jax.sharding import PartitionSpec as P

HD = 128
PAGE = 16
NEG = -1e30
VMEM_LIMIT = 48 * 1024 * 1024


def attention_kernel(heads, span, info, slots, q_ref, kv_ref, start_ref, out_ref, cache_ref, acc, top):
    index = info[0]
    first = info[1]
    factor = HD**-0.5 * math.log2(math.e)
    columns = lax.broadcasted_iota(jnp.int32, (span, span), 1)
    rows = lax.broadcasted_iota(jnp.int32, (span, span), 0)

    def block(j, diagonal):
        at = pl.multiple_of(j * span, span)
        keys = kv_ref[pl.ds(at, span), :HD]
        values = jnp.concatenate(
            [kv_ref[pl.ds(at, span), HD:], jnp.ones((span, HD), jnp.bfloat16)], axis=1
        )
        allowed = columns >= start_ref[...] - at
        if diagonal:
            allowed = allowed & (columns <= rows)
        for g in range(heads):
            scores = lax.dot_general(
                q_ref[:, g * HD : (g + 1) * HD],
                keys,
                (((1,), (1,)), ((), ())),
                preferred_element_type=jnp.float32,
            )
            scores = jnp.where(allowed, scores, NEG)
            peak = jnp.max(scores, axis=1, keepdims=True)
            if not diagonal:
                before = top[g]
                peak = jnp.maximum(peak, before)
            weights = jnp.exp2(scores * factor - peak * factor).astype(jnp.bfloat16)
            mixed = jnp.dot(weights, values, preferred_element_type=jnp.float32)
            if not diagonal:
                mixed = mixed + acc[g] * jnp.exp2((before - peak) * factor)
            top[g] = peak
            acc[g] = mixed

    block(index, True)

    @pl.loop(first, index)
    def _(j):
        block(j, False)

    for g in range(heads):
        mixed = acc[g]
        out_ref[:, g * HD : (g + 1) * HD] = (mixed[:, :HD] / mixed[:, HD:]).astype(out_ref.dtype)

    capacity = cache_ref.shape[1] // PAGE
    for s in range(cache_ref.shape[0]):

        @pl.loop(0, capacity)
        def _(r):
            page = slots[s * capacity + r]
            held = kv_ref[pl.ds(pl.multiple_of(jnp.maximum(page, 0) * PAGE, PAGE), PAGE), :]
            cache_ref[s, pl.ds(pl.multiple_of(r * PAGE, PAGE), PAGE), :] = jnp.where(
                page >= 0, held, jnp.zeros_like(held)
            )


def attention(info, slots, queries, kv, start, n_pre, capacity):
    span = queries.shape[0]
    heads = queries.shape[1] // HD
    return pl.pallas_call(
        functools.partial(attention_kernel, heads, span),
        in_specs=[
            pl.BlockSpec(memory_space=pltpu.SMEM),
            pl.BlockSpec(memory_space=pltpu.SMEM),
            pl.BlockSpec(memory_space=pltpu.VMEM),
            pl.BlockSpec(memory_space=pltpu.VMEM),
            pl.BlockSpec(memory_space=pltpu.VMEM),
        ],
        out_specs=[
            pl.BlockSpec(memory_space=pltpu.VMEM),
            pl.BlockSpec(memory_space=pltpu.VMEM),
        ],
        out_shape=[
            jax.ShapeDtypeStruct(queries.shape, jnp.bfloat16),
            jax.ShapeDtypeStruct((n_pre, capacity * PAGE, 2 * HD), jnp.bfloat16),
        ],
        scratch_shapes=[
            pltpu.VMEM((heads, span, 2 * HD), jnp.float32),
            pltpu.VMEM((heads, span, 1), jnp.float32),
        ],
        compiler_params=pltpu.CompilerParams(vmem_limit_bytes=VMEM_LIMIT),
        cost_estimate=pl.CostEstimate(
            flops=4 * heads * span * span * n_pre * HD,
            bytes_accessed=4 * queries.size * 2,
            transcendentals=heads * span * span * n_pre,
        ),
        name="attention",
    )(info, slots, queries, kv, start)


STEP = 1024


def project_kernel(mode, place, own_ref, outer_ref, kw_ref, vw_ref, *rest):
    if mode == "first":
        (acc,) = rest
    elif mode == "middle":
        before, acc = rest
    else:
        before, kb_ref, vb_ref, kv_ref, acc = rest
    k = pl.program_id(0)
    span = own_ref.shape[0]

    @pl.when(k == 0)
    def _():
        acc[...] = jnp.zeros_like(acc) if mode == "first" else before[...]

    weights = jnp.concatenate([kw_ref[...], vw_ref[...]], axis=1)
    acc[:span] += jnp.dot(own_ref[...], weights, preferred_element_type=jnp.float32)
    acc[span:] += jnp.dot(outer_ref[0], weights, preferred_element_type=jnp.float32)
    if mode == "last":

        @pl.when(k == pl.num_programs(0) - 1)
        def _():
            bias = jnp.concatenate([kb_ref[...], vb_ref[...]], axis=1).astype(jnp.float32)
            done = (acc[...] + bias).astype(jnp.bfloat16)
            own_at = pl.multiple_of(place[1] * span, span)
            outer_at = pl.multiple_of((1 - place[1]) * span, span)
            kv_ref[pl.ds(own_at, span), :] = done[:span]
            kv_ref[pl.ds(outer_at, span), :] = done[span:]


def project(mode, place, own, outer, key_weight, value_weight, before=None, biases=None):
    span = own.shape[0]
    depth = key_weight.shape[0]
    steps = depth // STEP
    columns = 2 * HD
    in_specs = [
        pl.BlockSpec((span, STEP), lambda k, place: (0, place[0] + k)),
        pl.BlockSpec((1, span, STEP), lambda k, place: (place[0] + k, 0, 0)),
        pl.BlockSpec((STEP, HD), lambda k, place: (k, 0)),
        pl.BlockSpec((STEP, HD), lambda k, place: (k, 0)),
    ]
    operands = [own, outer, key_weight, value_weight]
    whole = pl.BlockSpec((2 * span, columns), lambda k, place: (0, 0))
    if mode != "first":
        in_specs.append(whole)
        operands.append(before)
    out_shape = jax.ShapeDtypeStruct((2 * span, columns), jnp.float32)
    scratch = []
    if mode == "last":
        in_specs += [pl.BlockSpec((1, HD), lambda k, place: (0, 0))] * 2
        operands += biases
        out_shape = jax.ShapeDtypeStruct((2 * span, columns), jnp.bfloat16)
        scratch = [pltpu.VMEM((2 * span, columns), jnp.float32)]
    return pl.pallas_call(
        functools.partial(project_kernel, mode),
        grid_spec=pltpu.PrefetchScalarGridSpec(
            num_scalar_prefetch=1,
            grid=(steps,),
            in_specs=in_specs,
            out_specs=whole,
            scratch_shapes=scratch,
        ),
        out_shape=out_shape,
        compiler_params=pltpu.CompilerParams(
            vmem_limit_bytes=VMEM_LIMIT, dimension_semantics=("arbitrary",)
        ),
        cost_estimate=pl.CostEstimate(
            flops=4 * span * depth * columns,
            bytes_accessed=4 * span * depth + 2 * depth * columns + 8 * span * columns,
            transcendentals=0,
        ),
        name="project_" + mode,
    )(place, *operands)


INWARD = [(0, 1), (3, 2)]
ACROSS = [(1, 2), (2, 1)]
OUTWARD = [(1, 0), (2, 3)]


def line_of_four(hidden, key_weight, value_weight, key_bias, value_bias):
    index = lax.axis_index("pre")
    span, width = hidden.shape
    depth = key_weight.shape[0]
    share = width // lax.axis_size(("dec", "tp"))
    mine = lax.axis_index(("dec", "tp")) * share

    def send(x, pairs):
        return lax.ppermute(x, "pre", pairs)

    cut = lax.dynamic_slice_in_dim(hidden, mine, share, axis=1)
    cut = send(cut, INWARD)
    other = lax.all_gather(cut, ("dec", "tp"))
    half = depth // 2
    parts = [
        (key_weight[:half], value_weight[:half]),
        (key_weight[half:], value_weight[half:]),
    ]
    crossed = [send(key_weight, ACROSS), send(value_weight, ACROSS)]
    came, far = [], []
    for part in parts:
        got = [send(part[0], INWARD), send(part[1], INWARD)]
        came.append(got)
        far.append([send(got[0], ACROSS), send(got[1], ACROSS)])

    blocks = depth // STEP
    second = jnp.where(index < 2, 1, 0)
    facing = 3 - index

    def place(chunk, row=0):
        return jnp.stack([chunk * blocks + row // STEP, second]).astype(jnp.int32)

    acc = project("first", place(index), hidden, other, key_weight, value_weight)
    acc = project("middle", place(facing), hidden, other, crossed[0], crossed[1], acc)
    outer = jnp.bitwise_xor(index, 1)
    for i in range(2):
        acc = project("middle", place(outer, i * half), hidden, other, came[i][0], came[i][1], acc)
    distant = jnp.bitwise_xor(facing, 1)
    acc = project("middle", place(distant), hidden, other, far[0][0], far[0][1], acc)
    pair = project(
        "last",
        place(distant, half),
        hidden,
        other,
        far[1][0],
        far[1][1],
        acc,
        [key_bias[None, :], value_bias[None, :]],
    )
    facing_pair = send(pair, ACROSS)
    own_pair = send(pair, OUTWARD)
    far_pair = send(facing_pair, OUTWARD)
    low = jnp.where(
        index == 0, own_pair, jnp.where(index == 1, pair, jnp.where(index == 2, facing_pair, far_pair))
    )
    high = jnp.where(
        index == 3, own_pair, jnp.where(index == 2, pair, jnp.where(index == 1, facing_pair, far_pair))
    )
    return jnp.concatenate([low, high], axis=0)


def gathered(hidden, key_weight, value_weight, key_bias, value_bias):
    joined = jnp.concatenate([key_weight, value_weight], axis=1)
    joined = lax.all_gather(joined, "pre", axis=0, tiled=True)
    bias = jnp.concatenate([key_bias, value_bias]).astype(jnp.float32)
    local = jnp.dot(hidden, joined, preferred_element_type=jnp.float32) + bias
    return lax.all_gather(local.astype(jnp.bfloat16), "pre", axis=0, tiled=True)


def body(hidden, queries, key_weight, value_weight, key_bias, value_bias, segment_ids, page_owner):
    n_pre = lax.axis_size("pre")
    index = lax.axis_index("pre")
    span = hidden.shape[0]
    pages_dev = span // PAGE
    capacity = 2 * pages_dev // n_pre
    assert key_weight.shape[1] == HD

    owners = lax.all_gather(page_owner[:, 0], "pre")
    mine = (owners == index).astype(jnp.int32)
    rank = jnp.cumsum(mine, axis=1) - mine
    numbers = jnp.arange(n_pre * pages_dev, dtype=jnp.int32).reshape(n_pre, 1, pages_dev)
    wanted = (mine[:, None, :] == 1) & (
        rank[:, None, :] == jnp.arange(capacity, dtype=jnp.int32)[None, :, None]
    )
    slots = jnp.max(jnp.where(wanted, numbers, -1), axis=2).reshape(-1)

    own_segments = lax.dynamic_slice_in_dim(segment_ids, index * span, span)
    start = jnp.sum(
        (segment_ids[None, :] < own_segments[:, None]).astype(jnp.int32), axis=1, keepdims=True
    )
    info = jnp.stack([index, start[0, 0] // span]).astype(jnp.int32)

    project_all = line_of_four if n_pre == 4 else gathered
    kv = project_all(hidden, key_weight, value_weight, key_bias, value_bias)
    mixed, cache = attention(info, slots, queries, kv, start, n_pre, capacity)
    return (mixed, cache[None])


def solution(mesh):
    return jax.shard_map(
        body,
        mesh=mesh,
        in_specs=(
            P(("group", "pre"), None),
            P(("group", "pre"), ("dec", "tp")),
            P("pre", ("dec", "tp")),
            P("pre", ("dec", "tp")),
            P(("dec", "tp")),
            P(("dec", "tp")),
            P("group"),
            P(("group", "pre"), None),
        ),
        out_specs=(
            P(("group", "pre"), ("dec", "tp")),
            P(("group", "pre"), None, None, ("dec", "tp")),
        ),
        check_vma=False,
    )
```

time: 184 us -> 136 us (0.74)
  waiting for transfers between devices: 88.6 us -> 47.3 us
  Pallas kernels: 0 us -> 27.3 us
  matrix products: 24.3 us -> 0 us
  starting transfers between devices: 5.78 us -> 28.4 us
  blocking collectives: 29.4 us -> 6.99 us
  other arithmetic: 15.9 us -> 1.5 us
  between operations: 14.1 us -> 17 us
    all_gather x2 -> x1, waiting for transfers between devices: 87.3 us -> 1.47 us  [line_of_four(): other = lax.all_gather(cut, ('dec', 'tp'))]
    ppermute x0 -> x14, waiting for transfers between devices: none -> 45.8 us  [send(): return lax.ppermute(x, 'pre', pairs)]
    all_gather x2 -> x0, blocking collectives: 29.4 us -> none  [the longest x1 14.8 us: body(): lax.all_gather(key_local, 'pre', axis=0, tiled=True)]
    ppermute x0 -> x14, starting transfers between devices: none -> 28.3 us  [send(): return lax.ppermute(x, 'pre', pairs)]
    pallas_call x0 -> x7, Pallas kernels: none -> 27.3 us  [the longest x6 16.5 us: project(): pl.pallas_call(functools.partial(project_kernel, mode), grid_spec=pltpu.P...]
    dot_general x4 -> x0, matrix products: 24.3 us -> none  [the longest x1 9.33 us: attend(): jnp.einsum('lgij,jld->lgid', weights.astype(jnp.bfloat16), value_block, p...]
    reduce_sum x2 -> x1, other arithmetic: 11.8 us -> 0.39 us  [body(): jnp.sum((segment_ids[None, :] < own_segments[:, None]).astype(jnp.int32),...]
    unnamed x0 -> x1, blocking collectives: none -> 6.99 us
  transfers between devices with their start and end apart: 3 -> 15, of which waited for: 2 -> 7; matrix products, arithmetic and copies ran while one was open for 15% -> 3% of each run, Pallas kernels for 0% -> 10%
where the time goes in v1:
time: 136 us; the launch traced here: 134 us
  waiting for transfers between devices  47.3 us (35%)
  starting transfers between devices  28.4 us (21%)
  Pallas kernels  27.3 us (20%)
  between operations  17 us (12%)
  blocking collectives  6.99 us (5%)
  local copies, waits for them, and re-layouts  5.3 us (4%)
  other arithmetic  1.5 us (1%)
    ppermute x14, waiting for transfers between devices, send(): return lax.ppermute(x, 'pre', pairs)  45.8 us
    ppermute x14, starting transfers between devices, send(): return lax.ppermute(x, 'pre', pairs)  28.3 us
    pallas_call x6, Pallas kernels, project(): pl.pallas_call(functools.partial(project_kernel, mode), grid_spec=pltpu.P...  16.5 us
    pallas_call x1, Pallas kernels, attention(): pl.pallas_call(functools.partial(attention_kernel, heads, span), in_specs...  10.8 us
    unnamed x1, blocking collectives  6.99 us
  transfers between devices with their start and end apart: 15, of which 7 were waited for; matrix products, arithmetic and copies ran while one was open for 3% of the time, Pallas kernels for 10%

profile of v1, /device:TPU:16, one launch (start us, length us, event | category | flops | bytes accessed | tf_op | source)
XLA Modules:
  0.0 133.7 jit_solution(16250866850712322493)
XLA Ops:
  7.3 1.3 constant_dynamic-slice_fusion
  8.5 1.3 collective-permute-start
  9.8 19.9 %collective-permute-done = bf16[384,1024]{1,0:T(8,128)(2,1)S(1)} collective-permute-done((bf16[384,1024]{1,0:T(8,128)(2,1)S(1)}, bf16[384,1024]{1,0:T(8,128)(2,1)S(1)}, u32[]{:S(2)}, u32[]{:S(2)}) %collective-permute-start) | collective-permute-done | bytes 786464 | tf_op jit(solution)/shard_map/ppermute | solution.py:198
  29.7 0.9 copy-done.5
  30.6 2.4 %collective-permute-start.10 = (bf16[2048,128]{1,0:T(8,128)(2,1)S(1)}, bf16[2048,128]{1,0:T(8,128)(2,1)S(1)}, u32[]{:S(2)}, u32[]{:S(2)}) collective-permute-start(bf16[2048,128]{1,0:T(8,128)(2,1)S(1)} %copy-done), channel_id=1, source_target_pairs={{8,16},{16,8},{9,17},{17,9},{10,18},{18,10},{11,19},{19,11},{12,20... | collective-permute-start | bytes 1572872 | tf_op jit(solution)/shard_map/ppermute | solution.py:198
  33.0 3.5 %collective-permute-start.9 = (bf16[2048,128]{1,0:T(8,128)(2,1)S(1)}, bf16[2048,128]{1,0:T(8,128)(2,1)S(1)}, u32[]{:S(2)}, u32[]{:S(2)}) collective-permute-start(bf16[2048,128]{1,0:T(8,128)(2,1)S(1)} %copy-done.1), channel_id=1, source_target_pairs={{8,16},{16,8},{9,17},{17,9},{10,18},{18,10},{11,19},{19,11},{12,20... | collective-permute-start | bytes 1572872 | tf_op jit(solution)/shard_map/ppermute | solution.py:198
  36.5 0.7 fusion.2
  37.2 1.3 collective-permute-start.5
  38.5 0.7 fusion.1
  39.3 1.3 collective-permute-start.7
  40.5 1.3 collective-permute-start.1
  41.9 0.6 dynamic-slice
  43.0 0.1 bitcast_dynamic-update-slice_fusion
  43.1 0.1 pad_add_fusion.6.place
  43.3 5.1 %collective-permute-done.5.kw_ref = bf16[1024,128]{1,0:T(8,128)(2,1)S(1)} collective-permute-done((bf16[1024,128]{1,0:T(8,128)(2,1)S(1)}, bf16[1024,128]{1,0:T(8,128)(2,1)S(1)}, u32[]{:S(2)}, u32[]{:S(2)}) %collective-permute-start.5) | collective-permute-done | bytes 262176 | tf_op jit(solution)/shard_map/ppermute | solution.py:198
  48.3 1.3 collective-permute-start.3
  49.6 0.1 pad_add_fusion.4.place
  49.8 4.2 %collective-permute-done.7.vw_ref = bf16[1024,128]{1,0:T(8,128)(2,1)S(1)} collective-permute-done((bf16[1024,128]{1,0:T(8,128)(2,1)S(1)}, bf16[1024,128]{1,0:T(8,128)(2,1)S(1)}, u32[]{:S(2)}, u32[]{:S(2)}) %collective-permute-start.7) | collective-permute-done | bytes 262176 | tf_op jit(solution)/shard_map/ppermute | solution.py:198
  54.0 2.3 %collective-permute-start.6 = (bf16[1024,128]{1,0:T(8,128)(2,1)S(1)}, bf16[1024,128]{1,0:T(8,128)(2,1)S(1)}, u32[]{:S(2)}, u32[]{:S(2)}) collective-permute-start(bf16[1024,128]{1,0:T(8,128)(2,1)S(1)} %collective-permute-done.5.kw_ref), channel_id=1, source_target_pairs={{8,16},{16,8},{9,17},{17,9},{10,18},{18,10},{11,19},{19,11},{12,20... | collective-permute-start | bytes 786440 | tf_op jit(solution)/shard_map/ppermute | solution.py:198
  56.3 3.3 %collective-permute-done.1.kw_ref = bf16[1024,128]{1,0:T(8,128)(2,1)S(1)} collective-permute-done((bf16[1024,128]{1,0:T(8,128)(2,1)}, bf16[1024,128]{1,0:T(8,128)(2,1)S(1)}, u32[]{:S(2)}, u32[]{:S(2)}) %collective-permute-start.1) | collective-permute-done | bytes 262176 | tf_op jit(solution)/shard_map/ppermute | solution.py:198
  59.6 2.3 %collective-permute-start.8 = (bf16[1024,128]{1,0:T(8,128)(2,1)S(1)}, bf16[1024,128]{1,0:T(8,128)(2,1)}, u32[]{:S(2)}, u32[]{:S(2)}) collective-permute-start(bf16[1024,128]{1,0:T(8,128)(2,1)S(1)} %collective-permute-done.7.vw_ref), channel_id=1, source_target_pairs={{8,16},{16,8},{9,17},{17,9},{10,18},{18,10},{11,19},{19,11},{12,20... | collective-permute-start | bytes 786440 | tf_op jit(solution)/shard_map/ppermute | solution.py:198
  61.9 0.1 pad_add_fusion.3.place
  62.0 7.0 %all-reduce = s32[96]{0:T(128)S(1)} all-reduce(s32[96]{0:T(128)S(1)} %bitcast_dynamic-update-slice_fusion), channel_id=2, replica_groups=mesh['group'=1,'pre'=4,'dec'=4,'tp'=2] {'pre'}, use_global_device_ids=true, to_apply=%add | all-reduce | flops 96 | bytes 768
  69.0 2.3 %collective-permute-start.2 = (bf16[1024,128]{1,0:T(8,128)(2,1)S(1)}, bf16[1024,128]{1,0:T(8,128)(2,1)}, u32[]{:S(2)}, u32[]{:S(2)}) collective-permute-start(bf16[1024,128]{1,0:T(8,128)(2,1)S(1)} %collective-permute-done.1.kw_ref), channel_id=1, source_target_pairs={{8,16},{16,8},{9,17},{17,9},{10,18},{18,10},{11,19},{19,11},{12,20... | collective-permute-start | bytes 786440 | tf_op jit(solution)/shard_map/ppermute | solution.py:198
  71.4 3.5 %collective-permute-start.4 = (bf16[1024,128]{1,0:T(8,128)(2,1)S(1)}, bf16[1024,128]{1,0:T(8,128)(2,1)}, u32[]{:S(2)}, u32[]{:S(2)}) collective-permute-start(bf16[1024,128]{1,0:T(8,128)(2,1)S(1)} %collective-permute-done.3.vw_ref), channel_id=1, source_target_pairs={{8,16},{16,8},{9,17},{17,9},{10,18},{18,10},{11,19},{19,11},{12,20... | collective-permute-start | bytes 786440 | tf_op jit(solution)/shard_map/ppermute | solution.py:198
  74.9 1.5 %all-gather.4.cloned.1.call-done = bf16[3072,1024]{1,0:T(8,128)(2,1)} async-done(((bf16[384,1024]{1,0:T(8,128)(2,1)}), bf16[3072,1024]{1,0:T(8,128)(2,1)}) %all-gather.4.cloned.1.call-update) | async-done | bytes 6291472 | tf_op jit(solution)/shard_map/all_gather | solution.py:202
  76.3 3.2 %project_first.1.rest_0_ = f32[768,256]{1,0:T(8,128)S(1)} custom-call(s32[2]{0:T(128)S(1)} %pad_add_fusion.6.place, bf16[384,8192]{1,0:T(8,128)(2,1)} %own_ref.11, bf16[8,384,1024]{2,1,0:T(8,128)(2,1)} %bitcast.20, bf16[2048,128]{1,0:T(8,128)(2,1)S(1)} %copy-done.1, bf16[2048,128]{1,0:T(8,128)(2,1)S(1)} %copy-done), custom_call_target="tpu_custom_call" | custom-call | flops 805306368 | bytes 4980736 | tf_op jit(solution)/shard_map/project_first/pallas_call | solution.py:163
  79.5 3.2 %project_middle.4.rest_0_ = f32[768,256]{1,0:T(8,128)S(1)} custom-call(s32[2]{0:T(128)S(1)} %pad_add_fusion.5.place, bf16[384,8192]{1,0:T(8,128)(2,1)} %own_ref.11, bf16[8,384,1024]{2,1,0:T(8,128)(2,1)} %bitcast.21, bf16[2048,128]{1,0:T(8,128)(2,1)S(1)} %collective-permute-done.9.kw_ref, bf16[2048,128]{1,0:T(8,128)(2,1)S(1)} %collective-permute-done.10.vw_ref, ...), custom_call_target="tpu_custom_call" | custom-call | flops 805306368 | bytes 4980736 | tf_op jit(solution)/shard_map/project_middle/pallas_call | solution.py:163
  82.7 2.5 %project_middle.5.rest_0_ = f32[768,256]{1,0:T(8,128)S(1)} custom-call(s32[2]{0:T(128)S(1)} %pad_add_fusion.4.place, bf16[384,8192]{1,0:T(8,128)(2,1)} %own_ref.11, bf16[8,384,1024]{2,1,0:T(8,128)(2,1)} %bitcast.22, bf16[1024,128]{1,0:T(8,128)(2,1)S(1)} %collective-permute-done.5.kw_ref, bf16[1024,128]{1,0:T(8,128)(2,1)S(1)} %collective-permute-done.7.vw_ref, ...), custom_call_target="tpu_custom_call" | custom-call | flops 402653184 | bytes 2883584 | tf_op jit(solution)/shard_map/project_middle/pallas_call | solution.py:163
  85.2 2.5 %project_middle.6.rest_0_ = f32[768,256]{1,0:T(8,128)S(1)} custom-call(s32[2]{0:T(128)S(1)} %pad_add_fusion.3.place, bf16[384,8192]{1,0:T(8,128)(2,1)} %own_ref.11, bf16[8,384,1024]{2,1,0:T(8,128)(2,1)} %bitcast.23, bf16[1024,128]{1,0:T(8,128)(2,1)S(1)} %collective-permute-done.1.kw_ref, bf16[1024,128]{1,0:T(8,128)(2,1)S(1)} %collective-permute-done.3.vw_ref, ...), custom_call_target="tpu_custom_call" | custom-call | flops 402653184 | bytes 2883584 | tf_op jit(solution)/shard_map/project_middle/pallas_call | solution.py:163
  87.7 2.5 %project_middle.7.rest_0_ = f32[768,256]{1,0:T(8,128)S(1)} custom-call(s32[2]{0:T(128)S(1)} %get-tuple-element.13.place, bf16[384,8192]{1,0:T(8,128)(2,1)} %own_ref.11, bf16[8,384,1024]{2,1,0:T(8,128)(2,1)} %bitcast.24, bf16[1024,128]{1,0:T(8,128)(2,1)S(1)} %collective-permute-done.6.kw_ref, bf16[1024,128]{1,0:T(8,128)(2,1)} %collective-permute-done.8.vw_ref, ...), custom_call_target="tpu_custom_call" | custom-call | flops 402653184 | bytes 2883584 | tf_op jit(solution)/shard_map/project_middle/pallas_call | solution.py:163
  90.4 2.6 %project_last.1 = bf16[768,256]{1,0:T(8,128)(2,1)S(1)} custom-call(s32[2]{0:T(128)S(1)} %get-tuple-element.12.place, bf16[384,8192]{1,0:T(8,128)(2,1)} %own_ref.11, bf16[8,384,1024]{2,1,0:T(8,128)(2,1)} %bitcast.25, bf16[1024,128]{1,0:T(8,128)(2,1)} %collective-permute-done.2.kw_ref, bf16[1024,128]{1,0:T(8,128)(2,1)} %collective-permute-done.4.vw_ref, ...), custom_call_target="tpu_custom_call" | custom-call | flops 402653184 | bytes 2883584 | tf_op jit(solution)/shard_map/project_last/pallas_call | solution.py:163
  93.0 2.6 %collective-permute-start.12 = (bf16[768,256]{1,0:T(8,128)(2,1)S(1)}, bf16[768,256]{1,0:T(8,128)(2,1)S(1)}, u32[]{:S(2)}, u32[]{:S(2)}) collective-permute-start(bf16[768,256]{1,0:T(8,128)(2,1)S(1)} %project_last.1), channel_id=1, source_target_pairs={{8,16},{16,8},{9,17},{17,9},{10,18},{18,10},{11,19},{19,11},{12,20... | collective-permute-start | bytes 1179656 | tf_op jit(solution)/shard_map/ppermute | solution.py:198
  95.6 0.1 reshape.52
  95.7 0.1 dynamic_slice.6
  95.8 1.6 %collective-permute-start.11 = (bf16[768,256]{1,0:T(8,128)(2,1)S(1)}, bf16[768,256]{1,0:T(8,128)(2,1)S(1)}, u32[]{:S(2)}, u32[]{:S(2)}) collective-permute-start(bf16[768,256]{1,0:T(8,128)(2,1)S(1)} %project_last.1), channel_id=1, source_target_pairs={{8,0},{16,24},{9,1},{17,25},{10,2},{18,26},{11,3},{19,27},{12,4},{... | collective-permute-start | bytes 1179656 | tf_op jit(solution)/shard_map/ppermute | solution.py:198
  97.4 8.9 %collective-permute-done.12 = bf16[768,256]{1,0:T(8,128)(2,1)S(1)} collective-permute-done((bf16[768,256]{1,0:T(8,128)(2,1)S(1)}, bf16[768,256]{1,0:T(8,128)(2,1)S(1)}, u32[]{:S(2)}, u32[]{:S(2)}) %collective-permute-start.12) | collective-permute-done | bytes 393248 | tf_op jit(solution)/shard_map/ppermute | solution.py:198
  106.3 1.3 collective-permute-start.13
  107.6 0.4 convert_reduce_fusion
  108.0 0.5 slice.16
  110.5 0.2 reduce_window_sum.11
  110.7 0.1 broadcast_in_dim.35.start_ref
  110.8 0.3 select_reduce_fusion
  111.1 0.1 copy.11
  111.2 0.1 reshape.47.slots
  111.4 4.5 %collective-permute-done.13 = bf16[768,256]{1,0:T(8,128)(2,1)S(1)} collective-permute-done((bf16[768,256]{1,0:T(8,128)(2,1)S(1)}, bf16[768,256]{1,0:T(8,128)(2,1)S(1)}, u32[]{:S(2)}, u32[]{:S(2)}) %collective-permute-start.13) | collective-permute-done | bytes 393248 | tf_op jit(solution)/shard_map/ppermute | solution.py:198
  115.8 0.1 select_select_fusion.1
  116.0 10.8 %attention.1 = (bf16[384,1024]{1,0:T(8,128)(2,1)}, bf16[4,192,256]{2,1,0:T(8,128)(2,1)}) custom-call(s32[2]{0:T(128)S(1)} %pad_add_fusion.info, s32[48]{0:T(128)S(1)} %reshape.47.slots, bf16[384,1024]{1,0:T(8,128)(2,1)S(1)} %copy-done.4, bf16[1536,256]{1,0:T(8,128)(2,1)S(1)} %pad_maximum_fusion.kv_ref, s32[384,1]{1,0:T(8,128)S(1)} %broadcast_in_dim.35.start_ref), custom_call_target="tpu_custom_call" | custom-call | flops 2415919104 | bytes 3145728 | tf_op jit(solution)/shard_map/attention/pallas_call | solution.py:77
  (36 shorter events, 0.4 us)
Async XLA Ops:
  7.2 34.7 %copy-start.8 = (u32[32]{0:T(128)S(1)}, u32[32]{0:T(128)}, u32[]{:S(2)}) copy-start(u32[32]{0:T(128)} %constant.54) | copy-start | bytes 388
  7.2 23.4 %copy-start = (bf16[2048,128]{1,0:T(8,128)(2,1)S(1)}, bf16[2048,128]{1,0:T(8,128)(2,1)}, u32[]{:S(2)}) copy-start(bf16[2048,128]{1,0:T(8,128)(2,1)} %vw_ref.1) | copy-start | bytes 1572868
  7.2 25.8 %copy-start.1 = (bf16[2048,128]{1,0:T(8,128)(2,1)S(1)}, bf16[2048,128]{1,0:T(8,128)(2,1)}, u32[]{:S(2)}) copy-start(bf16[2048,128]{1,0:T(8,128)(2,1)} %kw_ref.1) | copy-start | bytes 1572868
  7.2 35.8 %copy-start.7 = (s32[24,1]{0,1:T(1,128)S(1)}, s32[24,1]{0,1:T(1,128)}, u32[]{:S(2)}) copy-start(s32[24,1]{0,1:T(1,128)} %param.15) | copy-start | bytes 292
  7.2 69.1 %all-gather.4.cloned.1.call-start = ((), (), s32[]{:S(2)}) async-start(), calls=%async_computation | async-start | bytes 7077888 | tf_op jit(solution)/shard_map/all_gather | solution.py:202
  8.5 21.2 %collective-permute-start = (bf16[384,1024]{1,0:T(8,128)(2,1)S(1)}, bf16[384,1024]{1,0:T(8,128)(2,1)S(1)}, u32[]{:S(2)}, u32[]{:S(2)}) collective-permute-start(bf16[384,1024]{1,0:T(8,128)(2,1)S(1)} %constant_dynamic-slice_fusion), channel_id=1, source_target_pairs={{0,8},{24,16},{1,9},{25,17},{2,10},{26,18},{3,11},{27,19},{4,12},{... | collective-permute-start | bytes 2359304 | tf_op jit(solution)/shard_map/ppermute | solution.py:198
  29.7 0.9 copy-start.5
  30.6 40.8 %collective-permute-start.10 = (bf16[2048,128]{1,0:T(8,128)(2,1)S(1)}, bf16[2048,128]{1,0:T(8,128)(2,1)S(1)}, u32[]{:S(2)}, u32[]{:S(2)}) collective-permute-start(bf16[2048,128]{1,0:T(8,128)(2,1)S(1)} %copy-done), channel_id=1, source_target_pairs={{8,16},{16,8},{9,17},{17,9},{10,18},{18,10},{11,19},{19,11},{12,20... | collective-permute-start | bytes 1572872 | tf_op jit(solution)/shard_map/ppermute | solution.py:198
  33.0 46.5 %collective-permute-start.9 = (bf16[2048,128]{1,0:T(8,128)(2,1)S(1)}, bf16[2048,128]{1,0:T(8,128)(2,1)S(1)}, u32[]{:S(2)}, u32[]{:S(2)}) collective-permute-start(bf16[2048,128]{1,0:T(8,128)(2,1)S(1)} %copy-done.1), channel_id=1, source_target_pairs={{8,16},{16,8},{9,17},{17,9},{10,18},{18,10},{11,19},{19,11},{12,20... | collective-permute-start | bytes 1572872 | tf_op jit(solution)/shard_map/ppermute | solution.py:198
  37.2 11.1 %collective-permute-start.5 = (bf16[1024,128]{1,0:T(8,128)(2,1)S(1)}, bf16[1024,128]{1,0:T(8,128)(2,1)S(1)}, u32[]{:S(2)}, u32[]{:S(2)}) collective-permute-start(bf16[1024,128]{1,0:T(8,128)(2,1)S(1)} %get-tuple-element.10), channel_id=1, source_target_pairs={{0,8},{24,16},{1,9},{25,17},{2,10},{26,18},{3,11},{27,19},{4,12},{... | collective-permute-start | bytes 786440 | tf_op jit(solution)/shard_map/ppermute | solution.py:198
  39.3 14.7 %collective-permute-start.7 = (bf16[1024,128]{1,0:T(8,128)(2,1)S(1)}, bf16[1024,128]{1,0:T(8,128)(2,1)S(1)}, u32[]{:S(2)}, u32[]{:S(2)}) collective-permute-start(bf16[1024,128]{1,0:T(8,128)(2,1)S(1)} %get-tuple-element.8), channel_id=1, source_target_pairs={{0,8},{24,16},{1,9},{25,17},{2,10},{26,18},{3,11},{27,19},{4,12},{... | collective-permute-start | bytes 786440 | tf_op jit(solution)/shard_map/ppermute | solution.py:198
  40.5 19.0 %collective-permute-start.1 = (bf16[1024,128]{1,0:T(8,128)(2,1)}, bf16[1024,128]{1,0:T(8,128)(2,1)S(1)}, u32[]{:S(2)}, u32[]{:S(2)}) collective-permute-start(bf16[1024,128]{1,0:T(8,128)(2,1)} %get-tuple-element.11), channel_id=1, source_target_pairs={{0,8},{24,16},{1,9},{25,17},{2,10},{26,18},{3,11},{27,19},{4,12},{... | collective-permute-start | bytes 786440 | tf_op jit(solution)/shard_map/ppermute | solution.py:198
  48.3 20.7 %collective-permute-start.3 = (bf16[1024,128]{1,0:T(8,128)(2,1)}, bf16[1024,128]{1,0:T(8,128)(2,1)S(1)}, u32[]{:S(2)}, u32[]{:S(2)}) collective-permute-start(bf16[1024,128]{1,0:T(8,128)(2,1)} %get-tuple-element.9), channel_id=1, source_target_pairs={{0,8},{24,16},{1,9},{25,17},{2,10},{26,18},{3,11},{27,19},{4,12},{... | collective-permute-start | bytes 786440 | tf_op jit(solution)/shard_map/ppermute | solution.py:198
  54.0 33.7 %collective-permute-start.6 = (bf16[1024,128]{1,0:T(8,128)(2,1)S(1)}, bf16[1024,128]{1,0:T(8,128)(2,1)S(1)}, u32[]{:S(2)}, u32[]{:S(2)}) collective-permute-start(bf16[1024,128]{1,0:T(8,128)(2,1)S(1)} %collective-permute-done.5.kw_ref), channel_id=1, source_target_pairs={{8,16},{16,8},{9,17},{17,9},{10,18},{18,10},{11,19},{19,11},{12,20... | collective-permute-start | bytes 786440 | tf_op jit(solution)/shard_map/ppermute | solution.py:198
  59.6 28.1 %collective-permute-start.8 = (bf16[1024,128]{1,0:T(8,128)(2,1)S(1)}, bf16[1024,128]{1,0:T(8,128)(2,1)}, u32[]{:S(2)}, u32[]{:S(2)}) collective-permute-start(bf16[1024,128]{1,0:T(8,128)(2,1)S(1)} %collective-permute-done.7.vw_ref), channel_id=1, source_target_pairs={{8,16},{16,8},{9,17},{17,9},{10,18},{18,10},{11,19},{19,11},{12,20... | collective-permute-start | bytes 786440 | tf_op jit(solution)/shard_map/ppermute | solution.py:198
  69.0 21.3 %collective-permute-start.2 = (bf16[1024,128]{1,0:T(8,128)(2,1)S(1)}, bf16[1024,128]{1,0:T(8,128)(2,1)}, u32[]{:S(2)}, u32[]{:S(2)}) collective-permute-start(bf16[1024,128]{1,0:T(8,128)(2,1)S(1)} %collective-permute-done.1.kw_ref), channel_id=1, source_target_pairs={{8,16},{16,8},{9,17},{17,9},{10,18},{18,10},{11,19},{19,11},{12,20... | collective-permute-start | bytes 786440 | tf_op jit(solution)/shard_map/ppermute | solution.py:198
  71.4 18.9 %collective-permute-start.4 = (bf16[1024,128]{1,0:T(8,128)(2,1)S(1)}, bf16[1024,128]{1,0:T(8,128)(2,1)}, u32[]{:S(2)}, u32[]{:S(2)}) collective-permute-start(bf16[1024,128]{1,0:T(8,128)(2,1)S(1)} %collective-permute-done.3.vw_ref), channel_id=1, source_target_pairs={{8,16},{16,8},{9,17},{17,9},{10,18},{18,10},{11,19},{19,11},{12,20... | collective-permute-start | bytes 786440 | tf_op jit(solution)/shard_map/ppermute | solution.py:198
  87.7 2.6 %copy-start.2 = (bf16[128]{0:T(256)(128)(2,1)S(1)}, bf16[128]{0:T(256)(128)(2,1)}, u32[]{:S(2)}) copy-start(bf16[128]{0:T(256)(128)(2,1)} %param.12) | copy-start | bytes 772
  87.7 2.6 %copy-start.3 = (bf16[128]{0:T(256)(128)(2,1)S(1)}, bf16[128]{0:T(256)(128)(2,1)}, u32[]{:S(2)}) copy-start(bf16[128]{0:T(256)(128)(2,1)} %param.13) | copy-start | bytes 772
  90.3 5.4 %copy-start.6 = (s32[1536]{0:T(1024)S(1)}, s32[1536]{0:T(1024)}, u32[]{:S(2)}) copy-start(s32[1536]{0:T(1024)} %param.14) | copy-start | bytes 18436
  93.0 23.0 %copy-start.4 = (bf16[384,1024]{1,0:T(8,128)(2,1)S(1)}, bf16[384,1024]{1,0:T(8,128)(2,1)}, u32[]{:S(2)}) copy-start(bf16[384,1024]{1,0:T(8,128)(2,1)} %q_ref.1) | copy-start | bytes 2359300
  93.0 13.3 %collective-permute-start.12 = (bf16[768,256]{1,0:T(8,128)(2,1)S(1)}, bf16[768,256]{1,0:T(8,128)(2,1)S(1)}, u32[]{:S(2)}, u32[]{:S(2)}) collective-permute-start(bf16[768,256]{1,0:T(8,128)(2,1)S(1)} %project_last.1), channel_id=1, source_target_pairs={{8,16},{16,8},{9,17},{17,9},{10,18},{18,10},{11,19},{19,11},{12,20... | collective-permute-start | bytes 1179656 | tf_op jit(solution)/shard_map/ppermute | solution.py:198
  95.8 15.6 %collective-permute-start.11 = (bf16[768,256]{1,0:T(8,128)(2,1)S(1)}, bf16[768,256]{1,0:T(8,128)(2,1)S(1)}, u32[]{:S(2)}, u32[]{:S(2)}) collective-permute-start(bf16[768,256]{1,0:T(8,128)(2,1)S(1)} %project_last.1), channel_id=1, source_target_pairs={{8,0},{16,24},{9,1},{17,25},{10,2},{18,26},{11,3},{19,27},{12,4},{... | collective-permute-start | bytes 1179656 | tf_op jit(solution)/shard_map/ppermute | solution.py:198
  106.3 9.5 %collective-permute-start.13 = (bf16[768,256]{1,0:T(8,128)(2,1)S(1)}, bf16[768,256]{1,0:T(8,128)(2,1)S(1)}, u32[]{:S(2)}, u32[]{:S(2)}) collective-permute-start(bf16[768,256]{1,0:T(8,128)(2,1)S(1)} %collective-permute-done.12), channel_id=1, source_target_pairs={{8,0},{16,24},{9,1},{17,25},{10,2},{18,26},{11,3},{19,27},{12,4},{... | collective-permute-start | bytes 1179656 | tf_op jit(solution)/shard_map/ppermute | solution.py:198
Sparse Core Ops, SparseCore 0:
  30.7 45.5 all-gather.3

commit v2 on v1

v2 whole, which is shorter than its diff:
```python
import functools
import math

import jax
import jax.numpy as jnp
from jax import lax
from jax.experimental import pallas as pl
from jax.experimental.pallas import tpu as pltpu
from jax.sharding import PartitionSpec as P

HD = 128
PAGE = 16
NEG = -1e30
VMEM_LIMIT = 48 * 1024 * 1024


def attention_kernel(heads, span, info, slots, q_ref, k_ref, v_ref, start_ref, out_ref, cache_ref, acc, top):
    index = info[0]
    first = info[1]
    factor = HD**-0.5 * math.log2(math.e)
    columns = lax.broadcasted_iota(jnp.int32, (span, span), 1)
    rows = lax.broadcasted_iota(jnp.int32, (span, span), 0)

    def block(j, diagonal):
        at = pl.multiple_of(j * span, span)
        keys = k_ref[pl.ds(at, span), :]
        values = jnp.concatenate(
            [v_ref[pl.ds(at, span), :], jnp.ones((span, HD), jnp.bfloat16)], axis=1
        )
        allowed = columns >= start_ref[...] - at
        if diagonal:
            allowed = allowed & (columns <= rows)
        for g in range(heads):
            scores = lax.dot_general(
                q_ref[:, g * HD : (g + 1) * HD],
                keys,
                (((1,), (1,)), ((), ())),
                preferred_element_type=jnp.float32,
            )
            scores = jnp.where(allowed, scores, NEG)
            peak = jnp.max(scores, axis=1, keepdims=True)
            if not diagonal:
                before = top[g]
                peak = jnp.maximum(peak, before)
            weights = jnp.exp2(scores * factor - peak * factor).astype(jnp.bfloat16)
            mixed = jnp.dot(weights, values, preferred_element_type=jnp.float32)
            if not diagonal:
                mixed = mixed + acc[g] * jnp.exp2((before - peak) * factor)
            top[g] = peak
            acc[g] = mixed

    block(index, True)

    @pl.loop(first, index)
    def _(j):
        block(j, False)

    for g in range(heads):
        mixed = acc[g]
        out_ref[:, g * HD : (g + 1) * HD] = (mixed[:, :HD] / mixed[:, HD:]).astype(out_ref.dtype)

    pick_pages(slots, k_ref, v_ref, cache_ref)


def attention(info, slots, queries, keys, values, start, n_pre, capacity):
    span = queries.shape[0]
    heads = queries.shape[1] // HD
    return pl.pallas_call(
        functools.partial(attention_kernel, heads, span),
        in_specs=[
            pl.BlockSpec(memory_space=pltpu.SMEM),
            pl.BlockSpec(memory_space=pltpu.SMEM),
            pl.BlockSpec(memory_space=pltpu.VMEM),
            pl.BlockSpec(memory_space=pltpu.VMEM),
            pl.BlockSpec(memory_space=pltpu.VMEM),
            pl.BlockSpec(memory_space=pltpu.VMEM),
        ],
        out_specs=[
            pl.BlockSpec(memory_space=pltpu.VMEM),
            pl.BlockSpec(memory_space=pltpu.VMEM),
        ],
        out_shape=[
            jax.ShapeDtypeStruct(queries.shape, jnp.bfloat16),
            jax.ShapeDtypeStruct((n_pre, capacity * PAGE, 2 * HD), jnp.bfloat16),
        ],
        scratch_shapes=[
            pltpu.VMEM((heads, span, 2 * HD), jnp.float32),
            pltpu.VMEM((heads, span, 1), jnp.float32),
        ],
        compiler_params=pltpu.CompilerParams(vmem_limit_bytes=VMEM_LIMIT),
        cost_estimate=pl.CostEstimate(
            flops=4 * heads * span * span * n_pre * HD,
            bytes_accessed=4 * queries.size * 2,
            transcendentals=heads * span * span * n_pre,
        ),
        name="attention",
    )(info, slots, queries, keys, values, start)


STEP = 1024


def near_kernel(place, own_ref, kw_ref, vw_ref, kx_ref, vx_ref, out_ref):
    k = pl.program_id(0)

    @pl.when(k == 0)
    def _():
        out_ref[...] = jnp.zeros_like(out_ref)

    def add(key_ref, value_ref):
        weight = jnp.concatenate([key_ref[...], value_ref[...]], axis=1)
        out_ref[...] += jnp.dot(own_ref[...], weight, preferred_element_type=jnp.float32)

    @pl.when(k < pl.num_programs(0) // 2)
    def _():
        add(kw_ref, vw_ref)

    @pl.when(k >= pl.num_programs(0) // 2)
    def _():
        add(kx_ref, vx_ref)


def facing_kernel(place, own_ref, other_ref, kw_ref, vw_ref, out_ref):
    k = pl.program_id(0)
    span = own_ref.shape[0]
    share = other_ref.shape[3]

    @pl.when(k == 0)
    def _():
        out_ref[...] = jnp.zeros_like(out_ref)

    weight = jnp.concatenate([kw_ref[...], vw_ref[...]], axis=1)
    other = jnp.concatenate([other_ref[i, 0] for i in range(STEP // share)], axis=1)
    out_ref[:span] += jnp.dot(own_ref[...], weight, preferred_element_type=jnp.float32)
    out_ref[span:] += jnp.dot(other, weight, preferred_element_type=jnp.float32)


def distant_kernel(
    place, own_ref, other_ref, w_ref, near_ref, outer_ref, facing_ref, bias_ref, out_ref, acc
):
    k = pl.program_id(0)
    span = own_ref.shape[0]
    share = other_ref.shape[3]

    @pl.when(k == 0)
    def _():
        bias = bias_ref[...].astype(jnp.float32)
        acc[:span] = near_ref[...] + facing_ref[:span] + bias
        acc[span:] = outer_ref[...] + facing_ref[span:] + bias

    weight = w_ref[...]
    other = jnp.concatenate([other_ref[i, 0] for i in range(STEP // share)], axis=1)
    acc[:span] += jnp.dot(own_ref[...], weight, preferred_element_type=jnp.float32)
    acc[span:] += jnp.dot(other, weight, preferred_element_type=jnp.float32)

    @pl.when(k == pl.num_programs(0) - 1)
    def _():
        own_at = pl.multiple_of(place[2] * span, span)
        outer_at = pl.multiple_of((1 - place[2]) * span, span)
        out_ref[pl.ds(own_at, span), :] = acc[:span].astype(jnp.bfloat16)
        out_ref[pl.ds(outer_at, span), :] = acc[span:].astype(jnp.bfloat16)


def call_project(kernel, name, place, operands, in_specs, steps, rows, columns, kind, scratch=()):
    return pl.pallas_call(
        kernel,
        grid_spec=pltpu.PrefetchScalarGridSpec(
            num_scalar_prefetch=1,
            grid=(steps,),
            in_specs=in_specs,
            out_specs=pl.BlockSpec((rows, columns), lambda k, place: (0, 0)),
            scratch_shapes=list(scratch),
        ),
        out_shape=jax.ShapeDtypeStruct((rows, columns), kind),
        compiler_params=pltpu.CompilerParams(
            vmem_limit_bytes=VMEM_LIMIT, dimension_semantics=("arbitrary",)
        ),
        cost_estimate=pl.CostEstimate(
            flops=2 * rows * STEP * steps * columns,
            bytes_accessed=2 * rows * STEP * steps + 2 * STEP * steps * columns,
            transcendentals=0,
        ),
        name=name,
    )(place, *operands)


def project_near(place, own, key_weight, value_weight, key_swapped, value_swapped):
    span = own.shape[0]
    steps = key_weight.shape[0] // STEP
    first = pl.BlockSpec((STEP, HD), lambda k, place: (jnp.minimum(k, steps - 1), 0))
    second = pl.BlockSpec((STEP, HD), lambda k, place: (jnp.maximum(k - steps, 0), 0))
    in_specs = [
        pl.BlockSpec((span, STEP), lambda k, place: (0, place[k // steps] + lax.rem(k, steps))),
        first,
        first,
        second,
        second,
    ]
    operands = [own, key_weight, value_weight, key_swapped, value_swapped]
    return call_project(
        near_kernel, "near", place, operands, in_specs, 2 * steps, span, 2 * HD, jnp.float32
    )


def far_specs(span, share):
    return [
        pl.BlockSpec((span, STEP), lambda k, place: (0, place[0] + k)),
        pl.BlockSpec((STEP // share, 1, span, share), lambda k, place: (0, place[1] + k, 0, 0)),
    ]


def project_facing(place, own, other, key_weight, value_weight):
    span = own.shape[0]
    weight = pl.BlockSpec((STEP, HD), lambda k, place: (k, 0))
    in_specs = far_specs(span, other.shape[3]) + [weight, weight]
    operands = [own, other, key_weight, value_weight]
    steps = key_weight.shape[0] // STEP
    return call_project(
        facing_kernel, "facing", place, operands, in_specs, steps, 2 * span, 2 * HD, jnp.float32
    )


def project_distant(place, column, own, other, weight, near, outer, facing, bias):
    span = own.shape[0]
    part = pl.BlockSpec((span, HD), lambda k, place: (0, column))
    in_specs = far_specs(span, other.shape[3]) + [
        pl.BlockSpec((STEP, HD), lambda k, place: (k, 0)),
        part,
        part,
        pl.BlockSpec((2 * span, HD), lambda k, place: (0, column)),
        pl.BlockSpec((1, HD), lambda k, place: (0, 0)),
    ]
    operands = [own, other, weight, near, outer, facing, bias]
    return call_project(
        distant_kernel,
        "distant",
        place,
        operands,
        in_specs,
        weight.shape[0] // STEP,
        2 * span,
        HD,
        jnp.bfloat16,
        [pltpu.VMEM((2 * span, HD), jnp.float32)],
    )


INWARD = [(0, 1), (3, 2)]
ACROSS = [(1, 2), (2, 1)]
OUTWARD = [(1, 0), (2, 3)]
SWAP = [(0, 1), (1, 0), (2, 3), (3, 2)]


def line_of_four(hidden, key_weight, value_weight, key_bias, value_bias, owners):
    index = lax.axis_index("pre")
    width = hidden.shape[1]
    blocks = key_weight.shape[0] // STEP
    share = width // 2 // lax.axis_size(("dec", "tp"))
    facing = 3 - index
    near = jnp.bitwise_xor(index, 1)
    distant = jnp.bitwise_xor(facing, 1)
    second = (index < 2).astype(jnp.int32)

    def send(x, pairs):
        return lax.ppermute(x, "pre", pairs)

    mine = second * (width // 2) + lax.axis_index(("dec", "tp")) * share
    cut = send(lax.dynamic_slice_in_dim(hidden, mine, share, axis=1), INWARD)
    key_facing = send(key_weight, ACROSS)
    cut, key_facing, owners = lax.optimization_barrier((cut, key_facing, owners))
    other = lax.all_gather(cut, "dec")
    value_facing = send(value_weight, ACROSS)
    key_swapped = send(key_weight, SWAP)
    other, value_facing, key_swapped = lax.optimization_barrier((other, value_facing, key_swapped))
    other = lax.all_gather(other, "tp")
    value_swapped = send(value_weight, SWAP)
    key_distant = send(key_swapped, ACROSS)
    value_distant = send(value_swapped, ACROSS)

    def place(chunk):
        return jnp.stack([chunk * blocks, lax.rem(chunk, 2) * blocks, second])

    at_near = jnp.stack([index * blocks, near * blocks])
    own_part = project_near(
        at_near, hidden, key_weight, value_weight, key_swapped, value_swapped
    )
    outer_part = send(own_part, INWARD)
    faced = project_facing(place(facing), hidden, other, key_facing, value_facing)

    def finish(column, weight, bias):
        pair = project_distant(
            place(distant), column, hidden, other, weight, own_part, outer_part, faced, bias[None, :]
        )
        across = send(pair, ACROSS)
        return pair, send(pair, OUTWARD), across, send(across, OUTWARD)

    keys = finish(0, key_distant, key_bias)
    values = finish(1, value_distant, value_bias)
    return keys, values, owners


def softmax_step(q, keys, values, allowed, before):
    factor = HD**-0.5 * math.log2(math.e)
    scores = lax.dot_general(q, keys, (((1,), (1,)), ((), ())), preferred_element_type=jnp.float32)
    scores = jnp.where(allowed, scores, NEG)
    peak = jnp.max(scores, axis=1, keepdims=True)
    if before is not None:
        peak = jnp.maximum(peak, before[0])
    weights = jnp.exp2(scores * factor - peak * factor).astype(jnp.bfloat16)
    mixed = jnp.dot(weights, values, preferred_element_type=jnp.float32)
    total, mixed = mixed[:, HD:], mixed[:, :HD]
    if before is not None:
        shrink = jnp.exp2((before[0] - peak) * factor)
        total = total + before[1] * shrink
        mixed = mixed + before[2] * shrink
    return peak, total, mixed


def with_ones(values):
    return jnp.concatenate([values, jnp.ones_like(values)], axis=1)


def own_kernel(heads, info, q_ref, start_ref, k_in, k_out, v_in, v_out, top, total, mix):
    span = q_ref.shape[0]
    index = info[0]
    inner = (index == 1) | (index == 2)
    keys = jnp.where(inner, k_in[...], k_out[...])
    values = with_ones(jnp.where(inner, v_in[...], v_out[...]))
    columns = lax.broadcasted_iota(jnp.int32, (span, 2 * span), 1)
    rows = lax.broadcasted_iota(jnp.int32, (span, 2 * span), 0)
    allowed = (columns <= rows + lax.rem(index, 2) * span) & (
        columns >= start_ref[...] - (index // 2) * 2 * span
    )
    for g in range(heads):
        q = q_ref[:, g * HD : (g + 1) * HD]
        peak, sums, mixed = softmax_step(q, keys, values, allowed, None)
        top[g] = peak
        total[g] = sums[:, :1]
        mix[g] = mixed


def far_kernel(
    heads,
    info,
    slots,
    q_ref,
    start_ref,
    k_in,
    k_out,
    k_across,
    k_far,
    v_in,
    v_out,
    v_across,
    v_far,
    top,
    total,
    mix,
    out_ref,
    cache_ref,
    held_k,
    held_v,
):
    span = q_ref.shape[0]
    index = info[0]
    inner = (index == 1) | (index == 2)
    own_at = pl.multiple_of((index // 2) * 2 * span, 2 * span)
    far_at = pl.multiple_of((1 - index // 2) * 2 * span, 2 * span)
    held_k[pl.ds(own_at, 2 * span), :] = jnp.where(inner, k_in[...], k_out[...])
    held_v[pl.ds(own_at, 2 * span), :] = jnp.where(inner, v_in[...], v_out[...])
    held_k[pl.ds(far_at, 2 * span), :] = jnp.where(inner, k_across[...], k_far[...])
    held_v[pl.ds(far_at, 2 * span), :] = jnp.where(inner, v_across[...], v_far[...])

    @pl.when((index < 2) | (info[1] >= 2))
    def _():
        for g in range(heads):
            out_ref[:, g * HD : (g + 1) * HD] = (mix[g] / total[g]).astype(out_ref.dtype)

    @pl.when((index >= 2) & (info[1] < 2))
    def _():
        keys = held_k[: 2 * span]
        values = with_ones(held_v[: 2 * span])
        columns = lax.broadcasted_iota(jnp.int32, (span, 2 * span), 1)
        allowed = columns >= start_ref[...]
        for g in range(heads):
            q = q_ref[:, g * HD : (g + 1) * HD]
            _, sums, mixed = softmax_step(q, keys, values, allowed, (top[g], total[g], mix[g]))
            out_ref[:, g * HD : (g + 1) * HD] = (mixed / sums).astype(out_ref.dtype)

    pick_pages(slots, held_k, held_v, cache_ref)


def pick_pages(slots, k_ref, v_ref, cache_ref):
    capacity = cache_ref.shape[1] // PAGE
    empty = jnp.zeros((PAGE, HD), cache_ref.dtype)
    for s in range(cache_ref.shape[0]):

        @pl.loop(0, capacity)
        def _(r):
            page = slots[s * capacity + r]
            token = pl.ds(pl.multiple_of(jnp.maximum(page, 0) * PAGE, PAGE), PAGE)
            row = pl.ds(pl.multiple_of(r * PAGE, PAGE), PAGE)
            cache_ref[s, row, :HD] = jnp.where(page >= 0, k_ref[token, :], empty)
            cache_ref[s, row, HD:] = jnp.where(page >= 0, v_ref[token, :], empty)


def attention_of_pairs(info, slots, queries, start, keys, values, capacity):
    span = queries.shape[0]
    heads = queries.shape[1] // HD
    smem = pl.BlockSpec(memory_space=pltpu.SMEM)
    vmem = pl.BlockSpec(memory_space=pltpu.VMEM)
    cost = pl.CostEstimate(
        flops=8 * heads * span * span * HD,
        bytes_accessed=4 * queries.size * 2,
        transcendentals=2 * heads * span * span,
    )
    params = pltpu.CompilerParams(vmem_limit_bytes=VMEM_LIMIT)
    state = pl.pallas_call(
        functools.partial(own_kernel, heads),
        in_specs=[smem] + [vmem] * 6,
        out_specs=[vmem] * 3,
        out_shape=[
            jax.ShapeDtypeStruct((heads, span, 1), jnp.float32),
            jax.ShapeDtypeStruct((heads, span, 1), jnp.float32),
            jax.ShapeDtypeStruct((heads, span, HD), jnp.float32),
        ],
        compiler_params=params,
        cost_estimate=cost,
        name="attend_own",
    )(info, queries, start, keys[0], keys[1], values[0], values[1])
    return pl.pallas_call(
        functools.partial(far_kernel, heads),
        in_specs=[smem, smem] + [vmem] * 13,
        out_specs=[vmem] * 2,
        out_shape=[
            jax.ShapeDtypeStruct(queries.shape, jnp.bfloat16),
            jax.ShapeDtypeStruct((4, capacity * PAGE, 2 * HD), jnp.bfloat16),
        ],
        scratch_shapes=[pltpu.VMEM((4 * span, HD), jnp.bfloat16)] * 2,
        compiler_params=params,
        cost_estimate=cost,
        name="attend_far",
    )(info, slots, queries, start, *keys, *values, *state)


def gathered(hidden, key_weight, value_weight, key_bias, value_bias):
    joined = jnp.concatenate([key_weight, value_weight], axis=1)
    joined = lax.all_gather(joined, "pre", axis=0, tiled=True)
    bias = jnp.concatenate([key_bias, value_bias]).astype(jnp.float32)
    local = jnp.dot(hidden, joined, preferred_element_type=jnp.float32) + bias
    both = lax.all_gather(local.astype(jnp.bfloat16), "pre", axis=0, tiled=True)
    return both[:, :HD], both[:, HD:]


def body(hidden, queries, key_weight, value_weight, key_bias, value_bias, segment_ids, page_owner):
    n_pre = lax.axis_size("pre")
    index = lax.axis_index("pre")
    span = hidden.shape[0]
    pages_dev = span // PAGE
    capacity = 2 * pages_dev // n_pre
    assert key_weight.shape[1] == HD

    own_segments = lax.dynamic_slice_in_dim(segment_ids, index * span, span)
    start = jnp.sum(
        (segment_ids[None, :] < own_segments[:, None]).astype(jnp.int32), axis=1, keepdims=True
    )
    info = jnp.stack([index, start[0, 0] // span]).astype(jnp.int32)
    owners = lax.all_to_all(
        jnp.broadcast_to(page_owner[:, 0], (n_pre, pages_dev)), "pre", 0, 0, tiled=True
    )
    arrays = (hidden, key_weight, value_weight, key_bias, value_bias)
    if n_pre == 4:
        keys, values, owners = line_of_four(*arrays, owners)
    else:
        keys, values = gathered(*arrays)

    mine = (owners == index).astype(jnp.int32)
    rank = jnp.cumsum(mine, axis=1) - mine
    numbers = jnp.arange(n_pre * pages_dev, dtype=jnp.int32).reshape(n_pre, 1, pages_dev)
    wanted = (mine[:, None, :] == 1) & (
        rank[:, None, :] == jnp.arange(capacity, dtype=jnp.int32)[None, :, None]
    )
    slots = jnp.max(jnp.where(wanted, numbers, -1), axis=2).reshape(-1)
    if n_pre == 4:
        mixed, cache = attention_of_pairs(info, slots, queries, start, keys, values, capacity)
    else:
        mixed, cache = attention(info, slots, queries, keys, values, start, n_pre, capacity)
    return (mixed, cache[None])


def solution(mesh):
    return jax.shard_map(
        body,
        mesh=mesh,
        in_specs=(
            P(("group", "pre"), None),
            P(("group", "pre"), ("dec", "tp")),
            P("pre", ("dec", "tp")),
            P("pre", ("dec", "tp")),
            P(("dec", "tp")),
            P(("dec", "tp")),
            P("group"),
            P(("group", "pre"), None),
        ),
        out_specs=(
            P(("group", "pre"), ("dec", "tp")),
            P(("group", "pre"), None, None, ("dec", "tp")),
        ),
        check_vma=False,
    )
```

time: 136 us -> 131 us (0.963)
  waiting for transfers between devices: 47.3 us -> 42.7 us
  blocking collectives: 6.99 us -> 11.5 us
  starting transfers between devices: 28.4 us -> 25.9 us
    ppermute x14, waiting for transfers between devices: 45.8 us -> 26.2 us  [send(): return lax.ppermute(x, 'pre', pairs)]
    all_gather x1 -> x2, waiting for transfers between devices: 1.47 us -> 16.5 us  [the longest x1 16.5 us: line_of_four(): other = lax.all_gather(cut, 'dec')]
    all_to_all x0 -> x1, blocking collectives: none -> 11.5 us  [body(): lax.all_to_all(jnp.broadcast_to(page_owner[:, 0], (n_pre, pages_dev)), 'p...]
    unnamed x1 -> x0, blocking collectives: 6.99 us -> none
    ppermute x14, starting transfers between devices: 28.3 us -> 25.9 us  [send(): return lax.ppermute(x, 'pre', pairs)]
    slice x2 -> x0, local copies, waits for them, and re-layouts: 1.48 us -> none  [the longest x1 0.74 us: line_of_four(): value_weight[:half]]
    pallas_call x7 -> x6, Pallas kernels: 27.3 us -> 27 us  [the longest x4 13.6 us: call_project(): pl.pallas_call(kernel, grid_spec=pltpu.PrefetchScalarGridSpec(num_scalar_...]
  transfers between devices with their start and end apart: 15 -> 16, of which waited for: 7 -> 6; matrix products, arithmetic and copies ran while one was open for 3% -> 3% of each run, Pallas kernels for 10% -> 15%
where the time goes in v2:
time: 131 us; the launch traced here: 130 us
  waiting for transfers between devices  42.7 us (33%)
  Pallas kernels  27 us (21%)
  starting transfers between devices  25.9 us (20%)
  between operations  16.3 us (12%)
  blocking collectives  11.5 us (9%)
  local copies, waits for them, and re-layouts  5.22 us (4%)
    ppermute x14, waiting for transfers between devices, send(): return lax.ppermute(x, 'pre', pairs)  26.2 us
    ppermute x14, starting transfers between devices, send(): return lax.ppermute(x, 'pre', pairs)  25.9 us
    all_gather x1, waiting for transfers between devices, line_of_four(): other = lax.all_gather(cut, 'dec')  16.5 us
    pallas_call x4, Pallas kernels, call_project(): pl.pallas_call(kernel, grid_spec=pltpu.PrefetchScalarGridSpec(num_scalar_...  13.6 us
    all_to_all x1, blocking collectives, body(): lax.all_to_all(jnp.broadcast_to(page_owner[:, 0], (n_pre, pages_dev)), 'p...  11.5 us
    pallas_call x1, Pallas kernels, attention_of_pairs(): pl.pallas_call(functools.partial(far_kernel, heads), in_specs=[smem, smem...  7.79 us
    pallas_call x1, Pallas kernels, attention_of_pairs(): pl.pallas_call(functools.partial(own_kernel, heads), in_specs=[smem] + [v...  5.64 us
    unnamed x18, local copies, waits for them, and re-layouts  2.67 us
  transfers between devices with their start and end apart: 16, of which 6 were waited for; matrix products, arithmetic and copies ran while one was open for 3% of the time, Pallas kernels for 15%

profile of v2, /device:TPU:16, one launch (start us, length us, event | category | flops | bytes accessed | tf_op | source)
XLA Modules:
  0.0 129.8 jit_solution(14511021743644267501)
XLA Ops:
  7.2 0.0 copy-start.3
  7.2 0.0 copy-start.4
  7.2 0.0 all-gather.5.cloned.1.call-start
  7.2 2.5 %collective-permute-start.1 = (bf16[2048,128]{1,0:T(8,128)(2,1)}, bf16[2048,128]{1,0:T(8,128)(2,1)S(1)}, u32[]{:S(2)}, u32[]{:S(2)}) collective-permute-start(bf16[2048,128]{1,0:T(8,128)(2,1)} %kw_ref.1), channel_id=1, source_target_pairs={{8,16},{16,8},{9,17},{17,9},{10,18},{18,10},{11,19},{19,11},{12,20... | collective-permute-start | bytes 1572872 | tf_op jit(solution)/shard_map/ppermute | solution.py:265
  9.8 1.0 constant_dynamic-slice_fusion
  10.8 1.3 collective-permute-start
  12.1 0.7 broadcast_in_dim.35
  12.7 11.5 %all_to_all.9 = s32[4,1,24]{2,1,0:T(1,128)S(1)} all-to-all(s32[4,1,24]{2,1,0:T(1,128)S(1)} %broadcast_in_dim.35), channel_id=1, replica_groups=mesh['group'=1,'pre'=4,'dec'=4,'tp'=2] {'pre'}, dimensions={0} | all-to-all | bytes 768 | tf_op jit(solution)/shard_map/all_to_all | solution.py:468
  24.3 0.7 copy-done.7
  25.0 0.0 all-gather.5.cloned.1.call-update
  25.0 0.0 all-gather.7.cloned.1.call-start
  25.1 1.5 %collective-permute-start.3 = (bf16[2048,128]{1,0:T(8,128)(2,1)}, bf16[2048,128]{1,0:T(8,128)(2,1)S(1)}, u32[]{:S(2)}, u32[]{:S(2)}) collective-permute-start(bf16[2048,128]{1,0:T(8,128)(2,1)} %kw_ref.1), channel_id=1, source_target_pairs={{0,8},{8,0},{16,24},{24,16},{1,9},{9,1},{17,25},{25,17},{2,10},{10... | collective-permute-start | bytes 1572872 | tf_op jit(solution)/shard_map/ppermute | solution.py:265
  26.6 2.3 %collective-permute-start.2 = (bf16[2048,128]{1,0:T(8,128)(2,1)}, bf16[2048,128]{1,0:T(8,128)(2,1)S(1)}, u32[]{:S(2)}, u32[]{:S(2)}) collective-permute-start(bf16[2048,128]{1,0:T(8,128)(2,1)} %vw_ref.1), channel_id=1, source_target_pairs={{8,16},{16,8},{9,17},{17,9},{10,18},{18,10},{11,19},{19,11},{12,20... | collective-permute-start | bytes 1572872 | tf_op jit(solution)/shard_map/ppermute | solution.py:265
  29.0 8.6 %collective-permute-done.3.kx_ref = bf16[2048,128]{1,0:T(8,128)(2,1)S(1)} collective-permute-done((bf16[2048,128]{1,0:T(8,128)(2,1)}, bf16[2048,128]{1,0:T(8,128)(2,1)S(1)}, u32[]{:S(2)}, u32[]{:S(2)}) %collective-permute-start.3) | collective-permute-done | bytes 524320 | tf_op jit(solution)/shard_map/ppermute | solution.py:265
  37.6 3.1 %collective-permute-done.2.vw_ref = bf16[2048,128]{1,0:T(8,128)(2,1)S(1)} collective-permute-done((bf16[2048,128]{1,0:T(8,128)(2,1)}, bf16[2048,128]{1,0:T(8,128)(2,1)S(1)}, u32[]{:S(2)}, u32[]{:S(2)}) %collective-permute-start.2) | collective-permute-done | bytes 524320 | tf_op jit(solution)/shard_map/ppermute | solution.py:265
  40.6 16.5 %all-gather.5.cloned.1.call-done = bf16[1536,512]{1,0:T(8,128)(2,1)} async-done(((bf16[384,512]{1,0:T(8,128)(2,1)}), bf16[1536,512]{1,0:T(8,128)(2,1)}) %all-gather.5.cloned.1.call-update) | async-done | bytes 1572880 | tf_op jit(solution)/shard_map/all_gather | solution.py:271
  57.1 0.0 all-gather.7.cloned.1.call-update
  57.2 1.6 %collective-permute-start.5 = (bf16[2048,128]{1,0:T(8,128)(2,1)S(1)}, bf16[2048,128]{1,0:T(8,128)(2,1)}, u32[]{:S(2)}, u32[]{:S(2)}) collective-permute-start(bf16[2048,128]{1,0:T(8,128)(2,1)S(1)} %copy-done.4), channel_id=1, source_target_pairs={{0,8},{8,0},{16,24},{24,16},{1,9},{9,1},{17,25},{25,17},{2,10},{10... | collective-permute-start | bytes 1572872 | tf_op jit(solution)/shard_map/ppermute | solution.py:265
  58.7 0.1 dynamic_slice.6
  58.8 0.4 convert_reduce_fusion
  59.2 1.9 %collective-permute-start.4 = (bf16[2048,128]{1,0:T(8,128)(2,1)S(1)}, bf16[2048,128]{1,0:T(8,128)(2,1)}, u32[]{:S(2)}, u32[]{:S(2)}) collective-permute-start(bf16[2048,128]{1,0:T(8,128)(2,1)S(1)} %collective-permute-done.3.kx_ref), channel_id=1, source_target_pairs={{8,16},{16,8},{9,17},{17,9},{10,18},{18,10},{11,19},{19,11},{12,20... | collective-permute-start | bytes 1572872 | tf_op jit(solution)/shard_map/ppermute | solution.py:265
  61.1 0.1 pad_add_fusion.1.place
  61.2 0.5 slice.4
  63.7 0.1 broadcast_in_dim.42.start_ref
  63.8 7.2 %collective-permute-done.5.vx_ref = bf16[2048,128]{1,0:T(8,128)(2,1)} collective-permute-done((bf16[2048,128]{1,0:T(8,128)(2,1)S(1)}, bf16[2048,128]{1,0:T(8,128)(2,1)}, u32[]{:S(2)}, u32[]{:S(2)}) %collective-permute-start.5) | collective-permute-done | bytes 524320 | tf_op jit(solution)/shard_map/ppermute | solution.py:265
  71.0 2.4 %collective-permute-start.10 = (bf16[2048,128]{1,0:T(8,128)(2,1)}, bf16[2048,128]{1,0:T(8,128)(2,1)}, u32[]{:S(2)}, u32[]{:S(2)}) collective-permute-start(bf16[2048,128]{1,0:T(8,128)(2,1)} %collective-permute-done.5.vx_ref), channel_id=1, source_target_pairs={{8,16},{16,8},{9,17},{17,9},{10,18},{18,10},{11,19},{19,11},{12,20... | collective-permute-start | bytes 1572872 | tf_op jit(solution)/shard_map/ppermute | solution.py:265
  73.5 4.3 %near.1.near_ref = f32[384,256]{1,0:T(8,128)S(1)} custom-call(s32[2]{0:T(128)S(1)} %pad_add_fusion.1.place, bf16[384,8192]{1,0:T(8,128)(2,1)} %own_ref.7, bf16[2048,128]{1,0:T(8,128)(2,1)S(1)} %copy-done.3, bf16[2048,128]{1,0:T(8,128)(2,1)S(1)} %copy-done.4, bf16[2048,128]{1,0:T(8,128)(2,1)S(1)} %collective-permute-done.3.kx_ref, ...), custom_call_target="tpu_custom_call" | custom-call | flops 805306368 | bytes 5242880 | tf_op jit(solution)/shard_map/near/pallas_call | solution.py:165
  77.7 1.3 collective-permute-start.6
  79.0 0.1 pad_add_fusion.info
  79.1 0.1 add_add_fusion
  79.2 1.9 %copy-done = bf16[8,384,512]{2,1,0:T(8,128)(2,1)S(1)} copy-done((bf16[8,384,512]{2,1,0:T(8,128)(2,1)S(1)}, bf16[8,384,512]{2,1,0:T(8,128)(2,1)}, u32[]{:S(2)}) %copy-start) | copy-done | bytes 3145752
  81.1 3.2 %facing.1.facing_ref = f32[768,256]{1,0:T(8,128)S(1)} custom-call(s32[3]{0:T(128)S(1)} %get-tuple-element.27.place, bf16[384,8192]{1,0:T(8,128)(2,1)} %own_ref.7, bf16[2,4,384,512]{3,2,1,0:T(8,128)(2,1)S(1)} %bitcast.18, bf16[2048,128]{1,0:T(8,128)(2,1)S(1)} %collective-permute-done.1.kw_ref, bf16[2048,128]{1,0:T(8,128)(2,1)S(1)} %collective-permute-done.2.vw_ref), custom_call_target="tpu_custom_call" | custom-call | flops 805306368 | bytes 4194304 | tf_op jit(solution)/shard_map/facing/pallas_call | solution.py:165
  84.3 5.0 %collective-permute-done.6.outer_ref = f32[384,256]{1,0:T(8,128)S(1)} collective-permute-done((f32[384,256]{1,0:T(8,128)S(1)}, f32[384,256]{1,0:T(8,128)S(1)}, u32[]{:S(2)}, u32[]{:S(2)}) %collective-permute-start.6) | collective-permute-done | bytes 393248 | tf_op jit(solution)/shard_map/ppermute | solution.py:265
  89.3 3.1 %distant.2.k_in = bf16[768,128]{1,0:T(8,128)(2,1)S(1)} custom-call(s32[3]{0:T(128)S(1)} %get-tuple-element.26.place, bf16[384,8192]{1,0:T(8,128)(2,1)} %own_ref.7, bf16[2,4,384,512]{3,2,1,0:T(8,128)(2,1)S(1)} %bitcast.19, bf16[2048,128]{1,0:T(8,128)(2,1)} %collective-permute-done.4.w_ref, f32[384,256]{1,0:T(8,128)S(1)} %near.1.near_ref, ...), custom_call_target="tpu_custom_call" | custom-call | flops 402653184 | bytes 3670016 | tf_op jit(solution)/shard_map/distant/pallas_call | solution.py:165
  92.4 3.4 %collective-permute-start.8 = (bf16[768,128]{1,0:T(8,128)(2,1)S(1)}, bf16[768,128]{1,0:T(8,128)(2,1)S(1)}, u32[]{:S(2)}, u32[]{:S(2)}) collective-permute-start(bf16[768,128]{1,0:T(8,128)(2,1)S(1)} %distant.2.k_in), channel_id=1, source_target_pairs={{8,16},{16,8},{9,17},{17,9},{10,18},{18,10},{11,19},{19,11},{12,20... | collective-permute-start | bytes 589832 | tf_op jit(solution)/shard_map/ppermute | solution.py:265
  95.8 1.3 %collective-permute-start.7 = (bf16[768,128]{1,0:T(8,128)(2,1)S(1)}, bf16[768,128]{1,0:T(8,128)(2,1)S(1)}, u32[]{:S(2)}, u32[]{:S(2)}) collective-permute-start(bf16[768,128]{1,0:T(8,128)(2,1)S(1)} %distant.2.k_in), channel_id=1, source_target_pairs={{8,0},{16,24},{9,1},{17,25},{10,2},{18,26},{11,3},{19,27},{12,4},{... | collective-permute-start | bytes 589832 | tf_op jit(solution)/shard_map/ppermute | solution.py:265
  97.2 3.1 %distant.3.v_in = bf16[768,128]{1,0:T(8,128)(2,1)S(1)} custom-call(s32[3]{0:T(128)S(1)} %get-tuple-element.26.place, bf16[384,8192]{1,0:T(8,128)(2,1)} %own_ref.7, bf16[2,4,384,512]{3,2,1,0:T(8,128)(2,1)S(1)} %bitcast.20, bf16[2048,128]{1,0:T(8,128)(2,1)} %collective-permute-done.10.w_ref, f32[384,256]{1,0:T(8,128)S(1)} %near.1.near_ref, ...), custom_call_target="tpu_custom_call" | custom-call | flops 402653184 | bytes 3670016 | tf_op jit(solution)/shard_map/distant/pallas_call | solution.py:165
  100.2 2.5 %collective-permute-start.12 = (bf16[768,128]{1,0:T(8,128)(2,1)S(1)}, bf16[768,128]{1,0:T(8,128)(2,1)S(1)}, u32[]{:S(2)}, u32[]{:S(2)}) collective-permute-start(bf16[768,128]{1,0:T(8,128)(2,1)S(1)} %distant.3.v_in), channel_id=1, source_target_pairs={{8,16},{16,8},{9,17},{17,9},{10,18},{18,10},{11,19},{19,11},{12,20... | collective-permute-start | bytes 589832 | tf_op jit(solution)/shard_map/ppermute | solution.py:265
  102.7 1.3 %collective-permute-start.11 = (bf16[768,128]{1,0:T(8,128)(2,1)S(1)}, bf16[768,128]{1,0:T(8,128)(2,1)S(1)}, u32[]{:S(2)}, u32[]{:S(2)}) collective-permute-start(bf16[768,128]{1,0:T(8,128)(2,1)S(1)} %distant.3.v_in), channel_id=1, source_target_pairs={{8,0},{16,24},{9,1},{17,25},{10,2},{18,26},{11,3},{19,27},{12,4},{... | collective-permute-start | bytes 589832 | tf_op jit(solution)/shard_map/ppermute | solution.py:265
  104.0 0.2 reduce_window_sum.11
  104.2 1.3 collective-permute-start.9
  105.5 2.3 %collective-permute-done.12.v_across = bf16[768,128]{1,0:T(8,128)(2,1)S(1)} collective-permute-done((bf16[768,128]{1,0:T(8,128)(2,1)S(1)}, bf16[768,128]{1,0:T(8,128)(2,1)S(1)}, u32[]{:S(2)}, u32[]{:S(2)}) %collective-permute-start.12) | collective-permute-done | bytes 196640 | tf_op jit(solution)/shard_map/ppermute | solution.py:265
  107.8 1.3 collective-permute-start.13
  109.1 0.3 select_reduce_fusion
  109.4 0.1 copy.14
  109.5 0.1 reshape.54.slots
  109.6 5.6 %attend_own.1 = (f32[8,384,1]{2,1,0:T(8,128)S(1)}, f32[8,384,1]{2,1,0:T(8,128)S(1)}, f32[8,384,128]{2,1,0:T(8,128)}) custom-call(s32[2]{0:T(128)S(1)} %pad_add_fusion.info, bf16[384,1024]{1,0:T(8,128)(2,1)S(1)} %copy-done.2, s32[384,1]{1,0:T(8,128)S(1)} %broadcast_in_dim.42.start_ref, bf16[768,128]{1,0:T(8,128)(2,1)S(1)} %distant.2.k_in, ...), custom_call_target="tpu_custom_call" | custom-call | flops 1207959552 | bytes 3145728 | tf_op jit(solution)/shard_map/attend_own/pallas_call | solution.py:418
  115.2 7.8 %attend_far.1 = (bf16[384,1024]{1,0:T(8,128)(2,1)}, bf16[4,192,256]{2,1,0:T(8,128)(2,1)}) custom-call(s32[2]{0:T(128)S(1)} %pad_add_fusion.info, s32[48]{0:T(128)S(1)} %reshape.54.slots, bf16[384,1024]{1,0:T(8,128)(2,1)S(1)} %copy-done.2, s32[384,1]{1,0:T(8,128)S(1)} %broadcast_in_dim.42.start_ref, bf16[768,128]{1,0:T(8,128)(2,1)S(1)} %distant.2.k_in, ...), custom_call_target="tpu_custom_call" | custom-call | flops 1207959552 | bytes 3145728 | tf_op jit(solution)/shard_map/attend_far/pallas_call | solution.py:431
  (27 shorter events, 0.1 us)
Async XLA Ops:
  7.2 66.3 %copy-start.3 = (bf16[2048,128]{1,0:T(8,128)(2,1)S(1)}, bf16[2048,128]{1,0:T(8,128)(2,1)}, u32[]{:S(2)}) copy-start(bf16[2048,128]{1,0:T(8,128)(2,1)} %kw_ref.1) | copy-start | bytes 1572868
  7.2 50.0 %copy-start.4 = (bf16[2048,128]{1,0:T(8,128)(2,1)S(1)}, bf16[2048,128]{1,0:T(8,128)(2,1)}, u32[]{:S(2)}) copy-start(bf16[2048,128]{1,0:T(8,128)(2,1)} %vw_ref.1) | copy-start | bytes 1572868
  7.2 51.5 %copy-start.8 = (s32[1536]{0:T(1024)S(1)}, s32[1536]{0:T(1024)}, u32[]{:S(2)}) copy-start(s32[1536]{0:T(1024)} %param.14) | copy-start | bytes 18436
  7.2 49.9 %all-gather.5.cloned.1.call-start = ((), (), s32[]{:S(2)}) async-start(), calls=%async_computation.1 | async-start | bytes 1966080 | tf_op jit(solution)/shard_map/all_gather | solution.py:271
  7.2 17.0 %collective-permute-start.1 = (bf16[2048,128]{1,0:T(8,128)(2,1)}, bf16[2048,128]{1,0:T(8,128)(2,1)S(1)}, u32[]{:S(2)}, u32[]{:S(2)}) collective-permute-start(bf16[2048,128]{1,0:T(8,128)(2,1)} %kw_ref.1), channel_id=1, source_target_pairs={{8,16},{16,8},{9,17},{17,9},{10,18},{18,10},{11,19},{19,11},{12,20... | collective-permute-start | bytes 1572872 | tf_op jit(solution)/shard_map/ppermute | solution.py:265
  10.8 13.5 %collective-permute-start = (bf16[384,512]{1,0:T(8,128)(2,1)S(1)}, bf16[384,512]{1,0:T(8,128)(2,1)S(1)}, u32[]{:S(2)}, u32[]{:S(2)}) collective-permute-start(bf16[384,512]{1,0:T(8,128)(2,1)S(1)} %constant_dynamic-slice_fusion), channel_id=1, source_target_pairs={{0,8},{24,16},{1,9},{25,17},{2,10},{26,18},{3,11},{27,19},{4,12},{... | collective-permute-start | bytes 1179656 | tf_op jit(solution)/shard_map/ppermute | solution.py:265
  24.3 0.7 copy-start.7
  25.0 54.1 %all-gather.7.cloned.1.call-start = ((), (), s32[]{:S(2)}) async-start(), calls=%async_computation.2 | async-start | bytes 4718592 | tf_op jit(solution)/shard_map/all_gather | solution.py:275
  25.1 12.5 %collective-permute-start.3 = (bf16[2048,128]{1,0:T(8,128)(2,1)}, bf16[2048,128]{1,0:T(8,128)(2,1)S(1)}, u32[]{:S(2)}, u32[]{:S(2)}) collective-permute-start(bf16[2048,128]{1,0:T(8,128)(2,1)} %kw_ref.1), channel_id=1, source_target_pairs={{0,8},{8,0},{16,24},{24,16},{1,9},{9,1},{17,25},{25,17},{2,10},{10... | collective-permute-start | bytes 1572872 | tf_op jit(solution)/shard_map/ppermute | solution.py:265
  26.6 14.0 %collective-permute-start.2 = (bf16[2048,128]{1,0:T(8,128)(2,1)}, bf16[2048,128]{1,0:T(8,128)(2,1)S(1)}, u32[]{:S(2)}, u32[]{:S(2)}) collective-permute-start(bf16[2048,128]{1,0:T(8,128)(2,1)} %vw_ref.1), channel_id=1, source_target_pairs={{8,16},{16,8},{9,17},{17,9},{10,18},{18,10},{11,19},{19,11},{12,20... | collective-permute-start | bytes 1572872 | tf_op jit(solution)/shard_map/ppermute | solution.py:265
  57.2 13.8 %collective-permute-start.5 = (bf16[2048,128]{1,0:T(8,128)(2,1)S(1)}, bf16[2048,128]{1,0:T(8,128)(2,1)}, u32[]{:S(2)}, u32[]{:S(2)}) collective-permute-start(bf16[2048,128]{1,0:T(8,128)(2,1)S(1)} %copy-done.4), channel_id=1, source_target_pairs={{0,8},{8,0},{16,24},{24,16},{1,9},{9,1},{17,25},{25,17},{2,10},{10... | collective-permute-start | bytes 1572872 | tf_op jit(solution)/shard_map/ppermute | solution.py:265
  59.2 30.1 %collective-permute-start.4 = (bf16[2048,128]{1,0:T(8,128)(2,1)S(1)}, bf16[2048,128]{1,0:T(8,128)(2,1)}, u32[]{:S(2)}, u32[]{:S(2)}) collective-permute-start(bf16[2048,128]{1,0:T(8,128)(2,1)S(1)} %collective-permute-done.3.kx_ref), channel_id=1, source_target_pairs={{8,16},{16,8},{9,17},{17,9},{10,18},{18,10},{11,19},{19,11},{12,20... | collective-permute-start | bytes 1572872 | tf_op jit(solution)/shard_map/ppermute | solution.py:265
  71.0 26.1 %collective-permute-start.10 = (bf16[2048,128]{1,0:T(8,128)(2,1)}, bf16[2048,128]{1,0:T(8,128)(2,1)}, u32[]{:S(2)}, u32[]{:S(2)}) collective-permute-start(bf16[2048,128]{1,0:T(8,128)(2,1)} %collective-permute-done.5.vx_ref), channel_id=1, source_target_pairs={{8,16},{16,8},{9,17},{17,9},{10,18},{18,10},{11,19},{19,11},{12,20... | collective-permute-start | bytes 1572872 | tf_op jit(solution)/shard_map/ppermute | solution.py:265
  77.7 11.6 %collective-permute-start.6 = (f32[384,256]{1,0:T(8,128)S(1)}, f32[384,256]{1,0:T(8,128)S(1)}, u32[]{:S(2)}, u32[]{:S(2)}) collective-permute-start(f32[384,256]{1,0:T(8,128)S(1)} %near.1.near_ref), channel_id=1, source_target_pairs={{0,8},{24,16},{1,9},{25,17},{2,10},{26,18},{3,11},{27,19},{4,12},{... | collective-permute-start | bytes 1179656 | tf_op jit(solution)/shard_map/ppermute | solution.py:265
  79.2 1.9 %copy-start = (bf16[8,384,512]{2,1,0:T(8,128)(2,1)S(1)}, bf16[8,384,512]{2,1,0:T(8,128)(2,1)}, u32[]{:S(2)}) copy-start(bf16[8,384,512]{2,1,0:T(8,128)(2,1)} %all-gather.7.cloned.1.call-done) | copy-start | bytes 9437188
  81.1 8.2 %copy-start.1 = (bf16[8,384,512]{2,1,0:T(8,128)(2,1)S(1)}, bf16[8,384,512]{2,1,0:T(8,128)(2,1)}, u32[]{:S(2)}) copy-start(bf16[8,384,512]{2,1,0:T(8,128)(2,1)} %all-gather.7.cloned.1.call-done) | copy-start | bytes 9437188
  81.1 8.2 %copy-start.5 = (bf16[128]{0:T(256)(128)(2,1)S(1)}, bf16[128]{0:T(256)(128)(2,1)}, u32[]{:S(2)}) copy-start(bf16[128]{0:T(256)(128)(2,1)} %param.12) | copy-start | bytes 772
  89.3 7.8 %copy-start.6 = (bf16[128]{0:T(256)(128)(2,1)S(1)}, bf16[128]{0:T(256)(128)(2,1)}, u32[]{:S(2)}) copy-start(bf16[128]{0:T(256)(128)(2,1)} %param.13) | copy-start | bytes 772
  92.4 11.8 %collective-permute-start.8 = (bf16[768,128]{1,0:T(8,128)(2,1)S(1)}, bf16[768,128]{1,0:T(8,128)(2,1)S(1)}, u32[]{:S(2)}, u32[]{:S(2)}) collective-permute-start(bf16[768,128]{1,0:T(8,128)(2,1)S(1)} %distant.2.k_in), channel_id=1, source_target_pairs={{8,16},{16,8},{9,17},{17,9},{10,18},{18,10},{11,19},{19,11},{12,20... | collective-permute-start | bytes 589832 | tf_op jit(solution)/shard_map/ppermute | solution.py:265
  95.8 13.7 %collective-permute-start.7 = (bf16[768,128]{1,0:T(8,128)(2,1)S(1)}, bf16[768,128]{1,0:T(8,128)(2,1)S(1)}, u32[]{:S(2)}, u32[]{:S(2)}) collective-permute-start(bf16[768,128]{1,0:T(8,128)(2,1)S(1)} %distant.2.k_in), channel_id=1, source_target_pairs={{8,0},{16,24},{9,1},{17,25},{10,2},{18,26},{11,3},{19,27},{12,4},{... | collective-permute-start | bytes 589832 | tf_op jit(solution)/shard_map/ppermute | solution.py:265
  97.1 12.4 %copy-start.2 = (bf16[384,1024]{1,0:T(8,128)(2,1)S(1)}, bf16[384,1024]{1,0:T(8,128)(2,1)}, u32[]{:S(2)}) copy-start(bf16[384,1024]{1,0:T(8,128)(2,1)} %q_ref.3) | copy-start | bytes 2359300
  100.2 7.6 %collective-permute-start.12 = (bf16[768,128]{1,0:T(8,128)(2,1)S(1)}, bf16[768,128]{1,0:T(8,128)(2,1)S(1)}, u32[]{:S(2)}, u32[]{:S(2)}) collective-permute-start(bf16[768,128]{1,0:T(8,128)(2,1)S(1)} %distant.3.v_in), channel_id=1, source_target_pairs={{8,16},{16,8},{9,17},{17,9},{10,18},{18,10},{11,19},{19,11},{12,20... | collective-permute-start | bytes 589832 | tf_op jit(solution)/shard_map/ppermute | solution.py:265
  102.7 6.9 %collective-permute-start.11 = (bf16[768,128]{1,0:T(8,128)(2,1)S(1)}, bf16[768,128]{1,0:T(8,128)(2,1)S(1)}, u32[]{:S(2)}, u32[]{:S(2)}) collective-permute-start(bf16[768,128]{1,0:T(8,128)(2,1)S(1)} %distant.3.v_in), channel_id=1, source_target_pairs={{8,0},{16,24},{9,1},{17,25},{10,2},{18,26},{11,3},{19,27},{12,4},{... | collective-permute-start | bytes 589832 | tf_op jit(solution)/shard_map/ppermute | solution.py:265
  104.2 11.0 %collective-permute-start.9 = (bf16[768,128]{1,0:T(8,128)(2,1)S(1)}, bf16[768,128]{1,0:T(8,128)(2,1)S(1)}, u32[]{:S(2)}, u32[]{:S(2)}) collective-permute-start(bf16[768,128]{1,0:T(8,128)(2,1)S(1)} %collective-permute-done.8.k_across), channel_id=1, source_target_pairs={{8,0},{16,24},{9,1},{17,25},{10,2},{18,26},{11,3},{19,27},{12,4},{... | collective-permute-start | bytes 589832 | tf_op jit(solution)/shard_map/ppermute | solution.py:265
  107.8 7.4 %collective-permute-start.13 = (bf16[768,128]{1,0:T(8,128)(2,1)S(1)}, bf16[768,128]{1,0:T(8,128)(2,1)S(1)}, u32[]{:S(2)}, u32[]{:S(2)}) collective-permute-start(bf16[768,128]{1,0:T(8,128)(2,1)S(1)} %collective-permute-done.12.v_across), channel_id=1, source_target_pairs={{8,0},{16,24},{9,1},{17,25},{10,2},{18,26},{11,3},{19,27},{12,4},{... | collective-permute-start | bytes 589832 | tf_op jit(solution)/shard_map/ppermute | solution.py:265
Sparse Core Ops, SparseCore 0:
  25.2 31.9 all-gather.4
  58.7 12.3 all-gather.6

commit v3 on v2

v3 whole, which is shorter than its diff:
```python
import functools
import math

import jax
import jax.numpy as jnp
from jax import lax
from jax.experimental import pallas as pl
from jax.experimental.pallas import tpu as pltpu
from jax.sharding import PartitionSpec as P

HD = 128
PAGE = 16
NEG = -1e30
VMEM_LIMIT = 24 * 1024 * 1024
PROJECT_VMEM = 24 * 1024 * 1024


def attention_kernel(heads, span, info, slots, q_ref, k_ref, v_ref, start_ref, out_ref, cache_ref, acc, top):
    index = info[0]
    first = info[1]
    factor = HD**-0.5 * math.log2(math.e)
    columns = lax.broadcasted_iota(jnp.int32, (span, span), 1)
    rows = lax.broadcasted_iota(jnp.int32, (span, span), 0)

    def block(j, diagonal):
        at = pl.multiple_of(j * span, span)
        keys = k_ref[pl.ds(at, span), :]
        values = jnp.concatenate(
            [v_ref[pl.ds(at, span), :], jnp.ones((span, HD), jnp.bfloat16)], axis=1
        )
        allowed = columns >= start_ref[...] - at
        if diagonal:
            allowed = allowed & (columns <= rows)
        for g in range(heads):
            scores = lax.dot_general(
                q_ref[:, g * HD : (g + 1) * HD],
                keys,
                (((1,), (1,)), ((), ())),
                preferred_element_type=jnp.float32,
            )
            scores = jnp.where(allowed, scores, NEG)
            peak = jnp.max(scores, axis=1, keepdims=True)
            if not diagonal:
                before = top[g]
                peak = jnp.maximum(peak, before)
            weights = jnp.exp2(scores * factor - peak * factor).astype(jnp.bfloat16)
            mixed = jnp.dot(weights, values, preferred_element_type=jnp.float32)
            if not diagonal:
                mixed = mixed + acc[g] * jnp.exp2((before - peak) * factor)
            top[g] = peak
            acc[g] = mixed

    block(index, True)

    @pl.loop(first, index)
    def _(j):
        block(j, False)

    for g in range(heads):
        mixed = acc[g]
        out_ref[:, g * HD : (g + 1) * HD] = (mixed[:, :HD] / mixed[:, HD:]).astype(out_ref.dtype)

    pick_pages(slots, 0, cache_ref.shape[0], k_ref, v_ref, cache_ref)


def attention(info, slots, queries, keys, values, start, n_pre, capacity):
    span = queries.shape[0]
    heads = queries.shape[1] // HD
    return pl.pallas_call(
        functools.partial(attention_kernel, heads, span),
        in_specs=[
            pl.BlockSpec(memory_space=pltpu.SMEM),
            pl.BlockSpec(memory_space=pltpu.SMEM),
            pl.BlockSpec(memory_space=pltpu.VMEM),
            pl.BlockSpec(memory_space=pltpu.VMEM),
            pl.BlockSpec(memory_space=pltpu.VMEM),
            pl.BlockSpec(memory_space=pltpu.VMEM),
        ],
        out_specs=[
            pl.BlockSpec(memory_space=pltpu.VMEM),
            pl.BlockSpec(memory_space=pltpu.VMEM),
        ],
        out_shape=[
            jax.ShapeDtypeStruct(queries.shape, jnp.bfloat16),
            jax.ShapeDtypeStruct((n_pre, capacity * PAGE, 2 * HD), jnp.bfloat16),
        ],
        scratch_shapes=[
            pltpu.VMEM((heads, span, 2 * HD), jnp.float32),
            pltpu.VMEM((heads, span, 1), jnp.float32),
        ],
        compiler_params=pltpu.CompilerParams(vmem_limit_bytes=VMEM_LIMIT),
        cost_estimate=pl.CostEstimate(
            flops=4 * heads * span * span * n_pre * HD,
            bytes_accessed=4 * queries.size * 2,
            transcendentals=heads * span * span * n_pre,
        ),
        name="attention",
    )(info, slots, queries, keys, values, start)


PIECES = 8


def near_kernel(place, own_ref, near_ref, kw_ref, vw_ref, kx_ref, vx_ref, out_ref):
    def part(h_ref, key_ref, value_ref):
        weight = jnp.concatenate([key_ref[...], value_ref[...]], axis=1)
        return jnp.dot(h_ref[...], weight, preferred_element_type=jnp.float32)

    out_ref[...] = part(own_ref, kw_ref, vw_ref) + part(near_ref, kx_ref, vx_ref)


def add_pieces(member, chunk, pieces, w_ref, acc_ref):
    share = pieces[0].shape[1]
    half = PIECES // 2
    for side in range(2):

        @pl.when(jnp.bitwise_xor(member // half, side) == lax.rem(chunk, 2))
        def _():
            total = acc_ref[...]
            for j in range(side * half, side * half + half):
                row = lax.rem(jnp.bitwise_xor(member, j), half) * share
                total += jnp.dot(
                    pieces[j][...],
                    w_ref[pl.ds(pl.multiple_of(row, share), share), :],
                    preferred_element_type=jnp.float32,
                )
            acc_ref[...] = total


def facing_kernel(place, own_ref, *refs):
    pieces = refs[:PIECES]
    kw_ref, vw_ref, out_ref, w_ref = refs[PIECES:]
    span = own_ref.shape[0]
    w_ref[:, :HD] = kw_ref[...]
    w_ref[:, HD:] = vw_ref[...]
    out_ref[:span] = jnp.dot(own_ref[...], w_ref[...], preferred_element_type=jnp.float32)
    out_ref[span:] = jnp.zeros((span, 2 * HD), jnp.float32)
    add_pieces(place[2], place[0], pieces, w_ref, out_ref.at[pl.ds(span, span)])


def distant_kernel(place, own_ref, *refs):
    pieces = refs[:PIECES]
    w_ref, near_ref, outer_ref, facing_ref, bias_ref, out_ref, acc = refs[PIECES:]
    span = own_ref.shape[0]
    bias = bias_ref[...].astype(jnp.float32)
    own = jnp.dot(own_ref[...], w_ref[...], preferred_element_type=jnp.float32)
    own = own + near_ref[...] + facing_ref[:span] + bias
    acc[...] = outer_ref[...] + facing_ref[span:] + bias
    add_pieces(place[2], place[0], pieces, w_ref, acc)
    own_at = pl.multiple_of(place[1] * span, span)
    outer_at = pl.multiple_of((1 - place[1]) * span, span)
    out_ref[pl.ds(own_at, span), :] = own.astype(jnp.bfloat16)
    out_ref[pl.ds(outer_at, span), :] = acc[...].astype(jnp.bfloat16)


def call_project(kernel, name, place, operands, in_specs, depth, rows, columns, kind, scratch=()):
    return pl.pallas_call(
        kernel,
        grid_spec=pltpu.PrefetchScalarGridSpec(
            num_scalar_prefetch=1,
            grid=(1,),
            in_specs=in_specs,
            out_specs=pl.BlockSpec((rows, columns), lambda k, place: (0, 0)),
            scratch_shapes=list(scratch),
        ),
        out_shape=jax.ShapeDtypeStruct((rows, columns), kind),
        compiler_params=pltpu.CompilerParams(vmem_limit_bytes=PROJECT_VMEM),
        cost_estimate=pl.CostEstimate(flops=0, bytes_accessed=0, transcendentals=0),
        name=name,
    )(place, *operands)


def all_of(x, column=0, columns=None):
    shape = (x.shape[0], columns or x.shape[1])
    return pl.BlockSpec(shape, lambda k, place: (0, column))


def project_near(place, own, key_weight, value_weight, key_swapped, value_swapped):
    span, depth = own.shape[0], key_weight.shape[0]
    weights = [key_weight, value_weight, key_swapped, value_swapped]
    in_specs = [
        pl.BlockSpec((span, depth), lambda k, place: (0, place[0])),
        pl.BlockSpec((span, depth), lambda k, place: (0, place[1])),
    ] + [all_of(w) for w in weights]
    operands = [own, own] + weights
    return call_project(
        near_kernel, "near", place, operands, in_specs, 2 * depth, span, 2 * HD, jnp.float32
    )


def project_facing(place, own, pieces, key_weight, value_weight):
    span, depth = own.shape[0], key_weight.shape[0]
    others = list(pieces) + [key_weight, value_weight]
    in_specs = [pl.BlockSpec((span, depth), lambda k, place: (0, place[0]))]
    in_specs += [all_of(x) for x in others]
    return call_project(
        facing_kernel,
        "facing",
        place,
        [own] + others,
        in_specs,
        depth,
        2 * span,
        2 * HD,
        jnp.float32,
        [pltpu.VMEM((depth, 2 * HD), jnp.bfloat16)],
    )


def project_distant(place, column, own, pieces, weight, near, outer, facing, bias):
    span, depth = own.shape[0], weight.shape[0]
    others = list(pieces) + [weight]
    parts = [near, outer, facing]
    in_specs = [pl.BlockSpec((span, depth), lambda k, place: (0, place[0]))]
    in_specs += [all_of(x) for x in others] + [all_of(x, column, HD) for x in parts]
    in_specs.append(all_of(bias))
    return call_project(
        distant_kernel,
        "distant",
        place,
        [own] + others + parts + [bias],
        in_specs,
        depth,
        2 * span,
        HD,
        jnp.bfloat16,
        [pltpu.VMEM((span, HD), jnp.float32)],
    )


INWARD = [(0, 1), (3, 2)]
ACROSS = [(1, 2), (2, 1)]
OUTWARD = [(1, 0), (2, 3)]
SWAP = [(0, 1), (1, 0), (2, 3), (3, 2)]


def spread_owners(page_owner):
    index = lax.axis_index("pre")
    mine = page_owner.T
    mate = lax.ppermute(mine, "pre", SWAP)
    even = lax.rem(index, 2) == 0
    pair = jnp.concatenate([jnp.where(even, mine, mate), jnp.where(even, mate, mine)], axis=0)
    across = lax.ppermute(pair, "pre", ACROSS)
    far = lax.ppermute(across, "pre", OUTWARD)
    other = jnp.where((index == 1) | (index == 2), across, far)
    return jnp.concatenate(
        [jnp.where(index < 2, pair, other), jnp.where(index < 2, other, pair)], axis=0
    )


def line_of_four(hidden, key_weight, value_weight, key_bias, value_bias):
    index = lax.axis_index("pre")
    member = lax.axis_index(("dec", "tp"))
    width = hidden.shape[1]
    share = width // 2 // PIECES
    facing = 3 - index
    near = jnp.bitwise_xor(index, 1)
    distant = jnp.bitwise_xor(facing, 1)
    second = (index < 2).astype(jnp.int32)

    def send(x, pairs):
        return lax.ppermute(x, "pre", pairs)

    def trade(x, apart):
        return lax.ppermute(x, ("dec", "tp"), [(m, m ^ apart) for m in range(PIECES)])

    mine = second * (width // 2) + member * share
    cut = send(lax.dynamic_slice_in_dim(hidden, mine, share, axis=1), INWARD)
    key_facing = send(key_weight, ACROSS)
    cut, key_facing, key_weight, value_weight = lax.optimization_barrier(
        (cut, key_facing, key_weight, value_weight)
    )
    chips = [cut, trade(cut, 2), trade(cut, 4), trade(cut, 6)]
    value_facing = send(value_weight, ACROSS)
    key_swapped = send(key_weight, SWAP)
    value_swapped = send(value_weight, SWAP)
    key_distant = send(key_swapped, ACROSS)
    value_distant = send(value_swapped, ACROSS)
    mates = [trade(x, 1) for x in chips]
    pieces = [x for both in zip(chips, mates) for x in both]

    def place(chunk):
        return jnp.stack([chunk, second, member])

    own_part = project_near(
        jnp.stack([index, near]), hidden, key_weight, value_weight, key_swapped, value_swapped
    )
    outer_part = send(own_part, INWARD)
    faced = project_facing(place(facing), hidden, pieces, key_facing, value_facing)

    def finish(column, weight, bias):
        pair = project_distant(
            place(distant), column, hidden, pieces, weight, own_part, outer_part, faced, bias[None, :]
        )
        out = send(pair, OUTWARD)
        across = send(pair, ACROSS)
        return pair, out, across, send(across, OUTWARD)

    keys = finish(0, key_distant, key_bias)
    values = finish(1, value_distant, value_bias)
    return keys, values


def softmax_step(q, keys, values, allowed, before):
    factor = HD**-0.5 * math.log2(math.e)
    scores = lax.dot_general(q, keys, (((1,), (1,)), ((), ())), preferred_element_type=jnp.float32)
    scores = jnp.where(allowed, scores, NEG)
    peak = jnp.max(scores, axis=1, keepdims=True)
    if before is not None:
        peak = jnp.maximum(peak, before[0])
    weights = jnp.exp2(scores * factor - peak * factor).astype(jnp.bfloat16)
    mixed = jnp.dot(weights, values, preferred_element_type=jnp.float32)
    total, mixed = mixed[:, HD:], mixed[:, :HD]
    if before is not None:
        shrink = jnp.exp2((before[0] - peak) * factor)
        total = total + before[1] * shrink
        mixed = mixed + before[2] * shrink
    return peak, total, mixed


def with_ones(values):
    return jnp.concatenate([values, jnp.ones_like(values)], axis=1)


def own_kernel(
    heads, info, slots, q_ref, start_ref, k_in, k_out, v_in, v_out, top, total, mix, cache_ref, held_k, held_v
):
    span = q_ref.shape[0]
    index = info[0]
    inner = (index == 1) | (index == 2)
    held_k[...] = jnp.where(inner, k_in[...], k_out[...])
    held_v[...] = jnp.where(inner, v_in[...], v_out[...])
    pick_pages(slots, 0, 2, held_k, held_v, cache_ref)
    values = with_ones(held_v[...])
    columns = lax.broadcasted_iota(jnp.int32, (span, 2 * span), 1)
    rows = lax.broadcasted_iota(jnp.int32, (span, 2 * span), 0)
    allowed = (columns <= rows + lax.rem(index, 2) * span) & (
        columns >= start_ref[...] - (index // 2) * 2 * span
    )
    for g in range(heads):
        q = q_ref[:, g * HD : (g + 1) * HD]
        peak, sums, mixed = softmax_step(q, held_k[...], values, allowed, None)
        top[g] = peak
        total[g] = sums[:, :1]
        mix[g] = mixed


def far_kernel(
    heads,
    info,
    slots,
    q_ref,
    start_ref,
    k_across,
    k_far,
    v_across,
    v_far,
    top,
    total,
    mix,
    own_cache,
    out_ref,
    cache_ref,
    held_k,
    held_v,
):
    span = q_ref.shape[0]
    index = info[0]
    inner = (index == 1) | (index == 2)
    held_k[...] = jnp.where(inner, k_across[...], k_far[...])
    held_v[...] = jnp.where(inner, v_across[...], v_far[...])

    @pl.when((index < 2) | (info[1] >= 2))
    def _():
        for g in range(heads):
            out_ref[:, g * HD : (g + 1) * HD] = (mix[g] / total[g]).astype(out_ref.dtype)

    @pl.when((index >= 2) & (info[1] < 2))
    def _():
        keys = held_k[...]
        values = with_ones(held_v[...])
        columns = lax.broadcasted_iota(jnp.int32, (span, 2 * span), 1)
        allowed = columns >= start_ref[...]
        for g in range(heads):
            q = q_ref[:, g * HD : (g + 1) * HD]
            _, sums, mixed = softmax_step(q, keys, values, allowed, (top[g], total[g], mix[g]))
            out_ref[:, g * HD : (g + 1) * HD] = (mixed / sums).astype(out_ref.dtype)

    cache_ref[pl.ds(index // 2 * 2, 2)] = own_cache[...]
    pick_pages(slots, 2, 2, held_k, held_v, cache_ref.at[pl.ds((1 - index // 2) * 2, 2)])


def pick_pages(slots, first, sources, k_ref, v_ref, cache_ref):
    capacity = cache_ref.shape[1] // PAGE
    empty = jnp.zeros((PAGE, HD), cache_ref.dtype)
    for s in range(sources):
        for r in range(capacity):
            page = slots[(first + s) * capacity + r]
            token = pl.ds(pl.multiple_of(jnp.maximum(page, 0) * PAGE, PAGE), PAGE)
            row = pl.ds(r * PAGE, PAGE)
            cache_ref[s, row, :HD] = jnp.where(page >= 0, k_ref[token, :], empty)
            cache_ref[s, row, HD:] = jnp.where(page >= 0, v_ref[token, :], empty)


def attention_of_pairs(info, slots, queries, start, keys, values, capacity):
    span = queries.shape[0]
    heads = queries.shape[1] // HD
    smem = pl.BlockSpec(memory_space=pltpu.SMEM)
    vmem = pl.BlockSpec(memory_space=pltpu.VMEM)
    cost = pl.CostEstimate(
        flops=8 * heads * span * span * HD,
        bytes_accessed=4 * queries.size * 2,
        transcendentals=2 * heads * span * span,
    )
    params = pltpu.CompilerParams(vmem_limit_bytes=VMEM_LIMIT)
    held = [pltpu.VMEM((2 * span, HD), jnp.bfloat16)] * 2
    state = pl.pallas_call(
        functools.partial(own_kernel, heads),
        in_specs=[smem] * 2 + [vmem] * 6,
        out_specs=[vmem] * 4,
        out_shape=[
            jax.ShapeDtypeStruct((heads, span, 1), jnp.float32),
            jax.ShapeDtypeStruct((heads, span, 1), jnp.float32),
            jax.ShapeDtypeStruct((heads, span, HD), jnp.float32),
            jax.ShapeDtypeStruct((2, capacity * PAGE, 2 * HD), jnp.bfloat16),
        ],
        scratch_shapes=held,
        compiler_params=params,
        cost_estimate=cost,
        name="attend_own",
    )(info, slots, queries, start, *keys[:2], *values[:2])
    return pl.pallas_call(
        functools.partial(far_kernel, heads),
        in_specs=[smem] * 2 + [vmem] * 10,
        out_specs=[vmem] * 2,
        out_shape=[
            jax.ShapeDtypeStruct(queries.shape, jnp.bfloat16),
            jax.ShapeDtypeStruct((4, capacity * PAGE, 2 * HD), jnp.bfloat16),
        ],
        scratch_shapes=held,
        compiler_params=params,
        cost_estimate=cost,
        name="attend_far",
    )(info, slots, queries, start, *keys[2:], *values[2:], *state)


def gathered(hidden, key_weight, value_weight, key_bias, value_bias):
    joined = jnp.concatenate([key_weight, value_weight], axis=1)
    joined = lax.all_gather(joined, "pre", axis=0, tiled=True)
    bias = jnp.concatenate([key_bias, value_bias]).astype(jnp.float32)
    local = jnp.dot(hidden, joined, preferred_element_type=jnp.float32) + bias
    both = lax.all_gather(local.astype(jnp.bfloat16), "pre", axis=0, tiled=True)
    return both[:, :HD], both[:, HD:]


def body(hidden, queries, key_weight, value_weight, key_bias, value_bias, segment_ids, page_owner):
    n_pre = lax.axis_size("pre")
    index = lax.axis_index("pre")
    span = hidden.shape[0]
    pages_dev = span // PAGE
    capacity = 2 * pages_dev // n_pre
    assert key_weight.shape[1] == HD

    own_segments = lax.dynamic_slice_in_dim(segment_ids, index * span, span)
    start = jnp.sum(
        (segment_ids[None, :] < own_segments[:, None]).astype(jnp.int32), axis=1, keepdims=True
    )
    info = jnp.stack([index, start[0, 0] // span]).astype(jnp.int32)
    arrays = (hidden, key_weight, value_weight, key_bias, value_bias)
    if n_pre == 4:
        owners = spread_owners(page_owner)
        keys, values = line_of_four(*arrays)
    else:
        owners = lax.all_gather(page_owner[:, 0], "pre")
        keys, values = gathered(*arrays)

    mine = (owners == index).astype(jnp.int32)
    rank = jnp.cumsum(mine, axis=1) - mine
    numbers = jnp.arange(n_pre * pages_dev, dtype=jnp.int32).reshape(n_pre, 1, pages_dev)
    wanted = (mine[:, None, :] == 1) & (
        rank[:, None, :] == jnp.arange(capacity, dtype=jnp.int32)[None, :, None]
    )
    slots = jnp.max(jnp.where(wanted, numbers, -1), axis=2)
    if n_pre == 4:
        low, high = slots[:2], jnp.where(slots[2:] < 0, -1, slots[2:] - 2 * pages_dev)
        slots = jnp.where(index < 2, jnp.stack([low, high]), jnp.stack([high, low]))
        mixed, cache = attention_of_pairs(
            info, slots.reshape(-1), queries, start, keys, values, capacity
        )
    else:
        slots = slots.reshape(-1)
        mixed, cache = attention(info, slots, queries, keys, values, start, n_pre, capacity)
    return (mixed, cache[None])


def solution(mesh):
    return jax.shard_map(
        body,
        mesh=mesh,
        in_specs=(
            P(("group", "pre"), None),
            P(("group", "pre"), ("dec", "tp")),
            P("pre", ("dec", "tp")),
            P("pre", ("dec", "tp")),
            P(("dec", "tp")),
            P(("dec", "tp")),
            P("group"),
            P(("group", "pre"), None),
        ),
        out_specs=(
            P(("group", "pre"), ("dec", "tp")),
            P(("group", "pre"), None, None, ("dec", "tp")),
        ),
        check_vma=False,
    )
```

time: 131 us -> 118 us (0.901)
  waiting for transfers between devices: 42.7 us -> 23.2 us
  starting transfers between devices: 25.9 us -> 43.4 us
  between operations: 16.3 us -> 2.95 us
  local copies, waits for them, and re-layouts: 5.22 us -> 17.7 us
  blocking collectives: 11.5 us -> 0 us
  other arithmetic: 1.12 us -> 5.68 us
  Pallas kernels: 27 us -> 23.5 us
    all_gather x2 -> x0, waiting for transfers between devices: 16.5 us -> none  [the longest x1 16.5 us: line_of_four(): other = lax.all_gather(cut, 'dec')]
    ppermute x0 -> x10, starting transfers between devices: none -> 12.1 us  [the longest x7 4.58 us: trade(): lax.ppermute(x, ('dec', 'tp'), [(m, m ^ apart) for m in range(PIECES)])]
    unnamed x18 -> x38, local copies, waits for them, and re-layouts: 2.67 us -> 14.3 us
    all_to_all x1 -> x0, blocking collectives: 11.5 us -> none  [body(): lax.all_to_all(jnp.broadcast_to(page_owner[:, 0], (n_pre, pages_dev)), 'p...]
    ppermute x14, starting transfers between devices: 25.9 us -> 31.3 us  [send(): return lax.ppermute(x, 'pre', pairs)]
    ppermute x14, waiting for transfers between devices: 26.2 us -> 20.8 us  [send(): return lax.ppermute(x, 'pre', pairs)]
    ppermute x0 -> x10, waiting for transfers between devices: none -> 2.49 us  [the longest x1 1.97 us: spread_owners(): across = lax.ppermute(pair, 'pre', ACROSS)]
    pallas_call x4, Pallas kernels: 13.6 us -> 11.8 us  [call_project(): pl.pallas_call(kernel, grid_spec=pltpu.PrefetchScalarGridSpec(num_scalar_...]
  transfers between devices with their start and end apart: 16 -> 24, of which waited for: 6 -> 7; matrix products, arithmetic and copies ran while one was open for 3% -> 8% of each run, Pallas kernels for 15% -> 14%
where the time goes in v3:
time: 118 us; the launch traced here: 116 us
  starting transfers between devices  43.4 us (37%)
  Pallas kernels  23.5 us (20%)
  waiting for transfers between devices  23.2 us (20%)
  local copies, waits for them, and re-layouts  17.7 us (15%)
  other arithmetic  5.68 us (5%)
  between operations  2.95 us (2%)
    ppermute x14, starting transfers between devices, send(): return lax.ppermute(x, 'pre', pairs)  31.3 us
    ppermute x14, waiting for transfers between devices, send(): return lax.ppermute(x, 'pre', pairs)  20.8 us
    unnamed x38, local copies, waits for them, and re-layouts  14.3 us
    pallas_call x4, Pallas kernels, call_project(): pl.pallas_call(kernel, grid_spec=pltpu.PrefetchScalarGridSpec(num_scalar_...  11.8 us
    pallas_call x1, Pallas kernels, attention_of_pairs(): pl.pallas_call(functools.partial(far_kernel, heads), in_specs=[smem] * 2...  6.69 us
    pallas_call x1, Pallas kernels, attention_of_pairs(): pl.pallas_call(functools.partial(own_kernel, heads), in_specs=[smem] * 2...  5.09 us
    ppermute x7, starting transfers between devices, trade(): lax.ppermute(x, ('dec', 'tp'), [(m, m ^ apart) for m in range(PIECES)])  4.58 us
    ppermute x1, starting transfers between devices, spread_owners(): across = lax.ppermute(pair, 'pre', ACROSS)  3.48 us
  transfers between devices with their start and end apart: 24, of which 7 were waited for; matrix products, arithmetic and copies ran while one was open for 8% of the time, Pallas kernels for 14%

profile of v3, /device:TPU:16, one launch (start us, length us, event | category | flops | bytes accessed | tf_op | source)
XLA Modules:
  0.0 116.5 jit_solution(3799582591366649700)
XLA Ops:
  0.6 2.4 %collective-permute-start.4 = (bf16[2048,128]{1,0:T(8,128)(2,1)}, bf16[2048,128]{1,0:T(8,128)(2,1)S(1)}, u32[]{:S(2)}, u32[]{:S(2)}) collective-permute-start(bf16[2048,128]{1,0:T(8,128)(2,1)} %kw_ref), channel_id=1, source_target_pairs={{8,16},{16,8},{9,17},{17,9},{10,18},{18,10},{11,19},{19,11},{12,20... | collective-permute-start | bytes 1572872 | tf_op jit(solution)/shard_map/ppermute | solution.py:262
  3.0 1.0 constant_dynamic-slice_fusion
  4.0 1.3 %collective-permute-start.3 = (bf16[384,512]{1,0:T(8,128)(2,1)S(1)}, bf16[384,512]{1,0:T(8,128)(2,1)S(1)}, u32[]{:S(2)}, u32[]{:S(2)}) collective-permute-start(bf16[384,512]{1,0:T(8,128)(2,1)S(1)} %constant_dynamic-slice_fusion), channel_id=1, source_target_pairs={{0,8},{24,16},{1,9},{25,17},{2,10},{26,18},{3,11},{27,19},{4,12},{... | collective-permute-start | bytes 1179656 | tf_op jit(solution)/shard_map/ppermute | solution.py:262
  5.3 2.7 %collective-permute-start = (s32[1,24]{1,0:T(1,128)}, s32[1,24]{1,0:T(1,128)S(1)}, u32[]{:S(2)}, u32[]{:S(2)}) collective-permute-start(s32[1,24]{1,0:T(1,128)} %bitcast.21), channel_id=1, source_target_pairs={{0,8},{8,0},{16,24},{24,16},{1,9},{9,1},{17,25},{25,17},{2,10},{10... | collective-permute-start | bytes 296 | tf_op jit(solution)/shard_map/ppermute | solution.py:240
  8.1 8.4 %collective-permute-done.3.refs_0_ = bf16[384,512]{1,0:T(8,128)(2,1)S(1)} collective-permute-done((bf16[384,512]{1,0:T(8,128)(2,1)S(1)}, bf16[384,512]{1,0:T(8,128)(2,1)S(1)}, u32[]{:S(2)}, u32[]{:S(2)}) %collective-permute-start.3) | collective-permute-done | bytes 393248 | tf_op jit(solution)/shard_map/ppermute | solution.py:262
  16.5 0.8 copy-done.7
  17.3 2.4 %collective-permute-start.10 = (bf16[384,512]{1,0:T(8,128)(2,1)S(1)}, bf16[384,512]{1,0:T(8,128)(2,1)S(1)}, u32[]{:S(2)}, u32[]{:S(2)}) collective-permute-start(bf16[384,512]{1,0:T(8,128)(2,1)S(1)} %collective-permute-done.3.refs_0_), channel_id=1, source_target_pairs={{0,6},{1,7},{2,4},{3,5},{4,2},{5,3},{6,0},{7,1},{8,14},{9,15},{10,... | collective-permute-start | bytes 1179656 | tf_op jit(solution)/shard_map/ppermute | solution.py:265
  20.8 0.7 broadcast_select_fusion.2
  21.5 3.5 %collective-permute-start.1 = (s32[2,24]{1,0:T(2,128)S(1)}, s32[2,24]{1,0:T(2,128)S(1)}, u32[]{:S(2)}, u32[]{:S(2)}) collective-permute-start(s32[2,24]{1,0:T(2,128)S(1)} %pad_add_fusion), channel_id=1, source_target_pairs={{8,16},{16,8},{9,17},{17,9},{10,18},{18,10},{11,19},{19,11},{12,20... | collective-permute-start | bytes 584 | tf_op jit(solution)/shard_map/ppermute | solution.py:243
  25.0 2.0 %collective-permute-done.1 = s32[2,24]{1,0:T(2,128)S(1)} collective-permute-done((s32[2,24]{1,0:T(2,128)S(1)}, s32[2,24]{1,0:T(2,128)S(1)}, u32[]{:S(2)}, u32[]{:S(2)}) %collective-permute-start.1) | collective-permute-done | bytes 224 | tf_op jit(solution)/shard_map/ppermute | solution.py:243
  26.9 1.3 %collective-permute-start.2 = (s32[2,24]{1,0:T(2,128)S(1)}, s32[2,24]{1,0:T(2,128)S(1)}, u32[]{:S(2)}, u32[]{:S(2)}) collective-permute-start(s32[2,24]{1,0:T(2,128)S(1)} %collective-permute-done.1), channel_id=1, source_target_pairs={{8,0},{16,24},{9,1},{17,25},{10,2},{18,26},{11,3},{19,27},{12,4},{... | collective-permute-start | bytes 584 | tf_op jit(solution)/shard_map/ppermute | solution.py:244
  28.2 0.8 dynamic_slice.6
  29.5 2.3 %collective-permute-start.14 = (bf16[2048,128]{1,0:T(8,128)(2,1)}, bf16[2048,128]{1,0:T(8,128)(2,1)}, u32[]{:S(2)}, u32[]{:S(2)}) collective-permute-start(bf16[2048,128]{1,0:T(8,128)(2,1)} %vw_ref), channel_id=1, source_target_pairs={{0,8},{8,0},{16,24},{24,16},{1,9},{9,1},{17,25},{25,17},{2,10},{10... | collective-permute-start | bytes 1572872 | tf_op jit(solution)/shard_map/ppermute | solution.py:262
  31.9 1.1 convert_reduce_fusion
  35.4 0.8 broadcast_in_dim.40.start_ref
  36.2 3.5 %collective-permute-start.16 = (bf16[2048,128]{1,0:T(8,128)(2,1)}, bf16[2048,128]{1,0:T(8,128)(2,1)S(1)}, u32[]{:S(2)}, u32[]{:S(2)}) collective-permute-start(bf16[2048,128]{1,0:T(8,128)(2,1)} %vw_ref), channel_id=1, source_target_pairs={{8,16},{16,8},{9,17},{17,9},{10,18},{18,10},{11,19},{19,11},{12,20... | collective-permute-start | bytes 1572872 | tf_op jit(solution)/shard_map/ppermute | solution.py:262
  41.1 3.1 %collective-permute-done.12.kx_ref = bf16[2048,128]{1,0:T(8,128)(2,1)} collective-permute-done((bf16[2048,128]{1,0:T(8,128)(2,1)}, bf16[2048,128]{1,0:T(8,128)(2,1)}, u32[]{:S(2)}, u32[]{:S(2)}) %collective-permute-start.12) | collective-permute-done | bytes 524320 | tf_op jit(solution)/shard_map/ppermute | solution.py:262
  44.2 3.5 %collective-permute-start.13 = (bf16[2048,128]{1,0:T(8,128)(2,1)}, bf16[2048,128]{1,0:T(8,128)(2,1)}, u32[]{:S(2)}, u32[]{:S(2)}) collective-permute-start(bf16[2048,128]{1,0:T(8,128)(2,1)} %collective-permute-done.12.kx_ref), channel_id=1, source_target_pairs={{8,16},{16,8},{9,17},{17,9},{10,18},{18,10},{11,19},{19,11},{12,20... | collective-permute-start | bytes 1572872 | tf_op jit(solution)/shard_map/ppermute | solution.py:262
  47.7 3.9 %collective-permute-done.14.vx_ref = bf16[2048,128]{1,0:T(8,128)(2,1)} collective-permute-done((bf16[2048,128]{1,0:T(8,128)(2,1)}, bf16[2048,128]{1,0:T(8,128)(2,1)}, u32[]{:S(2)}, u32[]{:S(2)}) %collective-permute-start.14) | collective-permute-done | bytes 524320 | tf_op jit(solution)/shard_map/ppermute | solution.py:262
  51.5 3.3 %collective-permute-start.19 = (bf16[2048,128]{1,0:T(8,128)(2,1)}, bf16[2048,128]{1,0:T(8,128)(2,1)}, u32[]{:S(2)}, u32[]{:S(2)}) collective-permute-start(bf16[2048,128]{1,0:T(8,128)(2,1)} %collective-permute-done.14.vx_ref), channel_id=1, source_target_pairs={{8,16},{16,8},{9,17},{17,9},{10,18},{18,10},{11,19},{19,11},{12,20... | collective-permute-start | bytes 1572872 | tf_op jit(solution)/shard_map/ppermute | solution.py:262
  54.9 2.8 %copy-done = bf16[384,8192]{1,0:T(8,128)(2,1)S(1)} copy-done((bf16[384,8192]{1,0:T(8,128)(2,1)S(1)}, bf16[384,8192]{1,0:T(8,128)(2,1)}, u32[]{:S(2)}) %copy-start) | copy-done | bytes 6291480
  57.7 1.0 copy-done.5
  58.7 1.0 copy-done.6
  59.8 2.8 %near.1.refs_9_ = f32[384,256]{1,0:T(8,128)S(1)} custom-call(s32[2]{0:T(128)S(1)} %pad_add_fusion.2.place, bf16[384,8192]{1,0:T(8,128)(2,1)S(1)} %copy-done, bf16[384,8192]{1,0:T(8,128)(2,1)S(1)} %copy-done, bf16[2048,128]{1,0:T(8,128)(2,1)S(1)} %copy-done.5, bf16[2048,128]{1,0:T(8,128)(2,1)S(1)} %copy-done.6, ...), custom_call_target="tpu_custom_call" | custom-call | tf_op jit(solution)/shard_map/near/pallas_call | solution.py:157
  62.7 0.8 copy-done.9
  64.0 1.3 %collective-permute-start.15 = (f32[384,256]{1,0:T(8,128)S(1)}, f32[384,256]{1,0:T(8,128)}, u32[]{:S(2)}, u32[]{:S(2)}) collective-permute-start(f32[384,256]{1,0:T(8,128)S(1)} %near.1.refs_9_), channel_id=1, source_target_pairs={{0,8},{24,16},{1,9},{25,17},{2,10},{26,18},{3,11},{27,19},{4,12},{... | collective-permute-start | bytes 1179656 | tf_op jit(solution)/shard_map/ppermute | solution.py:262
  65.9 0.8 reduce_window_sum.11
  66.6 0.7 sub.18
  67.3 1.0 select_reduce_fusion
  68.3 2.8 %copy-done.1 = bf16[384,8192]{1,0:T(8,128)(2,1)S(1)} copy-done((bf16[384,8192]{1,0:T(8,128)(2,1)S(1)}, bf16[384,8192]{1,0:T(8,128)(2,1)}, u32[]{:S(2)}) %copy-start.1) | copy-done | bytes 6291480
  71.1 1.0 copy-done.8
  72.1 1.0 copy-done.10
  73.2 1.8 %facing.1.refs_11_ = f32[768,256]{1,0:T(8,128)S(1)} custom-call(s32[3]{0:T(128)S(1)} %add_add_fusion.1.place, bf16[384,8192]{1,0:T(8,128)(2,1)S(1)} %copy-done.1, bf16[384,512]{1,0:T(8,128)(2,1)S(1)} %collective-permute-done.3.refs_0_, bf16[384,512]{1,0:T(8,128)(2,1)S(1)} %collective-permute-done.5.refs_1_, ...), custom_call_target="tpu_custom_call" | custom-call | tf_op jit(solution)/shard_map/facing/pallas_call | solution.py:157
  75.0 2.1 %collective-permute-done.15.refs_10_ = f32[384,256]{1,0:T(8,128)} collective-permute-done((f32[384,256]{1,0:T(8,128)S(1)}, f32[384,256]{1,0:T(8,128)}, u32[]{:S(2)}, u32[]{:S(2)}) %collective-permute-start.15) | collective-permute-done | bytes 393248 | tf_op jit(solution)/shard_map/ppermute | solution.py:262
  77.0 3.6 %distant.2.k_in = bf16[768,128]{1,0:T(8,128)(2,1)} custom-call(s32[3]{0:T(128)S(1)} %add_add_fusion.place, bf16[384,8192]{1,0:T(8,128)(2,1)S(1)} %copy-done.1, bf16[384,512]{1,0:T(8,128)(2,1)S(1)} %collective-permute-done.3.refs_0_, bf16[384,512]{1,0:T(8,128)(2,1)S(1)} %collective-permute-done.5.refs_1_, ...), custom_call_target="tpu_custom_call" | custom-call | tf_op jit(solution)/shard_map/distant/pallas_call | solution.py:157
  80.6 3.9 %collective-permute-start.22 = (bf16[768,128]{1,0:T(8,128)(2,1)}, bf16[768,128]{1,0:T(8,128)(2,1)}, u32[]{:S(2)}, u32[]{:S(2)}) collective-permute-start(bf16[768,128]{1,0:T(8,128)(2,1)} %distant.2.k_in), channel_id=1, source_target_pairs={{8,0},{16,24},{9,1},{17,25},{10,2},{18,26},{11,3},{19,27},{12,4},{... | collective-permute-start | bytes 589832 | tf_op jit(solution)/shard_map/ppermute | solution.py:262
  84.5 2.6 %collective-permute-start.17 = (bf16[768,128]{1,0:T(8,128)(2,1)}, bf16[768,128]{1,0:T(8,128)(2,1)}, u32[]{:S(2)}, u32[]{:S(2)}) collective-permute-start(bf16[768,128]{1,0:T(8,128)(2,1)} %distant.2.k_in), channel_id=1, source_target_pairs={{8,16},{16,8},{9,17},{17,9},{10,18},{18,10},{11,19},{19,11},{12,20... | collective-permute-start | bytes 589832 | tf_op jit(solution)/shard_map/ppermute | solution.py:262
  87.1 3.6 %distant.3.v_in = bf16[768,128]{1,0:T(8,128)(2,1)} custom-call(s32[3]{0:T(128)S(1)} %add_add_fusion.place, bf16[384,8192]{1,0:T(8,128)(2,1)S(1)} %copy-done.1, bf16[384,512]{1,0:T(8,128)(2,1)S(1)} %collective-permute-done.3.refs_0_, bf16[384,512]{1,0:T(8,128)(2,1)S(1)} %collective-permute-done.5.refs_1_, ...), custom_call_target="tpu_custom_call" | custom-call | tf_op jit(solution)/shard_map/distant/pallas_call | solution.py:157
  90.7 1.3 %collective-permute-start.23 = (bf16[768,128]{1,0:T(8,128)(2,1)}, bf16[768,128]{1,0:T(8,128)(2,1)S(1)}, u32[]{:S(2)}, u32[]{:S(2)}) collective-permute-start(bf16[768,128]{1,0:T(8,128)(2,1)} %distant.3.v_in), channel_id=1, source_target_pairs={{8,0},{16,24},{9,1},{17,25},{10,2},{18,26},{11,3},{19,27},{12,4},{... | collective-permute-start | bytes 589832 | tf_op jit(solution)/shard_map/ppermute | solution.py:262
  92.0 3.3 %collective-permute-start.20 = (bf16[768,128]{1,0:T(8,128)(2,1)}, bf16[768,128]{1,0:T(8,128)(2,1)S(1)}, u32[]{:S(2)}, u32[]{:S(2)}) collective-permute-start(bf16[768,128]{1,0:T(8,128)(2,1)} %distant.3.v_in), channel_id=1, source_target_pairs={{8,16},{16,8},{9,17},{17,9},{10,18},{18,10},{11,19},{19,11},{12,20... | collective-permute-start | bytes 589832 | tf_op jit(solution)/shard_map/ppermute | solution.py:262
  95.6 1.3 %collective-permute-start.18 = (bf16[768,128]{1,0:T(8,128)(2,1)}, bf16[768,128]{1,0:T(8,128)(2,1)S(1)}, u32[]{:S(2)}, u32[]{:S(2)}) collective-permute-start(bf16[768,128]{1,0:T(8,128)(2,1)} %collective-permute-done.17.k_across), channel_id=1, source_target_pairs={{8,0},{16,24},{9,1},{17,25},{10,2},{18,26},{11,3},{19,27},{12,4},{... | collective-permute-start | bytes 589832 | tf_op jit(solution)/shard_map/ppermute | solution.py:262
  96.9 3.3 %collective-permute-done.20.v_across = bf16[768,128]{1,0:T(8,128)(2,1)S(1)} collective-permute-done((bf16[768,128]{1,0:T(8,128)(2,1)}, bf16[768,128]{1,0:T(8,128)(2,1)S(1)}, u32[]{:S(2)}, u32[]{:S(2)}) %collective-permute-start.20) | collective-permute-done | bytes 196640 | tf_op jit(solution)/shard_map/ppermute | solution.py:262
  100.1 1.5 %collective-permute-start.21 = (bf16[768,128]{1,0:T(8,128)(2,1)S(1)}, bf16[768,128]{1,0:T(8,128)(2,1)S(1)}, u32[]{:S(2)}, u32[]{:S(2)}) collective-permute-start(bf16[768,128]{1,0:T(8,128)(2,1)S(1)} %collective-permute-done.20.v_across), channel_id=1, source_target_pairs={{8,0},{16,24},{9,1},{17,25},{10,2},{18,26},{11,3},{19,27},{12,4},{... | collective-permute-start | bytes 589832 | tf_op jit(solution)/shard_map/ppermute | solution.py:262
  101.7 0.9 copy-done.2
  102.6 1.1 copy-done.4
  103.8 5.1 %attend_own.1 = (f32[8,384,1]{2,1,0:T(8,128)S(1)}, f32[8,384,1]{2,1,0:T(8,128)S(1)}, f32[8,384,128]{2,1,0:T(8,128)S(1)}, bf16[2,192,256]{2,1,0:T(8,128)(2,1)S(1)}) custom-call(s32[2]{0:T(128)S(1)} %pad_add_fusion.1.info, s32[48]{0:T(128)S(1)} %select_n.75.slots, bf16[384,1024]{1,0:T(8,128)(2,1)S(1)} %copy-done.4, s32[384,1]{1,0:T(8,128)S(1)} %copy-done.2, ...), custom_call_target="tpu_custom_call" | custom-call | flops 1207959552 | bytes 3145728 | tf_op jit(solution)/shard_map/attend_own/pallas_call | solution.py:417
  108.9 0.9 copy-done.3
  109.8 6.7 %attend_far.1 = (bf16[384,1024]{1,0:T(8,128)(2,1)}, bf16[4,192,256]{2,1,0:T(8,128)(2,1)}) custom-call(s32[2]{0:T(128)S(1)} %pad_add_fusion.1.info, s32[48]{0:T(128)S(1)} %select_n.75.slots, bf16[384,1024]{1,0:T(8,128)(2,1)S(1)} %copy-done.4, s32[384,1]{1,0:T(8,128)S(1)} %copy-done.3, bf16[768,128]{1,0:T(8,128)(2,1)} %collective-permute-done.17.k_across, ...), custom_call_target="tpu_custom_call" | custom-call | flops 1207959552 | bytes 3145728 | tf_op jit(solution)/shard_map/attend_far/pallas_call | solution.py:432
  (66 shorter events, 5.1 us)
Async XLA Ops:
  0.6 15.9 %collective-permute-start.4 = (bf16[2048,128]{1,0:T(8,128)(2,1)}, bf16[2048,128]{1,0:T(8,128)(2,1)S(1)}, u32[]{:S(2)}, u32[]{:S(2)}) collective-permute-start(bf16[2048,128]{1,0:T(8,128)(2,1)} %kw_ref), channel_id=1, source_target_pairs={{8,16},{16,8},{9,17},{17,9},{10,18},{18,10},{11,19},{19,11},{12,20... | collective-permute-start | bytes 1572872 | tf_op jit(solution)/shard_map/ppermute | solution.py:262
  4.0 12.5 %collective-permute-start.3 = (bf16[384,512]{1,0:T(8,128)(2,1)S(1)}, bf16[384,512]{1,0:T(8,128)(2,1)S(1)}, u32[]{:S(2)}, u32[]{:S(2)}) collective-permute-start(bf16[384,512]{1,0:T(8,128)(2,1)S(1)} %constant_dynamic-slice_fusion), channel_id=1, source_target_pairs={{0,8},{24,16},{1,9},{25,17},{2,10},{26,18},{3,11},{27,19},{4,12},{... | collective-permute-start | bytes 1179656 | tf_op jit(solution)/shard_map/ppermute | solution.py:262
  5.3 15.5 %collective-permute-start = (s32[1,24]{1,0:T(1,128)}, s32[1,24]{1,0:T(1,128)S(1)}, u32[]{:S(2)}, u32[]{:S(2)}) collective-permute-start(s32[1,24]{1,0:T(1,128)} %bitcast.21), channel_id=1, source_target_pairs={{0,8},{8,0},{16,24},{24,16},{1,9},{9,1},{17,25},{25,17},{2,10},{10... | collective-permute-start | bytes 296 | tf_op jit(solution)/shard_map/ppermute | solution.py:240
  16.5 0.8 copy-start.7
  17.3 18.9 %collective-permute-start.10 = (bf16[384,512]{1,0:T(8,128)(2,1)S(1)}, bf16[384,512]{1,0:T(8,128)(2,1)S(1)}, u32[]{:S(2)}, u32[]{:S(2)}) collective-permute-start(bf16[384,512]{1,0:T(8,128)(2,1)S(1)} %collective-permute-done.3.refs_0_), channel_id=1, source_target_pairs={{0,6},{1,7},{2,4},{3,5},{4,2},{5,3},{6,0},{7,1},{8,14},{9,15},{10,... | collective-permute-start | bytes 1179656 | tf_op jit(solution)/shard_map/ppermute | solution.py:265
  19.8 20.0 %collective-permute-start.8 = (bf16[384,512]{1,0:T(8,128)(2,1)S(1)}, bf16[384,512]{1,0:T(8,128)(2,1)S(1)}, u32[]{:S(2)}, u32[]{:S(2)}) collective-permute-start(bf16[384,512]{1,0:T(8,128)(2,1)S(1)} %collective-permute-done.3.refs_0_), channel_id=1, source_target_pairs={{0,4},{1,5},{2,6},{3,7},{4,0},{5,1},{6,2},{7,3},{8,12},{9,13},{10,... | collective-permute-start | bytes 1179656 | tf_op jit(solution)/shard_map/ppermute | solution.py:265
  20.3 19.6 %collective-permute-start.6 = (bf16[384,512]{1,0:T(8,128)(2,1)S(1)}, bf16[384,512]{1,0:T(8,128)(2,1)S(1)}, u32[]{:S(2)}, u32[]{:S(2)}) collective-permute-start(bf16[384,512]{1,0:T(8,128)(2,1)S(1)} %collective-permute-done.3.refs_0_), channel_id=1, source_target_pairs={{0,2},{1,3},{2,0},{3,1},{4,6},{5,7},{6,4},{7,5},{8,10},{9,11},{10,... | collective-permute-start | bytes 1179656 | tf_op jit(solution)/shard_map/ppermute | solution.py:265
  21.5 33.4 %copy-start.13 = (s32[1,24]{1,0:T(1,128)}, s32[1,24]{1,0:T(1,128)S(1)}, u32[]{:S(2)}) copy-start(s32[1,24]{1,0:T(1,128)S(1)} %get-tuple-element.29) | copy-start | bytes 292
  21.5 5.5 %collective-permute-start.1 = (s32[2,24]{1,0:T(2,128)S(1)}, s32[2,24]{1,0:T(2,128)S(1)}, u32[]{:S(2)}, u32[]{:S(2)}) collective-permute-start(s32[2,24]{1,0:T(2,128)S(1)} %pad_add_fusion), channel_id=1, source_target_pairs={{8,16},{16,8},{9,17},{17,9},{10,18},{18,10},{11,19},{19,11},{12,20... | collective-permute-start | bytes 584 | tf_op jit(solution)/shard_map/ppermute | solution.py:243
  26.9 12.8 %copy-start.15 = (s32[2,24]{1,0:T(2,128)}, s32[2,24]{1,0:T(2,128)S(1)}, u32[]{:S(2)}) copy-start(s32[2,24]{1,0:T(2,128)S(1)} %collective-permute-done.1) | copy-start | bytes 580
  26.9 2.6 %collective-permute-start.2 = (s32[2,24]{1,0:T(2,128)S(1)}, s32[2,24]{1,0:T(2,128)S(1)}, u32[]{:S(2)}, u32[]{:S(2)}) collective-permute-start(s32[2,24]{1,0:T(2,128)S(1)} %collective-permute-done.1), channel_id=1, source_target_pairs={{8,0},{16,24},{9,1},{17,25},{10,2},{18,26},{11,3},{19,27},{12,4},{... | collective-permute-start | bytes 584 | tf_op jit(solution)/shard_map/ppermute | solution.py:244
  29.0 15.2 %collective-permute-start.12 = (bf16[2048,128]{1,0:T(8,128)(2,1)}, bf16[2048,128]{1,0:T(8,128)(2,1)}, u32[]{:S(2)}, u32[]{:S(2)}) collective-permute-start(bf16[2048,128]{1,0:T(8,128)(2,1)} %kw_ref), channel_id=1, source_target_pairs={{0,8},{8,0},{16,24},{24,16},{1,9},{9,1},{17,25},{25,17},{2,10},{10... | collective-permute-start | bytes 1572872 | tf_op jit(solution)/shard_map/ppermute | solution.py:262
  29.5 10.2 %copy-start.17 = (s32[2,24]{1,0:T(2,128)}, s32[2,24]{1,0:T(2,128)S(1)}, u32[]{:S(2)}) copy-start(s32[2,24]{1,0:T(2,128)S(1)} %collective-permute-done.2) | copy-start | bytes 580
  29.5 22.0 %collective-permute-start.14 = (bf16[2048,128]{1,0:T(8,128)(2,1)}, bf16[2048,128]{1,0:T(8,128)(2,1)}, u32[]{:S(2)}, u32[]{:S(2)}) collective-permute-start(bf16[2048,128]{1,0:T(8,128)(2,1)} %vw_ref), channel_id=1, source_target_pairs={{0,8},{8,0},{16,24},{24,16},{1,9},{9,1},{17,25},{25,17},{2,10},{10... | collective-permute-start | bytes 1572872 | tf_op jit(solution)/shard_map/ppermute | solution.py:262
  36.2 26.5 %collective-permute-start.16 = (bf16[2048,128]{1,0:T(8,128)(2,1)}, bf16[2048,128]{1,0:T(8,128)(2,1)S(1)}, u32[]{:S(2)}, u32[]{:S(2)}) collective-permute-start(bf16[2048,128]{1,0:T(8,128)(2,1)} %vw_ref), channel_id=1, source_target_pairs={{8,16},{16,8},{9,17},{17,9},{10,18},{18,10},{11,19},{19,11},{12,20... | collective-permute-start | bytes 1572872 | tf_op jit(solution)/shard_map/ppermute | solution.py:262
  39.8 22.8 %collective-permute-start.5 = (bf16[384,512]{1,0:T(8,128)(2,1)S(1)}, bf16[384,512]{1,0:T(8,128)(2,1)S(1)}, u32[]{:S(2)}, u32[]{:S(2)}) collective-permute-start(bf16[384,512]{1,0:T(8,128)(2,1)S(1)} %collective-permute-done.3.refs_0_), channel_id=1, source_target_pairs={{0,1},{1,0},{2,3},{3,2},{4,5},{5,4},{6,7},{7,6},{8,9},{9,8},{10,11... | collective-permute-start | bytes 1179656 | tf_op jit(solution)/shard_map/ppermute | solution.py:265
  39.8 24.1 %collective-permute-start.11 = (bf16[384,512]{1,0:T(8,128)(2,1)S(1)}, bf16[384,512]{1,0:T(8,128)(2,1)S(1)}, u32[]{:S(2)}, u32[]{:S(2)}) collective-permute-start(bf16[384,512]{1,0:T(8,128)(2,1)S(1)} %collective-permute-done.10.refs_6_), channel_id=1, source_target_pairs={{0,1},{1,0},{2,3},{3,2},{4,5},{5,4},{6,7},{7,6},{8,9},{9,8},{10,11... | collective-permute-start | bytes 1179656 | tf_op jit(solution)/shard_map/ppermute | solution.py:265
  44.2 32.8 %collective-permute-start.13 = (bf16[2048,128]{1,0:T(8,128)(2,1)}, bf16[2048,128]{1,0:T(8,128)(2,1)}, u32[]{:S(2)}, u32[]{:S(2)}) collective-permute-start(bf16[2048,128]{1,0:T(8,128)(2,1)} %collective-permute-done.12.kx_ref), channel_id=1, source_target_pairs={{8,16},{16,8},{9,17},{17,9},{10,18},{18,10},{11,19},{19,11},{12,20... | collective-permute-start | bytes 1572872 | tf_op jit(solution)/shard_map/ppermute | solution.py:262
  51.5 35.6 %collective-permute-start.19 = (bf16[2048,128]{1,0:T(8,128)(2,1)}, bf16[2048,128]{1,0:T(8,128)(2,1)}, u32[]{:S(2)}, u32[]{:S(2)}) collective-permute-start(bf16[2048,128]{1,0:T(8,128)(2,1)} %collective-permute-done.14.vx_ref), channel_id=1, source_target_pairs={{8,16},{16,8},{9,17},{17,9},{10,18},{18,10},{11,19},{19,11},{12,20... | collective-permute-start | bytes 1572872 | tf_op jit(solution)/shard_map/ppermute | solution.py:262
  54.9 2.8 %copy-start = (bf16[384,8192]{1,0:T(8,128)(2,1)S(1)}, bf16[384,8192]{1,0:T(8,128)(2,1)}, u32[]{:S(2)}) copy-start(bf16[384,8192]{1,0:T(8,128)(2,1)} %own_ref.7) | copy-start | bytes 18874372
  57.7 1.0 copy-start.5
  58.7 1.0 copy-start.6
  59.8 5.5 %copy-start.14 = (s32[1,24]{1,0:T(1,128)S(1)}, s32[1,24]{1,0:T(1,128)}, u32[]{:S(2)}) copy-start(s32[1,24]{1,0:T(1,128)} %copy-done.13) | copy-start | bytes 292
  59.8 5.5 %copy-start.16 = (s32[2,24]{1,0:T(2,128)S(1)}, s32[2,24]{1,0:T(2,128)}, u32[]{:S(2)}) copy-start(s32[2,24]{1,0:T(2,128)} %copy-done.15) | copy-start | bytes 580
  59.8 5.5 %copy-start.18 = (s32[2,24]{1,0:T(2,128)S(1)}, s32[2,24]{1,0:T(2,128)}, u32[]{:S(2)}) copy-start(s32[2,24]{1,0:T(2,128)} %copy-done.17) | copy-start | bytes 580
  62.6 5.7 %collective-permute-start.9 = (bf16[384,512]{1,0:T(8,128)(2,1)S(1)}, bf16[384,512]{1,0:T(8,128)(2,1)S(1)}, u32[]{:S(2)}, u32[]{:S(2)}) collective-permute-start(bf16[384,512]{1,0:T(8,128)(2,1)S(1)} %collective-permute-done.8.refs_4_), channel_id=1, source_target_pairs={{0,1},{1,0},{2,3},{3,2},{4,5},{5,4},{6,7},{7,6},{8,9},{9,8},{10,11... | collective-permute-start | bytes 1179656 | tf_op jit(solution)/shard_map/ppermute | solution.py:265
  62.7 0.8 copy-start.9
  63.5 4.8 %collective-permute-start.7 = (bf16[384,512]{1,0:T(8,128)(2,1)S(1)}, bf16[384,512]{1,0:T(8,128)(2,1)S(1)}, u32[]{:S(2)}, u32[]{:S(2)}) collective-permute-start(bf16[384,512]{1,0:T(8,128)(2,1)S(1)} %collective-permute-done.6.refs_2_), channel_id=1, source_target_pairs={{0,1},{1,0},{2,3},{3,2},{4,5},{5,4},{6,7},{7,6},{8,9},{9,8},{10,11... | collective-permute-start | bytes 1179656 | tf_op jit(solution)/shard_map/ppermute | solution.py:265
  64.0 13.0 %collective-permute-start.15 = (f32[384,256]{1,0:T(8,128)S(1)}, f32[384,256]{1,0:T(8,128)}, u32[]{:S(2)}, u32[]{:S(2)}) collective-permute-start(f32[384,256]{1,0:T(8,128)S(1)} %near.1.refs_9_), channel_id=1, source_target_pairs={{0,8},{24,16},{1,9},{25,17},{2,10},{26,18},{3,11},{27,19},{4,12},{... | collective-permute-start | bytes 1179656 | tf_op jit(solution)/shard_map/ppermute | solution.py:262
  67.3 9.7 %copy-start.11 = (bf16[128]{0:T(256)(128)(2,1)S(1)}, bf16[128]{0:T(256)(128)(2,1)}, u32[]{:S(2)}) copy-start(bf16[128]{0:T(256)(128)(2,1)} %param.12) | copy-start | bytes 772
  68.3 2.8 %copy-start.1 = (bf16[384,8192]{1,0:T(8,128)(2,1)S(1)}, bf16[384,8192]{1,0:T(8,128)(2,1)}, u32[]{:S(2)}) copy-start(bf16[384,8192]{1,0:T(8,128)(2,1)} %own_ref.7) | copy-start | bytes 18874372
  71.1 1.0 copy-start.8
  72.1 1.0 copy-start.10
  77.0 10.1 %copy-start.12 = (bf16[128]{0:T(256)(128)(2,1)S(1)}, bf16[128]{0:T(256)(128)(2,1)}, u32[]{:S(2)}) copy-start(bf16[128]{0:T(256)(128)(2,1)} %param.13) | copy-start | bytes 772
  80.6 21.1 %collective-permute-start.22 = (bf16[768,128]{1,0:T(8,128)(2,1)}, bf16[768,128]{1,0:T(8,128)(2,1)}, u32[]{:S(2)}, u32[]{:S(2)}) collective-permute-start(bf16[768,128]{1,0:T(8,128)(2,1)} %distant.2.k_in), channel_id=1, source_target_pairs={{8,0},{16,24},{9,1},{17,25},{10,2},{18,26},{11,3},{19,27},{12,4},{... | collective-permute-start | bytes 589832 | tf_op jit(solution)/shard_map/ppermute | solution.py:262
  84.5 11.0 %collective-permute-start.17 = (bf16[768,128]{1,0:T(8,128)(2,1)}, bf16[768,128]{1,0:T(8,128)(2,1)}, u32[]{:S(2)}, u32[]{:S(2)}) collective-permute-start(bf16[768,128]{1,0:T(8,128)(2,1)} %distant.2.k_in), channel_id=1, source_target_pairs={{8,16},{16,8},{9,17},{17,9},{10,18},{18,10},{11,19},{19,11},{12,20... | collective-permute-start | bytes 589832 | tf_op jit(solution)/shard_map/ppermute | solution.py:262
  90.7 11.0 %collective-permute-start.23 = (bf16[768,128]{1,0:T(8,128)(2,1)}, bf16[768,128]{1,0:T(8,128)(2,1)S(1)}, u32[]{:S(2)}, u32[]{:S(2)}) collective-permute-start(bf16[768,128]{1,0:T(8,128)(2,1)} %distant.3.v_in), channel_id=1, source_target_pairs={{8,0},{16,24},{9,1},{17,25},{10,2},{18,26},{11,3},{19,27},{12,4},{... | collective-permute-start | bytes 589832 | tf_op jit(solution)/shard_map/ppermute | solution.py:262
  92.0 8.1 %collective-permute-start.20 = (bf16[768,128]{1,0:T(8,128)(2,1)}, bf16[768,128]{1,0:T(8,128)(2,1)S(1)}, u32[]{:S(2)}, u32[]{:S(2)}) collective-permute-start(bf16[768,128]{1,0:T(8,128)(2,1)} %distant.3.v_in), channel_id=1, source_target_pairs={{8,16},{16,8},{9,17},{17,9},{10,18},{18,10},{11,19},{19,11},{12,20... | collective-permute-start | bytes 589832 | tf_op jit(solution)/shard_map/ppermute | solution.py:262
  95.6 13.3 %collective-permute-start.18 = (bf16[768,128]{1,0:T(8,128)(2,1)}, bf16[768,128]{1,0:T(8,128)(2,1)S(1)}, u32[]{:S(2)}, u32[]{:S(2)}) collective-permute-start(bf16[768,128]{1,0:T(8,128)(2,1)} %collective-permute-done.17.k_across), channel_id=1, source_target_pairs={{8,0},{16,24},{9,1},{17,25},{10,2},{18,26},{11,3},{19,27},{12,4},{... | collective-permute-start | bytes 589832 | tf_op jit(solution)/shard_map/ppermute | solution.py:262
  100.1 8.8 %collective-permute-start.21 = (bf16[768,128]{1,0:T(8,128)(2,1)S(1)}, bf16[768,128]{1,0:T(8,128)(2,1)S(1)}, u32[]{:S(2)}, u32[]{:S(2)}) collective-permute-start(bf16[768,128]{1,0:T(8,128)(2,1)S(1)} %collective-permute-done.20.v_across), channel_id=1, source_target_pairs={{8,0},{16,24},{9,1},{17,25},{10,2},{18,26},{11,3},{19,27},{12,4},{... | collective-permute-start | bytes 589832 | tf_op jit(solution)/shard_map/ppermute | solution.py:262
  101.7 0.9 copy-start.2
  102.6 1.1 copy-start.4
  108.9 0.9 copy-start.3

commit v4 on v3

--- a/solution.py
+++ b/solution.py
@@ -11,8 +11,8 @@
 HD = 128
 PAGE = 16
 NEG = -1e30
-VMEM_LIMIT = 24 * 1024 * 1024
-PROJECT_VMEM = 24 * 1024 * 1024
+VMEM_LIMIT = 48 * 1024 * 1024
+PROJECT_VMEM = 48 * 1024 * 1024
 
 
 def attention_kernel(heads, span, info, slots, q_ref, k_ref, v_ref, start_ref, out_ref, cache_ref, acc, top):
@@ -101,59 +101,91 @@
 PIECES = 8
 
 
-def near_kernel(place, own_ref, near_ref, kw_ref, vw_ref, kx_ref, vx_ref, out_ref):
-    def part(h_ref, key_ref, value_ref):
-        weight = jnp.concatenate([key_ref[...], value_ref[...]], axis=1)
-        return jnp.dot(h_ref[...], weight, preferred_element_type=jnp.float32)
-
-    out_ref[...] = part(own_ref, kw_ref, vw_ref) + part(near_ref, kx_ref, vx_ref)
-
-
-def add_pieces(member, chunk, pieces, w_ref, acc_ref):
+def chunk_of(h_ref, chunk, depth):
+    return h_ref.at[:, pl.ds(pl.multiple_of(chunk * depth, depth), depth)]
+
+
+def add_pieces(member, chunk, pieces, w_ref, acc_ref, held, sems):
     share = pieces[0].shape[1]
     half = PIECES // 2
     for side in range(2):
 
         @pl.when(jnp.bitwise_xor(member // half, side) == lax.rem(chunk, 2))
         def _():
-            total = acc_ref[...]
-            for j in range(side * half, side * half + half):
-                row = lax.rem(jnp.bitwise_xor(member, j), half) * share
-                total += jnp.dot(
-                    pieces[j][...],
-                    w_ref[pl.ds(pl.multiple_of(row, share), share), :],
-                    preferred_element_type=jnp.float32,
-                )
-            acc_ref[...] = total
-
-
-def facing_kernel(place, own_ref, *refs):
+            copies = [
+                pltpu.make_async_copy(pieces[side * half + t], held.at[t], sems.at[t])
+                for t in range(half)
+            ]
+            for copy in copies:
+                copy.start()
+            for t in range(half):
+                row = lax.rem(jnp.bitwise_xor(member, side * half + t), half) * share
+                weight = w_ref[pl.ds(pl.multiple_of(row, share), share), :]
+                copies[t].wait()
+                acc_ref[...] += jnp.dot(held[t], weight, preferred_element_type=jnp.float32)
+
+
+def near_kernel(chained, place, h_ref, k_ref, v_ref, *refs):
+    before = refs[0] if chained else None
+    out_ref, h_buf, w_buf, sems = refs[1:] if chained else refs
+    copies = [
+        pltpu.make_async_copy(k_ref, w_buf.at[:, pl.ds(0, HD)], sems.at[0]),
+        pltpu.make_async_copy(v_ref, w_buf.at[:, pl.ds(HD, HD)], sems.at[1]),
+        pltpu.make_async_copy(chunk_of(h_ref, place[0], h_buf.shape[1]), h_buf, sems.at[2]),
+    ]
+    for copy in copies:
+        copy.start()
+    for copy in copies:
+        copy.wait()
+    part = jnp.dot(h_buf[...], w_buf[...], preferred_element_type=jnp.float32)
+    out_ref[...] = part + before[...] if chained else part
+
+
+def facing_kernel(place, h_ref, k_ref, v_ref, *refs):
     pieces = refs[:PIECES]
-    kw_ref, vw_ref, out_ref, w_ref = refs[PIECES:]
-    span = own_ref.shape[0]
-    w_ref[:, :HD] = kw_ref[...]
-    w_ref[:, HD:] = vw_ref[...]
-    out_ref[:span] = jnp.dot(own_ref[...], w_ref[...], preferred_element_type=jnp.float32)
+    out_ref, h_buf, w_buf, held, sems = refs[PIECES:]
+    span = h_buf.shape[0]
+    copies = [
+        pltpu.make_async_copy(k_ref, w_buf.at[:, pl.ds(0, HD)], sems.at[4]),
+        pltpu.make_async_copy(v_ref, w_buf.at[:, pl.ds(HD, HD)], sems.at[5]),
+        pltpu.make_async_copy(chunk_of(h_ref, place[0], h_buf.shape[1]), h_buf, sems.at[6]),
+    ]
+    for copy in copies:
+        copy.start()
+    for copy in copies:
+        copy.wait()
+    out_ref[:span] = jnp.dot(h_buf[...], w_buf[...], preferred_element_type=jnp.float32)
     out_ref[span:] = jnp.zeros((span, 2 * HD), jnp.float32)
-    add_pieces(place[2], place[0], pieces, w_ref, out_ref.at[pl.ds(span, span)])
-
-
-def distant_kernel(place, own_ref, *refs):
+    add_pieces(place[2], place[0], pieces, w_buf, out_ref.at[pl.ds(span, span)], held, sems)
+
+
+def distant_kernel(place, h_ref, w_ref, near_ref, outer_ref, facing_ref, bias_ref, *refs):
     pieces = refs[:PIECES]
-    w_ref, near_ref, outer_ref, facing_ref, bias_ref, out_ref, acc = refs[PIECES:]
-    span = own_ref.shape[0]
+    out_ref, h_buf, w_buf, held, acc, sems = refs[PIECES:]
+    span = h_buf.shape[0]
+    copies = [
+        pltpu.make_async_copy(w_ref, w_buf, sems.at[4]),
+        pltpu.make_async_copy(chunk_of(h_ref, place[0], h_buf.shape[1]), h_buf, sems.at[5]),
+    ]
+    for copy in copies:
+        copy.start()
     bias = bias_ref[...].astype(jnp.float32)
-    own = jnp.dot(own_ref[...], w_ref[...], preferred_element_type=jnp.float32)
-    own = own + near_ref[...] + facing_ref[:span] + bias
     acc[...] = outer_ref[...] + facing_ref[span:] + bias
-    add_pieces(place[2], place[0], pieces, w_ref, acc)
+    own = near_ref[...] + facing_ref[:span] + bias
+    for copy in copies:
+        copy.wait()
+    own += jnp.dot(h_buf[...], w_buf[...], preferred_element_type=jnp.float32)
     own_at = pl.multiple_of(place[1] * span, span)
     outer_at = pl.multiple_of((1 - place[1]) * span, span)
     out_ref[pl.ds(own_at, span), :] = own.astype(jnp.bfloat16)
+    add_pieces(place[2], place[0], pieces, w_buf, acc, held, sems)
     out_ref[pl.ds(outer_at, span), :] = acc[...].astype(jnp.bfloat16)
 
 
-def call_project(kernel, name, place, operands, in_specs, depth, rows, columns, kind, scratch=()):
+ANY = pl.BlockSpec(memory_space=pl.ANY)
+
+
+def call_project(kernel, name, place, operands, in_specs, rows, columns, kind, scratch):
     return pl.pallas_call(
         kernel,
         grid_spec=pltpu.PrefetchScalarGridSpec(
@@ -175,56 +207,65 @@
     return pl.BlockSpec(shape, lambda k, place: (0, column))
 
 
-def project_near(place, own, key_weight, value_weight, key_swapped, value_swapped):
+def project_near(place, own, key_weight, value_weight, before=None):
     span, depth = own.shape[0], key_weight.shape[0]
-    weights = [key_weight, value_weight, key_swapped, value_swapped]
-    in_specs = [
-        pl.BlockSpec((span, depth), lambda k, place: (0, place[0])),
-        pl.BlockSpec((span, depth), lambda k, place: (0, place[1])),
-    ] + [all_of(w) for w in weights]
-    operands = [own, own] + weights
+    chained = before is not None
     return call_project(
-        near_kernel, "near", place, operands, in_specs, 2 * depth, span, 2 * HD, jnp.float32
+        functools.partial(near_kernel, chained),
+        "near",
+        place,
+        [own, key_weight, value_weight] + [before] * chained,
+        [ANY] * 3 + ([all_of(before)] if chained else []),
+        span,
+        2 * HD,
+        jnp.float32,
+        [
+            pltpu.VMEM((span, depth), jnp.bfloat16),
+            pltpu.VMEM((depth, 2 * HD), jnp.bfloat16),
+            pltpu.SemaphoreType.DMA((3,)),
+        ],
     )
 
 
 def project_facing(place, own, pieces, key_weight, value_weight):
     span, depth = own.shape[0], key_weight.shape[0]
-    others = list(pieces) + [key_weight, value_weight]
-    in_specs = [pl.BlockSpec((span, depth), lambda k, place: (0, place[0]))]
-    in_specs += [all_of(x) for x in others]
     return call_project(
         facing_kernel,
         "facing",
         place,
-        [own] + others,
-        in_specs,
-        depth,
+        [own, key_weight, value_weight] + pieces,
+        [ANY] * (3 + PIECES),
         2 * span,
         2 * HD,
         jnp.float32,
-        [pltpu.VMEM((depth, 2 * HD), jnp.bfloat16)],
+        [
+            pltpu.VMEM((span, depth), jnp.bfloat16),
+            pltpu.VMEM((depth, 2 * HD), jnp.bfloat16),
+            pltpu.VMEM((PIECES // 2,) + pieces[0].shape, jnp.bfloat16),
+            pltpu.SemaphoreType.DMA((7,)),
+        ],
     )
 
 
 def project_distant(place, column, own, pieces, weight, near, outer, facing, bias):
     span, depth = own.shape[0], weight.shape[0]
-    others = list(pieces) + [weight]
     parts = [near, outer, facing]
-    in_specs = [pl.BlockSpec((span, depth), lambda k, place: (0, place[0]))]
-    in_specs += [all_of(x) for x in others] + [all_of(x, column, HD) for x in parts]
-    in_specs.append(all_of(bias))
     return call_project(
         distant_kernel,
         "distant",
         place,
-        [own] + others + parts + [bias],
-        in_specs,
-        depth,
+        [own, weight] + parts + [bias] + pieces,
+        [ANY] * 2 + [all_of(x, column, HD) for x in parts] + [all_of(bias)] + [ANY] * PIECES,
         2 * span,
         HD,
         jnp.bfloat16,
-        [pltpu.VMEM((span, HD), jnp.float32)],
+        [
+            pltpu.VMEM((span, depth), jnp.bfloat16),
+            pltpu.VMEM((depth, HD), jnp.bfloat16),
+            pltpu.VMEM((PIECES // 2,) + pieces[0].shape, jnp.bfloat16),
+            pltpu.VMEM((span, HD), jnp.float32),
+            pltpu.SemaphoreType.DMA((6,)),
+        ],
     )
 
 
@@ -240,15 +281,13 @@
     mate = lax.ppermute(mine, "pre", SWAP)
     even = lax.rem(index, 2) == 0
     pair = jnp.concatenate([jnp.where(even, mine, mate), jnp.where(even, mate, mine)], axis=0)
-    across = lax.ppermute(pair, "pre", ACROSS)
-    far = lax.ppermute(across, "pre", OUTWARD)
-    other = jnp.where((index == 1) | (index == 2), across, far)
+    other = lax.ppermute(pair, "pre", [(p, p ^ 2) for p in range(4)])
     return jnp.concatenate(
         [jnp.where(index < 2, pair, other), jnp.where(index < 2, other, pair)], axis=0
     )
 
 
-def line_of_four(hidden, key_weight, value_weight, key_bias, value_bias):
+def line_of_four(hidden, key_weight, value_weight, key_bias, value_bias, page_owner):
     index = lax.axis_index("pre")
     member = lax.axis_index(("dec", "tp"))
     width = hidden.shape[1]
@@ -267,9 +306,8 @@
     mine = second * (width // 2) + member * share
     cut = send(lax.dynamic_slice_in_dim(hidden, mine, share, axis=1), INWARD)
     key_facing = send(key_weight, ACROSS)
-    cut, key_facing, key_weight, value_weight = lax.optimization_barrier(
-        (cut, key_facing, key_weight, value_weight)
-    )
+    cut, page_owner = lax.optimization_barrier((cut, page_owner))
+    owners = spread_owners(page_owner)
     chips = [cut, trade(cut, 2), trade(cut, 4), trade(cut, 6)]
     value_facing = send(value_weight, ACROSS)
     key_swapped = send(key_weight, SWAP)
@@ -282,9 +320,8 @@
     def place(chunk):
         return jnp.stack([chunk, second, member])
 
-    own_part = project_near(
-        jnp.stack([index, near]), hidden, key_weight, value_weight, key_swapped, value_swapped
-    )
+    own_part = project_near(index[None], hidden, key_weight, value_weight)
+    own_part = project_near(near[None], hidden, key_swapped, value_swapped, own_part)
     outer_part = send(own_part, INWARD)
     faced = project_facing(place(facing), hidden, pieces, key_facing, value_facing)
 
@@ -298,7 +335,7 @@
 
     keys = finish(0, key_distant, key_bias)
     values = finish(1, value_distant, value_bias)
-    return keys, values
+    return keys, values, owners
 
 
 def softmax_step(q, keys, values, allowed, before):
@@ -468,8 +505,7 @@
     info = jnp.stack([index, start[0, 0] // span]).astype(jnp.int32)
     arrays = (hidden, key_weight, value_weight, key_bias, value_bias)
     if n_pre == 4:
-        owners = spread_owners(page_owner)
-        keys, values = line_of_four(*arrays)
+        keys, values, owners = line_of_four(*arrays, page_owner)
     else:
         owners = lax.all_gather(page_owner[:, 0], "pre")
         keys, values = gathered(*arrays)

time: 118 us -> 128 us (1.085)
  waiting for transfers between devices: 23.2 us -> 37.2 us
  Pallas kernels: 23.5 us -> 35.3 us
  local copies, waits for them, and re-layouts: 17.7 us -> 9.36 us
  starting transfers between devices: 43.4 us -> 36.6 us
    ppermute x1, waiting for transfers between devices: 0.01 us -> 19 us  [spread_owners(): mate = lax.ppermute(mine, 'pre', SWAP)]
    pallas_call x4 -> x5, Pallas kernels: 11.8 us -> 21.9 us  [call_project(): pl.pallas_call(kernel, grid_spec=pltpu.PrefetchScalarGridSpec(num_scalar_...]
    unnamed x38 -> x24, local copies, waits for them, and re-layouts: 14.3 us -> 5.98 us
    ppermute x14, waiting for transfers between devices: 20.8 us -> 13.8 us  [send(): return lax.ppermute(x, 'pre', pairs)]
    ppermute x2 -> x1, starting transfers between devices: 4.76 us -> 0.07 us  [spread_owners(): other = lax.ppermute(pair, 'pre', [(p, p ^ 2) for p in range(4)])]
    ppermute x1, starting transfers between devices: 2.73 us -> 0.01 us  [spread_owners(): mate = lax.ppermute(mine, 'pre', SWAP)]
    ppermute x7, starting transfers between devices: 4.58 us -> 6.59 us  [trade(): lax.ppermute(x, ('dec', 'tp'), [(m, m ^ apart) for m in range(PIECES)])]
    ppermute x2 -> x1, waiting for transfers between devices: 2.47 us -> 4.45 us  [spread_owners(): other = lax.ppermute(pair, 'pre', [(p, p ^ 2) for p in range(4)])]
  transfers between devices with their start and end apart: 24 -> 23, of which waited for: 7 -> 5; matrix products, arithmetic and copies ran while one was open for 8% -> 6% of each run, Pallas kernels for 14% -> 22%
where the time goes in v4:
time: 128 us; the launch traced here: 127 us
  waiting for transfers between devices  37.2 us (29%)
  starting transfers between devices  36.6 us (29%)
  Pallas kernels  35.3 us (28%)
  local copies, waits for them, and re-layouts  9.36 us (7%)
  other arithmetic  5.56 us (4%)
  between operations  2.93 us (2%)
    ppermute x14, starting transfers between devices, send(): return lax.ppermute(x, 'pre', pairs)  29.9 us
    pallas_call x5, Pallas kernels, call_project(): pl.pallas_call(kernel, grid_spec=pltpu.PrefetchScalarGridSpec(num_scalar_...  21.9 us
    ppermute x1, waiting for transfers between devices, spread_owners(): mate = lax.ppermute(mine, 'pre', SWAP)  19 us
    ppermute x14, waiting for transfers between devices, send(): return lax.ppermute(x, 'pre', pairs)  13.8 us
    pallas_call x1, Pallas kernels, attention_of_pairs(): pl.pallas_call(functools.partial(far_kernel, heads), in_specs=[smem] * 2...  7.23 us
    ppermute x7, starting transfers between devices, trade(): lax.ppermute(x, ('dec', 'tp'), [(m, m ^ apart) for m in range(PIECES)])  6.59 us
    pallas_call x1, Pallas kernels, attention_of_pairs(): pl.pallas_call(functools.partial(own_kernel, heads), in_specs=[smem] * 2...  6.18 us
    unnamed x24, local copies, waits for them, and re-layouts  5.98 us
  transfers between devices with their start and end apart: 23, of which 5 were waited for; matrix products, arithmetic and copies ran while one was open for 6% of the time, Pallas kernels for 22%

profile of v4, /device:TPU:16, one launch (start us, length us, event | category | flops | bytes accessed | tf_op | source)
XLA Modules:
  0.0 127.0 jit_solution(2982740260697442954)
XLA Ops:
  0.6 1.0 constant_dynamic-slice_fusion
  1.7 1.3 %collective-permute-start = (bf16[384,512]{1,0:T(8,128)(2,1)S(1)}, bf16[384,512]{1,0:T(8,128)(2,1)S(1)}, u32[]{:S(2)}, u32[]{:S(2)}) collective-permute-start(bf16[384,512]{1,0:T(8,128)(2,1)S(1)} %constant_dynamic-slice_fusion), channel_id=1, source_target_pairs={{0,8},{24,16},{1,9},{25,17},{2,10},{26,18},{3,11},{27,19},{4,12},{... | collective-permute-start | bytes 1179656 | tf_op jit(solution)/shard_map/ppermute | solution.py:301
  3.0 2.7 %collective-permute-start.3 = (bf16[2048,128]{1,0:T(8,128)(2,1)}, bf16[2048,128]{1,0:T(8,128)(2,1)}, u32[]{:S(2)}, u32[]{:S(2)}) collective-permute-start(bf16[2048,128]{1,0:T(8,128)(2,1)} %k_ref.1), channel_id=1, source_target_pairs={{0,8},{8,0},{16,24},{24,16},{1,9},{9,1},{17,25},{25,17},{2,10},{10... | collective-permute-start | bytes 1572872 | tf_op jit(solution)/shard_map/ppermute | solution.py:301
  5.7 2.3 %collective-permute-start.7 = (bf16[2048,128]{1,0:T(8,128)(2,1)}, bf16[2048,128]{1,0:T(8,128)(2,1)S(1)}, u32[]{:S(2)}, u32[]{:S(2)}) collective-permute-start(bf16[2048,128]{1,0:T(8,128)(2,1)} %k_ref.1), channel_id=1, source_target_pairs={{8,16},{16,8},{9,17},{17,9},{10,18},{18,10},{11,19},{19,11},{12,20... | collective-permute-start | bytes 1572872 | tf_op jit(solution)/shard_map/ppermute | solution.py:301
  8.1 7.4 %collective-permute-done.refs_0_ = bf16[384,512]{1,0:T(8,128)(2,1)S(1)} collective-permute-done((bf16[384,512]{1,0:T(8,128)(2,1)S(1)}, bf16[384,512]{1,0:T(8,128)(2,1)S(1)}, u32[]{:S(2)}, u32[]{:S(2)}) %collective-permute-start) | collective-permute-done | bytes 393248 | tf_op jit(solution)/shard_map/ppermute | solution.py:301
  15.6 2.4 %collective-permute-start.14 = (bf16[384,512]{1,0:T(8,128)(2,1)S(1)}, bf16[384,512]{1,0:T(8,128)(2,1)S(1)}, u32[]{:S(2)}, u32[]{:S(2)}) collective-permute-start(bf16[384,512]{1,0:T(8,128)(2,1)S(1)} %collective-permute-done.refs_0_), channel_id=1, source_target_pairs={{0,6},{1,7},{2,4},{3,5},{4,2},{5,3},{6,0},{7,1},{8,14},{9,15},{10,... | collective-permute-start | bytes 1179656 | tf_op jit(solution)/shard_map/ppermute | solution.py:304
  18.0 19.0 %collective-permute-done.1 = s32[1,24]{1,0:T(1,128)S(1)} collective-permute-done((s32[1,24]{1,0:T(1,128)}, s32[1,24]{1,0:T(1,128)S(1)}, u32[]{:S(2)}, u32[]{:S(2)}) %collective-permute-start.1) | collective-permute-done | bytes 128 | tf_op jit(solution)/shard_map/ppermute | solution.py:281
  37.0 0.7 broadcast_select_fusion.1
  37.8 4.5 %collective-permute-done.2 = s32[2,24]{1,0:T(2,128)S(1)} collective-permute-done((s32[2,24]{1,0:T(2,128)S(1)}, s32[2,24]{1,0:T(2,128)S(1)}, u32[]{:S(2)}, u32[]{:S(2)}) %collective-permute-start.2) | collective-permute-done | bytes 224 | tf_op jit(solution)/shard_map/ppermute | solution.py:284
  42.2 2.3 %collective-permute-start.8 = (bf16[2048,128]{1,0:T(8,128)(2,1)}, bf16[2048,128]{1,0:T(8,128)(2,1)}, u32[]{:S(2)}, u32[]{:S(2)}) collective-permute-start(bf16[2048,128]{1,0:T(8,128)(2,1)} %v_ref.1), channel_id=1, source_target_pairs={{8,16},{16,8},{9,17},{17,9},{10,18},{18,10},{11,19},{19,11},{12,20... | collective-permute-start | bytes 1572872 | tf_op jit(solution)/shard_map/ppermute | solution.py:301
  44.6 0.8 dynamic_slice.6
  45.4 1.6 %collective-permute-start.12 = (bf16[384,512]{1,0:T(8,128)(2,1)S(1)}, bf16[384,512]{1,0:T(8,128)(2,1)S(1)}, u32[]{:S(2)}, u32[]{:S(2)}) collective-permute-start(bf16[384,512]{1,0:T(8,128)(2,1)S(1)} %collective-permute-done.refs_0_), channel_id=1, source_target_pairs={{0,4},{1,5},{2,6},{3,7},{4,0},{5,1},{6,2},{7,3},{8,12},{9,13},{10,... | collective-permute-start | bytes 1179656 | tf_op jit(solution)/shard_map/ppermute | solution.py:304
  46.9 1.1 convert_reduce_fusion
  48.0 0.5 slice.11
  50.5 0.8 broadcast_in_dim.45.start_ref
  51.3 1.0 copy-done.4
  52.3 1.0 copy-done.5
  53.4 2.2 %near.2.refs_0_ = f32[384,256]{1,0:T(8,128)S(1)} custom-call(s32[1]{0:T(128)} %bitcast.place, bf16[384,8192]{1,0:T(8,128)(2,1)} %h_ref.9, bf16[2048,128]{1,0:T(8,128)(2,1)S(1)} %copy-done.4, bf16[2048,128]{1,0:T(8,128)(2,1)S(1)} %copy-done.5), custom_call_target="tpu_custom_call" | custom-call | tf_op jit(solution)/shard_map/near/pallas_call | solution.py:189
  55.6 0.8 copy-done.2
  56.4 1.5 %collective-permute-start.10 = (bf16[384,512]{1,0:T(8,128)(2,1)S(1)}, bf16[384,512]{1,0:T(8,128)(2,1)S(1)}, u32[]{:S(2)}, u32[]{:S(2)}) collective-permute-start(bf16[384,512]{1,0:T(8,128)(2,1)S(1)} %collective-permute-done.refs_0_), channel_id=1, source_target_pairs={{0,2},{1,3},{2,0},{3,1},{4,6},{5,7},{6,4},{7,5},{8,10},{9,11},{10,... | collective-permute-start | bytes 1179656 | tf_op jit(solution)/shard_map/ppermute | solution.py:304
  57.9 0.5 collective-permute-start.15
  58.5 0.6 multiply_add_fusion
  59.1 3.5 %collective-permute-start.4 = (bf16[2048,128]{1,0:T(8,128)(2,1)}, bf16[2048,128]{1,0:T(8,128)(2,1)}, u32[]{:S(2)}, u32[]{:S(2)}) collective-permute-start(bf16[2048,128]{1,0:T(8,128)(2,1)} %collective-permute-done.3.k_ref), channel_id=1, source_target_pairs={{8,16},{16,8},{9,17},{17,9},{10,18},{18,10},{11,19},{19,11},{12,20... | collective-permute-start | bytes 1572872 | tf_op jit(solution)/shard_map/ppermute | solution.py:301
  62.6 2.4 %collective-permute-start.18 = (bf16[2048,128]{1,0:T(8,128)(2,1)}, bf16[2048,128]{1,0:T(8,128)(2,1)}, u32[]{:S(2)}, u32[]{:S(2)}) collective-permute-start(bf16[2048,128]{1,0:T(8,128)(2,1)} %collective-permute-done.5.v_ref), channel_id=1, source_target_pairs={{8,16},{16,8},{9,17},{17,9},{10,18},{18,10},{11,19},{19,11},{12,20... | collective-permute-start | bytes 1572872 | tf_op jit(solution)/shard_map/ppermute | solution.py:301
  65.1 2.3 %near.3.near_ref = f32[384,256]{1,0:T(8,128)S(1)} custom-call(s32[1]{0:T(128)} %bitcast.10.place, bf16[384,8192]{1,0:T(8,128)(2,1)} %h_ref.9, bf16[2048,128]{1,0:T(8,128)(2,1)} %collective-permute-done.3.k_ref, bf16[2048,128]{1,0:T(8,128)(2,1)} %collective-permute-done.5.v_ref, f32[384,256]{1,0:T(8,128)S(1)} %near.2.refs_0_), custom_call_target="tpu_custom_call" | custom-call | tf_op jit(solution)/shard_map/near/pallas_call | solution.py:189
  67.4 1.3 %collective-permute-start.6 = (f32[384,256]{1,0:T(8,128)S(1)}, f32[384,256]{1,0:T(8,128)}, u32[]{:S(2)}, u32[]{:S(2)}) collective-permute-start(f32[384,256]{1,0:T(8,128)S(1)} %near.3.near_ref), channel_id=1, source_target_pairs={{0,8},{24,16},{1,9},{25,17},{2,10},{26,18},{3,11},{27,19},{4,12},{... | collective-permute-start | bytes 1179656 | tf_op jit(solution)/shard_map/ppermute | solution.py:301
  68.8 0.5 collective-permute-start.11
  69.3 0.5 broadcast_compare_fusion
  69.9 0.8 reduce_window_sum.11
  70.6 0.7 sub.18
  71.3 1.0 select_reduce_fusion
  72.3 1.0 copy-done.3
  73.3 4.8 %facing.1.facing_ref = f32[768,256]{1,0:T(8,128)S(1)} custom-call(s32[3]{0:T(128)S(1)} %add_add_fusion.1.place, bf16[384,8192]{1,0:T(8,128)(2,1)} %h_ref.9, bf16[2048,128]{1,0:T(8,128)(2,1)S(1)} %copy-done.3, bf16[2048,128]{1,0:T(8,128)(2,1)} %collective-permute-done.8.v_ref, bf16[384,512]{1,0:T(8,128)(2,1)S(1)} %collective-permute-done.refs_0_, ...), custom_call_target="tpu_custom_call" | custom-call | tf_op jit(solution)/shard_map/facing/pallas_call | solution.py:189
  78.1 1.8 %collective-permute-done.6.outer_ref = f32[384,256]{1,0:T(8,128)} collective-permute-done((f32[384,256]{1,0:T(8,128)S(1)}, f32[384,256]{1,0:T(8,128)}, u32[]{:S(2)}, u32[]{:S(2)}) %collective-permute-start.6) | collective-permute-done | bytes 393248 | tf_op jit(solution)/shard_map/ppermute | solution.py:301
  80.0 6.3 %distant.2.k_in = bf16[768,128]{1,0:T(8,128)(2,1)} custom-call(s32[3]{0:T(128)S(1)} %add_add_fusion.place, bf16[384,8192]{1,0:T(8,128)(2,1)} %h_ref.9, bf16[2048,128]{1,0:T(8,128)(2,1)} %collective-permute-done.4.w_ref, f32[384,256]{1,0:T(8,128)S(1)} %near.3.near_ref, f32[384,256]{1,0:T(8,128)} %collective-permute-done.6.outer_ref, ...), custom_call_target="tpu_custom_call" | custom-call | tf_op jit(solution)/shard_map/distant/pallas_call | solution.py:189
  86.3 4.1 %collective-permute-start.21 = (bf16[768,128]{1,0:T(8,128)(2,1)}, bf16[768,128]{1,0:T(8,128)(2,1)}, u32[]{:S(2)}, u32[]{:S(2)}) collective-permute-start(bf16[768,128]{1,0:T(8,128)(2,1)} %distant.2.k_in), channel_id=1, source_target_pairs={{8,0},{16,24},{9,1},{17,25},{10,2},{18,26},{11,3},{19,27},{12,4},{... | collective-permute-start | bytes 589832 | tf_op jit(solution)/shard_map/ppermute | solution.py:301
  90.4 3.5 %collective-permute-start.16 = (bf16[768,128]{1,0:T(8,128)(2,1)}, bf16[768,128]{1,0:T(8,128)(2,1)}, u32[]{:S(2)}, u32[]{:S(2)}) collective-permute-start(bf16[768,128]{1,0:T(8,128)(2,1)} %distant.2.k_in), channel_id=1, source_target_pairs={{8,16},{16,8},{9,17},{17,9},{10,18},{18,10},{11,19},{19,11},{12,20... | collective-permute-start | bytes 589832 | tf_op jit(solution)/shard_map/ppermute | solution.py:301
  93.9 6.3 %distant.3.v_in = bf16[768,128]{1,0:T(8,128)(2,1)} custom-call(s32[3]{0:T(128)S(1)} %add_add_fusion.place, bf16[384,8192]{1,0:T(8,128)(2,1)} %h_ref.9, bf16[2048,128]{1,0:T(8,128)(2,1)} %collective-permute-done.18.w_ref, f32[384,256]{1,0:T(8,128)S(1)} %near.3.near_ref, f32[384,256]{1,0:T(8,128)} %collective-permute-done.6.outer_ref, ...), custom_call_target="tpu_custom_call" | custom-call | tf_op jit(solution)/shard_map/distant/pallas_call | solution.py:189
  100.2 1.3 %collective-permute-start.22 = (bf16[768,128]{1,0:T(8,128)(2,1)}, bf16[768,128]{1,0:T(8,128)(2,1)S(1)}, u32[]{:S(2)}, u32[]{:S(2)}) collective-permute-start(bf16[768,128]{1,0:T(8,128)(2,1)} %distant.3.v_in), channel_id=1, source_target_pairs={{8,0},{16,24},{9,1},{17,25},{10,2},{18,26},{11,3},{19,27},{12,4},{... | collective-permute-start | bytes 589832 | tf_op jit(solution)/shard_map/ppermute | solution.py:301
  101.5 2.4 %collective-permute-start.19 = (bf16[768,128]{1,0:T(8,128)(2,1)}, bf16[768,128]{1,0:T(8,128)(2,1)S(1)}, u32[]{:S(2)}, u32[]{:S(2)}) collective-permute-start(bf16[768,128]{1,0:T(8,128)(2,1)} %distant.3.v_in), channel_id=1, source_target_pairs={{8,16},{16,8},{9,17},{17,9},{10,18},{18,10},{11,19},{19,11},{12,20... | collective-permute-start | bytes 589832 | tf_op jit(solution)/shard_map/ppermute | solution.py:301
  104.0 0.1 copy.12
  104.2 1.3 %collective-permute-start.17 = (bf16[768,128]{1,0:T(8,128)(2,1)}, bf16[768,128]{1,0:T(8,128)(2,1)S(1)}, u32[]{:S(2)}, u32[]{:S(2)}) collective-permute-start(bf16[768,128]{1,0:T(8,128)(2,1)} %collective-permute-done.16.k_across), channel_id=1, source_target_pairs={{8,0},{16,24},{9,1},{17,25},{10,2},{18,26},{11,3},{19,27},{12,4},{... | collective-permute-start | bytes 589832 | tf_op jit(solution)/shard_map/ppermute | solution.py:301
  105.5 4.5 %collective-permute-done.19.v_across = bf16[768,128]{1,0:T(8,128)(2,1)S(1)} collective-permute-done((bf16[768,128]{1,0:T(8,128)(2,1)}, bf16[768,128]{1,0:T(8,128)(2,1)S(1)}, u32[]{:S(2)}, u32[]{:S(2)}) %collective-permute-start.19) | collective-permute-done | bytes 196640 | tf_op jit(solution)/shard_map/ppermute | solution.py:301
  110.0 1.5 %collective-permute-start.20 = (bf16[768,128]{1,0:T(8,128)(2,1)S(1)}, bf16[768,128]{1,0:T(8,128)(2,1)S(1)}, u32[]{:S(2)}, u32[]{:S(2)}) collective-permute-start(bf16[768,128]{1,0:T(8,128)(2,1)S(1)} %collective-permute-done.19.v_across), channel_id=1, source_target_pairs={{8,0},{16,24},{9,1},{17,25},{10,2},{18,26},{11,3},{19,27},{12,4},{... | collective-permute-start | bytes 589832 | tf_op jit(solution)/shard_map/ppermute | solution.py:301
  111.6 0.9 copy-done
  112.5 1.1 copy-done.1
  113.6 6.2 %attend_own.1 = (f32[8,384,1]{2,1,0:T(8,128)S(1)}, f32[8,384,1]{2,1,0:T(8,128)S(1)}, f32[8,384,128]{2,1,0:T(8,128)}, bf16[2,192,256]{2,1,0:T(8,128)(2,1)S(1)}) custom-call(s32[2]{0:T(128)S(1)} %pad_add_fusion.1.info, s32[48]{0:T(128)S(1)} %select_n.68.slots, bf16[384,1024]{1,0:T(8,128)(2,1)S(1)} %copy-done.1, s32[384,1]{1,0:T(8,128)S(1)} %copy-done, ...), custom_call_target="tpu_custom_call" | custom-call | flops 1207959552 | bytes 3145728 | tf_op jit(solution)/shard_map/attend_own/pallas_call | solution.py:454
  119.8 7.2 %attend_far.1 = (bf16[384,1024]{1,0:T(8,128)(2,1)}, bf16[4,192,256]{2,1,0:T(8,128)(2,1)}) custom-call(s32[2]{0:T(128)S(1)} %pad_add_fusion.1.info, s32[48]{0:T(128)S(1)} %select_n.68.slots, bf16[384,1024]{1,0:T(8,128)(2,1)S(1)} %copy-done.1, s32[384,1]{1,0:T(8,128)S(1)} %copy-done, bf16[768,128]{1,0:T(8,128)(2,1)} %collective-permute-done.16.k_across, ...), custom_call_target="tpu_custom_call" | custom-call | flops 1207959552 | bytes 3145728 | tf_op jit(solution)/shard_map/attend_far/pallas_call | solution.py:469
  (50 shorter events, 0.8 us)
Async XLA Ops:
  1.7 13.9 %collective-permute-start = (bf16[384,512]{1,0:T(8,128)(2,1)S(1)}, bf16[384,512]{1,0:T(8,128)(2,1)S(1)}, u32[]{:S(2)}, u32[]{:S(2)}) collective-permute-start(bf16[384,512]{1,0:T(8,128)(2,1)S(1)} %constant_dynamic-slice_fusion), channel_id=1, source_target_pairs={{0,8},{24,16},{1,9},{25,17},{2,10},{26,18},{3,11},{27,19},{4,12},{... | collective-permute-start | bytes 1179656 | tf_op jit(solution)/shard_map/ppermute | solution.py:301
  3.0 42.4 %collective-permute-start.3 = (bf16[2048,128]{1,0:T(8,128)(2,1)}, bf16[2048,128]{1,0:T(8,128)(2,1)}, u32[]{:S(2)}, u32[]{:S(2)}) collective-permute-start(bf16[2048,128]{1,0:T(8,128)(2,1)} %k_ref.1), channel_id=1, source_target_pairs={{0,8},{8,0},{16,24},{24,16},{1,9},{9,1},{17,25},{25,17},{2,10},{10... | collective-permute-start | bytes 1572872 | tf_op jit(solution)/shard_map/ppermute | solution.py:301
  5.7 49.9 %collective-permute-start.7 = (bf16[2048,128]{1,0:T(8,128)(2,1)}, bf16[2048,128]{1,0:T(8,128)(2,1)S(1)}, u32[]{:S(2)}, u32[]{:S(2)}) collective-permute-start(bf16[2048,128]{1,0:T(8,128)(2,1)} %k_ref.1), channel_id=1, source_target_pairs={{8,16},{16,8},{9,17},{17,9},{10,18},{18,10},{11,19},{19,11},{12,20... | collective-permute-start | bytes 1572872 | tf_op jit(solution)/shard_map/ppermute | solution.py:301
  8.1 49.8 %collective-permute-start.5 = (bf16[2048,128]{1,0:T(8,128)(2,1)}, bf16[2048,128]{1,0:T(8,128)(2,1)}, u32[]{:S(2)}, u32[]{:S(2)}) collective-permute-start(bf16[2048,128]{1,0:T(8,128)(2,1)} %v_ref.1), channel_id=1, source_target_pairs={{0,8},{8,0},{16,24},{24,16},{1,9},{9,1},{17,25},{25,17},{2,10},{10... | collective-permute-start | bytes 1572872 | tf_op jit(solution)/shard_map/ppermute | solution.py:301
  15.6 21.4 %collective-permute-start.1 = (s32[1,24]{1,0:T(1,128)}, s32[1,24]{1,0:T(1,128)S(1)}, u32[]{:S(2)}, u32[]{:S(2)}) collective-permute-start(s32[1,24]{1,0:T(1,128)} %bitcast.21), channel_id=1, source_target_pairs={{0,8},{8,0},{16,24},{24,16},{1,9},{9,1},{17,25},{25,17},{2,10},{10... | collective-permute-start | bytes 296 | tf_op jit(solution)/shard_map/ppermute | solution.py:281
  15.6 42.3 %collective-permute-start.14 = (bf16[384,512]{1,0:T(8,128)(2,1)S(1)}, bf16[384,512]{1,0:T(8,128)(2,1)S(1)}, u32[]{:S(2)}, u32[]{:S(2)}) collective-permute-start(bf16[384,512]{1,0:T(8,128)(2,1)S(1)} %collective-permute-done.refs_0_), channel_id=1, source_target_pairs={{0,6},{1,7},{2,4},{3,5},{4,2},{5,3},{6,0},{7,1},{8,14},{9,15},{10,... | collective-permute-start | bytes 1179656 | tf_op jit(solution)/shard_map/ppermute | solution.py:304
  37.7 7.7 %copy-start.8 = (s32[1,24]{1,0:T(1,128)}, s32[1,24]{1,0:T(1,128)S(1)}, u32[]{:S(2)}) copy-start(s32[1,24]{1,0:T(1,128)S(1)} %get-tuple-element.25) | copy-start | bytes 292
  37.7 4.5 %collective-permute-start.2 = (s32[2,24]{1,0:T(2,128)S(1)}, s32[2,24]{1,0:T(2,128)S(1)}, u32[]{:S(2)}, u32[]{:S(2)}) collective-permute-start(s32[2,24]{1,0:T(2,128)S(1)} %pad_add_fusion), channel_id=1, source_target_pairs={{0,16},{8,24},{16,0},{24,8},{1,17},{9,25},{17,1},{25,9},{2,18},{10... | collective-permute-start | bytes 584 | tf_op jit(solution)/shard_map/ppermute | solution.py:284
  42.2 3.1 %copy-start.10 = (s32[2,24]{1,0:T(2,128)}, s32[2,24]{1,0:T(2,128)S(1)}, u32[]{:S(2)}) copy-start(s32[2,24]{1,0:T(2,128)S(1)} %collective-permute-done.2) | copy-start | bytes 580
  42.2 16.9 %collective-permute-start.8 = (bf16[2048,128]{1,0:T(8,128)(2,1)}, bf16[2048,128]{1,0:T(8,128)(2,1)}, u32[]{:S(2)}, u32[]{:S(2)}) collective-permute-start(bf16[2048,128]{1,0:T(8,128)(2,1)} %v_ref.1), channel_id=1, source_target_pairs={{8,16},{16,8},{9,17},{17,9},{10,18},{18,10},{11,19},{19,11},{12,20... | collective-permute-start | bytes 1572872 | tf_op jit(solution)/shard_map/ppermute | solution.py:301
  45.4 17.3 %collective-permute-start.12 = (bf16[384,512]{1,0:T(8,128)(2,1)S(1)}, bf16[384,512]{1,0:T(8,128)(2,1)S(1)}, u32[]{:S(2)}, u32[]{:S(2)}) collective-permute-start(bf16[384,512]{1,0:T(8,128)(2,1)S(1)} %collective-permute-done.refs_0_), channel_id=1, source_target_pairs={{0,4},{1,5},{2,6},{3,7},{4,0},{5,1},{6,2},{7,3},{8,12},{9,13},{10,... | collective-permute-start | bytes 1179656 | tf_op jit(solution)/shard_map/ppermute | solution.py:304
  51.3 1.0 copy-start.4
  52.3 1.0 copy-start.5
  55.6 0.8 copy-start.2
  56.4 11.0 %collective-permute-start.10 = (bf16[384,512]{1,0:T(8,128)(2,1)S(1)}, bf16[384,512]{1,0:T(8,128)(2,1)S(1)}, u32[]{:S(2)}, u32[]{:S(2)}) collective-permute-start(bf16[384,512]{1,0:T(8,128)(2,1)S(1)} %collective-permute-done.refs_0_), channel_id=1, source_target_pairs={{0,2},{1,3},{2,0},{3,1},{4,6},{5,7},{6,4},{7,5},{8,10},{9,11},{10,... | collective-permute-start | bytes 1179656 | tf_op jit(solution)/shard_map/ppermute | solution.py:304
  57.9 10.9 %collective-permute-start.9 = (bf16[384,512]{1,0:T(8,128)(2,1)S(1)}, bf16[384,512]{1,0:T(8,128)(2,1)S(1)}, u32[]{:S(2)}, u32[]{:S(2)}) collective-permute-start(bf16[384,512]{1,0:T(8,128)(2,1)S(1)} %collective-permute-done.refs_0_), channel_id=1, source_target_pairs={{0,1},{1,0},{2,3},{3,2},{4,5},{5,4},{6,7},{7,6},{8,9},{9,8},{10,11... | collective-permute-start | bytes 1179656 | tf_op jit(solution)/shard_map/ppermute | solution.py:304
  57.9 10.9 %collective-permute-start.15 = (bf16[384,512]{1,0:T(8,128)(2,1)S(1)}, bf16[384,512]{1,0:T(8,128)(2,1)S(1)}, u32[]{:S(2)}, u32[]{:S(2)}) collective-permute-start(bf16[384,512]{1,0:T(8,128)(2,1)S(1)} %collective-permute-done.14.refs_6_), channel_id=1, source_target_pairs={{0,1},{1,0},{2,3},{3,2},{4,5},{5,4},{6,7},{7,6},{8,9},{9,8},{10,11... | collective-permute-start | bytes 1179656 | tf_op jit(solution)/shard_map/ppermute | solution.py:304
  59.1 20.8 %collective-permute-start.4 = (bf16[2048,128]{1,0:T(8,128)(2,1)}, bf16[2048,128]{1,0:T(8,128)(2,1)}, u32[]{:S(2)}, u32[]{:S(2)}) collective-permute-start(bf16[2048,128]{1,0:T(8,128)(2,1)} %collective-permute-done.3.k_ref), channel_id=1, source_target_pairs={{8,16},{16,8},{9,17},{17,9},{10,18},{18,10},{11,19},{19,11},{12,20... | collective-permute-start | bytes 1572872 | tf_op jit(solution)/shard_map/ppermute | solution.py:301
  62.6 31.3 %collective-permute-start.18 = (bf16[2048,128]{1,0:T(8,128)(2,1)}, bf16[2048,128]{1,0:T(8,128)(2,1)}, u32[]{:S(2)}, u32[]{:S(2)}) collective-permute-start(bf16[2048,128]{1,0:T(8,128)(2,1)} %collective-permute-done.5.v_ref), channel_id=1, source_target_pairs={{8,16},{16,8},{9,17},{17,9},{10,18},{18,10},{11,19},{19,11},{12,20... | collective-permute-start | bytes 1572872 | tf_op jit(solution)/shard_map/ppermute | solution.py:301
  65.1 4.3 %copy-start.9 = (s32[1,24]{1,0:T(1,128)S(1)}, s32[1,24]{1,0:T(1,128)}, u32[]{:S(2)}) copy-start(s32[1,24]{1,0:T(1,128)} %copy-done.8) | copy-start | bytes 292
  65.1 4.3 %copy-start.11 = (s32[2,24]{1,0:T(2,128)S(1)}, s32[2,24]{1,0:T(2,128)}, u32[]{:S(2)}) copy-start(s32[2,24]{1,0:T(2,128)} %copy-done.10) | copy-start | bytes 580
  67.4 12.5 %collective-permute-start.6 = (f32[384,256]{1,0:T(8,128)S(1)}, f32[384,256]{1,0:T(8,128)}, u32[]{:S(2)}, u32[]{:S(2)}) collective-permute-start(f32[384,256]{1,0:T(8,128)S(1)} %near.3.near_ref), channel_id=1, source_target_pairs={{0,8},{24,16},{1,9},{25,17},{2,10},{26,18},{3,11},{27,19},{4,12},{... | collective-permute-start | bytes 1179656 | tf_op jit(solution)/shard_map/ppermute | solution.py:301
  68.7 3.5 %collective-permute-start.13 = (bf16[384,512]{1,0:T(8,128)(2,1)S(1)}, bf16[384,512]{1,0:T(8,128)(2,1)S(1)}, u32[]{:S(2)}, u32[]{:S(2)}) collective-permute-start(bf16[384,512]{1,0:T(8,128)(2,1)S(1)} %collective-permute-done.12.refs_4_), channel_id=1, source_target_pairs={{0,1},{1,0},{2,3},{3,2},{4,5},{5,4},{6,7},{7,6},{8,9},{9,8},{10,11... | collective-permute-start | bytes 1179656 | tf_op jit(solution)/shard_map/ppermute | solution.py:304
  68.8 3.5 %collective-permute-start.11 = (bf16[384,512]{1,0:T(8,128)(2,1)S(1)}, bf16[384,512]{1,0:T(8,128)(2,1)S(1)}, u32[]{:S(2)}, u32[]{:S(2)}) collective-permute-start(bf16[384,512]{1,0:T(8,128)(2,1)S(1)} %collective-permute-done.10.refs_2_), channel_id=1, source_target_pairs={{0,1},{1,0},{2,3},{3,2},{4,5},{5,4},{6,7},{7,6},{8,9},{9,8},{10,11... | collective-permute-start | bytes 1179656 | tf_op jit(solution)/shard_map/ppermute | solution.py:304
  71.3 8.7 %copy-start.6 = (bf16[128]{0:T(256)(128)(2,1)S(1)}, bf16[128]{0:T(256)(128)(2,1)}, u32[]{:S(2)}) copy-start(bf16[128]{0:T(256)(128)(2,1)} %param.12) | copy-start | bytes 772
  72.3 1.0 copy-start.3
  80.0 13.9 %copy-start.7 = (bf16[128]{0:T(256)(128)(2,1)S(1)}, bf16[128]{0:T(256)(128)(2,1)}, u32[]{:S(2)}) copy-start(bf16[128]{0:T(256)(128)(2,1)} %param.13) | copy-start | bytes 772
  86.3 25.3 %collective-permute-start.21 = (bf16[768,128]{1,0:T(8,128)(2,1)}, bf16[768,128]{1,0:T(8,128)(2,1)}, u32[]{:S(2)}, u32[]{:S(2)}) collective-permute-start(bf16[768,128]{1,0:T(8,128)(2,1)} %distant.2.k_in), channel_id=1, source_target_pairs={{8,0},{16,24},{9,1},{17,25},{10,2},{18,26},{11,3},{19,27},{12,4},{... | collective-permute-start | bytes 589832 | tf_op jit(solution)/shard_map/ppermute | solution.py:301
  90.4 13.8 %collective-permute-start.16 = (bf16[768,128]{1,0:T(8,128)(2,1)}, bf16[768,128]{1,0:T(8,128)(2,1)}, u32[]{:S(2)}, u32[]{:S(2)}) collective-permute-start(bf16[768,128]{1,0:T(8,128)(2,1)} %distant.2.k_in), channel_id=1, source_target_pairs={{8,16},{16,8},{9,17},{17,9},{10,18},{18,10},{11,19},{19,11},{12,20... | collective-permute-start | bytes 589832 | tf_op jit(solution)/shard_map/ppermute | solution.py:301
  100.2 11.3 %collective-permute-start.22 = (bf16[768,128]{1,0:T(8,128)(2,1)}, bf16[768,128]{1,0:T(8,128)(2,1)S(1)}, u32[]{:S(2)}, u32[]{:S(2)}) collective-permute-start(bf16[768,128]{1,0:T(8,128)(2,1)} %distant.3.v_in), channel_id=1, source_target_pairs={{8,0},{16,24},{9,1},{17,25},{10,2},{18,26},{11,3},{19,27},{12,4},{... | collective-permute-start | bytes 589832 | tf_op jit(solution)/shard_map/ppermute | solution.py:301
  101.5 8.4 %collective-permute-start.19 = (bf16[768,128]{1,0:T(8,128)(2,1)}, bf16[768,128]{1,0:T(8,128)(2,1)S(1)}, u32[]{:S(2)}, u32[]{:S(2)}) collective-permute-start(bf16[768,128]{1,0:T(8,128)(2,1)} %distant.3.v_in), channel_id=1, source_target_pairs={{8,16},{16,8},{9,17},{17,9},{10,18},{18,10},{11,19},{19,11},{12,20... | collective-permute-start | bytes 589832 | tf_op jit(solution)/shard_map/ppermute | solution.py:301
  104.2 15.6 %collective-permute-start.17 = (bf16[768,128]{1,0:T(8,128)(2,1)}, bf16[768,128]{1,0:T(8,128)(2,1)S(1)}, u32[]{:S(2)}, u32[]{:S(2)}) collective-permute-start(bf16[768,128]{1,0:T(8,128)(2,1)} %collective-permute-done.16.k_across), channel_id=1, source_target_pairs={{8,0},{16,24},{9,1},{17,25},{10,2},{18,26},{11,3},{19,27},{12,4},{... | collective-permute-start | bytes 589832 | tf_op jit(solution)/shard_map/ppermute | solution.py:301
  110.0 9.8 %collective-permute-start.20 = (bf16[768,128]{1,0:T(8,128)(2,1)S(1)}, bf16[768,128]{1,0:T(8,128)(2,1)S(1)}, u32[]{:S(2)}, u32[]{:S(2)}) collective-permute-start(bf16[768,128]{1,0:T(8,128)(2,1)S(1)} %collective-permute-done.19.v_across), channel_id=1, source_target_pairs={{8,0},{16,24},{9,1},{17,25},{10,2},{18,26},{11,3},{19,27},{12,4},{... | collective-permute-start | bytes 589832 | tf_op jit(solution)/shard_map/ppermute | solution.py:301
  111.5 0.9 copy-start
  112.5 1.1 copy-start.1

commit v5 on v3

v5 whole, which is shorter than its diff:
```python
import functools
import math

import jax
import jax.numpy as jnp
from jax import lax
from jax.experimental import pallas as pl
from jax.experimental.pallas import tpu as pltpu
from jax.sharding import PartitionSpec as P

HD = 128
PAGE = 16
NEG = -1e30
KERNEL_VMEM = 48 * 1024 * 1024
PROMPTS = 4


def attention_kernel(heads, span, info, slots, q_ref, k_ref, v_ref, start_ref, out_ref, cache_ref, acc, top):
    index = info[0]
    first = info[1]
    factor = HD**-0.5 * math.log2(math.e)
    columns = lax.broadcasted_iota(jnp.int32, (span, span), 1)
    rows = lax.broadcasted_iota(jnp.int32, (span, span), 0)

    def block(j, diagonal):
        at = pl.multiple_of(j * span, span)
        keys = k_ref[pl.ds(at, span), :]
        values = jnp.concatenate(
            [v_ref[pl.ds(at, span), :], jnp.ones((span, HD), jnp.bfloat16)], axis=1
        )
        allowed = columns >= start_ref[...] - at
        if diagonal:
            allowed = allowed & (columns <= rows)
        for g in range(heads):
            scores = lax.dot_general(
                q_ref[:, g * HD : (g + 1) * HD],
                keys,
                (((1,), (1,)), ((), ())),
                preferred_element_type=jnp.float32,
            )
            scores = jnp.where(allowed, scores, NEG)
            peak = jnp.max(scores, axis=1, keepdims=True)
            if not diagonal:
                before = top[g]
                peak = jnp.maximum(peak, before)
            weights = jnp.exp2(scores * factor - peak * factor).astype(jnp.bfloat16)
            mixed = jnp.dot(weights, values, preferred_element_type=jnp.float32)
            if not diagonal:
                mixed = mixed + acc[g] * jnp.exp2((before - peak) * factor)
            top[g] = peak
            acc[g] = mixed

    block(index, True)

    @pl.loop(first, index)
    def _(j):
        block(j, False)

    for g in range(heads):
        mixed = acc[g]
        out_ref[:, g * HD : (g + 1) * HD] = (mixed[:, :HD] / mixed[:, HD:]).astype(out_ref.dtype)

    capacity = cache_ref.shape[1] // PAGE
    empty = jnp.zeros((PAGE, HD), cache_ref.dtype)
    for s in range(cache_ref.shape[0]):

        @pl.loop(0, capacity)
        def _(r):
            page = slots[s * capacity + r]
            token = pl.ds(pl.multiple_of(jnp.maximum(page, 0) * PAGE, PAGE), PAGE)
            row = pl.ds(pl.multiple_of(r * PAGE, PAGE), PAGE)
            cache_ref[s, row, :HD] = jnp.where(page >= 0, k_ref[token, :], empty)
            cache_ref[s, row, HD:] = jnp.where(page >= 0, v_ref[token, :], empty)


def attention(info, slots, queries, keys, values, start, n_pre, capacity):
    span = queries.shape[0]
    heads = queries.shape[1] // HD
    return pl.pallas_call(
        functools.partial(attention_kernel, heads, span),
        in_specs=[
            pl.BlockSpec(memory_space=pltpu.SMEM),
            pl.BlockSpec(memory_space=pltpu.SMEM),
            pl.BlockSpec(memory_space=pltpu.VMEM),
            pl.BlockSpec(memory_space=pltpu.VMEM),
            pl.BlockSpec(memory_space=pltpu.VMEM),
            pl.BlockSpec(memory_space=pltpu.VMEM),
        ],
        out_specs=[
            pl.BlockSpec(memory_space=pltpu.VMEM),
            pl.BlockSpec(memory_space=pltpu.VMEM),
        ],
        out_shape=[
            jax.ShapeDtypeStruct(queries.shape, jnp.bfloat16),
            jax.ShapeDtypeStruct((n_pre, capacity * PAGE, 2 * HD), jnp.bfloat16),
        ],
        scratch_shapes=[
            pltpu.VMEM((heads, span, 2 * HD), jnp.float32),
            pltpu.VMEM((heads, span, 1), jnp.float32),
        ],
        compiler_params=pltpu.CompilerParams(vmem_limit_bytes=KERNEL_VMEM),
        cost_estimate=pl.CostEstimate(
            flops=4 * heads * span * span * n_pre * HD,
            bytes_accessed=4 * queries.size * 2,
            transcendentals=heads * span * span * n_pre,
        ),
        name="attention",
    )(info, slots, queries, keys, values, start)


PIECES = 8


def chunk_copy(h_ref, chunk, h_buf, sem):
    depth = h_buf.shape[1]
    columns = pl.ds(pl.multiple_of(chunk * depth, depth), depth)
    return pltpu.make_async_copy(h_ref.at[:, columns], h_buf, sem)


def add_pieces(member, chunk, pieces, w_ref, acc_ref):
    share = pieces[0].shape[1]
    half = PIECES // 2
    for side in range(2):

        @pl.when(jnp.bitwise_xor(member // half, side) == lax.rem(chunk, 2))
        def _():
            total = acc_ref[...]
            for j in range(side * half, side * half + half):
                row = lax.rem(jnp.bitwise_xor(member, j), half) * share
                total += jnp.dot(
                    pieces[j][...],
                    w_ref[pl.ds(pl.multiple_of(row, share), share), :],
                    preferred_element_type=jnp.float32,
                )
            acc_ref[...] = total


def near_kernel(place, h_ref, kw_ref, vw_ref, out_ref, h_buf, sem):
    copy = chunk_copy(h_ref, place[0], h_buf, sem)
    copy.start()
    weight = jnp.concatenate([kw_ref[...], vw_ref[...]], axis=1)
    copy.wait()
    out_ref[...] = jnp.dot(h_buf[...], weight, preferred_element_type=jnp.float32)


def partial_kernel(place, h_ref, kw_ref, vw_ref, before_ref, owner_ref, out_ref, h_buf, sem):
    copy = chunk_copy(h_ref, place[0], h_buf, sem)
    copy.start()
    span = h_buf.shape[0]
    weight = jnp.concatenate([kw_ref[...], vw_ref[...]], axis=1)
    out_ref[span:, :HD] = owner_ref[...]
    out_ref[span:, HD:] = owner_ref[...]
    copy.wait()
    out_ref[:span] = before_ref[...] + jnp.dot(
        h_buf[...], weight, preferred_element_type=jnp.float32
    )


def facing_kernel(place, h_ref, kw_ref, vw_ref, *refs):
    pieces = refs[:PIECES]
    out_ref, h_buf, w_buf, sem = refs[PIECES:]
    copy = chunk_copy(h_ref, place[0], h_buf, sem)
    copy.start()
    span = h_buf.shape[0]
    w_buf[:, :HD] = kw_ref[...]
    w_buf[:, HD:] = vw_ref[...]
    out_ref[span:] = jnp.zeros((span, 2 * HD), jnp.float32)
    add_pieces(place[2], place[0], pieces, w_buf, out_ref.at[pl.ds(span, span)])
    copy.wait()
    out_ref[:span] = jnp.dot(h_buf[...], w_buf[...], preferred_element_type=jnp.float32)


def distant_kernel(column, place, h_ref, w_ref, near_ref, outer_ref, facing_ref, bias_ref, *refs):
    pieces = refs[:PIECES]
    out_ref, h_buf, acc, sem = refs[PIECES:]
    copy = chunk_copy(h_ref, place[0], h_buf, sem)
    copy.start()
    span = h_buf.shape[0]
    part = slice(column * HD, column * HD + HD)
    own_at = pl.multiple_of(place[1] * span, span)
    outer_at = pl.multiple_of((1 - place[1]) * span, span)
    bias = bias_ref[...].astype(jnp.float32)
    acc[...] = outer_ref[:span, part] + facing_ref[span:, part] + bias
    add_pieces(place[2], place[0], pieces, w_ref, acc)
    out_ref[pl.ds(outer_at, span), :] = acc[...].astype(jnp.bfloat16)
    own = near_ref[:span, part] + facing_ref[:span, part] + bias
    copy.wait()
    own += jnp.dot(h_buf[...], w_ref[...], preferred_element_type=jnp.float32)
    out_ref[pl.ds(own_at, span), :] = own.astype(jnp.bfloat16)
    if column == 0:
        mine, theirs = near_ref[span:, :HD], outer_ref[span:, :HD]
        lower = jnp.where(place[1] == 0, mine, theirs)
        upper = jnp.where(place[1] == 0, theirs, mine)
        out_ref[2 * span :] = jnp.concatenate([lower, upper], axis=0).astype(jnp.bfloat16)


ANY = pl.BlockSpec(memory_space=pl.ANY)
EXTRA = 8


def call_project(kernel, name, place, operands, rows, columns, kind, scratch):
    whole = [pl.BlockSpec(x.shape, lambda k, place: (0, 0)) for x in operands[1:]]
    return pl.pallas_call(
        kernel,
        grid_spec=pltpu.PrefetchScalarGridSpec(
            num_scalar_prefetch=1,
            grid=(1,),
            in_specs=[ANY] + whole,
            out_specs=pl.BlockSpec((rows, columns), lambda k, place: (0, 0)),
            scratch_shapes=scratch + [pltpu.SemaphoreType.DMA],
        ),
        out_shape=jax.ShapeDtypeStruct((rows, columns), kind),
        compiler_params=pltpu.CompilerParams(vmem_limit_bytes=KERNEL_VMEM),
        cost_estimate=pl.CostEstimate(flops=0, bytes_accessed=0, transcendentals=0),
        name=name,
    )(place, *operands)


INWARD = [(0, 1), (3, 2)]
ACROSS = [(1, 2), (2, 1)]
OUTWARD = [(1, 0), (2, 3)]
SWAP = [(0, 1), (1, 0), (2, 3), (3, 2)]


def line_of_four(hidden, key_weight, value_weight, key_bias, value_bias, page_owner):
    index = lax.axis_index("pre")
    member = lax.axis_index(("dec", "tp"))
    span, width = hidden.shape
    depth = key_weight.shape[0]
    share = width // 2 // PIECES
    facing = 3 - index
    near = jnp.bitwise_xor(index, 1)
    distant = jnp.bitwise_xor(facing, 1)
    second = (index < 2).astype(jnp.int32)

    def send(x, pairs):
        return lax.ppermute(x, "pre", pairs)

    def trade(x, apart):
        return lax.ppermute(x, ("dec", "tp"), [(m, m ^ apart) for m in range(PIECES)])

    mine = second * (width // 2) + member * share
    cut = lax.dynamic_slice_in_dim(hidden, mine, share, axis=1)
    tie = lax.optimization_barrier
    key_facing = send(key_weight, ACROSS)
    cut = send(cut, INWARD)
    cut, key_after = tie((cut, key_weight))
    key_swapped = send(key_after, SWAP)
    key_facing, value_after = tie((key_facing, value_weight))
    value_facing = send(value_after, ACROSS)
    key_swapped, value_after = tie((key_swapped, value_weight))
    value_swapped = send(value_after, SWAP)
    chips = [trade(cut, 2), trade(cut, 4), trade(cut, 6)]
    chips, value_facing = tie((chips, value_facing))
    chips = [cut] + chips
    mates = [trade(x, 1) for x in chips]
    pieces = [x for both in zip(chips, mates) for x in both]
    key_distant = send(key_swapped, ACROSS)
    value_distant = send(value_swapped, ACROSS)

    def place(chunk):
        return jnp.stack([chunk, second, member])

    block = pltpu.VMEM((span, depth), jnp.bfloat16)
    both = pltpu.VMEM((depth, 2 * HD), jnp.bfloat16)
    own_part = call_project(
        near_kernel,
        "near",
        index[None],
        [hidden, key_weight, value_weight],
        span,
        2 * HD,
        jnp.float32,
        [block],
    )
    faced = call_project(
        facing_kernel,
        "facing",
        place(facing),
        [hidden, key_facing, value_facing] + pieces,
        2 * span,
        2 * HD,
        jnp.float32,
        [block, both],
    )
    faced, own_part, key_distant = tie((faced, own_part, key_distant))
    owners = jnp.broadcast_to(page_owner.T.astype(jnp.float32), (EXTRA, page_owner.shape[0]))
    owners = jnp.pad(owners, ((0, 0), (0, HD - page_owner.shape[0])))
    own_part = call_project(
        partial_kernel,
        "partial",
        near[None],
        [hidden, key_swapped, value_swapped, own_part, owners],
        span + EXTRA,
        2 * HD,
        jnp.float32,
        [block],
    )
    outer_part = send(own_part, INWARD)

    def finish(column, weight, bias):
        pair = call_project(
            functools.partial(distant_kernel, column),
            "distant",
            place(distant),
            [hidden, weight, own_part, outer_part, faced, bias[None, :]] + pieces,
            2 * span + (2 * EXTRA if column == 0 else 0),
            HD,
            jnp.bfloat16,
            [block, pltpu.VMEM((span, HD), jnp.float32)],
        )
        out = send(pair, OUTWARD)
        across = send(pair, ACROSS)
        return pair, out, across, send(across, OUTWARD)

    keys = finish(0, key_distant, key_bias)
    values = finish(1, value_distant, value_bias)
    return keys, values


def softmax_step(q, keys, values, allowed, before):
    factor = HD**-0.5 * math.log2(math.e)
    scores = lax.dot_general(q, keys, (((1,), (1,)), ((), ())), preferred_element_type=jnp.float32)
    scores = jnp.where(allowed, scores, NEG)
    peak = jnp.max(scores, axis=1, keepdims=True)
    if before is not None:
        peak = jnp.maximum(peak, before[0])
    weights = jnp.exp2(scores * factor - peak * factor).astype(jnp.bfloat16)
    mixed = jnp.dot(weights, values, preferred_element_type=jnp.float32)
    total, mixed = mixed[:, HD:], mixed[:, :HD]
    if before is not None:
        shrink = jnp.exp2((before[0] - peak) * factor)
        total = total + before[1] * shrink
        mixed = mixed + before[2] * shrink
    return peak, total, mixed


def with_ones(values):
    return jnp.concatenate([values, jnp.ones_like(values)], axis=1)


def prompt_starts(seg_ref, first, span):
    seg = seg_ref[...]
    position = (lax.broadcasted_iota(jnp.int32, (span, 1), 0) + first).astype(jnp.float32)
    start = jnp.zeros((span, 1), jnp.float32)
    for v in range(1, PROMPTS):
        lower = jnp.where(seg < v, 1.0, 0.0)
        bound = jnp.sum(jnp.sum(lower, axis=1, keepdims=True), axis=0, keepdims=True)
        start = jnp.where(position >= bound, bound, start)
    return start.astype(jnp.int32)


def read_owners(held_k, span, listed, named, sem):
    listed[...] = held_k[2 * span :].astype(jnp.float32).astype(jnp.int32)
    copy = pltpu.make_async_copy(listed, named, sem)
    copy.start()
    return copy


def place_pages(index, span, named, held_k, held_v, cache_ref):
    cache_ref[...] = jnp.zeros(cache_ref.shape, cache_ref.dtype)
    for s in range(2):
        rank = jnp.int32(0)
        for p in range(span // PAGE):
            owned = named[s * EXTRA, p] == index
            tokens = pl.ds(s * span + p * PAGE, PAGE)
            at = pl.ds(pl.multiple_of(rank * PAGE, PAGE), PAGE)

            @pl.when(owned)
            def _():
                cache_ref[s, at, :HD] = held_k[tokens, :]
                cache_ref[s, at, HD:] = held_v[tokens, :]

            rank = rank + owned.astype(jnp.int32)


def own_kernel(
    heads,
    info,
    q_ref,
    seg_ref,
    k_in,
    k_out,
    v_in,
    v_out,
    top,
    total,
    mix,
    cache_ref,
    held_k,
    held_v,
    q_buf,
    listed,
    named,
    sems,
):
    copy = pltpu.make_async_copy(q_ref, q_buf, sems.at[0])
    copy.start()
    span = q_buf.shape[0]
    index = info[0]
    inner = (index == 1) | (index == 2)
    held_k[...] = jnp.where(inner, k_in[...], k_out[...])
    held_v[...] = jnp.where(inner, v_in[...], v_out[...])
    owners = read_owners(held_k, span, listed, named, sems.at[1])
    keys = held_k[: 2 * span]
    values = with_ones(held_v[...])
    columns = lax.broadcasted_iota(jnp.int32, (span, 2 * span), 1)
    rows = lax.broadcasted_iota(jnp.int32, (span, 2 * span), 0)
    start = prompt_starts(seg_ref, index * span, span)
    allowed = (columns <= rows + lax.rem(index, 2) * span) & (
        columns >= start - (index // 2) * 2 * span
    )
    copy.wait()
    for g in range(heads):
        q = q_buf[:, g * HD : (g + 1) * HD]
        peak, sums, mixed = softmax_step(q, keys, values, allowed, None)
        top[g] = peak
        total[g] = sums[:, :1]
        mix[g] = mixed
    owners.wait()
    place_pages(index, span, named, held_k, held_v, cache_ref)


def far_kernel(
    heads,
    info,
    q_ref,
    seg_ref,
    k_across,
    k_far,
    v_across,
    v_far,
    top,
    total,
    mix,
    own_cache,
    out_ref,
    cache_ref,
    held_k,
    held_v,
    q_buf,
    listed,
    named,
    sems,
):
    copy = pltpu.make_async_copy(q_ref, q_buf, sems.at[0])
    copy.start()
    span = q_buf.shape[0]
    index = info[0]
    inner = (index == 1) | (index == 2)
    held_k[...] = jnp.where(inner, k_across[...], k_far[...])
    held_v[...] = jnp.where(inner, v_across[...], v_far[...])
    cache_ref[pl.ds(index // 2 * 2, 2)] = own_cache[...]
    owners = read_owners(held_k, span, listed, named, sems.at[1])
    copy.wait()

    @pl.when(index < 2)
    def _():
        for g in range(heads):
            out_ref[:, g * HD : (g + 1) * HD] = (mix[g] / total[g]).astype(out_ref.dtype)

    @pl.when(index >= 2)
    def _():
        keys = held_k[: 2 * span]
        values = with_ones(held_v[...])
        columns = lax.broadcasted_iota(jnp.int32, (span, 2 * span), 1)
        allowed = columns >= prompt_starts(seg_ref, index * span, span)
        for g in range(heads):
            q = q_buf[:, g * HD : (g + 1) * HD]
            _, sums, mixed = softmax_step(q, keys, values, allowed, (top[g], total[g], mix[g]))
            out_ref[:, g * HD : (g + 1) * HD] = (mixed / sums).astype(out_ref.dtype)

    owners.wait()
    far_cache = cache_ref.at[pl.ds((1 - index // 2) * 2, 2)]
    place_pages(index, span, named, held_k, held_v, far_cache)


def attention_of_pairs(queries, segment_ids, keys, values, capacity):
    span = queries.shape[0]
    heads = queries.shape[1] // HD
    info = lax.axis_index("pre").astype(jnp.int32)[None]
    segments = segment_ids.reshape(-1, HD)
    smem = pl.BlockSpec(memory_space=pltpu.SMEM)
    vmem = pl.BlockSpec(memory_space=pltpu.VMEM)
    cost = pl.CostEstimate(flops=0, bytes_accessed=0, transcendentals=0)
    params = pltpu.CompilerParams(vmem_limit_bytes=KERNEL_VMEM)
    scratch = [
        pltpu.VMEM((2 * span + 2 * EXTRA, HD), jnp.bfloat16),
        pltpu.VMEM((2 * span, HD), jnp.bfloat16),
        pltpu.VMEM(queries.shape, jnp.bfloat16),
        pltpu.VMEM((2 * EXTRA, HD), jnp.int32),
        pltpu.SMEM((2 * EXTRA, HD), jnp.int32),
        pltpu.SemaphoreType.DMA((2,)),
    ]
    state = pl.pallas_call(
        functools.partial(own_kernel, heads),
        in_specs=[smem, ANY] + [vmem] * 5,
        out_specs=[vmem] * 4,
        out_shape=[
            jax.ShapeDtypeStruct((heads, span, 1), jnp.float32),
            jax.ShapeDtypeStruct((heads, span, 1), jnp.float32),
            jax.ShapeDtypeStruct((heads, span, HD), jnp.float32),
            jax.ShapeDtypeStruct((2, capacity * PAGE, 2 * HD), jnp.bfloat16),
        ],
        scratch_shapes=scratch,
        compiler_params=params,
        cost_estimate=cost,
        name="attend_own",
    )(info, queries, segments, *keys[:2], *values[:2])
    return pl.pallas_call(
        functools.partial(far_kernel, heads),
        in_specs=[smem, ANY] + [vmem] * 9,
        out_specs=[vmem] * 2,
        out_shape=[
            jax.ShapeDtypeStruct(queries.shape, jnp.bfloat16),
            jax.ShapeDtypeStruct((4, capacity * PAGE, 2 * HD), jnp.bfloat16),
        ],
        scratch_shapes=scratch,
        compiler_params=params,
        cost_estimate=cost,
        name="attend_far",
    )(info, queries, segments, *keys[2:], *values[2:], *state)


def gathered(hidden, key_weight, value_weight, key_bias, value_bias):
    joined = jnp.concatenate([key_weight, value_weight], axis=1)
    joined = lax.all_gather(joined, "pre", axis=0, tiled=True)
    bias = jnp.concatenate([key_bias, value_bias]).astype(jnp.float32)
    local = jnp.dot(hidden, joined, preferred_element_type=jnp.float32) + bias
    both = lax.all_gather(local.astype(jnp.bfloat16), "pre", axis=0, tiled=True)
    return both[:, :HD], both[:, HD:]


def body(hidden, queries, key_weight, value_weight, key_bias, value_bias, segment_ids, page_owner):
    n_pre = lax.axis_size("pre")
    index = lax.axis_index("pre")
    span = hidden.shape[0]
    pages_dev = span // PAGE
    capacity = 2 * pages_dev // n_pre
    assert key_weight.shape[1] == HD
    arrays = (hidden, key_weight, value_weight, key_bias, value_bias)
    if n_pre == 4:
        keys, values = line_of_four(*arrays, page_owner)
        mixed, cache = attention_of_pairs(queries, segment_ids, keys, values, capacity)
        return (mixed, cache[None])

    own_segments = lax.dynamic_slice_in_dim(segment_ids, index * span, span)
    start = jnp.sum(
        (segment_ids[None, :] < own_segments[:, None]).astype(jnp.int32), axis=1, keepdims=True
    )
    info = jnp.stack([index, start[0, 0] // span]).astype(jnp.int32)
    owners = lax.all_gather(page_owner[:, 0], "pre")
    keys, values = gathered(*arrays)
    mine = (owners == index).astype(jnp.int32)
    rank = jnp.cumsum(mine, axis=1) - mine
    numbers = jnp.arange(n_pre * pages_dev, dtype=jnp.int32).reshape(n_pre, 1, pages_dev)
    wanted = (mine[:, None, :] == 1) & (
        rank[:, None, :] == jnp.arange(capacity, dtype=jnp.int32)[None, :, None]
    )
    slots = jnp.max(jnp.where(wanted, numbers, -1), axis=2).reshape(-1)
    mixed, cache = attention(info, slots, queries, keys, values, start, n_pre, capacity)
    return (mixed, cache[None])


def solution(mesh):
    return jax.shard_map(
        body,
        mesh=mesh,
        in_specs=(
            P(("group", "pre"), None),
            P(("group", "pre"), ("dec", "tp")),
            P("pre", ("dec", "tp")),
            P("pre", ("dec", "tp")),
            P(("dec", "tp")),
            P(("dec", "tp")),
            P("group"),
            P(("group", "pre"), None),
        ),
        out_specs=(
            P(("group", "pre"), ("dec", "tp")),
            P(("group", "pre"), None, None, ("dec", "tp")),
        ),
        check_vma=False,
    )
```

time: 118 us -> 122 us (1.034)
  waiting for transfers between devices: 23.2 us -> 47.8 us
  starting transfers between devices: 43.4 us -> 30.5 us
  local copies, waits for them, and re-layouts: 17.7 us -> 11.3 us
  Pallas kernels: 23.5 us -> 28.6 us
  other arithmetic: 5.68 us -> 0.81 us
  between operations: 2.95 us -> 1.14 us
    ppermute x14, waiting for transfers between devices: 20.8 us -> 38 us  [send(): return lax.ppermute(x, 'pre', pairs)]
    ppermute x7, waiting for transfers between devices: 0.02 us -> 9.84 us  [trade(): lax.ppermute(x, ('dec', 'tp'), [(m, m ^ apart) for m in range(PIECES)])]
    ppermute x3 -> x0, starting transfers between devices: 7.49 us -> none  [the longest x1 3.48 us: spread_owners(): across = lax.ppermute(pair, 'pre', ACROSS)]
    ppermute x14, starting transfers between devices: 31.3 us -> 24.5 us  [send(): return lax.ppermute(x, 'pre', pairs)]
    unnamed x38 -> x34, local copies, waits for them, and re-layouts: 14.3 us -> 10.3 us
    pallas_call x4 -> x5, Pallas kernels: 11.8 us -> 15.1 us  [call_project(): pl.pallas_call(kernel, grid_spec=pltpu.PrefetchScalarGridSpec(num_scalar_...]
    ppermute x3 -> x0, waiting for transfers between devices: 2.47 us -> none  [the longest x1 1.97 us: spread_owners(): across = lax.ppermute(pair, 'pre', ACROSS)]
    pallas_call x2, Pallas kernels: 11.8 us -> 13.5 us  [the longest x1 7.77 us: attention_of_pairs(): pl.pallas_call(functools.partial(far_kernel, heads), in_specs=[smem, ANY]...]
  transfers between devices with their start and end apart: 24 -> 21, of which waited for: 7 -> 7; matrix products, arithmetic and copies ran while one was open for 8% -> 1% of each run, Pallas kernels for 14% -> 17%
where the time goes in v5:
time: 122 us; the launch traced here: 120 us
  waiting for transfers between devices  47.8 us (39%)
  starting transfers between devices  30.5 us (25%)
  Pallas kernels  28.6 us (23%)
  local copies, waits for them, and re-layouts  11.3 us (9%)
    ppermute x14, waiting for transfers between devices, send(): return lax.ppermute(x, 'pre', pairs)  38 us
    ppermute x14, starting transfers between devices, send(): return lax.ppermute(x, 'pre', pairs)  24.5 us
    pallas_call x5, Pallas kernels, call_project(): pl.pallas_call(kernel, grid_spec=pltpu.PrefetchScalarGridSpec(num_scalar_...  15.1 us
    unnamed x34, local copies, waits for them, and re-layouts  10.3 us
    ppermute x7, waiting for transfers between devices, trade(): lax.ppermute(x, ('dec', 'tp'), [(m, m ^ apart) for m in range(PIECES)])  9.84 us
    pallas_call x1, Pallas kernels, attention_of_pairs(): pl.pallas_call(functools.partial(far_kernel, heads), in_specs=[smem, ANY]...  7.77 us
    ppermute x7, starting transfers between devices, trade(): lax.ppermute(x, ('dec', 'tp'), [(m, m ^ apart) for m in range(PIECES)])  6.04 us
    pallas_call x1, Pallas kernels, attention_of_pairs(): pl.pallas_call(functools.partial(own_kernel, heads), in_specs=[smem, ANY]...  5.7 us
  transfers between devices with their start and end apart: 21, of which 7 were waited for; matrix products, arithmetic and copies ran while one was open for 1% of the time, Pallas kernels for 17%

profile of v5, /device:TPU:16, one launch (start us, length us, event | category | flops | bytes accessed | tf_op | source)
XLA Modules:
  0.0 120.2 jit_solution(4029525378929354724)
XLA Ops:
  0.6 1.0 constant_dynamic-slice_fusion
  1.7 1.3 %collective-permute-start.1 = (bf16[384,512]{1,0:T(8,128)(2,1)S(1)}, bf16[384,512]{1,0:T(8,128)(2,1)S(1)}, u32[]{:S(2)}, u32[]{:S(2)}) collective-permute-start(bf16[384,512]{1,0:T(8,128)(2,1)S(1)} %constant_dynamic-slice_fusion), channel_id=1, source_target_pairs={{0,8},{24,16},{1,9},{25,17},{2,10},{26,18},{3,11},{27,19},{4,12},{... | collective-permute-start | bytes 1179656 | tf_op jit(solution)/shard_map/ppermute | solution.py:237
  3.0 2.4 %collective-permute-start = (bf16[2048,128]{1,0:T(8,128)(2,1)}, bf16[2048,128]{1,0:T(8,128)(2,1)S(1)}, u32[]{:S(2)}, u32[]{:S(2)}) collective-permute-start(bf16[2048,128]{1,0:T(8,128)(2,1)} %kw_ref.1), channel_id=1, source_target_pairs={{8,16},{16,8},{9,17},{17,9},{10,18},{18,10},{11,19},{19,11},{12,20... | collective-permute-start | bytes 1572872 | tf_op jit(solution)/shard_map/ppermute | solution.py:237
  5.3 9.1 %collective-permute-done.1.refs_0_ = bf16[384,512]{1,0:T(8,128)(2,1)S(1)} collective-permute-done((bf16[384,512]{1,0:T(8,128)(2,1)S(1)}, bf16[384,512]{1,0:T(8,128)(2,1)S(1)}, u32[]{:S(2)}, u32[]{:S(2)}) %collective-permute-start.1) | collective-permute-done | bytes 393248 | tf_op jit(solution)/shard_map/ppermute | solution.py:237
  14.4 1.5 %collective-permute-start.2 = (bf16[384,512]{1,0:T(8,128)(2,1)S(1)}, bf16[384,512]{1,0:T(8,128)(2,1)S(1)}, u32[]{:S(2)}, u32[]{:S(2)}) collective-permute-start(bf16[384,512]{1,0:T(8,128)(2,1)S(1)} %collective-permute-done.1.refs_0_), channel_id=1, source_target_pairs={{0,2},{1,3},{2,0},{3,1},{4,6},{5,7},{6,4},{7,5},{8,10},{9,11},{10,... | collective-permute-start | bytes 1179656 | tf_op jit(solution)/shard_map/ppermute | solution.py:240
  15.9 2.8 %collective-permute-done.kw_ref = bf16[2048,128]{1,0:T(8,128)(2,1)S(1)} collective-permute-done((bf16[2048,128]{1,0:T(8,128)(2,1)}, bf16[2048,128]{1,0:T(8,128)(2,1)S(1)}, u32[]{:S(2)}, u32[]{:S(2)}) %collective-permute-start) | collective-permute-done | bytes 524320 | tf_op jit(solution)/shard_map/ppermute | solution.py:237
  18.7 0.8 copy-done.8
  19.5 2.3 %collective-permute-start.5 = (bf16[2048,128]{1,0:T(8,128)(2,1)}, bf16[2048,128]{1,0:T(8,128)(2,1)S(1)}, u32[]{:S(2)}, u32[]{:S(2)}) collective-permute-start(bf16[2048,128]{1,0:T(8,128)(2,1)} %vw_ref.1), channel_id=1, source_target_pairs={{8,16},{16,8},{9,17},{17,9},{10,18},{18,10},{11,19},{19,11},{12,20... | collective-permute-start | bytes 1572872 | tf_op jit(solution)/shard_map/ppermute | solution.py:237
  21.9 1.6 %collective-permute-start.3 = (bf16[384,512]{1,0:T(8,128)(2,1)S(1)}, bf16[384,512]{1,0:T(8,128)(2,1)S(1)}, u32[]{:S(2)}, u32[]{:S(2)}) collective-permute-start(bf16[384,512]{1,0:T(8,128)(2,1)S(1)} %collective-permute-done.1.refs_0_), channel_id=1, source_target_pairs={{0,4},{1,5},{2,6},{3,7},{4,0},{5,1},{6,2},{7,3},{8,12},{9,13},{10,... | collective-permute-start | bytes 1179656 | tf_op jit(solution)/shard_map/ppermute | solution.py:240
  23.5 4.1 %collective-permute-done.10.kw_ref = bf16[2048,128]{1,0:T(8,128)(2,1)} collective-permute-done((bf16[2048,128]{1,0:T(8,128)(2,1)}, bf16[2048,128]{1,0:T(8,128)(2,1)}, u32[]{:S(2)}, u32[]{:S(2)}) %collective-permute-start.10) | collective-permute-done | bytes 524320 | tf_op jit(solution)/shard_map/ppermute | solution.py:237
  27.5 0.3 collective-permute-start.12
  27.8 2.4 %collective-permute-start.4 = (bf16[384,512]{1,0:T(8,128)(2,1)S(1)}, bf16[384,512]{1,0:T(8,128)(2,1)S(1)}, u32[]{:S(2)}, u32[]{:S(2)}) collective-permute-start(bf16[384,512]{1,0:T(8,128)(2,1)S(1)} %collective-permute-done.1.refs_0_), channel_id=1, source_target_pairs={{0,6},{1,7},{2,4},{3,5},{4,2},{5,3},{6,0},{7,1},{8,14},{9,15},{10,... | collective-permute-start | bytes 1179656 | tf_op jit(solution)/shard_map/ppermute | solution.py:240
  30.3 9.8 %collective-permute-done.3.refs_4_ = bf16[384,512]{1,0:T(8,128)(2,1)S(1)} collective-permute-done((bf16[384,512]{1,0:T(8,128)(2,1)S(1)}, bf16[384,512]{1,0:T(8,128)(2,1)S(1)}, u32[]{:S(2)}, u32[]{:S(2)}) %collective-permute-start.3) | collective-permute-done | bytes 393248 | tf_op jit(solution)/shard_map/ppermute | solution.py:240
  40.1 3.5 %collective-permute-start.11 = (bf16[2048,128]{1,0:T(8,128)(2,1)}, bf16[2048,128]{1,0:T(8,128)(2,1)}, u32[]{:S(2)}, u32[]{:S(2)}) collective-permute-start(bf16[2048,128]{1,0:T(8,128)(2,1)} %collective-permute-done.10.kw_ref), channel_id=1, source_target_pairs={{8,16},{16,8},{9,17},{17,9},{10,18},{18,10},{11,19},{19,11},{12,20... | collective-permute-start | bytes 1572872 | tf_op jit(solution)/shard_map/ppermute | solution.py:237
  43.6 0.8 copy-done.10
  44.4 0.5 collective-permute-start.8
  44.9 2.4 %collective-permute-start.16 = (bf16[2048,128]{1,0:T(8,128)(2,1)}, bf16[2048,128]{1,0:T(8,128)(2,1)}, u32[]{:S(2)}, u32[]{:S(2)}) collective-permute-start(bf16[2048,128]{1,0:T(8,128)(2,1)} %collective-permute-done.12.vw_ref), channel_id=1, source_target_pairs={{8,16},{16,8},{9,17},{17,9},{10,18},{18,10},{11,19},{19,11},{12,20... | collective-permute-start | bytes 1572872 | tf_op jit(solution)/shard_map/ppermute | solution.py:237
  47.3 0.7 convert_bitcast_fusion
  48.0 1.0 copy-done.12
  49.0 1.0 copy-done.13
  50.0 2.0 %near.1.before_ref = f32[384,256]{1,0:T(8,128)S(1)} custom-call(s32[1]{0:T(128)} %bitcast.place.info, bf16[384,8192]{1,0:T(8,128)(2,1)} %h_ref.9, bf16[2048,128]{1,0:T(8,128)(2,1)S(1)} %copy-done.12, bf16[2048,128]{1,0:T(8,128)(2,1)S(1)} %copy-done.13), custom_call_target="tpu_custom_call" | custom-call | tf_op jit(solution)/shard_map/near/pallas_call | solution.py:203
  52.0 0.0 copy-start.6
  52.0 0.7 copy-done.6
  52.8 0.1 add_add_fusion.1.place
  52.9 0.8 copy-done.2
  53.7 1.0 copy-done.3
  54.7 1.0 copy-done.9
  55.7 1.0 copy-done.11
  56.7 2.5 %facing.1.facing_ref = f32[768,256]{1,0:T(8,128)S(1)} custom-call(s32[3]{0:T(128)S(1)} %add_add_fusion.1.place, bf16[384,8192]{1,0:T(8,128)(2,1)} %h_ref.9, bf16[2048,128]{1,0:T(8,128)(2,1)S(1)} %copy-done.9, bf16[2048,128]{1,0:T(8,128)(2,1)S(1)} %copy-done.11, bf16[384,512]{1,0:T(8,128)(2,1)S(1)} %collective-permute-done.1.refs_0_, ...), custom_call_target="tpu_custom_call" | custom-call | tf_op jit(solution)/shard_map/facing/pallas_call | solution.py:203
  59.3 0.0 copy-start.15
  59.3 3.2 %partial.1.near_ref = f32[392,256]{1,0:T(8,128)S(1)} custom-call(s32[1]{0:T(128)} %bitcast.6.place, bf16[384,8192]{1,0:T(8,128)(2,1)} %h_ref.9, bf16[2048,128]{1,0:T(8,128)(2,1)} %collective-permute-done.10.kw_ref, bf16[2048,128]{1,0:T(8,128)(2,1)} %collective-permute-done.12.vw_ref, f32[384,256]{1,0:T(8,128)S(1)} %copy-done.7, f32[8,128]{1,0:T(8,128)S(1)} %pad.7.owner_ref), custom_call_target="tpu_custom_call" | custom-call | tf_op jit(solution)/shard_map/partial/pallas_call | solution.py:203
  62.5 1.3 %collective-permute-start.13 = (f32[392,256]{1,0:T(8,128)S(1)}, f32[392,256]{1,0:T(8,128)}, u32[]{:S(2)}, u32[]{:S(2)}) collective-permute-start(f32[392,256]{1,0:T(8,128)S(1)} %partial.1.near_ref), channel_id=1, source_target_pairs={{0,8},{24,16},{1,9},{25,17},{2,10},{26,18},{3,11},{27,19},{4,12},{... | collective-permute-start | bytes 1204232 | tf_op jit(solution)/shard_map/ppermute | solution.py:237
  63.8 0.1 add_add_fusion.place
  63.9 12.0 %collective-permute-done.13.outer_ref = f32[392,256]{1,0:T(8,128)} collective-permute-done((f32[392,256]{1,0:T(8,128)S(1)}, f32[392,256]{1,0:T(8,128)}, u32[]{:S(2)}, u32[]{:S(2)}) %collective-permute-start.13) | collective-permute-done | bytes 401440 | tf_op jit(solution)/shard_map/ppermute | solution.py:237
  76.0 1.0 copy-done.1
  77.0 1.0 copy-done.4
  78.0 3.7 %distant.2.k_in = bf16[784,128]{1,0:T(8,128)(2,1)S(1)} custom-call(s32[3]{0:T(128)S(1)} %add_add_fusion.place, bf16[384,8192]{1,0:T(8,128)(2,1)} %h_ref.9, bf16[2048,128]{1,0:T(8,128)(2,1)} %collective-permute-done.11.w_ref, f32[392,256]{1,0:T(8,128)S(1)} %partial.1.near_ref, f32[392,256]{1,0:T(8,128)} %collective-permute-done.13.outer_ref, ...), custom_call_target="tpu_custom_call" | custom-call | tf_op jit(solution)/shard_map/distant/pallas_call | solution.py:203
  81.7 3.5 %collective-permute-start.14 = (bf16[784,128]{1,0:T(8,128)(2,1)S(1)}, bf16[784,128]{1,0:T(8,128)(2,1)S(1)}, u32[]{:S(2)}, u32[]{:S(2)}) collective-permute-start(bf16[784,128]{1,0:T(8,128)(2,1)S(1)} %distant.2.k_in), channel_id=1, source_target_pairs={{8,16},{16,8},{9,17},{17,9},{10,18},{18,10},{11,19},{19,11},{12,20... | collective-permute-start | bytes 602120 | tf_op jit(solution)/shard_map/ppermute | solution.py:237
  85.2 3.7 %distant.3.v_in = bf16[768,128]{1,0:T(8,128)(2,1)S(1)} custom-call(s32[3]{0:T(128)S(1)} %add_add_fusion.place, bf16[384,8192]{1,0:T(8,128)(2,1)} %h_ref.9, bf16[2048,128]{1,0:T(8,128)(2,1)} %collective-permute-done.16.w_ref, f32[392,256]{1,0:T(8,128)S(1)} %partial.1.near_ref, f32[392,256]{1,0:T(8,128)} %collective-permute-done.13.outer_ref, ...), custom_call_target="tpu_custom_call" | custom-call | tf_op jit(solution)/shard_map/distant/pallas_call | solution.py:203
  88.9 2.4 %collective-permute-start.17 = (bf16[768,128]{1,0:T(8,128)(2,1)S(1)}, bf16[768,128]{1,0:T(8,128)(2,1)S(1)}, u32[]{:S(2)}, u32[]{:S(2)}) collective-permute-start(bf16[768,128]{1,0:T(8,128)(2,1)S(1)} %distant.3.v_in), channel_id=1, source_target_pairs={{8,16},{16,8},{9,17},{17,9},{10,18},{18,10},{11,19},{19,11},{12,20... | collective-permute-start | bytes 589832 | tf_op jit(solution)/shard_map/ppermute | solution.py:237
  91.3 1.3 %collective-permute-start.19 = (bf16[784,128]{1,0:T(8,128)(2,1)S(1)}, bf16[784,128]{1,0:T(8,128)(2,1)S(1)}, u32[]{:S(2)}, u32[]{:S(2)}) collective-permute-start(bf16[784,128]{1,0:T(8,128)(2,1)S(1)} %distant.2.k_in), channel_id=1, source_target_pairs={{8,0},{16,24},{9,1},{17,25},{10,2},{18,26},{11,3},{19,27},{12,4},{... | collective-permute-start | bytes 602120 | tf_op jit(solution)/shard_map/ppermute | solution.py:237
  92.6 1.3 %collective-permute-start.15 = (bf16[784,128]{1,0:T(8,128)(2,1)S(1)}, bf16[784,128]{1,0:T(8,128)(2,1)S(1)}, u32[]{:S(2)}, u32[]{:S(2)}) collective-permute-start(bf16[784,128]{1,0:T(8,128)(2,1)S(1)} %collective-permute-done.14.k_across), channel_id=1, source_target_pairs={{8,0},{16,24},{9,1},{17,25},{10,2},{18,26},{11,3},{19,27},{12,4},{... | collective-permute-start | bytes 602120 | tf_op jit(solution)/shard_map/ppermute | solution.py:237
  93.9 1.3 %collective-permute-start.20 = (bf16[768,128]{1,0:T(8,128)(2,1)S(1)}, bf16[768,128]{1,0:T(8,128)(2,1)S(1)}, u32[]{:S(2)}, u32[]{:S(2)}) collective-permute-start(bf16[768,128]{1,0:T(8,128)(2,1)S(1)} %distant.3.v_in), channel_id=1, source_target_pairs={{8,0},{16,24},{9,1},{17,25},{10,2},{18,26},{11,3},{19,27},{12,4},{... | collective-permute-start | bytes 589832 | tf_op jit(solution)/shard_map/ppermute | solution.py:237
  95.2 1.5 %collective-permute-done.17.v_across = bf16[768,128]{1,0:T(8,128)(2,1)S(1)} collective-permute-done((bf16[768,128]{1,0:T(8,128)(2,1)S(1)}, bf16[768,128]{1,0:T(8,128)(2,1)S(1)}, u32[]{:S(2)}, u32[]{:S(2)}) %collective-permute-start.17) | collective-permute-done | bytes 196640 | tf_op jit(solution)/shard_map/ppermute | solution.py:237
  96.7 1.3 %collective-permute-start.18 = (bf16[768,128]{1,0:T(8,128)(2,1)S(1)}, bf16[768,128]{1,0:T(8,128)(2,1)S(1)}, u32[]{:S(2)}, u32[]{:S(2)}) collective-permute-start(bf16[768,128]{1,0:T(8,128)(2,1)S(1)} %collective-permute-done.17.v_across), channel_id=1, source_target_pairs={{8,0},{16,24},{9,1},{17,25},{10,2},{18,26},{11,3},{19,27},{12,4},{... | collective-permute-start | bytes 589832 | tf_op jit(solution)/shard_map/ppermute | solution.py:237
  98.0 8.5 %collective-permute-done.20.v_out = bf16[768,128]{1,0:T(8,128)(2,1)S(1)} collective-permute-done((bf16[768,128]{1,0:T(8,128)(2,1)S(1)}, bf16[768,128]{1,0:T(8,128)(2,1)S(1)}, u32[]{:S(2)}, u32[]{:S(2)}) %collective-permute-start.20) | collective-permute-done | bytes 196640 | tf_op jit(solution)/shard_map/ppermute | solution.py:237
  106.5 5.7 %attend_own.1 = (f32[8,384,1]{2,1,0:T(8,128)S(1)}, f32[8,384,1]{2,1,0:T(8,128)S(1)}, f32[8,384,128]{2,1,0:T(8,128)}, bf16[2,192,256]{2,1,0:T(8,128)(2,1)S(1)}) custom-call(s32[1]{0:T(128)} %bitcast.place.info, bf16[384,1024]{1,0:T(8,128)(2,1)S(1)} %copy-done.5, s32[12,128]{1,0:T(8,128)S(1)} %bitcast.12, bf16[784,128]{1,0:T(8,128)(2,1)S(1)} %distant.2.k_in, ...), custom_call_target="tpu_custom_call" | custom-call | tf_op jit(solution)/shard_map/attend_own/pallas_call | solution.py:495
  112.2 7.8 %attend_far.1 = (bf16[384,1024]{1,0:T(8,128)(2,1)}, bf16[4,192,256]{2,1,0:T(8,128)(2,1)}) custom-call(s32[1]{0:T(128)} %bitcast.place.info, bf16[384,1024]{1,0:T(8,128)(2,1)S(1)} %copy-done.5, s32[12,128]{1,0:T(8,128)S(1)} %bitcast.13, bf16[784,128]{1,0:T(8,128)(2,1)S(1)} %collective-permute-done.14.k_across, ...), custom_call_target="tpu_custom_call" | custom-call | tf_op jit(solution)/shard_map/attend_far/pallas_call | solution.py:510
  (41 shorter events, 0.1 us)
Async XLA Ops:
  1.7 12.7 %collective-permute-start.1 = (bf16[384,512]{1,0:T(8,128)(2,1)S(1)}, bf16[384,512]{1,0:T(8,128)(2,1)S(1)}, u32[]{:S(2)}, u32[]{:S(2)}) collective-permute-start(bf16[384,512]{1,0:T(8,128)(2,1)S(1)} %constant_dynamic-slice_fusion), channel_id=1, source_target_pairs={{0,8},{24,16},{1,9},{25,17},{2,10},{26,18},{3,11},{27,19},{4,12},{... | collective-permute-start | bytes 1179656 | tf_op jit(solution)/shard_map/ppermute | solution.py:237
  3.0 15.8 %collective-permute-start = (bf16[2048,128]{1,0:T(8,128)(2,1)}, bf16[2048,128]{1,0:T(8,128)(2,1)S(1)}, u32[]{:S(2)}, u32[]{:S(2)}) collective-permute-start(bf16[2048,128]{1,0:T(8,128)(2,1)} %kw_ref.1), channel_id=1, source_target_pairs={{8,16},{16,8},{9,17},{17,9},{10,18},{18,10},{11,19},{19,11},{12,20... | collective-permute-start | bytes 1572872 | tf_op jit(solution)/shard_map/ppermute | solution.py:237
  14.4 13.1 %collective-permute-start.10 = (bf16[2048,128]{1,0:T(8,128)(2,1)}, bf16[2048,128]{1,0:T(8,128)(2,1)}, u32[]{:S(2)}, u32[]{:S(2)}) collective-permute-start(bf16[2048,128]{1,0:T(8,128)(2,1)} %kw_ref.1), channel_id=1, source_target_pairs={{0,8},{8,0},{16,24},{24,16},{1,9},{9,1},{17,25},{25,17},{2,10},{10... | collective-permute-start | bytes 1572872 | tf_op jit(solution)/shard_map/ppermute | solution.py:237
  14.4 15.8 %collective-permute-start.2 = (bf16[384,512]{1,0:T(8,128)(2,1)S(1)}, bf16[384,512]{1,0:T(8,128)(2,1)S(1)}, u32[]{:S(2)}, u32[]{:S(2)}) collective-permute-start(bf16[384,512]{1,0:T(8,128)(2,1)S(1)} %collective-permute-done.1.refs_0_), channel_id=1, source_target_pairs={{0,2},{1,3},{2,0},{3,1},{4,6},{5,7},{6,4},{7,5},{8,10},{9,11},{10,... | collective-permute-start | bytes 1179656 | tf_op jit(solution)/shard_map/ppermute | solution.py:240
  18.7 0.8 copy-start.8
  19.5 24.0 %collective-permute-start.5 = (bf16[2048,128]{1,0:T(8,128)(2,1)}, bf16[2048,128]{1,0:T(8,128)(2,1)S(1)}, u32[]{:S(2)}, u32[]{:S(2)}) collective-permute-start(bf16[2048,128]{1,0:T(8,128)(2,1)} %vw_ref.1), channel_id=1, source_target_pairs={{8,16},{16,8},{9,17},{17,9},{10,18},{18,10},{11,19},{19,11},{12,20... | collective-permute-start | bytes 1572872 | tf_op jit(solution)/shard_map/ppermute | solution.py:237
  21.9 18.2 %collective-permute-start.3 = (bf16[384,512]{1,0:T(8,128)(2,1)S(1)}, bf16[384,512]{1,0:T(8,128)(2,1)S(1)}, u32[]{:S(2)}, u32[]{:S(2)}) collective-permute-start(bf16[384,512]{1,0:T(8,128)(2,1)S(1)} %collective-permute-done.1.refs_0_), channel_id=1, source_target_pairs={{0,4},{1,5},{2,6},{3,7},{4,0},{5,1},{6,2},{7,3},{8,12},{9,13},{10,... | collective-permute-start | bytes 1179656 | tf_op jit(solution)/shard_map/ppermute | solution.py:240
  27.5 17.4 %collective-permute-start.12 = (bf16[2048,128]{1,0:T(8,128)(2,1)}, bf16[2048,128]{1,0:T(8,128)(2,1)}, u32[]{:S(2)}, u32[]{:S(2)}) collective-permute-start(bf16[2048,128]{1,0:T(8,128)(2,1)} %vw_ref.1), channel_id=1, source_target_pairs={{0,8},{8,0},{16,24},{24,16},{1,9},{9,1},{17,25},{25,17},{2,10},{10... | collective-permute-start | bytes 1572872 | tf_op jit(solution)/shard_map/ppermute | solution.py:237
  27.8 15.8 %collective-permute-start.4 = (bf16[384,512]{1,0:T(8,128)(2,1)S(1)}, bf16[384,512]{1,0:T(8,128)(2,1)S(1)}, u32[]{:S(2)}, u32[]{:S(2)}) collective-permute-start(bf16[384,512]{1,0:T(8,128)(2,1)S(1)} %collective-permute-done.1.refs_0_), channel_id=1, source_target_pairs={{0,6},{1,7},{2,4},{3,5},{4,2},{5,3},{6,0},{7,1},{8,14},{9,15},{10,... | collective-permute-start | bytes 1179656 | tf_op jit(solution)/shard_map/ppermute | solution.py:240
  30.3 14.6 %collective-permute-start.6 = (bf16[384,512]{1,0:T(8,128)(2,1)S(1)}, bf16[384,512]{1,0:T(8,128)(2,1)S(1)}, u32[]{:S(2)}, u32[]{:S(2)}) collective-permute-start(bf16[384,512]{1,0:T(8,128)(2,1)S(1)} %collective-permute-done.1.refs_0_), channel_id=1, source_target_pairs={{0,1},{1,0},{2,3},{3,2},{4,5},{5,4},{6,7},{7,6},{8,9},{9,8},{10,11... | collective-permute-start | bytes 1179656 | tf_op jit(solution)/shard_map/ppermute | solution.py:240
  40.1 19.2 %collective-permute-start.11 = (bf16[2048,128]{1,0:T(8,128)(2,1)}, bf16[2048,128]{1,0:T(8,128)(2,1)}, u32[]{:S(2)}, u32[]{:S(2)}) collective-permute-start(bf16[2048,128]{1,0:T(8,128)(2,1)} %collective-permute-done.10.kw_ref), channel_id=1, source_target_pairs={{8,16},{16,8},{9,17},{17,9},{10,18},{18,10},{11,19},{19,11},{12,20... | collective-permute-start | bytes 1572872 | tf_op jit(solution)/shard_map/ppermute | solution.py:237
  43.6 0.8 copy-start.10
  44.4 8.5 %collective-permute-start.7 = (bf16[384,512]{1,0:T(8,128)(2,1)S(1)}, bf16[384,512]{1,0:T(8,128)(2,1)S(1)}, u32[]{:S(2)}, u32[]{:S(2)}) collective-permute-start(bf16[384,512]{1,0:T(8,128)(2,1)S(1)} %collective-permute-done.2.refs_2_), channel_id=1, source_target_pairs={{0,1},{1,0},{2,3},{3,2},{4,5},{5,4},{6,7},{7,6},{8,9},{9,8},{10,11... | collective-permute-start | bytes 1179656 | tf_op jit(solution)/shard_map/ppermute | solution.py:240
  44.4 8.5 %collective-permute-start.8 = (bf16[384,512]{1,0:T(8,128)(2,1)S(1)}, bf16[384,512]{1,0:T(8,128)(2,1)S(1)}, u32[]{:S(2)}, u32[]{:S(2)}) collective-permute-start(bf16[384,512]{1,0:T(8,128)(2,1)S(1)} %collective-permute-done.3.refs_4_), channel_id=1, source_target_pairs={{0,1},{1,0},{2,3},{3,2},{4,5},{5,4},{6,7},{7,6},{8,9},{9,8},{10,11... | collective-permute-start | bytes 1179656 | tf_op jit(solution)/shard_map/ppermute | solution.py:240
  44.9 8.0 %collective-permute-start.9 = (bf16[384,512]{1,0:T(8,128)(2,1)S(1)}, bf16[384,512]{1,0:T(8,128)(2,1)S(1)}, u32[]{:S(2)}, u32[]{:S(2)}) collective-permute-start(bf16[384,512]{1,0:T(8,128)(2,1)S(1)} %collective-permute-done.4.refs_6_), channel_id=1, source_target_pairs={{0,1},{1,0},{2,3},{3,2},{4,5},{5,4},{6,7},{7,6},{8,9},{9,8},{10,11... | collective-permute-start | bytes 1179656 | tf_op jit(solution)/shard_map/ppermute | solution.py:240
  44.9 40.2 %collective-permute-start.16 = (bf16[2048,128]{1,0:T(8,128)(2,1)}, bf16[2048,128]{1,0:T(8,128)(2,1)}, u32[]{:S(2)}, u32[]{:S(2)}) collective-permute-start(bf16[2048,128]{1,0:T(8,128)(2,1)} %collective-permute-done.12.vw_ref), channel_id=1, source_target_pairs={{8,16},{16,8},{9,17},{17,9},{10,18},{18,10},{11,19},{19,11},{12,20... | collective-permute-start | bytes 1572872 | tf_op jit(solution)/shard_map/ppermute | solution.py:237
  47.9 1.0 copy-start.12
  49.0 1.0 copy-start.13
  52.0 0.7 copy-start.6
  52.9 6.4 %copy-start = (bf16[384,512]{1,0:T(8,128)(2,1)}, bf16[384,512]{1,0:T(8,128)(2,1)S(1)}, u32[]{:S(2)}) copy-start(bf16[384,512]{1,0:T(8,128)(2,1)S(1)} %collective-permute-done.8.refs_5_) | copy-start | bytes 1179652
  52.9 0.8 copy-start.2
  53.7 1.0 copy-start.3
  54.7 1.0 copy-start.9
  55.7 1.0 copy-start.11
  56.7 2.6 %copy-start.7 = (f32[384,256]{1,0:T(8,128)S(1)}, f32[384,256]{1,0:T(8,128)}, u32[]{:S(2)}) copy-start(f32[384,256]{1,0:T(8,128)} %copy-done.6) | copy-start | bytes 1179652
  59.3 16.6 %copy-start.15 = (bf16[128]{0:T(256)(128)(2,1)S(1)}, bf16[128]{0:T(256)(128)(2,1)}, u32[]{:S(2)}) copy-start(bf16[128]{0:T(256)(128)(2,1)} %param.12) | copy-start | bytes 772
  62.5 13.4 %collective-permute-start.13 = (f32[392,256]{1,0:T(8,128)S(1)}, f32[392,256]{1,0:T(8,128)}, u32[]{:S(2)}, u32[]{:S(2)}) collective-permute-start(f32[392,256]{1,0:T(8,128)S(1)} %partial.1.near_ref), channel_id=1, source_target_pairs={{0,8},{24,16},{1,9},{25,17},{2,10},{26,18},{3,11},{27,19},{4,12},{... | collective-permute-start | bytes 1204232 | tf_op jit(solution)/shard_map/ppermute | solution.py:237
  76.0 1.0 copy-start.1
  77.0 1.0 copy-start.4
  77.9 7.2 %copy-start.16 = (bf16[128]{0:T(256)(128)(2,1)S(1)}, bf16[128]{0:T(256)(128)(2,1)}, u32[]{:S(2)}) copy-start(bf16[128]{0:T(256)(128)(2,1)} %param.13) | copy-start | bytes 772
  81.7 10.9 %collective-permute-start.14 = (bf16[784,128]{1,0:T(8,128)(2,1)S(1)}, bf16[784,128]{1,0:T(8,128)(2,1)S(1)}, u32[]{:S(2)}, u32[]{:S(2)}) collective-permute-start(bf16[784,128]{1,0:T(8,128)(2,1)S(1)} %distant.2.k_in), channel_id=1, source_target_pairs={{8,16},{16,8},{9,17},{17,9},{10,18},{18,10},{11,19},{19,11},{12,20... | collective-permute-start | bytes 602120 | tf_op jit(solution)/shard_map/ppermute | solution.py:237
  85.2 21.3 %copy-start.5 = (bf16[384,1024]{1,0:T(8,128)(2,1)S(1)}, bf16[384,1024]{1,0:T(8,128)(2,1)}, u32[]{:S(2)}) copy-start(bf16[384,1024]{1,0:T(8,128)(2,1)} %q_ref.3) | copy-start | bytes 2359300
  85.2 21.3 %copy-start.14 = (s32[1536]{0:T(1024)S(1)}, s32[1536]{0:T(1024)}, u32[]{:S(2)}) copy-start(s32[1536]{0:T(1024)} %param.14) | copy-start | bytes 18436
  88.9 7.8 %collective-permute-start.17 = (bf16[768,128]{1,0:T(8,128)(2,1)S(1)}, bf16[768,128]{1,0:T(8,128)(2,1)S(1)}, u32[]{:S(2)}, u32[]{:S(2)}) collective-permute-start(bf16[768,128]{1,0:T(8,128)(2,1)S(1)} %distant.3.v_in), channel_id=1, source_target_pairs={{8,16},{16,8},{9,17},{17,9},{10,18},{18,10},{11,19},{19,11},{12,20... | collective-permute-start | bytes 589832 | tf_op jit(solution)/shard_map/ppermute | solution.py:237
  91.3 6.8 %collective-permute-start.19 = (bf16[784,128]{1,0:T(8,128)(2,1)S(1)}, bf16[784,128]{1,0:T(8,128)(2,1)S(1)}, u32[]{:S(2)}, u32[]{:S(2)}) collective-permute-start(bf16[784,128]{1,0:T(8,128)(2,1)S(1)} %distant.2.k_in), channel_id=1, source_target_pairs={{8,0},{16,24},{9,1},{17,25},{10,2},{18,26},{11,3},{19,27},{12,4},{... | collective-permute-start | bytes 602120 | tf_op jit(solution)/shard_map/ppermute | solution.py:237
  92.6 19.6 %collective-permute-start.15 = (bf16[784,128]{1,0:T(8,128)(2,1)S(1)}, bf16[784,128]{1,0:T(8,128)(2,1)S(1)}, u32[]{:S(2)}, u32[]{:S(2)}) collective-permute-start(bf16[784,128]{1,0:T(8,128)(2,1)S(1)} %collective-permute-done.14.k_across), channel_id=1, source_target_pairs={{8,0},{16,24},{9,1},{17,25},{10,2},{18,26},{11,3},{19,27},{12,4},{... | collective-permute-start | bytes 602120 | tf_op jit(solution)/shard_map/ppermute | solution.py:237
  93.9 12.6 %collective-permute-start.20 = (bf16[768,128]{1,0:T(8,128)(2,1)S(1)}, bf16[768,128]{1,0:T(8,128)(2,1)S(1)}, u32[]{:S(2)}, u32[]{:S(2)}) collective-permute-start(bf16[768,128]{1,0:T(8,128)(2,1)S(1)} %distant.3.v_in), channel_id=1, source_target_pairs={{8,0},{16,24},{9,1},{17,25},{10,2},{18,26},{11,3},{19,27},{12,4},{... | collective-permute-start | bytes 589832 | tf_op jit(solution)/shard_map/ppermute | solution.py:237
  96.7 15.5 %collective-permute-start.18 = (bf16[768,128]{1,0:T(8,128)(2,1)S(1)}, bf16[768,128]{1,0:T(8,128)(2,1)S(1)}, u32[]{:S(2)}, u32[]{:S(2)}) collective-permute-start(bf16[768,128]{1,0:T(8,128)(2,1)S(1)} %collective-permute-done.17.v_across), channel_id=1, source_target_pairs={{8,0},{16,24},{9,1},{17,25},{10,2},{18,26},{11,3},{19,27},{12,4},{... | collective-permute-start | bytes 589832 | tf_op jit(solution)/shard_map/ppermute | solution.py:237

commit v6 on v5

--- a/solution.py
+++ b/solution.py
@@ -11,7 +11,7 @@
 HD = 128
 PAGE = 16
 NEG = -1e30
-KERNEL_VMEM = 48 * 1024 * 1024
+KERNEL_VMEM = 24 * 1024 * 1024
 PROMPTS = 4
 
 
@@ -135,12 +135,17 @@
             acc_ref[...] = total
 
 
-def near_kernel(place, h_ref, kw_ref, vw_ref, out_ref, h_buf, sem):
-    copy = chunk_copy(h_ref, place[0], h_buf, sem)
-    copy.start()
-    weight = jnp.concatenate([kw_ref[...], vw_ref[...]], axis=1)
-    copy.wait()
-    out_ref[...] = jnp.dot(h_buf[...], weight, preferred_element_type=jnp.float32)
+def near_kernel(place, h_ref, kw_ref, vw_ref, out_ref, h_buf, w_buf, sems):
+    copies = [
+        chunk_copy(h_ref, place[0], h_buf, sems.at[0]),
+        pltpu.make_async_copy(kw_ref, w_buf.at[:, pl.ds(0, HD)], sems.at[1]),
+        pltpu.make_async_copy(vw_ref, w_buf.at[:, pl.ds(HD, HD)], sems.at[2]),
+    ]
+    for copy in copies:
+        copy.start()
+    for copy in copies:
+        copy.wait()
+    out_ref[...] = jnp.dot(h_buf[...], w_buf[...], preferred_element_type=jnp.float32)
 
 
 def partial_kernel(place, h_ref, kw_ref, vw_ref, before_ref, owner_ref, out_ref, h_buf, sem):
@@ -194,26 +199,27 @@
         out_ref[2 * span :] = jnp.concatenate([lower, upper], axis=0).astype(jnp.bfloat16)
 
 
-ANY = pl.BlockSpec(memory_space=pl.ANY)
 EXTRA = 8
-
-
-def call_project(kernel, name, place, operands, rows, columns, kind, scratch):
-    whole = [pl.BlockSpec(x.shape, lambda k, place: (0, 0)) for x in operands[1:]]
+HELD = pl.BlockSpec(memory_space=pltpu.HBM)
+FAST = pl.BlockSpec(memory_space=pltpu.VMEM)
+SCALAR = pl.BlockSpec(memory_space=pltpu.SMEM)
+
+
+def in_hbm(x):
+    return pltpu.with_memory_space_constraint(x, pltpu.HBM)
+
+
+def call_project(kernel, name, place, operands, rows, columns, kind, scratch, held=1, copies=()):
     return pl.pallas_call(
         kernel,
-        grid_spec=pltpu.PrefetchScalarGridSpec(
-            num_scalar_prefetch=1,
-            grid=(1,),
-            in_specs=[ANY] + whole,
-            out_specs=pl.BlockSpec((rows, columns), lambda k, place: (0, 0)),
-            scratch_shapes=scratch + [pltpu.SemaphoreType.DMA],
-        ),
+        in_specs=[SCALAR] + [HELD] * held + [FAST] * (len(operands) - held),
+        out_specs=FAST,
         out_shape=jax.ShapeDtypeStruct((rows, columns), kind),
+        scratch_shapes=scratch + [pltpu.SemaphoreType.DMA(copies)],
         compiler_params=pltpu.CompilerParams(vmem_limit_bytes=KERNEL_VMEM),
         cost_estimate=pl.CostEstimate(flops=0, bytes_accessed=0, transcendentals=0),
         name=name,
-    )(place, *operands)
+    )(place, *[in_hbm(x) for x in operands[:held]], *operands[held:])
 
 
 INWARD = [(0, 1), (3, 2)]
@@ -242,25 +248,6 @@
     mine = second * (width // 2) + member * share
     cut = lax.dynamic_slice_in_dim(hidden, mine, share, axis=1)
     tie = lax.optimization_barrier
-    key_facing = send(key_weight, ACROSS)
-    cut = send(cut, INWARD)
-    cut, key_after = tie((cut, key_weight))
-    key_swapped = send(key_after, SWAP)
-    key_facing, value_after = tie((key_facing, value_weight))
-    value_facing = send(value_after, ACROSS)
-    key_swapped, value_after = tie((key_swapped, value_weight))
-    value_swapped = send(value_after, SWAP)
-    chips = [trade(cut, 2), trade(cut, 4), trade(cut, 6)]
-    chips, value_facing = tie((chips, value_facing))
-    chips = [cut] + chips
-    mates = [trade(x, 1) for x in chips]
-    pieces = [x for both in zip(chips, mates) for x in both]
-    key_distant = send(key_swapped, ACROSS)
-    value_distant = send(value_swapped, ACROSS)
-
-    def place(chunk):
-        return jnp.stack([chunk, second, member])
-
     block = pltpu.VMEM((span, depth), jnp.bfloat16)
     both = pltpu.VMEM((depth, 2 * HD), jnp.bfloat16)
     own_part = call_project(
@@ -271,8 +258,28 @@
         span,
         2 * HD,
         jnp.float32,
-        [block],
-    )
+        [block, both],
+        held=3,
+        copies=(3,),
+    )
+    cut = send(cut, INWARD)
+    key_facing = send(key_weight, ACROSS)
+    key_facing, value_after = tie((key_facing, value_weight))
+    value_facing = send(value_after, ACROSS)
+    cut, key_after, own_part = tie((cut, key_weight, own_part))
+    key_swapped = send(key_after, SWAP)
+    key_swapped, value_after = tie((key_swapped, value_weight))
+    value_swapped = send(value_after, SWAP)
+    chips = [cut, trade(cut, 2), trade(cut, 4), trade(cut, 6)]
+    chips, value_facing = tie((chips, value_facing))
+    mates = [trade(x, 1) for x in chips]
+    pieces = [x for both_cores in zip(chips, mates) for x in both_cores]
+    key_distant = send(key_swapped, ACROSS)
+    value_distant = send(value_swapped, ACROSS)
+
+    def place(chunk):
+        return jnp.stack([chunk, second, member])
+
     faced = call_project(
         facing_kernel,
         "facing",
@@ -283,7 +290,7 @@
         jnp.float32,
         [block, both],
     )
-    faced, own_part, key_distant = tie((faced, own_part, key_distant))
+    own_part, key_distant = tie((own_part, key_distant))
     owners = jnp.broadcast_to(page_owner.T.astype(jnp.float32), (EXTRA, page_owner.shape[0]))
     owners = jnp.pad(owners, ((0, 0), (0, HD - page_owner.shape[0])))
     own_part = call_project(
@@ -299,7 +306,7 @@
     outer_part = send(own_part, INWARD)
 
     def finish(column, weight, bias):
-        pair = call_project(
+        return call_project(
             functools.partial(distant_kernel, column),
             "distant",
             place(distant),
@@ -309,13 +316,19 @@
             jnp.bfloat16,
             [block, pltpu.VMEM((span, HD), jnp.float32)],
         )
-        out = send(pair, OUTWARD)
-        across = send(pair, ACROSS)
-        return pair, out, across, send(across, OUTWARD)
 
     keys = finish(0, key_distant, key_bias)
+    keys_out, keys_across = send(keys, OUTWARD), send(keys, ACROSS)
     values = finish(1, value_distant, value_bias)
-    return keys, values
+    values_across = send(values, ACROSS)
+    keys_out, values_after = tie((keys_out, values))
+    values_out = send(values_after, OUTWARD)
+    keys_across, values_across = tie((keys_across, values_across))
+    keys_far, values_far = send(keys_across, OUTWARD), send(values_across, OUTWARD)
+    return (
+        (keys, keys_out, keys_across, keys_far),
+        (values, values_out, values_across, values_far),
+    )
 
 
 def softmax_step(q, keys, values, allowed, before):
@@ -480,9 +493,8 @@
     heads = queries.shape[1] // HD
     info = lax.axis_index("pre").astype(jnp.int32)[None]
     segments = segment_ids.reshape(-1, HD)
-    smem = pl.BlockSpec(memory_space=pltpu.SMEM)
-    vmem = pl.BlockSpec(memory_space=pltpu.VMEM)
-    cost = pl.CostEstimate(flops=0, bytes_accessed=0, transcendentals=0)
+    scores = heads * span * 2 * span
+    cost = pl.CostEstimate(flops=4 * scores * HD, bytes_accessed=8 * scores, transcendentals=scores)
     params = pltpu.CompilerParams(vmem_limit_bytes=KERNEL_VMEM)
     scratch = [
         pltpu.VMEM((2 * span + 2 * EXTRA, HD), jnp.bfloat16),
@@ -494,8 +506,8 @@
     ]
     state = pl.pallas_call(
         functools.partial(own_kernel, heads),
-        in_specs=[smem, ANY] + [vmem] * 5,
-        out_specs=[vmem] * 4,
+        in_specs=[SCALAR, HELD] + [FAST] * 5,
+        out_specs=[FAST] * 4,
         out_shape=[
             jax.ShapeDtypeStruct((heads, span, 1), jnp.float32),
             jax.ShapeDtypeStruct((heads, span, 1), jnp.float32),
@@ -506,11 +518,11 @@
         compiler_params=params,
         cost_estimate=cost,
         name="attend_own",
-    )(info, queries, segments, *keys[:2], *values[:2])
+    )(info, in_hbm(queries), segments, *keys[:2], *values[:2])
     return pl.pallas_call(
         functools.partial(far_kernel, heads),
-        in_specs=[smem, ANY] + [vmem] * 9,
-        out_specs=[vmem] * 2,
+        in_specs=[SCALAR, HELD] + [FAST] * 9,
+        out_specs=[FAST] * 2,
         out_shape=[
             jax.ShapeDtypeStruct(queries.shape, jnp.bfloat16),
             jax.ShapeDtypeStruct((4, capacity * PAGE, 2 * HD), jnp.bfloat16),
@@ -519,7 +531,7 @@
         compiler_params=params,
         cost_estimate=cost,
         name="attend_far",
-    )(info, queries, segments, *keys[2:], *values[2:], *state)
+    )(info, in_hbm(queries), segments, *keys[2:], *values[2:], *state)
 
 
 def gathered(hidden, key_weight, value_weight, key_bias, value_bias):

time: 122 us -> 99.9 us (0.82)
  waiting for transfers between devices: 47.8 us -> 33 us
  local copies, waits for them, and re-layouts: 11.3 us -> 4.74 us
  starting transfers between devices: 30.5 us -> 32.4 us
  Pallas kernels: 28.6 us -> 26.9 us
    ppermute x14, waiting for transfers between devices: 38 us -> 27 us  [send(): return lax.ppermute(x, 'pre', pairs)]
    unnamed x34 -> x24, local copies, waits for them, and re-layouts: 10.3 us -> 3.71 us
    ppermute x7, waiting for transfers between devices: 9.84 us -> 5.93 us  [trade(): lax.ppermute(x, ('dec', 'tp'), [(m, m ^ apart) for m in range(PIECES)])]
    ppermute x14, starting transfers between devices: 24.5 us -> 26.3 us  [send(): return lax.ppermute(x, 'pre', pairs)]
    pallas_call x7, Pallas kernels: 28.6 us -> 26.9 us  [the longest x5 14.5 us: call_project(): pl.pallas_call(kernel, in_specs=[SCALAR] + [HELD] * held + [FAST] * (len(...]
  transfers between devices with their start and end apart: 21 -> 21, of which waited for: 7 -> 14; matrix products, arithmetic and copies ran while one was open for 1% -> 0% of each run, Pallas kernels for 17% -> 20%
where the time goes in v6:
time: 99.9 us; the launch traced here: 98.3 us
  waiting for transfers between devices  33 us (33%)
  starting transfers between devices  32.4 us (32%)
  Pallas kernels  26.9 us (27%)
  local copies, waits for them, and re-layouts  4.74 us (5%)
  between operations  1.09 us (1%)
    ppermute x14, waiting for transfers between devices, send(): return lax.ppermute(x, 'pre', pairs)  27 us
    ppermute x14, starting transfers between devices, send(): return lax.ppermute(x, 'pre', pairs)  26.3 us
    pallas_call x5, Pallas kernels, call_project(): pl.pallas_call(kernel, in_specs=[SCALAR] + [HELD] * held + [FAST] * (len(...  14.5 us
    pallas_call x1, Pallas kernels, attention_of_pairs(): pl.pallas_call(functools.partial(far_kernel, heads), in_specs=[SCALAR, HE...  7.23 us
    ppermute x7, starting transfers between devices, trade(): lax.ppermute(x, ('dec', 'tp'), [(m, m ^ apart) for m in range(PIECES)])  6.17 us
    ppermute x7, waiting for transfers between devices, trade(): lax.ppermute(x, ('dec', 'tp'), [(m, m ^ apart) for m in range(PIECES)])  5.93 us
    pallas_call x1, Pallas kernels, attention_of_pairs(): pl.pallas_call(functools.partial(own_kernel, heads), in_specs=[SCALAR, HE...  5.17 us
    unnamed x24, local copies, waits for them, and re-layouts  3.71 us
  transfers between devices with their start and end apart: 21, of which 14 were waited for; matrix products, arithmetic and copies ran while one was open for 0% of the time, Pallas kernels for 20%

profile of v6, /device:TPU:16, one launch (start us, length us, event | category | flops | bytes accessed | tf_op | source)
XLA Modules:
  0.0 98.3 jit_solution(11608343770985008679)
XLA Ops:
  0.6 1.0 %constant_dynamic-slice_fusion = bf16[384,512]{1,0:T(8,128)(2,1)S(1)} fusion(bf16[384,8192]{1,0:T(8,128)(2,1)} %h_ref.9, s32[]{:T(128)S(6)} %select_n.3), kind=kLoop, calls=%fused_computation.3 | loop fusion | bytes 786436 | tf_op jit(solution)/shard_map/dynamic_slice | solution.py:249
  1.7 1.3 %collective-permute-start = (bf16[384,512]{1,0:T(8,128)(2,1)S(1)}, bf16[384,512]{1,0:T(8,128)(2,1)S(1)}, u32[]{:S(2)}, u32[]{:S(2)}) collective-permute-start(bf16[384,512]{1,0:T(8,128)(2,1)S(1)} %constant_dynamic-slice_fusion), channel_id=1, source_target_pairs={{0,8},{24,16},{1,9},{25,17},{2,10},{26,18},{3,11},{27,19},{4,12},{... | collective-permute-start | bytes 1179656 | tf_op jit(solution)/shard_map/ppermute | solution.py:243
  3.0 2.4 %collective-permute-start.5 = (bf16[2048,128]{1,0:T(8,128)(2,1)}, bf16[2048,128]{1,0:T(8,128)(2,1)S(1)}, u32[]{:S(2)}, u32[]{:S(2)}) collective-permute-start(bf16[2048,128]{1,0:T(8,128)(2,1)} %kw_ref.1), channel_id=1, source_target_pairs={{8,16},{16,8},{9,17},{17,9},{10,18},{18,10},{11,19},{19,11},{12,20... | collective-permute-start | bytes 1572872 | tf_op jit(solution)/shard_map/ppermute | solution.py:243
  5.3 0.0 copy-start.9
  5.4 2.4 %near.1.before_ref = f32[384,256]{1,0:T(8,128)S(1)} custom-call(s32[1]{0:T(128)} %bitcast.place.info, bf16[384,8192]{1,0:T(8,128)(2,1)} %h_ref.9, bf16[2048,128]{1,0:T(8,128)(2,1)} %kw_ref.1, bf16[2048,128]{1,0:T(8,128)(2,1)} %vw_ref.1), custom_call_target="tpu_custom_call" | custom-call | tf_op jit(solution)/shard_map/near/pallas_call | solution.py:213
  7.7 6.7 %collective-permute-done.refs_0_ = bf16[384,512]{1,0:T(8,128)(2,1)S(1)} collective-permute-done((bf16[384,512]{1,0:T(8,128)(2,1)S(1)}, bf16[384,512]{1,0:T(8,128)(2,1)S(1)}, u32[]{:S(2)}, u32[]{:S(2)}) %collective-permute-start) | collective-permute-done | bytes 393248 | tf_op jit(solution)/shard_map/ppermute | solution.py:243
  14.4 2.4 %collective-permute-start.8 = (bf16[384,512]{1,0:T(8,128)(2,1)S(1)}, bf16[384,512]{1,0:T(8,128)(2,1)S(1)}, u32[]{:S(2)}, u32[]{:S(2)}) collective-permute-start(bf16[384,512]{1,0:T(8,128)(2,1)S(1)} %collective-permute-done.refs_0_), channel_id=1, source_target_pairs={{0,6},{1,7},{2,4},{3,5},{4,2},{5,3},{6,0},{7,1},{8,14},{9,15},{10,... | collective-permute-start | bytes 1179656 | tf_op jit(solution)/shard_map/ppermute | solution.py:246
  16.9 1.9 %collective-permute-done.5.kw_ref = bf16[2048,128]{1,0:T(8,128)(2,1)S(1)} collective-permute-done((bf16[2048,128]{1,0:T(8,128)(2,1)}, bf16[2048,128]{1,0:T(8,128)(2,1)S(1)}, u32[]{:S(2)}, u32[]{:S(2)}) %collective-permute-start.5) | collective-permute-done | bytes 524320 | tf_op jit(solution)/shard_map/ppermute | solution.py:243
  18.7 0.8 copy-done
  19.5 2.3 %collective-permute-start.9 = (bf16[2048,128]{1,0:T(8,128)(2,1)S(1)}, bf16[2048,128]{1,0:T(8,128)(2,1)S(1)}, u32[]{:S(2)}, u32[]{:S(2)}) collective-permute-start(bf16[2048,128]{1,0:T(8,128)(2,1)S(1)} %copy-done.10), channel_id=1, source_target_pairs={{8,16},{16,8},{9,17},{17,9},{10,18},{18,10},{11,19},{19,11},{12,20... | collective-permute-start | bytes 1572872 | tf_op jit(solution)/shard_map/ppermute | solution.py:243
  21.9 1.6 %collective-permute-start.7 = (bf16[384,512]{1,0:T(8,128)(2,1)S(1)}, bf16[384,512]{1,0:T(8,128)(2,1)S(1)}, u32[]{:S(2)}, u32[]{:S(2)}) collective-permute-start(bf16[384,512]{1,0:T(8,128)(2,1)S(1)} %collective-permute-done.refs_0_), channel_id=1, source_target_pairs={{0,4},{1,5},{2,6},{3,7},{4,0},{5,1},{6,2},{7,3},{8,12},{9,13},{10,... | collective-permute-start | bytes 1179656 | tf_op jit(solution)/shard_map/ppermute | solution.py:246
  23.5 1.5 %collective-permute-start.6 = (bf16[384,512]{1,0:T(8,128)(2,1)S(1)}, bf16[384,512]{1,0:T(8,128)(2,1)S(1)}, u32[]{:S(2)}, u32[]{:S(2)}) collective-permute-start(bf16[384,512]{1,0:T(8,128)(2,1)S(1)} %collective-permute-done.refs_0_), channel_id=1, source_target_pairs={{0,2},{1,3},{2,0},{3,1},{4,6},{5,7},{6,4},{7,5},{8,10},{9,11},{10,... | collective-permute-start | bytes 1179656 | tf_op jit(solution)/shard_map/ppermute | solution.py:246
  25.0 2.3 %collective-permute-done.1.kw_ref = bf16[2048,128]{1,0:T(8,128)(2,1)} collective-permute-done((bf16[2048,128]{1,0:T(8,128)(2,1)S(1)}, bf16[2048,128]{1,0:T(8,128)(2,1)}, u32[]{:S(2)}, u32[]{:S(2)}) %collective-permute-start.1) | collective-permute-done | bytes 524320 | tf_op jit(solution)/shard_map/ppermute | solution.py:243
  27.3 0.3 collective-permute-start.3
  27.6 2.3 %collective-permute-start.2 = (bf16[2048,128]{1,0:T(8,128)(2,1)}, bf16[2048,128]{1,0:T(8,128)(2,1)S(1)}, u32[]{:S(2)}, u32[]{:S(2)}) collective-permute-start(bf16[2048,128]{1,0:T(8,128)(2,1)} %collective-permute-done.1.kw_ref), channel_id=1, source_target_pairs={{8,16},{16,8},{9,17},{17,9},{10,18},{18,10},{11,19},{19,11},{12,20... | collective-permute-start | bytes 1572872 | tf_op jit(solution)/shard_map/ppermute | solution.py:243
  30.0 3.8 %collective-permute-done.7.refs_4_ = bf16[384,512]{1,0:T(8,128)(2,1)S(1)} collective-permute-done((bf16[384,512]{1,0:T(8,128)(2,1)S(1)}, bf16[384,512]{1,0:T(8,128)(2,1)S(1)}, u32[]{:S(2)}, u32[]{:S(2)}) %collective-permute-start.7) | collective-permute-done | bytes 393248 | tf_op jit(solution)/shard_map/ppermute | solution.py:246
  33.7 0.1 collective-permute-done.6.refs_2_
  33.8 2.5 %collective-permute-done.9.vw_ref = bf16[2048,128]{1,0:T(8,128)(2,1)S(1)} collective-permute-done((bf16[2048,128]{1,0:T(8,128)(2,1)S(1)}, bf16[2048,128]{1,0:T(8,128)(2,1)S(1)}, u32[]{:S(2)}, u32[]{:S(2)}) %collective-permute-start.9) | collective-permute-done | bytes 524320 | tf_op jit(solution)/shard_map/ppermute | solution.py:243
  36.3 0.8 copy-done.2
  37.1 2.2 %collective-permute-done.3.vw_ref = bf16[2048,128]{1,0:T(8,128)(2,1)} collective-permute-done((bf16[2048,128]{1,0:T(8,128)(2,1)S(1)}, bf16[2048,128]{1,0:T(8,128)(2,1)}, u32[]{:S(2)}, u32[]{:S(2)}) %collective-permute-start.3) | collective-permute-done | bytes 524320 | tf_op jit(solution)/shard_map/ppermute | solution.py:243
  39.3 2.3 %collective-permute-start.15 = (bf16[2048,128]{1,0:T(8,128)(2,1)}, bf16[2048,128]{1,0:T(8,128)(2,1)}, u32[]{:S(2)}, u32[]{:S(2)}) collective-permute-start(bf16[2048,128]{1,0:T(8,128)(2,1)} %collective-permute-done.3.vw_ref), channel_id=1, source_target_pairs={{8,16},{16,8},{9,17},{17,9},{10,18},{18,10},{11,19},{19,11},{12,20... | collective-permute-start | bytes 1572872 | tf_op jit(solution)/shard_map/ppermute | solution.py:243
  41.7 5.8 %collective-permute-done.2.w_ref = bf16[2048,128]{1,0:T(8,128)(2,1)S(1)} collective-permute-done((bf16[2048,128]{1,0:T(8,128)(2,1)}, bf16[2048,128]{1,0:T(8,128)(2,1)S(1)}, u32[]{:S(2)}, u32[]{:S(2)}) %collective-permute-start.2) | collective-permute-done | bytes 524320 | tf_op jit(solution)/shard_map/ppermute | solution.py:243
  47.5 3.4 %partial.1.near_ref = f32[392,256]{1,0:T(8,128)S(1)} custom-call(s32[1]{0:T(128)} %bitcast.5.place, bf16[384,8192]{1,0:T(8,128)(2,1)} %h_ref.9, bf16[2048,128]{1,0:T(8,128)(2,1)} %collective-permute-done.1.kw_ref, bf16[2048,128]{1,0:T(8,128)(2,1)} %collective-permute-done.3.vw_ref, f32[384,256]{1,0:T(8,128)S(1)} %near.1.before_ref, f32[8,128]{1,0:T(8,128)S(1)} %pad.7.owner_ref), custom_call_target="tpu_custom_call" | custom-call | tf_op jit(solution)/shard_map/partial/pallas_call | solution.py:213
  50.9 1.3 %collective-permute-start.4 = (f32[392,256]{1,0:T(8,128)S(1)}, f32[392,256]{1,0:T(8,128)}, u32[]{:S(2)}, u32[]{:S(2)}) collective-permute-start(f32[392,256]{1,0:T(8,128)S(1)} %partial.1.near_ref), channel_id=1, source_target_pairs={{0,8},{24,16},{1,9},{25,17},{2,10},{26,18},{3,11},{27,19},{4,12},{... | collective-permute-start | bytes 1204232 | tf_op jit(solution)/shard_map/ppermute | solution.py:243
  52.2 0.1 collective-permute-start.11
  52.3 0.5 collective-permute-start.12
  52.8 0.1 collective-permute-start.13
  52.9 0.1 add_add_fusion.place
  53.0 0.1 add_add_fusion.1.place
  53.0 1.0 collective-permute-done.11.refs_3_
  54.0 0.6 collective-permute-done.12.refs_5_
  54.6 0.6 collective-permute-done.13.refs_7_
  55.1 1.0 %copy-done.1 = bf16[2048,128]{1,0:T(8,128)(2,1)S(1)} copy-done((bf16[2048,128]{1,0:T(8,128)(2,1)S(1)}, bf16[2048,128]{1,0:T(8,128)(2,1)}, u32[]{:S(2)}) %copy-start.1) | copy-done | bytes 524312
  56.2 1.0 %copy-done.3 = bf16[2048,128]{1,0:T(8,128)(2,1)S(1)} copy-done((bf16[2048,128]{1,0:T(8,128)(2,1)S(1)}, bf16[2048,128]{1,0:T(8,128)(2,1)}, u32[]{:S(2)}) %copy-start.3) | copy-done | bytes 524312
  57.2 2.5 %facing.1.facing_ref = f32[768,256]{1,0:T(8,128)S(1)} custom-call(s32[3]{0:T(128)S(1)} %add_add_fusion.1.place, bf16[384,8192]{1,0:T(8,128)(2,1)} %h_ref.9, bf16[2048,128]{1,0:T(8,128)(2,1)S(1)} %copy-done.1, bf16[2048,128]{1,0:T(8,128)(2,1)S(1)} %copy-done.3, bf16[384,512]{1,0:T(8,128)(2,1)S(1)} %collective-permute-done.refs_0_, ...), custom_call_target="tpu_custom_call" | custom-call | tf_op jit(solution)/shard_map/facing/pallas_call | solution.py:213
  59.8 1.0 %collective-permute-done.4.outer_ref = f32[392,256]{1,0:T(8,128)} collective-permute-done((f32[392,256]{1,0:T(8,128)S(1)}, f32[392,256]{1,0:T(8,128)}, u32[]{:S(2)}, u32[]{:S(2)}) %collective-permute-start.4) | collective-permute-done | bytes 401440 | tf_op jit(solution)/shard_map/ppermute | solution.py:243
  60.8 3.0 %distant.2.k_in = bf16[784,128]{1,0:T(8,128)(2,1)S(1)} custom-call(s32[3]{0:T(128)S(1)} %add_add_fusion.place, bf16[384,8192]{1,0:T(8,128)(2,1)} %h_ref.9, bf16[2048,128]{1,0:T(8,128)(2,1)S(1)} %copy-done.5, f32[392,256]{1,0:T(8,128)S(1)} %partial.1.near_ref, f32[392,256]{1,0:T(8,128)} %collective-permute-done.4.outer_ref, f32[768,256]{1,0:T(8,128)S(1)} %facing.1.facing_ref, ...), custom_call_target="tpu_custom_call" | custom-call | tf_op jit(solution)/shard_map/distant/pallas_call | solution.py:213
  63.8 4.3 %collective-permute-start.19 = (bf16[784,128]{1,0:T(8,128)(2,1)S(1)}, bf16[784,128]{1,0:T(8,128)(2,1)S(1)}, u32[]{:S(2)}, u32[]{:S(2)}) collective-permute-start(bf16[784,128]{1,0:T(8,128)(2,1)S(1)} %distant.2.k_in), channel_id=1, source_target_pairs={{8,0},{16,24},{9,1},{17,25},{10,2},{18,26},{11,3},{19,27},{12,4},{... | collective-permute-start | bytes 602120 | tf_op jit(solution)/shard_map/ppermute | solution.py:243
  68.1 2.4 %collective-permute-start.14 = (bf16[784,128]{1,0:T(8,128)(2,1)S(1)}, bf16[784,128]{1,0:T(8,128)(2,1)S(1)}, u32[]{:S(2)}, u32[]{:S(2)}) collective-permute-start(bf16[784,128]{1,0:T(8,128)(2,1)S(1)} %distant.2.k_in), channel_id=1, source_target_pairs={{8,16},{16,8},{9,17},{17,9},{10,18},{18,10},{11,19},{19,11},{12,20... | collective-permute-start | bytes 602120 | tf_op jit(solution)/shard_map/ppermute | solution.py:243
  70.5 3.2 %distant.3.v_in = bf16[768,128]{1,0:T(8,128)(2,1)S(1)} custom-call(s32[3]{0:T(128)S(1)} %add_add_fusion.place, bf16[384,8192]{1,0:T(8,128)(2,1)} %h_ref.9, bf16[2048,128]{1,0:T(8,128)(2,1)} %collective-permute-done.15.w_ref, f32[392,256]{1,0:T(8,128)S(1)} %partial.1.near_ref, f32[392,256]{1,0:T(8,128)} %collective-permute-done.4.outer_ref, ...), custom_call_target="tpu_custom_call" | custom-call | tf_op jit(solution)/shard_map/distant/pallas_call | solution.py:213
  73.7 3.5 %collective-permute-start.16 = (bf16[768,128]{1,0:T(8,128)(2,1)S(1)}, bf16[768,128]{1,0:T(8,128)(2,1)S(1)}, u32[]{:S(2)}, u32[]{:S(2)}) collective-permute-start(bf16[768,128]{1,0:T(8,128)(2,1)S(1)} %distant.3.v_in), channel_id=1, source_target_pairs={{8,16},{16,8},{9,17},{17,9},{10,18},{18,10},{11,19},{19,11},{12,20... | collective-permute-start | bytes 589832 | tf_op jit(solution)/shard_map/ppermute | solution.py:243
  77.2 1.3 %collective-permute-start.20 = (bf16[768,128]{1,0:T(8,128)(2,1)S(1)}, bf16[768,128]{1,0:T(8,128)(2,1)S(1)}, u32[]{:S(2)}, u32[]{:S(2)}) collective-permute-start(bf16[768,128]{1,0:T(8,128)(2,1)S(1)} %distant.3.v_in), channel_id=1, source_target_pairs={{8,0},{16,24},{9,1},{17,25},{10,2},{18,26},{11,3},{19,27},{12,4},{... | collective-permute-start | bytes 589832 | tf_op jit(solution)/shard_map/ppermute | solution.py:243
  78.5 3.5 %collective-permute-done.16.v_across = bf16[768,128]{1,0:T(8,128)(2,1)S(1)} collective-permute-done((bf16[768,128]{1,0:T(8,128)(2,1)S(1)}, bf16[768,128]{1,0:T(8,128)(2,1)S(1)}, u32[]{:S(2)}, u32[]{:S(2)}) %collective-permute-start.16) | collective-permute-done | bytes 196640 | tf_op jit(solution)/shard_map/ppermute | solution.py:243
  82.0 1.3 %collective-permute-start.17 = (bf16[784,128]{1,0:T(8,128)(2,1)S(1)}, bf16[784,128]{1,0:T(8,128)(2,1)S(1)}, u32[]{:S(2)}, u32[]{:S(2)}) collective-permute-start(bf16[784,128]{1,0:T(8,128)(2,1)S(1)} %collective-permute-done.14.k_across), channel_id=1, source_target_pairs={{8,0},{16,24},{9,1},{17,25},{10,2},{18,26},{11,3},{19,27},{12,4},{... | collective-permute-start | bytes 602120 | tf_op jit(solution)/shard_map/ppermute | solution.py:243
  83.3 1.3 %collective-permute-start.18 = (bf16[768,128]{1,0:T(8,128)(2,1)S(1)}, bf16[768,128]{1,0:T(8,128)(2,1)S(1)}, u32[]{:S(2)}, u32[]{:S(2)}) collective-permute-start(bf16[768,128]{1,0:T(8,128)(2,1)S(1)} %collective-permute-done.16.v_across), channel_id=1, source_target_pairs={{8,0},{16,24},{9,1},{17,25},{10,2},{18,26},{11,3},{19,27},{12,4},{... | collective-permute-start | bytes 589832 | tf_op jit(solution)/shard_map/ppermute | solution.py:243
  84.6 5.2 %attend_own.1 = (f32[8,384,1]{2,1,0:T(8,128)S(1)}, f32[8,384,1]{2,1,0:T(8,128)S(1)}, f32[8,384,128]{2,1,0:T(8,128)S(1)}, bf16[2,192,256]{2,1,0:T(8,128)(2,1)S(1)}) custom-call(s32[1]{0:T(128)} %bitcast.place.info, bf16[384,1024]{1,0:T(8,128)(2,1)} %q_ref.3, s32[12,128]{1,0:T(8,128)S(1)} %bitcast.12, bf16[784,128]{1,0:T(8,128)(2,1)S(1)} %distant.2.k_in, ...), custom_call_target="tpu_custom_call" | custom-call | flops 1207959552 | bytes 18874368 | tf_op jit(solution)/shard_map/attend_own/pallas_call | solution.py:507
  89.8 1.1 %collective-permute-done.18.v_far = bf16[768,128]{1,0:T(8,128)(2,1)S(1)} collective-permute-done((bf16[768,128]{1,0:T(8,128)(2,1)S(1)}, bf16[768,128]{1,0:T(8,128)(2,1)S(1)}, u32[]{:S(2)}, u32[]{:S(2)}) %collective-permute-start.18) | collective-permute-done | bytes 196640 | tf_op jit(solution)/shard_map/ppermute | solution.py:243
  90.9 7.2 %attend_far.1 = (bf16[384,1024]{1,0:T(8,128)(2,1)}, bf16[4,192,256]{2,1,0:T(8,128)(2,1)}) custom-call(s32[1]{0:T(128)} %bitcast.place.info, bf16[384,1024]{1,0:T(8,128)(2,1)} %q_ref.3, s32[12,128]{1,0:T(8,128)S(1)} %bitcast.13, bf16[784,128]{1,0:T(8,128)(2,1)S(1)} %collective-permute-done.14.k_across, bf16[784,128]{1,0:T(8,128)(2,1)S(1)} %collective-permute-done.17.k_far, ...), custom_call_target="tpu_custom_call" | custom-call | flops 1207959552 | bytes 18874368 | tf_op jit(solution)/shard_map/attend_far/pallas_call | solution.py:522
  (31 shorter events, 0.1 us)
Async XLA Ops:
  1.7 12.7 %collective-permute-start = (bf16[384,512]{1,0:T(8,128)(2,1)S(1)}, bf16[384,512]{1,0:T(8,128)(2,1)S(1)}, u32[]{:S(2)}, u32[]{:S(2)}) collective-permute-start(bf16[384,512]{1,0:T(8,128)(2,1)S(1)} %constant_dynamic-slice_fusion), channel_id=1, source_target_pairs={{0,8},{24,16},{1,9},{25,17},{2,10},{26,18},{3,11},{27,19},{4,12},{... | collective-permute-start | bytes 1179656 | tf_op jit(solution)/shard_map/ppermute | solution.py:243
  3.0 15.8 %collective-permute-start.5 = (bf16[2048,128]{1,0:T(8,128)(2,1)}, bf16[2048,128]{1,0:T(8,128)(2,1)S(1)}, u32[]{:S(2)}, u32[]{:S(2)}) collective-permute-start(bf16[2048,128]{1,0:T(8,128)(2,1)} %kw_ref.1), channel_id=1, source_target_pairs={{8,16},{16,8},{9,17},{17,9},{10,18},{18,10},{11,19},{19,11},{12,20... | collective-permute-start | bytes 1572872 | tf_op jit(solution)/shard_map/ppermute | solution.py:243
  5.3 9.1 %copy-start.9 = (bf16[2048,128]{1,0:T(8,128)(2,1)S(1)}, bf16[2048,128]{1,0:T(8,128)(2,1)}, u32[]{:S(2)}) copy-start(bf16[2048,128]{1,0:T(8,128)(2,1)} %kw_ref.1) | copy-start | bytes 1572868
  5.4 14.2 %copy-start.10 = (bf16[2048,128]{1,0:T(8,128)(2,1)S(1)}, bf16[2048,128]{1,0:T(8,128)(2,1)}, u32[]{:S(2)}) copy-start(bf16[2048,128]{1,0:T(8,128)(2,1)} %vw_ref.1) | copy-start | bytes 1572868
  5.4 36.3 %copy-start.11 = (s32[24,1]{0,1:T(1,128)S(1)}, s32[24,1]{0,1:T(1,128)}, u32[]{:S(2)}) copy-start(s32[24,1]{0,1:T(1,128)} %param.15) | copy-start | bytes 292
  14.4 12.9 %collective-permute-start.1 = (bf16[2048,128]{1,0:T(8,128)(2,1)S(1)}, bf16[2048,128]{1,0:T(8,128)(2,1)}, u32[]{:S(2)}, u32[]{:S(2)}) collective-permute-start(bf16[2048,128]{1,0:T(8,128)(2,1)S(1)} %copy-done.9), channel_id=1, source_target_pairs={{0,8},{8,0},{16,24},{24,16},{1,9},{9,1},{17,25},{25,17},{2,10},{10... | collective-permute-start | bytes 1572872 | tf_op jit(solution)/shard_map/ppermute | solution.py:243
  14.4 13.2 %collective-permute-start.8 = (bf16[384,512]{1,0:T(8,128)(2,1)S(1)}, bf16[384,512]{1,0:T(8,128)(2,1)S(1)}, u32[]{:S(2)}, u32[]{:S(2)}) collective-permute-start(bf16[384,512]{1,0:T(8,128)(2,1)S(1)} %collective-permute-done.refs_0_), channel_id=1, source_target_pairs={{0,6},{1,7},{2,4},{3,5},{4,2},{5,3},{6,0},{7,1},{8,14},{9,15},{10,... | collective-permute-start | bytes 1179656 | tf_op jit(solution)/shard_map/ppermute | solution.py:246
  18.7 0.8 copy-start
  19.5 16.7 %collective-permute-start.9 = (bf16[2048,128]{1,0:T(8,128)(2,1)S(1)}, bf16[2048,128]{1,0:T(8,128)(2,1)S(1)}, u32[]{:S(2)}, u32[]{:S(2)}) collective-permute-start(bf16[2048,128]{1,0:T(8,128)(2,1)S(1)} %copy-done.10), channel_id=1, source_target_pairs={{8,16},{16,8},{9,17},{17,9},{10,18},{18,10},{11,19},{19,11},{12,20... | collective-permute-start | bytes 1572872 | tf_op jit(solution)/shard_map/ppermute | solution.py:243
  21.9 11.8 %collective-permute-start.7 = (bf16[384,512]{1,0:T(8,128)(2,1)S(1)}, bf16[384,512]{1,0:T(8,128)(2,1)S(1)}, u32[]{:S(2)}, u32[]{:S(2)}) collective-permute-start(bf16[384,512]{1,0:T(8,128)(2,1)S(1)} %collective-permute-done.refs_0_), channel_id=1, source_target_pairs={{0,4},{1,5},{2,6},{3,7},{4,0},{5,1},{6,2},{7,3},{8,12},{9,13},{10,... | collective-permute-start | bytes 1179656 | tf_op jit(solution)/shard_map/ppermute | solution.py:246
  23.5 10.3 %collective-permute-start.6 = (bf16[384,512]{1,0:T(8,128)(2,1)S(1)}, bf16[384,512]{1,0:T(8,128)(2,1)S(1)}, u32[]{:S(2)}, u32[]{:S(2)}) collective-permute-start(bf16[384,512]{1,0:T(8,128)(2,1)S(1)} %collective-permute-done.refs_0_), channel_id=1, source_target_pairs={{0,2},{1,3},{2,0},{3,1},{4,6},{5,7},{6,4},{7,5},{8,10},{9,11},{10,... | collective-permute-start | bytes 1179656 | tf_op jit(solution)/shard_map/ppermute | solution.py:246
  27.3 12.0 %collective-permute-start.3 = (bf16[2048,128]{1,0:T(8,128)(2,1)S(1)}, bf16[2048,128]{1,0:T(8,128)(2,1)}, u32[]{:S(2)}, u32[]{:S(2)}) collective-permute-start(bf16[2048,128]{1,0:T(8,128)(2,1)S(1)} %copy-done.10), channel_id=1, source_target_pairs={{0,8},{8,0},{16,24},{24,16},{1,9},{9,1},{17,25},{25,17},{2,10},{10... | collective-permute-start | bytes 1572872 | tf_op jit(solution)/shard_map/ppermute | solution.py:243
  27.6 19.9 %collective-permute-start.2 = (bf16[2048,128]{1,0:T(8,128)(2,1)}, bf16[2048,128]{1,0:T(8,128)(2,1)S(1)}, u32[]{:S(2)}, u32[]{:S(2)}) collective-permute-start(bf16[2048,128]{1,0:T(8,128)(2,1)} %collective-permute-done.1.kw_ref), channel_id=1, source_target_pairs={{8,16},{16,8},{9,17},{17,9},{10,18},{18,10},{11,19},{19,11},{12,20... | collective-permute-start | bytes 1572872 | tf_op jit(solution)/shard_map/ppermute | solution.py:243
  36.3 0.8 copy-start.2
  37.1 15.7 %collective-permute-start.10 = (bf16[384,512]{1,0:T(8,128)(2,1)S(1)}, bf16[384,512]{1,0:T(8,128)(2,1)S(1)}, u32[]{:S(2)}, u32[]{:S(2)}) collective-permute-start(bf16[384,512]{1,0:T(8,128)(2,1)S(1)} %collective-permute-done.refs_0_), channel_id=1, source_target_pairs={{0,1},{1,0},{2,3},{3,2},{4,5},{5,4},{6,7},{7,6},{8,9},{9,8},{10,11... | collective-permute-start | bytes 1179656 | tf_op jit(solution)/shard_map/ppermute | solution.py:246
  39.3 31.2 %collective-permute-start.15 = (bf16[2048,128]{1,0:T(8,128)(2,1)}, bf16[2048,128]{1,0:T(8,128)(2,1)}, u32[]{:S(2)}, u32[]{:S(2)}) collective-permute-start(bf16[2048,128]{1,0:T(8,128)(2,1)} %collective-permute-done.3.vw_ref), channel_id=1, source_target_pairs={{8,16},{16,8},{9,17},{17,9},{10,18},{18,10},{11,19},{19,11},{12,20... | collective-permute-start | bytes 1572872 | tf_op jit(solution)/shard_map/ppermute | solution.py:243
  47.5 3.4 %copy-start.4 = (bf16[2048,128]{1,0:T(8,128)(2,1)}, bf16[2048,128]{1,0:T(8,128)(2,1)S(1)}, u32[]{:S(2)}) copy-start(bf16[2048,128]{1,0:T(8,128)(2,1)S(1)} %collective-permute-done.2.w_ref) | copy-start | bytes 1572868
  50.9 9.9 %collective-permute-start.4 = (f32[392,256]{1,0:T(8,128)S(1)}, f32[392,256]{1,0:T(8,128)}, u32[]{:S(2)}, u32[]{:S(2)}) collective-permute-start(f32[392,256]{1,0:T(8,128)S(1)} %partial.1.near_ref), channel_id=1, source_target_pairs={{0,8},{24,16},{1,9},{25,17},{2,10},{26,18},{3,11},{27,19},{4,12},{... | collective-permute-start | bytes 1204232 | tf_op jit(solution)/shard_map/ppermute | solution.py:243
  52.2 1.8 %collective-permute-start.11 = (bf16[384,512]{1,0:T(8,128)(2,1)S(1)}, bf16[384,512]{1,0:T(8,128)(2,1)S(1)}, u32[]{:S(2)}, u32[]{:S(2)}) collective-permute-start(bf16[384,512]{1,0:T(8,128)(2,1)S(1)} %collective-permute-done.6.refs_2_), channel_id=1, source_target_pairs={{0,1},{1,0},{2,3},{3,2},{4,5},{5,4},{6,7},{7,6},{8,9},{9,8},{10,11... | collective-permute-start | bytes 1179656 | tf_op jit(solution)/shard_map/ppermute | solution.py:246
  52.3 2.3 %collective-permute-start.12 = (bf16[384,512]{1,0:T(8,128)(2,1)S(1)}, bf16[384,512]{1,0:T(8,128)(2,1)S(1)}, u32[]{:S(2)}, u32[]{:S(2)}) collective-permute-start(bf16[384,512]{1,0:T(8,128)(2,1)S(1)} %collective-permute-done.7.refs_4_), channel_id=1, source_target_pairs={{0,1},{1,0},{2,3},{3,2},{4,5},{5,4},{6,7},{7,6},{8,9},{9,8},{10,11... | collective-permute-start | bytes 1179656 | tf_op jit(solution)/shard_map/ppermute | solution.py:246
  52.8 2.3 %collective-permute-start.13 = (bf16[384,512]{1,0:T(8,128)(2,1)S(1)}, bf16[384,512]{1,0:T(8,128)(2,1)S(1)}, u32[]{:S(2)}, u32[]{:S(2)}) collective-permute-start(bf16[384,512]{1,0:T(8,128)(2,1)S(1)} %collective-permute-done.8.refs_6_), channel_id=1, source_target_pairs={{0,1},{1,0},{2,3},{3,2},{4,5},{5,4},{6,7},{7,6},{8,9},{9,8},{10,11... | collective-permute-start | bytes 1179656 | tf_op jit(solution)/shard_map/ppermute | solution.py:246
  53.0 7.8 %copy-start.7 = (bf16[128]{0:T(256)(128)(2,1)S(1)}, bf16[128]{0:T(256)(128)(2,1)}, u32[]{:S(2)}) copy-start(bf16[128]{0:T(256)(128)(2,1)} %param.12) | copy-start | bytes 772
  55.1 1.0 %copy-start.1 = (bf16[2048,128]{1,0:T(8,128)(2,1)S(1)}, bf16[2048,128]{1,0:T(8,128)(2,1)}, u32[]{:S(2)}) copy-start(bf16[2048,128]{1,0:T(8,128)(2,1)} %copy-done) | copy-start | bytes 1572868
  56.2 1.0 %copy-start.3 = (bf16[2048,128]{1,0:T(8,128)(2,1)S(1)}, bf16[2048,128]{1,0:T(8,128)(2,1)}, u32[]{:S(2)}) copy-start(bf16[2048,128]{1,0:T(8,128)(2,1)} %copy-done.2) | copy-start | bytes 1572868
  57.2 3.6 %copy-start.5 = (bf16[2048,128]{1,0:T(8,128)(2,1)S(1)}, bf16[2048,128]{1,0:T(8,128)(2,1)}, u32[]{:S(2)}) copy-start(bf16[2048,128]{1,0:T(8,128)(2,1)} %copy-done.4) | copy-start | bytes 1572868
  60.8 9.7 %copy-start.8 = (bf16[128]{0:T(256)(128)(2,1)S(1)}, bf16[128]{0:T(256)(128)(2,1)}, u32[]{:S(2)}) copy-start(bf16[128]{0:T(256)(128)(2,1)} %param.13) | copy-start | bytes 772
  63.8 13.3 %collective-permute-start.19 = (bf16[784,128]{1,0:T(8,128)(2,1)S(1)}, bf16[784,128]{1,0:T(8,128)(2,1)S(1)}, u32[]{:S(2)}, u32[]{:S(2)}) collective-permute-start(bf16[784,128]{1,0:T(8,128)(2,1)S(1)} %distant.2.k_in), channel_id=1, source_target_pairs={{8,0},{16,24},{9,1},{17,25},{10,2},{18,26},{11,3},{19,27},{12,4},{... | collective-permute-start | bytes 602120 | tf_op jit(solution)/shard_map/ppermute | solution.py:243
  68.1 10.4 %collective-permute-start.14 = (bf16[784,128]{1,0:T(8,128)(2,1)S(1)}, bf16[784,128]{1,0:T(8,128)(2,1)S(1)}, u32[]{:S(2)}, u32[]{:S(2)}) collective-permute-start(bf16[784,128]{1,0:T(8,128)(2,1)S(1)} %distant.2.k_in), channel_id=1, source_target_pairs={{8,16},{16,8},{9,17},{17,9},{10,18},{18,10},{11,19},{19,11},{12,20... | collective-permute-start | bytes 602120 | tf_op jit(solution)/shard_map/ppermute | solution.py:243
  70.5 14.1 %copy-start.6 = (s32[1536]{0:T(1024)S(1)}, s32[1536]{0:T(1024)}, u32[]{:S(2)}) copy-start(s32[1536]{0:T(1024)} %param.14) | copy-start | bytes 18436
  73.7 8.3 %collective-permute-start.16 = (bf16[768,128]{1,0:T(8,128)(2,1)S(1)}, bf16[768,128]{1,0:T(8,128)(2,1)S(1)}, u32[]{:S(2)}, u32[]{:S(2)}) collective-permute-start(bf16[768,128]{1,0:T(8,128)(2,1)S(1)} %distant.3.v_in), channel_id=1, source_target_pairs={{8,16},{16,8},{9,17},{17,9},{10,18},{18,10},{11,19},{19,11},{12,20... | collective-permute-start | bytes 589832 | tf_op jit(solution)/shard_map/ppermute | solution.py:243
  77.2 7.4 %collective-permute-start.20 = (bf16[768,128]{1,0:T(8,128)(2,1)S(1)}, bf16[768,128]{1,0:T(8,128)(2,1)S(1)}, u32[]{:S(2)}, u32[]{:S(2)}) collective-permute-start(bf16[768,128]{1,0:T(8,128)(2,1)S(1)} %distant.3.v_in), channel_id=1, source_target_pairs={{8,0},{16,24},{9,1},{17,25},{10,2},{18,26},{11,3},{19,27},{12,4},{... | collective-permute-start | bytes 589832 | tf_op jit(solution)/shard_map/ppermute | solution.py:243
  82.0 8.9 %collective-permute-start.17 = (bf16[784,128]{1,0:T(8,128)(2,1)S(1)}, bf16[784,128]{1,0:T(8,128)(2,1)S(1)}, u32[]{:S(2)}, u32[]{:S(2)}) collective-permute-start(bf16[784,128]{1,0:T(8,128)(2,1)S(1)} %collective-permute-done.14.k_across), channel_id=1, source_target_pairs={{8,0},{16,24},{9,1},{17,25},{10,2},{18,26},{11,3},{19,27},{12,4},{... | collective-permute-start | bytes 602120 | tf_op jit(solution)/shard_map/ppermute | solution.py:243
  83.3 7.6 %collective-permute-start.18 = (bf16[768,128]{1,0:T(8,128)(2,1)S(1)}, bf16[768,128]{1,0:T(8,128)(2,1)S(1)}, u32[]{:S(2)}, u32[]{:S(2)}) collective-permute-start(bf16[768,128]{1,0:T(8,128)(2,1)S(1)} %collective-permute-done.16.v_across), channel_id=1, source_target_pairs={{8,0},{16,24},{9,1},{17,25},{10,2},{18,26},{11,3},{19,27},{12,4},{... | collective-permute-start | bytes 589832 | tf_op jit(solution)/shard_map/ppermute | solution.py:243

commit v7 on v6

--- a/solution.py
+++ b/solution.py
@@ -11,7 +11,7 @@
 HD = 128
 PAGE = 16
 NEG = -1e30
-KERNEL_VMEM = 24 * 1024 * 1024
+KERNEL_VMEM = 16 * 1024 * 1024
 PROMPTS = 4
 
 
@@ -148,16 +148,16 @@
     out_ref[...] = jnp.dot(h_buf[...], w_buf[...], preferred_element_type=jnp.float32)
 
 
-def partial_kernel(place, h_ref, kw_ref, vw_ref, before_ref, owner_ref, out_ref, h_buf, sem):
+def partial_kernel(column, place, h_ref, w_ref, before_ref, owner_ref, out_ref, h_buf, sem):
     copy = chunk_copy(h_ref, place[0], h_buf, sem)
     copy.start()
     span = h_buf.shape[0]
-    weight = jnp.concatenate([kw_ref[...], vw_ref[...]], axis=1)
-    out_ref[span:, :HD] = owner_ref[...]
-    out_ref[span:, HD:] = owner_ref[...]
+    part = slice(column * HD, column * HD + HD)
+    if column == 0:
+        out_ref[span:] = owner_ref[...]
     copy.wait()
-    out_ref[:span] = before_ref[...] + jnp.dot(
-        h_buf[...], weight, preferred_element_type=jnp.float32
+    out_ref[:span] = before_ref[:, part] + jnp.dot(
+        h_buf[...], w_ref[...], preferred_element_type=jnp.float32
     )
 
 
@@ -185,15 +185,15 @@
     own_at = pl.multiple_of(place[1] * span, span)
     outer_at = pl.multiple_of((1 - place[1]) * span, span)
     bias = bias_ref[...].astype(jnp.float32)
-    acc[...] = outer_ref[:span, part] + facing_ref[span:, part] + bias
+    acc[...] = outer_ref[:span] + facing_ref[span:, part] + bias
     add_pieces(place[2], place[0], pieces, w_ref, acc)
     out_ref[pl.ds(outer_at, span), :] = acc[...].astype(jnp.bfloat16)
-    own = near_ref[:span, part] + facing_ref[:span, part] + bias
+    own = near_ref[:span] + facing_ref[:span, part] + bias
     copy.wait()
     own += jnp.dot(h_buf[...], w_ref[...], preferred_element_type=jnp.float32)
     out_ref[pl.ds(own_at, span), :] = own.astype(jnp.bfloat16)
     if column == 0:
-        mine, theirs = near_ref[span:, :HD], outer_ref[span:, :HD]
+        mine, theirs = near_ref[span:], outer_ref[span:]
         lower = jnp.where(place[1] == 0, mine, theirs)
         upper = jnp.where(place[1] == 0, theirs, mine)
         out_ref[2 * span :] = jnp.concatenate([lower, upper], axis=0).astype(jnp.bfloat16)
@@ -250,6 +250,8 @@
     tie = lax.optimization_barrier
     block = pltpu.VMEM((span, depth), jnp.bfloat16)
     both = pltpu.VMEM((depth, 2 * HD), jnp.bfloat16)
+    key_facing = send(key_weight, ACROSS)
+    cut = send(cut, INWARD)
     own_part = call_project(
         near_kernel,
         "near",
@@ -262,24 +264,53 @@
         held=3,
         copies=(3,),
     )
-    cut = send(cut, INWARD)
-    key_facing = send(key_weight, ACROSS)
-    key_facing, value_after = tie((key_facing, value_weight))
+    cut, key_facing, key_after, value_after, own_part = tie(
+        (cut, key_facing, key_weight, value_weight, own_part)
+    )
     value_facing = send(value_after, ACROSS)
-    cut, key_after, own_part = tie((cut, key_weight, own_part))
     key_swapped = send(key_after, SWAP)
-    key_swapped, value_after = tie((key_swapped, value_weight))
     value_swapped = send(value_after, SWAP)
     chips = [cut, trade(cut, 2), trade(cut, 4), trade(cut, 6)]
-    chips, value_facing = tie((chips, value_facing))
+    key_swapped, value_facing = tie((key_swapped, value_facing))
+    key_distant = send(key_swapped, ACROSS)
+    value_distant = send(value_swapped, ACROSS)
+    chips[2], key_distant = tie((chips[2], key_distant))
     mates = [trade(x, 1) for x in chips]
     pieces = [x for both_cores in zip(chips, mates) for x in both_cores]
-    key_distant = send(key_swapped, ACROSS)
-    value_distant = send(value_swapped, ACROSS)
 
     def place(chunk):
         return jnp.stack([chunk, second, member])
 
+    owners = jnp.broadcast_to(page_owner.T.astype(jnp.float32), (EXTRA, page_owner.shape[0]))
+    owners = jnp.pad(owners, ((0, 0), (0, HD - page_owner.shape[0])))
+
+    def begin(column, weight):
+        part = call_project(
+            functools.partial(partial_kernel, column),
+            "partial",
+            near[None],
+            [hidden, weight, own_part, owners],
+            span + (EXTRA if column == 0 else 0),
+            HD,
+            jnp.float32,
+            [block],
+        )
+        return part, send(part, INWARD)
+
+    def finish(column, weight, parts, bias):
+        return call_project(
+            functools.partial(distant_kernel, column),
+            "distant",
+            place(distant),
+            [hidden, weight, *parts, faced, bias[None, :]] + pieces,
+            2 * span + (2 * EXTRA if column == 0 else 0),
+            HD,
+            jnp.bfloat16,
+            [block, pltpu.VMEM((span, HD), jnp.float32)],
+        )
+
+    key_parts = begin(0, key_swapped)
+    value_parts = begin(1, value_swapped)
     faced = call_project(
         facing_kernel,
         "facing",
@@ -290,40 +321,12 @@
         jnp.float32,
         [block, both],
     )
-    own_part, key_distant = tie((own_part, key_distant))
-    owners = jnp.broadcast_to(page_owner.T.astype(jnp.float32), (EXTRA, page_owner.shape[0]))
-    owners = jnp.pad(owners, ((0, 0), (0, HD - page_owner.shape[0])))
-    own_part = call_project(
-        partial_kernel,
-        "partial",
-        near[None],
-        [hidden, key_swapped, value_swapped, own_part, owners],
-        span + EXTRA,
-        2 * HD,
-        jnp.float32,
-        [block],
-    )
-    outer_part = send(own_part, INWARD)
-
-    def finish(column, weight, bias):
-        return call_project(
-            functools.partial(distant_kernel, column),
-            "distant",
-            place(distant),
-            [hidden, weight, own_part, outer_part, faced, bias[None, :]] + pieces,
-            2 * span + (2 * EXTRA if column == 0 else 0),
-            HD,
-            jnp.bfloat16,
-            [block, pltpu.VMEM((span, HD), jnp.float32)],
-        )
-
-    keys = finish(0, key_distant, key_bias)
+    keys = finish(0, key_distant, key_parts, key_bias)
     keys_out, keys_across = send(keys, OUTWARD), send(keys, ACROSS)
-    values = finish(1, value_distant, value_bias)
+    values = finish(1, value_distant, value_parts, value_bias)
     values_across = send(values, ACROSS)
     keys_out, values_after = tie((keys_out, values))
     values_out = send(values_after, OUTWARD)
-    keys_across, values_across = tie((keys_across, values_across))
     keys_far, values_far = send(keys_across, OUTWARD), send(values_across, OUTWARD)
     return (
         (keys, keys_out, keys_across, keys_far),
@@ -331,21 +334,35 @@
     )
 
 
-def softmax_step(q, keys, values, allowed, before):
+def head_of(x, g):
+    return x[:, g * HD : (g + 1) * HD]
+
+
+def attend(q_ref, heads, keys, values, allowed, before, store):
     factor = HD**-0.5 * math.log2(math.e)
-    scores = lax.dot_general(q, keys, (((1,), (1,)), ((), ())), preferred_element_type=jnp.float32)
-    scores = jnp.where(allowed, scores, NEG)
-    peak = jnp.max(scores, axis=1, keepdims=True)
-    if before is not None:
-        peak = jnp.maximum(peak, before[0])
-    weights = jnp.exp2(scores * factor - peak * factor).astype(jnp.bfloat16)
-    mixed = jnp.dot(weights, values, preferred_element_type=jnp.float32)
-    total, mixed = mixed[:, HD:], mixed[:, :HD]
-    if before is not None:
-        shrink = jnp.exp2((before[0] - peak) * factor)
-        total = total + before[1] * shrink
-        mixed = mixed + before[2] * shrink
-    return peak, total, mixed
+
+    def scores_of(g):
+        return lax.dot_general(
+            head_of(q_ref, g), keys, (((1,), (1,)), ((), ())), preferred_element_type=jnp.float32
+        )
+
+    following = scores_of(0)
+    for g in range(heads):
+        scores = jnp.where(allowed, following, NEG)
+        if g + 1 < heads:
+            following = scores_of(g + 1)
+        peak = jnp.max(scores, axis=1, keepdims=True)
+        if before is not None:
+            top, total, mix = before(g)
+            peak = jnp.maximum(peak, top)
+        weights = jnp.exp2(scores * factor - peak * factor).astype(jnp.bfloat16)
+        mixed = jnp.dot(weights, values, preferred_element_type=jnp.float32)
+        sums, mixed = mixed[:, HD:], mixed[:, :HD]
+        if before is not None:
+            shrink = jnp.exp2((top - peak) * factor)
+            sums = sums + total * shrink
+            mixed = mixed + mix * shrink
+        store(g, peak, sums, mixed)
 
 
 def with_ones(values):
@@ -370,21 +387,18 @@
     return copy
 
 
-def place_pages(index, span, named, held_k, held_v, cache_ref):
-    cache_ref[...] = jnp.zeros(cache_ref.shape, cache_ref.dtype)
+def place_pages(index, span, named, held_k, held_v, cache_ref, laid):
+    rows = cache_ref.shape[1]
+    row = lax.broadcasted_iota(jnp.int32, (rows, 2 * HD), 0)
     for s in range(2):
         rank = jnp.int32(0)
         for p in range(span // PAGE):
-            owned = named[s * EXTRA, p] == index
             tokens = pl.ds(s * span + p * PAGE, PAGE)
             at = pl.ds(pl.multiple_of(rank * PAGE, PAGE), PAGE)
-
-            @pl.when(owned)
-            def _():
-                cache_ref[s, at, :HD] = held_k[tokens, :]
-                cache_ref[s, at, HD:] = held_v[tokens, :]
-
-            rank = rank + owned.astype(jnp.int32)
+            laid[s, at, :HD] = held_k[tokens, :]
+            laid[s, at, HD:] = held_v[tokens, :]
+            rank = rank + (named[s * EXTRA, p] == index).astype(jnp.int32)
+        cache_ref[s] = jnp.where(row < rank * PAGE, laid[s, :rows], 0)
 
 
 def own_kernel(
@@ -405,6 +419,7 @@
     q_buf,
     listed,
     named,
+    laid,
     sems,
 ):
     copy = pltpu.make_async_copy(q_ref, q_buf, sems.at[0])
@@ -424,14 +439,15 @@
         columns >= start - (index // 2) * 2 * span
     )
     copy.wait()
-    for g in range(heads):
-        q = q_buf[:, g * HD : (g + 1) * HD]
-        peak, sums, mixed = softmax_step(q, keys, values, allowed, None)
+
+    def store(g, peak, sums, mixed):
         top[g] = peak
         total[g] = sums[:, :1]
         mix[g] = mixed
+
+    attend(q_buf, heads, keys, values, allowed, None, store)
     owners.wait()
-    place_pages(index, span, named, held_k, held_v, cache_ref)
+    place_pages(index, span, named, held_k, held_v, cache_ref, laid)
 
 
 def far_kernel(
@@ -454,6 +470,7 @@
     q_buf,
     listed,
     named,
+    laid,
     sems,
 ):
     copy = pltpu.make_async_copy(q_ref, q_buf, sems.at[0])
@@ -478,14 +495,15 @@
         values = with_ones(held_v[...])
         columns = lax.broadcasted_iota(jnp.int32, (span, 2 * span), 1)
         allowed = columns >= prompt_starts(seg_ref, index * span, span)
-        for g in range(heads):
-            q = q_buf[:, g * HD : (g + 1) * HD]
-            _, sums, mixed = softmax_step(q, keys, values, allowed, (top[g], total[g], mix[g]))
+
+        def store(g, peak, sums, mixed):
             out_ref[:, g * HD : (g + 1) * HD] = (mixed / sums).astype(out_ref.dtype)
+
+        attend(q_buf, heads, keys, values, allowed, lambda g: (top[g], total[g], mix[g]), store)
 
     owners.wait()
     far_cache = cache_ref.at[pl.ds((1 - index // 2) * 2, 2)]
-    place_pages(index, span, named, held_k, held_v, far_cache)
+    place_pages(index, span, named, held_k, held_v, far_cache, laid)
 
 
 def attention_of_pairs(queries, segment_ids, keys, values, capacity):
@@ -502,6 +520,7 @@
         pltpu.VMEM(queries.shape, jnp.bfloat16),
         pltpu.VMEM((2 * EXTRA, HD), jnp.int32),
         pltpu.SMEM((2 * EXTRA, HD), jnp.int32),
+        pltpu.VMEM((2, (capacity + 1) * PAGE, 2 * HD), jnp.bfloat16),
         pltpu.SemaphoreType.DMA((2,)),
     ]
     state = pl.pallas_call(

time: 99.9 us -> 98.4 us (0.985)
  waiting for transfers between devices: 33 us -> 29.4 us
  starting transfers between devices: 32.4 us -> 35.5 us
  local copies, waits for them, and re-layouts: 4.74 us -> 1.86 us
  Pallas kernels: 26.9 us -> 28.7 us
    ppermute x14 -> x15, waiting for transfers between devices: 27 us -> 23 us  [send(): return lax.ppermute(x, 'pre', pairs)]
    ppermute x14 -> x15, starting transfers between devices: 26.3 us -> 29.6 us  [send(): return lax.ppermute(x, 'pre', pairs)]
    unnamed x24 -> x14, local copies, waits for them, and re-layouts: 3.71 us -> 0.82 us
    pallas_call x5 -> x6, Pallas kernels: 14.5 us -> 16.6 us  [call_project(): pl.pallas_call(kernel, in_specs=[SCALAR] + [HELD] * held + [FAST] * (len(...]
  transfers between devices with their start and end apart: 21 -> 22, of which waited for: 14 -> 7; matrix products, arithmetic and copies ran while one was open for 0% -> 1% of each run, Pallas kernels for 20% -> 22%
where the time goes in v7:
time: 98.4 us; the launch traced here: 96.8 us
  starting transfers between devices  35.5 us (36%)
  waiting for transfers between devices  29.4 us (30%)
  Pallas kernels  28.7 us (29%)
  local copies, waits for them, and re-layouts  1.86 us (2%)
  between operations  1.11 us (1%)
    ppermute x15, starting transfers between devices, send(): return lax.ppermute(x, 'pre', pairs)  29.6 us
    ppermute x15, waiting for transfers between devices, send(): return lax.ppermute(x, 'pre', pairs)  23 us
    pallas_call x6, Pallas kernels, call_project(): pl.pallas_call(kernel, in_specs=[SCALAR] + [HELD] * held + [FAST] * (len(...  16.6 us
    pallas_call x1, Pallas kernels, attention_of_pairs(): pl.pallas_call(functools.partial(far_kernel, heads), in_specs=[SCALAR, HE...  7.13 us
    ppermute x7, waiting for transfers between devices, trade(): lax.ppermute(x, ('dec', 'tp'), [(m, m ^ apart) for m in range(PIECES)])  6.39 us
    ppermute x7, starting transfers between devices, trade(): lax.ppermute(x, ('dec', 'tp'), [(m, m ^ apart) for m in range(PIECES)])  5.89 us
    pallas_call x1, Pallas kernels, attention_of_pairs(): pl.pallas_call(functools.partial(own_kernel, heads), in_specs=[SCALAR, HE...  4.97 us
  transfers between devices with their start and end apart: 22, of which 7 were waited for; matrix products, arithmetic and copies ran while one was open for 1% of the time, Pallas kernels for 22%

profile of v7, /device:TPU:16, one launch (start us, length us, event | category | flops | bytes accessed | tf_op | source)
XLA Modules:
  0.0 96.8 jit_solution(14905847704563265555)
XLA Ops:
  0.6 2.4 %collective-permute-start.1 = (bf16[2048,128]{1,0:T(8,128)(2,1)}, bf16[2048,128]{1,0:T(8,128)(2,1)S(1)}, u32[]{:S(2)}, u32[]{:S(2)}) collective-permute-start(bf16[2048,128]{1,0:T(8,128)(2,1)} %kw_ref.1), channel_id=1, source_target_pairs={{8,16},{16,8},{9,17},{17,9},{10,18},{18,10},{11,19},{19,11},{12,20... | collective-permute-start | bytes 1572872 | tf_op jit(solution)/shard_map/ppermute | solution.py:243
  3.0 1.0 %constant_dynamic-slice_fusion = bf16[384,512]{1,0:T(8,128)(2,1)S(1)} fusion(bf16[384,8192]{1,0:T(8,128)(2,1)} %h_ref.11, s32[]{:T(128)S(6)} %select_n.3), kind=kLoop, calls=%fused_computation.3 | loop fusion | bytes 786436 | tf_op jit(solution)/shard_map/dynamic_slice | solution.py:249
  4.0 1.3 %collective-permute-start = (bf16[384,512]{1,0:T(8,128)(2,1)S(1)}, bf16[384,512]{1,0:T(8,128)(2,1)S(1)}, u32[]{:S(2)}, u32[]{:S(2)}) collective-permute-start(bf16[384,512]{1,0:T(8,128)(2,1)S(1)} %constant_dynamic-slice_fusion), channel_id=1, source_target_pairs={{0,8},{24,16},{1,9},{25,17},{2,10},{26,18},{3,11},{27,19},{4,12},{... | collective-permute-start | bytes 1179656 | tf_op jit(solution)/shard_map/ppermute | solution.py:243
  5.3 0.0 copy-start.5
  5.4 0.0 copy-start.6
  5.4 2.3 %near.1.before_ref = f32[384,256]{1,0:T(8,128)S(1)} custom-call(s32[1]{0:T(128)} %bitcast.place.info, bf16[384,8192]{1,0:T(8,128)(2,1)} %h_ref.11, bf16[2048,128]{1,0:T(8,128)(2,1)} %kw_ref.1, bf16[2048,128]{1,0:T(8,128)(2,1)} %vw_ref.1), custom_call_target="tpu_custom_call" | custom-call | tf_op jit(solution)/shard_map/near/pallas_call | solution.py:213
  7.7 8.8 %collective-permute-done.refs_0_ = bf16[384,512]{1,0:T(8,128)(2,1)S(1)} collective-permute-done((bf16[384,512]{1,0:T(8,128)(2,1)S(1)}, bf16[384,512]{1,0:T(8,128)(2,1)S(1)}, u32[]{:S(2)}, u32[]{:S(2)}) %collective-permute-start) | collective-permute-done | bytes 393248 | tf_op jit(solution)/shard_map/ppermute | solution.py:243
  16.5 0.0 collective-permute-done.1.kw_ref
  16.5 3.5 %collective-permute-start.4 = (bf16[2048,128]{1,0:T(8,128)(2,1)}, bf16[2048,128]{1,0:T(8,128)(2,1)S(1)}, u32[]{:S(2)}, u32[]{:S(2)}) collective-permute-start(bf16[2048,128]{1,0:T(8,128)(2,1)} %vw_ref.1), channel_id=1, source_target_pairs={{8,16},{16,8},{9,17},{17,9},{10,18},{18,10},{11,19},{19,11},{12,20... | collective-permute-start | bytes 1572872 | tf_op jit(solution)/shard_map/ppermute | solution.py:243
  20.0 2.5 %collective-permute-start.11 = (bf16[384,512]{1,0:T(8,128)(2,1)S(1)}, bf16[384,512]{1,0:T(8,128)(2,1)S(1)}, u32[]{:S(2)}, u32[]{:S(2)}) collective-permute-start(bf16[384,512]{1,0:T(8,128)(2,1)S(1)} %collective-permute-done.refs_0_), channel_id=1, source_target_pairs={{0,6},{1,7},{2,4},{3,5},{4,2},{5,3},{6,0},{7,1},{8,14},{9,15},{10,... | collective-permute-start | bytes 1179656 | tf_op jit(solution)/shard_map/ppermute | solution.py:246
  22.5 8.9 %collective-permute-done.3.w_ref = bf16[2048,128]{1,0:T(8,128)(2,1)} collective-permute-done((bf16[2048,128]{1,0:T(8,128)(2,1)S(1)}, bf16[2048,128]{1,0:T(8,128)(2,1)}, u32[]{:S(2)}, u32[]{:S(2)}) %collective-permute-start.3) | collective-permute-done | bytes 524320 | tf_op jit(solution)/shard_map/ppermute | solution.py:243
  31.5 0.0 collective-permute-done.4.vw_ref
  31.5 0.8 copy-done
  32.3 3.5 %collective-permute-start.5 = (bf16[2048,128]{1,0:T(8,128)(2,1)}, bf16[2048,128]{1,0:T(8,128)(2,1)}, u32[]{:S(2)}, u32[]{:S(2)}) collective-permute-start(bf16[2048,128]{1,0:T(8,128)(2,1)} %collective-permute-done.3.w_ref), channel_id=1, source_target_pairs={{8,16},{16,8},{9,17},{17,9},{10,18},{18,10},{11,19},{19,11},{12,20... | collective-permute-start | bytes 1572872 | tf_op jit(solution)/shard_map/ppermute | solution.py:243
  35.8 1.6 %collective-permute-start.8 = (bf16[384,512]{1,0:T(8,128)(2,1)S(1)}, bf16[384,512]{1,0:T(8,128)(2,1)S(1)}, u32[]{:S(2)}, u32[]{:S(2)}) collective-permute-start(bf16[384,512]{1,0:T(8,128)(2,1)S(1)} %collective-permute-done.refs_0_), channel_id=1, source_target_pairs={{0,2},{1,3},{2,0},{3,1},{4,6},{5,7},{6,4},{7,5},{8,10},{9,11},{10,... | collective-permute-start | bytes 1179656 | tf_op jit(solution)/shard_map/ppermute | solution.py:246
  37.3 1.5 %collective-permute-start.2 = (bf16[384,512]{1,0:T(8,128)(2,1)S(1)}, bf16[384,512]{1,0:T(8,128)(2,1)S(1)}, u32[]{:S(2)}, u32[]{:S(2)}) collective-permute-start(bf16[384,512]{1,0:T(8,128)(2,1)S(1)} %collective-permute-done.refs_0_), channel_id=1, source_target_pairs={{0,4},{1,5},{2,6},{3,7},{4,0},{5,1},{6,2},{7,3},{8,12},{9,13},{10,... | collective-permute-start | bytes 1179656 | tf_op jit(solution)/shard_map/ppermute | solution.py:246
  38.8 0.0 collective-permute-done.11.refs_6_
  38.8 0.0 collective-permute-start.7
  38.8 5.2 %collective-permute-done.8.refs_2_ = bf16[384,512]{1,0:T(8,128)(2,1)S(1)} collective-permute-done((bf16[384,512]{1,0:T(8,128)(2,1)S(1)}, bf16[384,512]{1,0:T(8,128)(2,1)S(1)}, u32[]{:S(2)}, u32[]{:S(2)}) %collective-permute-start.8) | collective-permute-done | bytes 393248 | tf_op jit(solution)/shard_map/ppermute | solution.py:246
  44.0 0.0 collective-permute-start.12
  44.0 1.2 %collective-permute-done.2.refs_4_ = bf16[384,512]{1,0:T(8,128)(2,1)S(1)} collective-permute-done((bf16[384,512]{1,0:T(8,128)(2,1)S(1)}, bf16[384,512]{1,0:T(8,128)(2,1)S(1)}, u32[]{:S(2)}, u32[]{:S(2)}) %collective-permute-start.2) | collective-permute-done | bytes 393248 | tf_op jit(solution)/shard_map/ppermute | solution.py:246
  45.2 0.0 collective-permute-start.9
  45.2 0.0 collective-permute-done.15.w_ref
  45.2 2.7 %collective-permute-start.16 = (bf16[2048,128]{1,0:T(8,128)(2,1)}, bf16[2048,128]{1,0:T(8,128)(2,1)S(1)}, u32[]{:S(2)}, u32[]{:S(2)}) collective-permute-start(bf16[2048,128]{1,0:T(8,128)(2,1)} %collective-permute-done.15.w_ref), channel_id=1, source_target_pairs={{8,16},{16,8},{9,17},{17,9},{10,18},{18,10},{11,19},{19,11},{12,20... | collective-permute-start | bytes 1572872 | tf_op jit(solution)/shard_map/ppermute | solution.py:243
  48.0 0.0 collective-permute-done.5.w_ref
  48.0 0.3 collective-permute-start.10
  48.3 3.0 %partial.2.near_ref = f32[392,128]{1,0:T(8,128)S(1)} custom-call(s32[1]{0:T(128)} %bitcast.5.place, bf16[384,8192]{1,0:T(8,128)(2,1)} %h_ref.11, bf16[2048,128]{1,0:T(8,128)(2,1)} %collective-permute-done.3.w_ref, f32[384,256]{1,0:T(8,128)S(1)} %near.1.before_ref, f32[8,128]{1,0:T(8,128)S(1)} %pad.7.owner_ref), custom_call_target="tpu_custom_call" | custom-call | tf_op jit(solution)/shard_map/partial/pallas_call | solution.py:213
  51.3 1.3 %collective-permute-start.6 = (f32[392,128]{1,0:T(8,128)S(1)}, f32[392,128]{1,0:T(8,128)S(1)}, u32[]{:S(2)}, u32[]{:S(2)}) collective-permute-start(f32[392,128]{1,0:T(8,128)S(1)} %partial.2.near_ref), channel_id=1, source_target_pairs={{0,8},{24,16},{1,9},{25,17},{2,10},{26,18},{3,11},{27,19},{4,12},{... | collective-permute-start | bytes 602120 | tf_op jit(solution)/shard_map/ppermute | solution.py:243
  52.6 0.1 add_add_fusion.place
  52.7 3.1 %partial.3.near_ref = f32[384,128]{1,0:T(8,128)S(1)} custom-call(s32[1]{0:T(128)} %bitcast.5.place, bf16[384,8192]{1,0:T(8,128)(2,1)} %h_ref.11, bf16[2048,128]{1,0:T(8,128)(2,1)} %collective-permute-done.15.w_ref, f32[384,256]{1,0:T(8,128)S(1)} %near.1.before_ref, f32[8,128]{1,0:T(8,128)S(1)} %pad.7.owner_ref), custom_call_target="tpu_custom_call" | custom-call | tf_op jit(solution)/shard_map/partial/pallas_call | solution.py:213
  55.8 0.0 collective-permute-done.12.refs_7_
  55.8 1.3 %collective-permute-start.17 = (f32[384,128]{1,0:T(8,128)S(1)}, f32[384,128]{1,0:T(8,128)S(1)}, u32[]{:S(2)}, u32[]{:S(2)}) collective-permute-start(f32[384,128]{1,0:T(8,128)S(1)} %partial.3.near_ref), channel_id=1, source_target_pairs={{0,8},{24,16},{1,9},{25,17},{2,10},{26,18},{3,11},{27,19},{4,12},{... | collective-permute-start | bytes 589832 | tf_op jit(solution)/shard_map/ppermute | solution.py:243
  57.1 0.1 add_add_fusion.1.place
  57.2 2.5 %facing.1.facing_ref = f32[768,256]{1,0:T(8,128)S(1)} custom-call(s32[3]{0:T(128)S(1)} %add_add_fusion.1.place, bf16[384,8192]{1,0:T(8,128)(2,1)} %h_ref.11, bf16[2048,128]{1,0:T(8,128)(2,1)S(1)} %collective-permute-done.1.kw_ref, bf16[2048,128]{1,0:T(8,128)(2,1)S(1)} %copy-done.1, bf16[384,512]{1,0:T(8,128)(2,1)S(1)} %collective-permute-done.refs_0_, ...), custom_call_target="tpu_custom_call" | custom-call | tf_op jit(solution)/shard_map/facing/pallas_call | solution.py:213
  59.8 0.6 collective-permute-done.6.outer_ref
  60.4 3.1 %distant.2.k_in = bf16[784,128]{1,0:T(8,128)(2,1)S(1)} custom-call(s32[3]{0:T(128)S(1)} %add_add_fusion.place, bf16[384,8192]{1,0:T(8,128)(2,1)} %h_ref.11, bf16[2048,128]{1,0:T(8,128)(2,1)} %collective-permute-done.5.w_ref, f32[392,128]{1,0:T(8,128)S(1)} %partial.2.near_ref, f32[392,128]{1,0:T(8,128)S(1)} %collective-permute-done.6.outer_ref, ...), custom_call_target="tpu_custom_call" | custom-call | tf_op jit(solution)/shard_map/distant/pallas_call | solution.py:213
  63.5 4.0 %collective-permute-start.20 = (bf16[784,128]{1,0:T(8,128)(2,1)S(1)}, bf16[784,128]{1,0:T(8,128)(2,1)S(1)}, u32[]{:S(2)}, u32[]{:S(2)}) collective-permute-start(bf16[784,128]{1,0:T(8,128)(2,1)S(1)} %distant.2.k_in), channel_id=1, source_target_pairs={{8,0},{16,24},{9,1},{17,25},{10,2},{18,26},{11,3},{19,27},{12,4},{... | collective-permute-start | bytes 602120 | tf_op jit(solution)/shard_map/ppermute | solution.py:243
  67.5 3.1 %collective-permute-start.13 = (bf16[784,128]{1,0:T(8,128)(2,1)S(1)}, bf16[784,128]{1,0:T(8,128)(2,1)S(1)}, u32[]{:S(2)}, u32[]{:S(2)}) collective-permute-start(bf16[784,128]{1,0:T(8,128)(2,1)S(1)} %distant.2.k_in), channel_id=1, source_target_pairs={{8,16},{16,8},{9,17},{17,9},{10,18},{18,10},{11,19},{19,11},{12,20... | collective-permute-start | bytes 602120 | tf_op jit(solution)/shard_map/ppermute | solution.py:243
  70.6 0.0 copy-start.2
  70.6 2.5 %distant.3.v_in = bf16[768,128]{1,0:T(8,128)(2,1)S(1)} custom-call(s32[3]{0:T(128)S(1)} %add_add_fusion.place, bf16[384,8192]{1,0:T(8,128)(2,1)} %h_ref.11, bf16[2048,128]{1,0:T(8,128)(2,1)S(1)} %collective-permute-done.16.w_ref, f32[384,128]{1,0:T(8,128)S(1)} %partial.3.near_ref, f32[384,128]{1,0:T(8,128)S(1)} %collective-permute-done.17.outer_ref, ...), custom_call_target="tpu_custom_call" | custom-call | tf_op jit(solution)/shard_map/distant/pallas_call | solution.py:213
  73.2 2.7 %collective-permute-start.18 = (bf16[768,128]{1,0:T(8,128)(2,1)S(1)}, bf16[768,128]{1,0:T(8,128)(2,1)S(1)}, u32[]{:S(2)}, u32[]{:S(2)}) collective-permute-start(bf16[768,128]{1,0:T(8,128)(2,1)S(1)} %distant.3.v_in), channel_id=1, source_target_pairs={{8,16},{16,8},{9,17},{17,9},{10,18},{18,10},{11,19},{19,11},{12,20... | collective-permute-start | bytes 589832 | tf_op jit(solution)/shard_map/ppermute | solution.py:243
  75.9 1.3 %collective-permute-start.21 = (bf16[768,128]{1,0:T(8,128)(2,1)S(1)}, bf16[768,128]{1,0:T(8,128)(2,1)S(1)}, u32[]{:S(2)}, u32[]{:S(2)}) collective-permute-start(bf16[768,128]{1,0:T(8,128)(2,1)S(1)} %distant.3.v_in), channel_id=1, source_target_pairs={{8,0},{16,24},{9,1},{17,25},{10,2},{18,26},{11,3},{19,27},{12,4},{... | collective-permute-start | bytes 589832 | tf_op jit(solution)/shard_map/ppermute | solution.py:243
  77.3 1.3 %collective-permute-start.14 = (bf16[784,128]{1,0:T(8,128)(2,1)S(1)}, bf16[784,128]{1,0:T(8,128)(2,1)S(1)}, u32[]{:S(2)}, u32[]{:S(2)}) collective-permute-start(bf16[784,128]{1,0:T(8,128)(2,1)S(1)} %collective-permute-done.13.k_across), channel_id=1, source_target_pairs={{8,0},{16,24},{9,1},{17,25},{10,2},{18,26},{11,3},{19,27},{12,4},{... | collective-permute-start | bytes 602120 | tf_op jit(solution)/shard_map/ppermute | solution.py:243
  78.6 2.8 %collective-permute-done.18.v_across = bf16[768,128]{1,0:T(8,128)(2,1)S(1)} collective-permute-done((bf16[768,128]{1,0:T(8,128)(2,1)S(1)}, bf16[768,128]{1,0:T(8,128)(2,1)S(1)}, u32[]{:S(2)}, u32[]{:S(2)}) %collective-permute-start.18) | collective-permute-done | bytes 196640 | tf_op jit(solution)/shard_map/ppermute | solution.py:243
  81.3 1.3 %collective-permute-start.19 = (bf16[768,128]{1,0:T(8,128)(2,1)S(1)}, bf16[768,128]{1,0:T(8,128)(2,1)S(1)}, u32[]{:S(2)}, u32[]{:S(2)}) collective-permute-start(bf16[768,128]{1,0:T(8,128)(2,1)S(1)} %collective-permute-done.18.v_across), channel_id=1, source_target_pairs={{8,0},{16,24},{9,1},{17,25},{10,2},{18,26},{11,3},{19,27},{12,4},{... | collective-permute-start | bytes 589832 | tf_op jit(solution)/shard_map/ppermute | solution.py:243
  82.7 5.0 %attend_own.1 = (f32[8,384,1]{2,1,0:T(8,128)S(1)}, f32[8,384,1]{2,1,0:T(8,128)S(1)}, f32[8,384,128]{2,1,0:T(8,128)S(1)}, bf16[2,192,256]{2,1,0:T(8,128)(2,1)S(1)}) custom-call(s32[1]{0:T(128)} %bitcast.place.info, bf16[384,1024]{1,0:T(8,128)(2,1)} %q_ref.3, s32[12,128]{1,0:T(8,128)S(1)} %bitcast.12, bf16[784,128]{1,0:T(8,128)(2,1)S(1)} %distant.2.k_in, ...), custom_call_target="tpu_custom_call" | custom-call | flops 1207959552 | bytes 18874368 | tf_op jit(solution)/shard_map/attend_own/pallas_call | solution.py:526
  87.6 1.9 %collective-permute-done.19.v_far = bf16[768,128]{1,0:T(8,128)(2,1)S(1)} collective-permute-done((bf16[768,128]{1,0:T(8,128)(2,1)S(1)}, bf16[768,128]{1,0:T(8,128)(2,1)S(1)}, u32[]{:S(2)}, u32[]{:S(2)}) %collective-permute-start.19) | collective-permute-done | bytes 196640 | tf_op jit(solution)/shard_map/ppermute | solution.py:243
  89.5 7.1 %attend_far.1 = (bf16[384,1024]{1,0:T(8,128)(2,1)}, bf16[4,192,256]{2,1,0:T(8,128)(2,1)}) custom-call(s32[1]{0:T(128)} %bitcast.place.info, bf16[384,1024]{1,0:T(8,128)(2,1)} %q_ref.3, s32[12,128]{1,0:T(8,128)S(1)} %bitcast.13, bf16[784,128]{1,0:T(8,128)(2,1)S(1)} %collective-permute-done.13.k_across, bf16[784,128]{1,0:T(8,128)(2,1)S(1)} %collective-permute-done.14.k_far, ...), custom_call_target="tpu_custom_call" | custom-call | flops 1207959552 | bytes 18874368 | tf_op jit(solution)/shard_map/attend_far/pallas_call | solution.py:541
  (24 shorter events, 0.1 us)
Async XLA Ops:
  0.6 15.9 %collective-permute-start.1 = (bf16[2048,128]{1,0:T(8,128)(2,1)}, bf16[2048,128]{1,0:T(8,128)(2,1)S(1)}, u32[]{:S(2)}, u32[]{:S(2)}) collective-permute-start(bf16[2048,128]{1,0:T(8,128)(2,1)} %kw_ref.1), channel_id=1, source_target_pairs={{8,16},{16,8},{9,17},{17,9},{10,18},{18,10},{11,19},{19,11},{12,20... | collective-permute-start | bytes 1572872 | tf_op jit(solution)/shard_map/ppermute | solution.py:243
  4.0 12.5 %collective-permute-start = (bf16[384,512]{1,0:T(8,128)(2,1)S(1)}, bf16[384,512]{1,0:T(8,128)(2,1)S(1)}, u32[]{:S(2)}, u32[]{:S(2)}) collective-permute-start(bf16[384,512]{1,0:T(8,128)(2,1)S(1)} %constant_dynamic-slice_fusion), channel_id=1, source_target_pairs={{0,8},{24,16},{1,9},{25,17},{2,10},{26,18},{3,11},{27,19},{4,12},{... | collective-permute-start | bytes 1179656 | tf_op jit(solution)/shard_map/ppermute | solution.py:243
  5.3 11.2 %copy-start.5 = (bf16[2048,128]{1,0:T(8,128)(2,1)S(1)}, bf16[2048,128]{1,0:T(8,128)(2,1)}, u32[]{:S(2)}) copy-start(bf16[2048,128]{1,0:T(8,128)(2,1)} %kw_ref.1) | copy-start | bytes 1572868
  5.4 42.9 %copy-start.6 = (s32[24,1]{0,1:T(1,128)S(1)}, s32[24,1]{0,1:T(1,128)}, u32[]{:S(2)}) copy-start(s32[24,1]{0,1:T(1,128)} %param.15) | copy-start | bytes 292
  16.5 15.0 %collective-permute-start.3 = (bf16[2048,128]{1,0:T(8,128)(2,1)S(1)}, bf16[2048,128]{1,0:T(8,128)(2,1)}, u32[]{:S(2)}, u32[]{:S(2)}) collective-permute-start(bf16[2048,128]{1,0:T(8,128)(2,1)S(1)} %copy-done.5), channel_id=1, source_target_pairs={{0,8},{8,0},{16,24},{24,16},{1,9},{9,1},{17,25},{25,17},{2,10},{10... | collective-permute-start | bytes 1572872 | tf_op jit(solution)/shard_map/ppermute | solution.py:243
  16.5 15.0 %collective-permute-start.4 = (bf16[2048,128]{1,0:T(8,128)(2,1)}, bf16[2048,128]{1,0:T(8,128)(2,1)S(1)}, u32[]{:S(2)}, u32[]{:S(2)}) collective-permute-start(bf16[2048,128]{1,0:T(8,128)(2,1)} %vw_ref.1), channel_id=1, source_target_pairs={{8,16},{16,8},{9,17},{17,9},{10,18},{18,10},{11,19},{19,11},{12,20... | collective-permute-start | bytes 1572872 | tf_op jit(solution)/shard_map/ppermute | solution.py:243
  20.0 18.8 %collective-permute-start.11 = (bf16[384,512]{1,0:T(8,128)(2,1)S(1)}, bf16[384,512]{1,0:T(8,128)(2,1)S(1)}, u32[]{:S(2)}, u32[]{:S(2)}) collective-permute-start(bf16[384,512]{1,0:T(8,128)(2,1)S(1)} %collective-permute-done.refs_0_), channel_id=1, source_target_pairs={{0,6},{1,7},{2,4},{3,5},{4,2},{5,3},{6,0},{7,1},{8,14},{9,15},{10,... | collective-permute-start | bytes 1179656 | tf_op jit(solution)/shard_map/ppermute | solution.py:246
  22.5 22.7 %collective-permute-start.15 = (bf16[2048,128]{1,0:T(8,128)(2,1)}, bf16[2048,128]{1,0:T(8,128)(2,1)}, u32[]{:S(2)}, u32[]{:S(2)}) collective-permute-start(bf16[2048,128]{1,0:T(8,128)(2,1)} %vw_ref.1), channel_id=1, source_target_pairs={{0,8},{8,0},{16,24},{24,16},{1,9},{9,1},{17,25},{25,17},{2,10},{10... | collective-permute-start | bytes 1572872 | tf_op jit(solution)/shard_map/ppermute | solution.py:243
  31.5 0.8 copy-start
  32.3 15.7 %collective-permute-start.5 = (bf16[2048,128]{1,0:T(8,128)(2,1)}, bf16[2048,128]{1,0:T(8,128)(2,1)}, u32[]{:S(2)}, u32[]{:S(2)}) collective-permute-start(bf16[2048,128]{1,0:T(8,128)(2,1)} %collective-permute-done.3.w_ref), channel_id=1, source_target_pairs={{8,16},{16,8},{9,17},{17,9},{10,18},{18,10},{11,19},{19,11},{12,20... | collective-permute-start | bytes 1572872 | tf_op jit(solution)/shard_map/ppermute | solution.py:243
  35.8 8.3 %collective-permute-start.8 = (bf16[384,512]{1,0:T(8,128)(2,1)S(1)}, bf16[384,512]{1,0:T(8,128)(2,1)S(1)}, u32[]{:S(2)}, u32[]{:S(2)}) collective-permute-start(bf16[384,512]{1,0:T(8,128)(2,1)S(1)} %collective-permute-done.refs_0_), channel_id=1, source_target_pairs={{0,2},{1,3},{2,0},{3,1},{4,6},{5,7},{6,4},{7,5},{8,10},{9,11},{10,... | collective-permute-start | bytes 1179656 | tf_op jit(solution)/shard_map/ppermute | solution.py:246
  37.3 7.9 %collective-permute-start.2 = (bf16[384,512]{1,0:T(8,128)(2,1)S(1)}, bf16[384,512]{1,0:T(8,128)(2,1)S(1)}, u32[]{:S(2)}, u32[]{:S(2)}) collective-permute-start(bf16[384,512]{1,0:T(8,128)(2,1)S(1)} %collective-permute-done.refs_0_), channel_id=1, source_target_pairs={{0,4},{1,5},{2,6},{3,7},{4,0},{5,1},{6,2},{7,3},{8,12},{9,13},{10,... | collective-permute-start | bytes 1179656 | tf_op jit(solution)/shard_map/ppermute | solution.py:246
  38.8 12.5 %collective-permute-start.7 = (bf16[384,512]{1,0:T(8,128)(2,1)S(1)}, bf16[384,512]{1,0:T(8,128)(2,1)S(1)}, u32[]{:S(2)}, u32[]{:S(2)}) collective-permute-start(bf16[384,512]{1,0:T(8,128)(2,1)S(1)} %collective-permute-done.refs_0_), channel_id=1, source_target_pairs={{0,1},{1,0},{2,3},{3,2},{4,5},{5,4},{6,7},{7,6},{8,9},{9,8},{10,11... | collective-permute-start | bytes 1179656 | tf_op jit(solution)/shard_map/ppermute | solution.py:246
  44.0 11.8 %collective-permute-start.12 = (bf16[384,512]{1,0:T(8,128)(2,1)S(1)}, bf16[384,512]{1,0:T(8,128)(2,1)S(1)}, u32[]{:S(2)}, u32[]{:S(2)}) collective-permute-start(bf16[384,512]{1,0:T(8,128)(2,1)S(1)} %collective-permute-done.11.refs_6_), channel_id=1, source_target_pairs={{0,1},{1,0},{2,3},{3,2},{4,5},{5,4},{6,7},{7,6},{8,9},{9,8},{10,11... | collective-permute-start | bytes 1179656 | tf_op jit(solution)/shard_map/ppermute | solution.py:246
  45.2 12.0 %collective-permute-start.9 = (bf16[384,512]{1,0:T(8,128)(2,1)S(1)}, bf16[384,512]{1,0:T(8,128)(2,1)S(1)}, u32[]{:S(2)}, u32[]{:S(2)}) collective-permute-start(bf16[384,512]{1,0:T(8,128)(2,1)S(1)} %collective-permute-done.8.refs_2_), channel_id=1, source_target_pairs={{0,1},{1,0},{2,3},{3,2},{4,5},{5,4},{6,7},{7,6},{8,9},{9,8},{10,11... | collective-permute-start | bytes 1179656 | tf_op jit(solution)/shard_map/ppermute | solution.py:246
  45.2 25.4 %collective-permute-start.16 = (bf16[2048,128]{1,0:T(8,128)(2,1)}, bf16[2048,128]{1,0:T(8,128)(2,1)S(1)}, u32[]{:S(2)}, u32[]{:S(2)}) collective-permute-start(bf16[2048,128]{1,0:T(8,128)(2,1)} %collective-permute-done.15.w_ref), channel_id=1, source_target_pairs={{8,16},{16,8},{9,17},{17,9},{10,18},{18,10},{11,19},{19,11},{12,20... | collective-permute-start | bytes 1572872 | tf_op jit(solution)/shard_map/ppermute | solution.py:243
  48.0 9.3 %collective-permute-start.10 = (bf16[384,512]{1,0:T(8,128)(2,1)S(1)}, bf16[384,512]{1,0:T(8,128)(2,1)S(1)}, u32[]{:S(2)}, u32[]{:S(2)}) collective-permute-start(bf16[384,512]{1,0:T(8,128)(2,1)S(1)} %collective-permute-done.2.refs_4_), channel_id=1, source_target_pairs={{0,1},{1,0},{2,3},{3,2},{4,5},{5,4},{6,7},{7,6},{8,9},{9,8},{10,11... | collective-permute-start | bytes 1179656 | tf_op jit(solution)/shard_map/ppermute | solution.py:246
  51.3 9.1 %collective-permute-start.6 = (f32[392,128]{1,0:T(8,128)S(1)}, f32[392,128]{1,0:T(8,128)S(1)}, u32[]{:S(2)}, u32[]{:S(2)}) collective-permute-start(f32[392,128]{1,0:T(8,128)S(1)} %partial.2.near_ref), channel_id=1, source_target_pairs={{0,8},{24,16},{1,9},{25,17},{2,10},{26,18},{3,11},{27,19},{4,12},{... | collective-permute-start | bytes 602120 | tf_op jit(solution)/shard_map/ppermute | solution.py:243
  52.7 4.5 %copy-start.1 = (bf16[2048,128]{1,0:T(8,128)(2,1)S(1)}, bf16[2048,128]{1,0:T(8,128)(2,1)}, u32[]{:S(2)}) copy-start(bf16[2048,128]{1,0:T(8,128)(2,1)} %copy-done) | copy-start | bytes 1572868
  55.8 14.8 %collective-permute-start.17 = (f32[384,128]{1,0:T(8,128)S(1)}, f32[384,128]{1,0:T(8,128)S(1)}, u32[]{:S(2)}, u32[]{:S(2)}) collective-permute-start(f32[384,128]{1,0:T(8,128)S(1)} %partial.3.near_ref), channel_id=1, source_target_pairs={{0,8},{24,16},{1,9},{25,17},{2,10},{26,18},{3,11},{27,19},{4,12},{... | collective-permute-start | bytes 589832 | tf_op jit(solution)/shard_map/ppermute | solution.py:243
  57.2 3.2 %copy-start.3 = (bf16[128]{0:T(256)(128)(2,1)S(1)}, bf16[128]{0:T(256)(128)(2,1)}, u32[]{:S(2)}) copy-start(bf16[128]{0:T(256)(128)(2,1)} %param.12) | copy-start | bytes 772
  60.4 10.2 %copy-start.4 = (bf16[128]{0:T(256)(128)(2,1)S(1)}, bf16[128]{0:T(256)(128)(2,1)}, u32[]{:S(2)}) copy-start(bf16[128]{0:T(256)(128)(2,1)} %param.13) | copy-start | bytes 772
  63.5 12.4 %collective-permute-start.20 = (bf16[784,128]{1,0:T(8,128)(2,1)S(1)}, bf16[784,128]{1,0:T(8,128)(2,1)S(1)}, u32[]{:S(2)}, u32[]{:S(2)}) collective-permute-start(bf16[784,128]{1,0:T(8,128)(2,1)S(1)} %distant.2.k_in), channel_id=1, source_target_pairs={{8,0},{16,24},{9,1},{17,25},{10,2},{18,26},{11,3},{19,27},{12,4},{... | collective-permute-start | bytes 602120 | tf_op jit(solution)/shard_map/ppermute | solution.py:243
  67.5 9.8 %collective-permute-start.13 = (bf16[784,128]{1,0:T(8,128)(2,1)S(1)}, bf16[784,128]{1,0:T(8,128)(2,1)S(1)}, u32[]{:S(2)}, u32[]{:S(2)}) collective-permute-start(bf16[784,128]{1,0:T(8,128)(2,1)S(1)} %distant.2.k_in), channel_id=1, source_target_pairs={{8,16},{16,8},{9,17},{17,9},{10,18},{18,10},{11,19},{19,11},{12,20... | collective-permute-start | bytes 602120 | tf_op jit(solution)/shard_map/ppermute | solution.py:243
  70.6 12.0 %copy-start.2 = (s32[1536]{0:T(1024)S(1)}, s32[1536]{0:T(1024)}, u32[]{:S(2)}) copy-start(s32[1536]{0:T(1024)} %param.14) | copy-start | bytes 18436
  73.2 8.1 %collective-permute-start.18 = (bf16[768,128]{1,0:T(8,128)(2,1)S(1)}, bf16[768,128]{1,0:T(8,128)(2,1)S(1)}, u32[]{:S(2)}, u32[]{:S(2)}) collective-permute-start(bf16[768,128]{1,0:T(8,128)(2,1)S(1)} %distant.3.v_in), channel_id=1, source_target_pairs={{8,16},{16,8},{9,17},{17,9},{10,18},{18,10},{11,19},{19,11},{12,20... | collective-permute-start | bytes 589832 | tf_op jit(solution)/shard_map/ppermute | solution.py:243
  75.9 6.7 %collective-permute-start.21 = (bf16[768,128]{1,0:T(8,128)(2,1)S(1)}, bf16[768,128]{1,0:T(8,128)(2,1)S(1)}, u32[]{:S(2)}, u32[]{:S(2)}) collective-permute-start(bf16[768,128]{1,0:T(8,128)(2,1)S(1)} %distant.3.v_in), channel_id=1, source_target_pairs={{8,0},{16,24},{9,1},{17,25},{10,2},{18,26},{11,3},{19,27},{12,4},{... | collective-permute-start | bytes 589832 | tf_op jit(solution)/shard_map/ppermute | solution.py:243
  77.3 12.2 %collective-permute-start.14 = (bf16[784,128]{1,0:T(8,128)(2,1)S(1)}, bf16[784,128]{1,0:T(8,128)(2,1)S(1)}, u32[]{:S(2)}, u32[]{:S(2)}) collective-permute-start(bf16[784,128]{1,0:T(8,128)(2,1)S(1)} %collective-permute-done.13.k_across), channel_id=1, source_target_pairs={{8,0},{16,24},{9,1},{17,25},{10,2},{18,26},{11,3},{19,27},{12,4},{... | collective-permute-start | bytes 602120 | tf_op jit(solution)/shard_map/ppermute | solution.py:243
  81.3 8.2 %collective-permute-start.19 = (bf16[768,128]{1,0:T(8,128)(2,1)S(1)}, bf16[768,128]{1,0:T(8,128)(2,1)S(1)}, u32[]{:S(2)}, u32[]{:S(2)}) collective-permute-start(bf16[768,128]{1,0:T(8,128)(2,1)S(1)} %collective-permute-done.18.v_across), channel_id=1, source_target_pairs={{8,0},{16,24},{9,1},{17,25},{10,2},{18,26},{11,3},{19,27},{12,4},{... | collective-permute-start | bytes 589832 | tf_op jit(solution)/shard_map/ppermute | solution.py:243

commit v8 on v7

--- a/solution.py
+++ b/solution.py
@@ -109,12 +109,7 @@
 
 
 PIECES = 8
-
-
-def chunk_copy(h_ref, chunk, h_buf, sem):
-    depth = h_buf.shape[1]
-    columns = pl.ds(pl.multiple_of(chunk * depth, depth), depth)
-    return pltpu.make_async_copy(h_ref.at[:, columns], h_buf, sem)
+PARTS = 4
 
 
 def add_pieces(member, chunk, pieces, w_ref, acc_ref):
@@ -135,68 +130,95 @@
             acc_ref[...] = total
 
 
-def near_kernel(place, h_ref, kw_ref, vw_ref, out_ref, h_buf, w_buf, sems):
+def chunk_copies(h_ref, chunk, h_buf, sems):
+    depth = h_buf.shape[1]
+    part = depth // PARTS
+    copies = []
+    for t in range(PARTS):
+        columns = pl.ds(pl.multiple_of(chunk * depth + t * part, part), part)
+        to = h_buf.at[:, pl.ds(t * part, part)]
+        copies.append(pltpu.make_async_copy(h_ref.at[:, columns], to, sems.at[t]))
+        copies[t].start()
+    return copies
+
+
+def chunk_product(copies, h_buf, w_ref):
+    part = h_buf.shape[1] // PARTS
+    total = None
+    for t, copy in enumerate(copies):
+        copy.wait()
+        at = slice(t * part, t * part + part)
+        product = jnp.dot(h_buf[:, at], w_ref[at, :], preferred_element_type=jnp.float32)
+        total = product if total is None else total + product
+    return total
+
+
+def weight_copies(kw_ref, vw_ref, w_buf, sems):
     copies = [
-        chunk_copy(h_ref, place[0], h_buf, sems.at[0]),
-        pltpu.make_async_copy(kw_ref, w_buf.at[:, pl.ds(0, HD)], sems.at[1]),
-        pltpu.make_async_copy(vw_ref, w_buf.at[:, pl.ds(HD, HD)], sems.at[2]),
+        pltpu.make_async_copy(kw_ref, w_buf.at[:, pl.ds(0, HD)], sems.at[PARTS]),
+        pltpu.make_async_copy(vw_ref, w_buf.at[:, pl.ds(HD, HD)], sems.at[PARTS + 1]),
     ]
     for copy in copies:
         copy.start()
-    for copy in copies:
+    return copies
+
+
+def near_kernel(place, h_ref, kw_ref, vw_ref, out_ref, h_buf, w_buf, sems):
+    weights = weight_copies(kw_ref, vw_ref, w_buf, sems)
+    copies = chunk_copies(h_ref, place[0], h_buf, sems)
+    for copy in weights:
         copy.wait()
-    out_ref[...] = jnp.dot(h_buf[...], w_buf[...], preferred_element_type=jnp.float32)
-
-
-def partial_kernel(column, place, h_ref, w_ref, before_ref, owner_ref, out_ref, h_buf, sem):
-    copy = chunk_copy(h_ref, place[0], h_buf, sem)
-    copy.start()
+    out_ref[...] = chunk_product(copies, h_buf, w_buf)
+
+
+def partial_kernel(column, place, h_ref, w_ref, before_ref, owner_ref, out_ref, h_buf, sems):
+    copies = chunk_copies(h_ref, place[0], h_buf, sems)
     span = h_buf.shape[0]
     part = slice(column * HD, column * HD + HD)
     if column == 0:
         out_ref[span:] = owner_ref[...]
-    copy.wait()
-    out_ref[:span] = before_ref[:, part] + jnp.dot(
-        h_buf[...], w_ref[...], preferred_element_type=jnp.float32
-    )
+    out_ref[:span] = before_ref[:, part] + chunk_product(copies, h_buf, w_ref)
 
 
 def facing_kernel(place, h_ref, kw_ref, vw_ref, *refs):
     pieces = refs[:PIECES]
-    out_ref, h_buf, w_buf, sem = refs[PIECES:]
-    copy = chunk_copy(h_ref, place[0], h_buf, sem)
-    copy.start()
+    out_ref, h_buf, w_buf, sems = refs[PIECES:]
     span = h_buf.shape[0]
-    w_buf[:, :HD] = kw_ref[...]
-    w_buf[:, HD:] = vw_ref[...]
-    out_ref[span:] = jnp.zeros((span, 2 * HD), jnp.float32)
-    add_pieces(place[2], place[0], pieces, w_buf, out_ref.at[pl.ds(span, span)])
-    copy.wait()
-    out_ref[:span] = jnp.dot(h_buf[...], w_buf[...], preferred_element_type=jnp.float32)
+
+    @pl.when(place[3] == 1)
+    def _():
+        weights = weight_copies(kw_ref, vw_ref, w_buf, sems)
+        copies = chunk_copies(h_ref, place[0], h_buf, sems)
+        for copy in weights:
+            copy.wait()
+        out_ref[span:] = jnp.zeros((span, 2 * HD), jnp.float32)
+        add_pieces(place[2], place[0], pieces, w_buf, out_ref.at[pl.ds(span, span)])
+        out_ref[:span] = chunk_product(copies, h_buf, w_buf)
 
 
 def distant_kernel(column, place, h_ref, w_ref, near_ref, outer_ref, facing_ref, bias_ref, *refs):
     pieces = refs[:PIECES]
-    out_ref, h_buf, acc, sem = refs[PIECES:]
-    copy = chunk_copy(h_ref, place[0], h_buf, sem)
-    copy.start()
+    out_ref, h_buf, acc, sems = refs[PIECES:]
     span = h_buf.shape[0]
     part = slice(column * HD, column * HD + HD)
-    own_at = pl.multiple_of(place[1] * span, span)
-    outer_at = pl.multiple_of((1 - place[1]) * span, span)
-    bias = bias_ref[...].astype(jnp.float32)
-    acc[...] = outer_ref[:span] + facing_ref[span:, part] + bias
-    add_pieces(place[2], place[0], pieces, w_ref, acc)
-    out_ref[pl.ds(outer_at, span), :] = acc[...].astype(jnp.bfloat16)
-    own = near_ref[:span] + facing_ref[:span, part] + bias
-    copy.wait()
-    own += jnp.dot(h_buf[...], w_ref[...], preferred_element_type=jnp.float32)
-    out_ref[pl.ds(own_at, span), :] = own.astype(jnp.bfloat16)
-    if column == 0:
-        mine, theirs = near_ref[span:], outer_ref[span:]
-        lower = jnp.where(place[1] == 0, mine, theirs)
-        upper = jnp.where(place[1] == 0, theirs, mine)
-        out_ref[2 * span :] = jnp.concatenate([lower, upper], axis=0).astype(jnp.bfloat16)
+
+    @pl.when(place[3] == 1)
+    def _():
+        copies = chunk_copies(h_ref, place[0], h_buf, sems)
+        own_at = pl.multiple_of(place[1] * span, span)
+        outer_at = pl.multiple_of((1 - place[1]) * span, span)
+        bias = bias_ref[...].astype(jnp.float32)
+        acc[...] = outer_ref[:span] + facing_ref[span:, part] + bias
+        add_pieces(place[2], place[0], pieces, w_ref, acc)
+        out_ref[pl.ds(outer_at, span), :] = acc[...].astype(jnp.bfloat16)
+        own = near_ref[:span] + facing_ref[:span, part] + bias
+        own += chunk_product(copies, h_buf, w_ref)
+        out_ref[pl.ds(own_at, span), :] = own.astype(jnp.bfloat16)
+        if column == 0:
+            mine, theirs = near_ref[span:], outer_ref[span:]
+            lower = jnp.where(place[1] == 0, mine, theirs)
+            upper = jnp.where(place[1] == 0, theirs, mine)
+            out_ref[2 * span :] = jnp.concatenate([lower, upper], axis=0).astype(jnp.bfloat16)
 
 
 EXTRA = 8
@@ -209,17 +231,18 @@
     return pltpu.with_memory_space_constraint(x, pltpu.HBM)
 
 
-def call_project(kernel, name, place, operands, rows, columns, kind, scratch, held=1, copies=()):
+def call_project(kernel, name, operands, in_specs, shapes, scratch=()):
+    many = isinstance(shapes, list)
     return pl.pallas_call(
         kernel,
-        in_specs=[SCALAR] + [HELD] * held + [FAST] * (len(operands) - held),
-        out_specs=FAST,
-        out_shape=jax.ShapeDtypeStruct((rows, columns), kind),
-        scratch_shapes=scratch + [pltpu.SemaphoreType.DMA(copies)],
+        in_specs=in_specs,
+        out_specs=[FAST] * len(shapes) if many else FAST,
+        out_shape=shapes,
+        scratch_shapes=list(scratch),
         compiler_params=pltpu.CompilerParams(vmem_limit_bytes=KERNEL_VMEM),
         cost_estimate=pl.CostEstimate(flops=0, bytes_accessed=0, transcendentals=0),
         name=name,
-    )(place, *[in_hbm(x) for x in operands[:held]], *operands[held:])
+    )(*operands)
 
 
 INWARD = [(0, 1), (3, 2)]
@@ -238,31 +261,40 @@
     near = jnp.bitwise_xor(index, 1)
     distant = jnp.bitwise_xor(facing, 1)
     second = (index < 2).astype(jnp.int32)
+    inner = ((index == 1) | (index == 2)).astype(jnp.int32)
+    tie = lax.optimization_barrier
 
     def send(x, pairs):
         return lax.ppermute(x, "pre", pairs)
 
     def trade(x, apart):
-        return lax.ppermute(x, ("dec", "tp"), [(m, m ^ apart) for m in range(PIECES)])
+        pairs = [(p * PIECES + m, p * PIECES + (m ^ apart)) for p in (1, 2) for m in range(PIECES)]
+        return lax.ppermute(x, ("pre", "dec", "tp"), pairs)
+
+    def place(chunk):
+        return jnp.stack([chunk, second, member, inner])
+
+    def f32(rows, columns):
+        return jax.ShapeDtypeStruct((rows, columns), jnp.float32)
+
+    def bf16(rows, columns):
+        return jax.ShapeDtypeStruct((rows, columns), jnp.bfloat16)
 
     mine = second * (width // 2) + member * share
     cut = lax.dynamic_slice_in_dim(hidden, mine, share, axis=1)
-    tie = lax.optimization_barrier
-    block = pltpu.VMEM((span, depth), jnp.bfloat16)
     both = pltpu.VMEM((depth, 2 * HD), jnp.bfloat16)
     key_facing = send(key_weight, ACROSS)
     cut = send(cut, INWARD)
+    block = [pltpu.VMEM((span, depth), jnp.bfloat16)]
+    parts = [pltpu.SemaphoreType.DMA((PARTS,))]
+    held = in_hbm(hidden)
     own_part = call_project(
         near_kernel,
         "near",
-        index[None],
-        [hidden, key_weight, value_weight],
-        span,
-        2 * HD,
-        jnp.float32,
-        [block, both],
-        held=3,
-        copies=(3,),
+        [index[None], held, in_hbm(key_weight), in_hbm(value_weight)],
+        [SCALAR] + [HELD] * 3,
+        f32(span, 2 * HD),
+        block + [both, pltpu.SemaphoreType.DMA((PARTS + 2,))],
     )
     cut, key_facing, key_after, value_after, own_part = tie(
         (cut, key_facing, key_weight, value_weight, own_part)
@@ -273,57 +305,49 @@
     chips = [cut, trade(cut, 2), trade(cut, 4), trade(cut, 6)]
     key_swapped, value_facing = tie((key_swapped, value_facing))
     key_distant = send(key_swapped, ACROSS)
+    owners = jnp.broadcast_to(page_owner.T.astype(jnp.float32), (EXTRA, page_owner.shape[0]))
+    owners = jnp.pad(owners, ((0, 0), (0, HD - page_owner.shape[0])))
+
+    def begin(column, weight):
+        return call_project(
+            functools.partial(partial_kernel, column),
+            "partial",
+            [near[None], held, weight, own_part, owners],
+            [SCALAR, HELD] + [FAST] * 3,
+            f32(span + (EXTRA if column == 0 else 0), HD),
+            block + parts,
+        )
+
+    key_part = begin(0, key_swapped)
+    key_part, value_swapped = tie((key_part, value_swapped))
     value_distant = send(value_swapped, ACROSS)
+    value_part = begin(1, value_swapped)
+    key_outer, value_outer = send(key_part, INWARD), send(value_part, INWARD)
     chips[2], key_distant = tie((chips[2], key_distant))
     mates = [trade(x, 1) for x in chips]
     pieces = [x for both_cores in zip(chips, mates) for x in both_cores]
-
-    def place(chunk):
-        return jnp.stack([chunk, second, member])
-
-    owners = jnp.broadcast_to(page_owner.T.astype(jnp.float32), (EXTRA, page_owner.shape[0]))
-    owners = jnp.pad(owners, ((0, 0), (0, HD - page_owner.shape[0])))
-
-    def begin(column, weight):
-        part = call_project(
-            functools.partial(partial_kernel, column),
-            "partial",
-            near[None],
-            [hidden, weight, own_part, owners],
-            span + (EXTRA if column == 0 else 0),
-            HD,
-            jnp.float32,
-            [block],
-        )
-        return part, send(part, INWARD)
-
-    def finish(column, weight, parts, bias):
+    faced = call_project(
+        facing_kernel,
+        "facing",
+        [place(facing), held, in_hbm(key_facing), in_hbm(value_facing)] + pieces,
+        [SCALAR] + [HELD] * 3 + [FAST] * PIECES,
+        f32(2 * span, 2 * HD),
+        block + [both, pltpu.SemaphoreType.DMA((PARTS + 2,))],
+    )
+
+    def finish(column, weight, part, outer, bias):
         return call_project(
             functools.partial(distant_kernel, column),
             "distant",
-            place(distant),
-            [hidden, weight, *parts, faced, bias[None, :]] + pieces,
-            2 * span + (2 * EXTRA if column == 0 else 0),
-            HD,
-            jnp.bfloat16,
-            [block, pltpu.VMEM((span, HD), jnp.float32)],
+            [place(distant), held, weight, part, outer, faced, bias[None, :]] + pieces,
+            [SCALAR, HELD] + [FAST] * (5 + PIECES),
+            bf16(2 * span + (2 * EXTRA if column == 0 else 0), HD),
+            block + [pltpu.VMEM((span, HD), jnp.float32)] + parts,
         )
 
-    key_parts = begin(0, key_swapped)
-    value_parts = begin(1, value_swapped)
-    faced = call_project(
-        facing_kernel,
-        "facing",
-        place(facing),
-        [hidden, key_facing, value_facing] + pieces,
-        2 * span,
-        2 * HD,
-        jnp.float32,
-        [block, both],
-    )
-    keys = finish(0, key_distant, key_parts, key_bias)
+    keys = finish(0, key_distant, key_part, key_outer, key_bias)
     keys_out, keys_across = send(keys, OUTWARD), send(keys, ACROSS)
-    values = finish(1, value_distant, value_parts, value_bias)
+    values = finish(1, value_distant, value_part, value_outer, value_bias)
     values_across = send(values, ACROSS)
     keys_out, values_after = tie((keys_out, values))
     values_out = send(values_after, OUTWARD)
@@ -472,6 +496,8 @@
     named,
     laid,
     sems,
+    out_buf,
+    far_cache,
 ):
     copy = pltpu.make_async_copy(q_ref, q_buf, sems.at[0])
     copy.start()
@@ -480,14 +506,27 @@
     inner = (index == 1) | (index == 2)
     held_k[...] = jnp.where(inner, k_across[...], k_far[...])
     held_v[...] = jnp.where(inner, v_across[...], v_far[...])
-    cache_ref[pl.ds(index // 2 * 2, 2)] = own_cache[...]
     owners = read_owners(held_k, span, listed, named, sems.at[1])
+    own_at, far_at = index // 2 * 2, (1 - index // 2) * 2
+    leaving = [pltpu.make_async_copy(own_cache, cache_ref.at[pl.ds(own_at, 2)], sems.at[2])]
+    leaving[0].start()
     copy.wait()
+
+    def leave(g):
+        columns = pl.ds(g * HD, HD)
+        return pltpu.make_async_copy(out_buf.at[:, columns], out_ref.at[:, columns], sems.at[4 + g])
+
+    def place_far():
+        owners.wait()
+        place_pages(index, span, named, held_k, held_v, far_cache, laid)
+        return pltpu.make_async_copy(far_cache, cache_ref.at[pl.ds(far_at, 2)], sems.at[3])
 
     @pl.when(index < 2)
     def _():
         for g in range(heads):
-            out_ref[:, g * HD : (g + 1) * HD] = (mix[g] / total[g]).astype(out_ref.dtype)
+            out_buf[:, g * HD : (g + 1) * HD] = (mix[g] / total[g]).astype(out_buf.dtype)
+            leave(g).start()
+        place_far().start()
 
     @pl.when(index >= 2)
     def _():
@@ -497,13 +536,17 @@
         allowed = columns >= prompt_starts(seg_ref, index * span, span)
 
         def store(g, peak, sums, mixed):
-            out_ref[:, g * HD : (g + 1) * HD] = (mixed / sums).astype(out_ref.dtype)
+            out_buf[:, g * HD : (g + 1) * HD] = (mixed / sums).astype(out_buf.dtype)
+            leave(g).start()
+            if g == heads // 2:
+                place_far().start()
 
         attend(q_buf, heads, keys, values, allowed, lambda g: (top[g], total[g], mix[g]), store)
 
-    owners.wait()
-    far_cache = cache_ref.at[pl.ds((1 - index // 2) * 2, 2)]
-    place_pages(index, span, named, held_k, held_v, far_cache, laid)
+    for g in range(heads):
+        leave(g).wait()
+    leaving[0].wait()
+    pltpu.make_async_copy(far_cache, cache_ref.at[pl.ds(far_at, 2)], sems.at[3]).wait()
 
 
 def attention_of_pairs(queries, segment_ids, keys, values, capacity):
@@ -521,7 +564,7 @@
         pltpu.VMEM((2 * EXTRA, HD), jnp.int32),
         pltpu.SMEM((2 * EXTRA, HD), jnp.int32),
         pltpu.VMEM((2, (capacity + 1) * PAGE, 2 * HD), jnp.bfloat16),
-        pltpu.SemaphoreType.DMA((2,)),
+        pltpu.SemaphoreType.DMA((4 + heads,)),
     ]
     state = pl.pallas_call(
         functools.partial(own_kernel, heads),
@@ -541,12 +584,16 @@
     return pl.pallas_call(
         functools.partial(far_kernel, heads),
         in_specs=[SCALAR, HELD] + [FAST] * 9,
-        out_specs=[FAST] * 2,
+        out_specs=[HELD] * 2,
         out_shape=[
             jax.ShapeDtypeStruct(queries.shape, jnp.bfloat16),
             jax.ShapeDtypeStruct((4, capacity * PAGE, 2 * HD), jnp.bfloat16),
         ],
-        scratch_shapes=scratch,
+        scratch_shapes=scratch
+        + [
+            pltpu.VMEM(queries.shape, jnp.bfloat16),
+            pltpu.VMEM((2, capacity * PAGE, 2 * HD), jnp.bfloat16),
+        ],
         compiler_params=params,
         cost_estimate=cost,
         name="attend_far",

time: 98.4 us -> 103 us (1.047)
  starting transfers between devices: 35.5 us -> 46.8 us
  waiting for transfers between devices: 29.4 us -> 20.1 us
  Pallas kernels: 28.7 us -> 30.6 us
    ppermute x7, starting transfers between devices: 5.89 us -> 19.8 us  [trade(): return lax.ppermute(x, ('pre', 'dec', 'tp'), pairs)]
    ppermute x7, waiting for transfers between devices: 6.39 us -> 0.02 us  [trade(): return lax.ppermute(x, ('pre', 'dec', 'tp'), pairs)]
    ppermute x15, waiting for transfers between devices: 23 us -> 20.1 us  [send(): return lax.ppermute(x, 'pre', pairs)]
    ppermute x15, starting transfers between devices: 29.6 us -> 26.9 us  [send(): return lax.ppermute(x, 'pre', pairs)]
    pallas_call x6, Pallas kernels: 16.6 us -> 18.8 us  [call_project(): pl.pallas_call(kernel, in_specs=in_specs, out_specs=[FAST] * len(shapes)...]
  transfers between devices with their start and end apart: 22 -> 22, of which waited for: 7 -> 4; matrix products, arithmetic and copies ran while one was open for 1% -> 1% of each run, Pallas kernels for 22% -> 23%
where the time goes in v8:
time: 103 us; the launch traced here: 101 us
  starting transfers between devices  46.8 us (45%)
  Pallas kernels  30.6 us (30%)
  waiting for transfers between devices  20.1 us (20%)
  local copies, waits for them, and re-layouts  2.55 us (2%)
  between operations  1.29 us (1%)
    ppermute x15, starting transfers between devices, send(): return lax.ppermute(x, 'pre', pairs)  26.9 us
    ppermute x15, waiting for transfers between devices, send(): return lax.ppermute(x, 'pre', pairs)  20.1 us
    ppermute x7, starting transfers between devices, trade(): return lax.ppermute(x, ('pre', 'dec', 'tp'), pairs)  19.8 us
    pallas_call x6, Pallas kernels, call_project(): pl.pallas_call(kernel, in_specs=in_specs, out_specs=[FAST] * len(shapes)...  18.8 us
    pallas_call x1, Pallas kernels, attention_of_pairs(): pl.pallas_call(functools.partial(far_kernel, heads), in_specs=[SCALAR, HE...  6.79 us
    pallas_call x1, Pallas kernels, attention_of_pairs(): pl.pallas_call(functools.partial(own_kernel, heads), in_specs=[SCALAR, HE...  5.06 us
  transfers between devices with their start and end apart: 22, of which 4 were waited for; matrix products, arithmetic and copies ran while one was open for 1% of the time, Pallas kernels for 23%

profile of v8, /device:TPU:16, one launch (start us, length us, event | category | flops | bytes accessed | tf_op | source)
XLA Modules:
  0.0 101.5 jit_solution(12127156299955653187)
XLA Ops:
  0.6 2.4 %collective-permute-start.1 = (bf16[2048,128]{1,0:T(8,128)(2,1)}, bf16[2048,128]{1,0:T(8,128)(2,1)S(1)}, u32[]{:S(2)}, u32[]{:S(2)}) collective-permute-start(bf16[2048,128]{1,0:T(8,128)(2,1)} %kw_ref.1), channel_id=1, source_target_pairs={{8,16},{16,8},{9,17},{17,9},{10,18},{18,10},{11,19},{19,11},{12,20... | collective-permute-start | bytes 1572872 | tf_op jit(solution)/shard_map/ppermute | solution.py:268
  3.0 1.0 %constant_dynamic-slice_fusion = bf16[384,512]{1,0:T(8,128)(2,1)S(1)} fusion(bf16[384,8192]{1,0:T(8,128)(2,1)} %h_ref.11, s32[]{:T(128)S(6)} %select_n.3), kind=kLoop, calls=%fused_computation.3 | loop fusion | bytes 786436 | tf_op jit(solution)/shard_map/dynamic_slice | solution.py:284
  4.0 1.3 %collective-permute-start = (bf16[384,512]{1,0:T(8,128)(2,1)S(1)}, bf16[384,512]{1,0:T(8,128)(2,1)S(1)}, u32[]{:S(2)}, u32[]{:S(2)}) collective-permute-start(bf16[384,512]{1,0:T(8,128)(2,1)S(1)} %constant_dynamic-slice_fusion), channel_id=1, source_target_pairs={{0,8},{24,16},{1,9},{25,17},{2,10},{26,18},{3,11},{27,19},{4,12},{... | collective-permute-start | bytes 1179656 | tf_op jit(solution)/shard_map/ppermute | solution.py:268
  5.3 0.0 copy-start.7
  5.4 0.0 copy-start.8
  5.4 0.0 copy-start.9
  5.4 2.7 %near.1.before_ref = f32[384,256]{1,0:T(8,128)S(1)} custom-call(s32[1]{0:T(128)} %bitcast.place.info, bf16[384,8192]{1,0:T(8,128)(2,1)} %h_ref.11, bf16[2048,128]{1,0:T(8,128)(2,1)} %kw_ref.1, bf16[2048,128]{1,0:T(8,128)(2,1)} %vw_ref.1), custom_call_target="tpu_custom_call" | custom-call | tf_op jit(solution)/shard_map/near/pallas_call | solution.py:236
  8.1 8.4 %collective-permute-done.refs_0_ = bf16[384,512]{1,0:T(8,128)(2,1)S(1)} collective-permute-done((bf16[384,512]{1,0:T(8,128)(2,1)S(1)}, bf16[384,512]{1,0:T(8,128)(2,1)S(1)}, u32[]{:S(2)}, u32[]{:S(2)}) %collective-permute-start) | collective-permute-done | bytes 393248 | tf_op jit(solution)/shard_map/ppermute | solution.py:268
  16.5 0.0 collective-permute-done.1.kw_ref
  16.5 0.1 collective-permute-start.3
  16.6 3.5 %collective-permute-start.4 = (bf16[2048,128]{1,0:T(8,128)(2,1)S(1)}, bf16[2048,128]{1,0:T(8,128)(2,1)S(1)}, u32[]{:S(2)}, u32[]{:S(2)}) collective-permute-start(bf16[2048,128]{1,0:T(8,128)(2,1)S(1)} %copy-done.8), channel_id=1, source_target_pairs={{8,16},{16,8},{9,17},{17,9},{10,18},{18,10},{11,19},{19,11},{12,20... | collective-permute-start | bytes 1572872 | tf_op jit(solution)/shard_map/ppermute | solution.py:268
  20.1 0.1 collective-permute-start.6
  20.2 4.4 %collective-permute-start.12 = (bf16[384,512]{1,0:T(8,128)(2,1)S(1)}, bf16[384,512]{1,0:T(8,128)(2,1)S(1)}, u32[]{:S(2)}, u32[]{:S(2)}) collective-permute-start(bf16[384,512]{1,0:T(8,128)(2,1)S(1)} %collective-permute-done.refs_0_), channel_id=1, source_target_pairs={{8,14},{9,15},{10,12},{11,13},{12,10},{13,11},{14,8},{15,9},{16,22... | collective-permute-start | bytes 1179656 | tf_op jit(solution)/shard_map/ppermute | solution.py:272
  24.6 7.0 %collective-permute-done.3.w_ref = bf16[2048,128]{1,0:T(8,128)(2,1)} collective-permute-done((bf16[2048,128]{1,0:T(8,128)(2,1)S(1)}, bf16[2048,128]{1,0:T(8,128)(2,1)}, u32[]{:S(2)}, u32[]{:S(2)}) %collective-permute-start.3) | collective-permute-done | bytes 524320 | tf_op jit(solution)/shard_map/ppermute | solution.py:268
  31.6 0.8 copy-done.6
  32.4 3.5 %collective-permute-start.5 = (bf16[2048,128]{1,0:T(8,128)(2,1)}, bf16[2048,128]{1,0:T(8,128)(2,1)}, u32[]{:S(2)}, u32[]{:S(2)}) collective-permute-start(bf16[2048,128]{1,0:T(8,128)(2,1)} %collective-permute-done.3.w_ref), channel_id=1, source_target_pairs={{8,16},{16,8},{9,17},{17,9},{10,18},{18,10},{11,19},{19,11},{12,20... | collective-permute-start | bytes 1572872 | tf_op jit(solution)/shard_map/ppermute | solution.py:268
  35.8 3.4 %collective-permute-start.9 = (bf16[384,512]{1,0:T(8,128)(2,1)S(1)}, bf16[384,512]{1,0:T(8,128)(2,1)S(1)}, u32[]{:S(2)}, u32[]{:S(2)}) collective-permute-start(bf16[384,512]{1,0:T(8,128)(2,1)S(1)} %collective-permute-done.refs_0_), channel_id=1, source_target_pairs={{8,10},{9,11},{10,8},{11,9},{12,14},{13,15},{14,12},{15,13},{16,18... | collective-permute-start | bytes 1179656 | tf_op jit(solution)/shard_map/ppermute | solution.py:272
  39.2 3.4 %collective-permute-start.2 = (bf16[384,512]{1,0:T(8,128)(2,1)S(1)}, bf16[384,512]{1,0:T(8,128)(2,1)S(1)}, u32[]{:S(2)}, u32[]{:S(2)}) collective-permute-start(bf16[384,512]{1,0:T(8,128)(2,1)S(1)} %collective-permute-done.refs_0_), channel_id=1, source_target_pairs={{8,12},{9,13},{10,14},{11,15},{12,8},{13,9},{14,10},{15,11},{16,20... | collective-permute-start | bytes 1179656 | tf_op jit(solution)/shard_map/ppermute | solution.py:272
  42.7 1.9 %collective-permute-start.8 = (bf16[384,512]{1,0:T(8,128)(2,1)S(1)}, bf16[384,512]{1,0:T(8,128)(2,1)S(1)}, u32[]{:S(2)}, u32[]{:S(2)}) collective-permute-start(bf16[384,512]{1,0:T(8,128)(2,1)S(1)} %collective-permute-done.refs_0_), channel_id=1, source_target_pairs={{8,9},{9,8},{10,11},{11,10},{12,13},{13,12},{14,15},{15,14},{16,17... | collective-permute-start | bytes 1179656 | tf_op jit(solution)/shard_map/ppermute | solution.py:272
  44.6 0.0 collective-permute-done.6.w_ref
  44.6 2.4 %collective-permute-start.13 = (bf16[384,512]{1,0:T(8,128)(2,1)S(1)}, bf16[384,512]{1,0:T(8,128)(2,1)S(1)}, u32[]{:S(2)}, u32[]{:S(2)}) collective-permute-start(bf16[384,512]{1,0:T(8,128)(2,1)S(1)} %collective-permute-done.12.refs_6_), channel_id=1, source_target_pairs={{8,9},{9,8},{10,11},{11,10},{12,13},{13,12},{14,15},{15,14},{16,17... | collective-permute-start | bytes 1179656 | tf_op jit(solution)/shard_map/ppermute | solution.py:272
  47.1 3.1 %partial.2.near_ref = f32[392,128]{1,0:T(8,128)S(1)} custom-call(s32[1]{0:T(128)} %bitcast.6.place, bf16[384,8192]{1,0:T(8,128)(2,1)} %h_ref.11, bf16[2048,128]{1,0:T(8,128)(2,1)} %collective-permute-done.3.w_ref, f32[384,256]{1,0:T(8,128)S(1)} %near.1.before_ref, f32[8,128]{1,0:T(8,128)S(1)} %pad.7.owner_ref), custom_call_target="tpu_custom_call" | custom-call | tf_op jit(solution)/shard_map/partial/pallas_call | solution.py:236
  50.2 0.0 copy-start
  50.2 0.7 copy-done
  50.9 0.0 collective-permute-done.9.refs_2_
  50.9 2.3 %collective-permute-start.16 = (bf16[2048,128]{1,0:T(8,128)(2,1)}, bf16[2048,128]{1,0:T(8,128)(2,1)}, u32[]{:S(2)}, u32[]{:S(2)}) collective-permute-start(bf16[2048,128]{1,0:T(8,128)(2,1)} %collective-permute-done.6.w_ref), channel_id=1, source_target_pairs={{8,16},{16,8},{9,17},{17,9},{10,18},{18,10},{11,19},{19,11},{12,20... | collective-permute-start | bytes 1572872 | tf_op jit(solution)/shard_map/ppermute | solution.py:268
  53.3 1.9 %collective-permute-start.10 = (bf16[384,512]{1,0:T(8,128)(2,1)S(1)}, bf16[384,512]{1,0:T(8,128)(2,1)S(1)}, u32[]{:S(2)}, u32[]{:S(2)}) collective-permute-start(bf16[384,512]{1,0:T(8,128)(2,1)S(1)} %collective-permute-done.9.refs_2_), channel_id=1, source_target_pairs={{8,9},{9,8},{10,11},{11,10},{12,13},{13,12},{14,15},{15,14},{16,17... | collective-permute-start | bytes 1179656 | tf_op jit(solution)/shard_map/ppermute | solution.py:272
  55.2 2.4 %collective-permute-start.11 = (bf16[384,512]{1,0:T(8,128)(2,1)S(1)}, bf16[384,512]{1,0:T(8,128)(2,1)S(1)}, u32[]{:S(2)}, u32[]{:S(2)}) collective-permute-start(bf16[384,512]{1,0:T(8,128)(2,1)S(1)} %collective-permute-done.2.refs_4_), channel_id=1, source_target_pairs={{8,9},{9,8},{10,11},{11,10},{12,13},{13,12},{14,15},{15,14},{16,17... | collective-permute-start | bytes 1179656 | tf_op jit(solution)/shard_map/ppermute | solution.py:272
  57.6 1.3 %collective-permute-start.7 = (f32[392,128]{1,0:T(8,128)}, f32[392,128]{1,0:T(8,128)S(1)}, u32[]{:S(2)}, u32[]{:S(2)}) collective-permute-start(f32[392,128]{1,0:T(8,128)} %copy-done), channel_id=1, source_target_pairs={{0,8},{24,16},{1,9},{25,17},{2,10},{26,18},{3,11},{27,19},{4,12},{... | collective-permute-start | bytes 602120 | tf_op jit(solution)/shard_map/ppermute | solution.py:268
  58.9 0.1 add_add_fusion.place
  59.0 3.1 %partial.3.near_ref = f32[384,128]{1,0:T(8,128)S(1)} custom-call(s32[1]{0:T(128)} %bitcast.6.place, bf16[384,8192]{1,0:T(8,128)(2,1)} %h_ref.11, bf16[2048,128]{1,0:T(8,128)(2,1)} %collective-permute-done.6.w_ref, f32[384,256]{1,0:T(8,128)S(1)} %near.1.before_ref, f32[8,128]{1,0:T(8,128)S(1)} %pad.7.owner_ref), custom_call_target="tpu_custom_call" | custom-call | tf_op jit(solution)/shard_map/partial/pallas_call | solution.py:236
  62.1 1.3 %collective-permute-start.17 = (f32[384,128]{1,0:T(8,128)S(1)}, f32[384,128]{1,0:T(8,128)S(1)}, u32[]{:S(2)}, u32[]{:S(2)}) collective-permute-start(f32[384,128]{1,0:T(8,128)S(1)} %partial.3.near_ref), channel_id=1, source_target_pairs={{0,8},{24,16},{1,9},{25,17},{2,10},{26,18},{3,11},{27,19},{4,12},{... | collective-permute-start | bytes 589832 | tf_op jit(solution)/shard_map/ppermute | solution.py:268
  63.4 0.1 add_add_fusion.1.place
  63.6 3.6 %facing.1.facing_ref = f32[768,256]{1,0:T(8,128)S(1)} custom-call(s32[4]{0:T(128)S(1)} %add_add_fusion.1.place, bf16[384,8192]{1,0:T(8,128)(2,1)} %h_ref.11, bf16[2048,128]{1,0:T(8,128)(2,1)} %copy-done.5, bf16[2048,128]{1,0:T(8,128)(2,1)} %copy-done.6, bf16[384,512]{1,0:T(8,128)(2,1)S(1)} %collective-permute-done.refs_0_, ...), custom_call_target="tpu_custom_call" | custom-call | tf_op jit(solution)/shard_map/facing/pallas_call | solution.py:236
  67.2 0.0 copy-start.4
  67.2 3.1 %distant.2.k_in = bf16[784,128]{1,0:T(8,128)(2,1)S(1)} custom-call(s32[4]{0:T(128)S(1)} %add_add_fusion.place, bf16[384,8192]{1,0:T(8,128)(2,1)} %h_ref.11, bf16[2048,128]{1,0:T(8,128)(2,1)} %collective-permute-done.5.w_ref, f32[392,128]{1,0:T(8,128)S(1)} %copy-done.1, f32[392,128]{1,0:T(8,128)S(1)} %collective-permute-done.7.outer_ref, ...), custom_call_target="tpu_custom_call" | custom-call | tf_op jit(solution)/shard_map/distant/pallas_call | solution.py:236
  70.3 1.3 %collective-permute-start.20 = (bf16[784,128]{1,0:T(8,128)(2,1)S(1)}, bf16[784,128]{1,0:T(8,128)(2,1)S(1)}, u32[]{:S(2)}, u32[]{:S(2)}) collective-permute-start(bf16[784,128]{1,0:T(8,128)(2,1)S(1)} %distant.2.k_in), channel_id=1, source_target_pairs={{8,0},{16,24},{9,1},{17,25},{10,2},{18,26},{11,3},{19,27},{12,4},{... | collective-permute-start | bytes 602120 | tf_op jit(solution)/shard_map/ppermute | solution.py:268
  71.6 3.5 %collective-permute-start.14 = (bf16[784,128]{1,0:T(8,128)(2,1)S(1)}, bf16[784,128]{1,0:T(8,128)(2,1)S(1)}, u32[]{:S(2)}, u32[]{:S(2)}) collective-permute-start(bf16[784,128]{1,0:T(8,128)(2,1)S(1)} %distant.2.k_in), channel_id=1, source_target_pairs={{8,16},{16,8},{9,17},{17,9},{10,18},{18,10},{11,19},{19,11},{12,20... | collective-permute-start | bytes 602120 | tf_op jit(solution)/shard_map/ppermute | solution.py:268
  75.1 0.0 copy-start.2
  75.2 3.1 %distant.3.v_in = bf16[768,128]{1,0:T(8,128)(2,1)S(1)} custom-call(s32[4]{0:T(128)S(1)} %add_add_fusion.place, bf16[384,8192]{1,0:T(8,128)(2,1)} %h_ref.11, bf16[2048,128]{1,0:T(8,128)(2,1)} %collective-permute-done.16.w_ref, f32[384,128]{1,0:T(8,128)S(1)} %partial.3.near_ref, f32[384,128]{1,0:T(8,128)S(1)} %collective-permute-done.17.outer_ref, ...), custom_call_target="tpu_custom_call" | custom-call | tf_op jit(solution)/shard_map/distant/pallas_call | solution.py:236
  78.3 2.4 %collective-permute-start.18 = (bf16[768,128]{1,0:T(8,128)(2,1)S(1)}, bf16[768,128]{1,0:T(8,128)(2,1)S(1)}, u32[]{:S(2)}, u32[]{:S(2)}) collective-permute-start(bf16[768,128]{1,0:T(8,128)(2,1)S(1)} %distant.3.v_in), channel_id=1, source_target_pairs={{8,16},{16,8},{9,17},{17,9},{10,18},{18,10},{11,19},{19,11},{12,20... | collective-permute-start | bytes 589832 | tf_op jit(solution)/shard_map/ppermute | solution.py:268
  80.7 1.3 %collective-permute-start.21 = (bf16[768,128]{1,0:T(8,128)(2,1)S(1)}, bf16[768,128]{1,0:T(8,128)(2,1)S(1)}, u32[]{:S(2)}, u32[]{:S(2)}) collective-permute-start(bf16[768,128]{1,0:T(8,128)(2,1)S(1)} %distant.3.v_in), channel_id=1, source_target_pairs={{8,0},{16,24},{9,1},{17,25},{10,2},{18,26},{11,3},{19,27},{12,4},{... | collective-permute-start | bytes 589832 | tf_op jit(solution)/shard_map/ppermute | solution.py:268
  82.0 1.3 %collective-permute-start.15 = (bf16[784,128]{1,0:T(8,128)(2,1)S(1)}, bf16[784,128]{1,0:T(8,128)(2,1)S(1)}, u32[]{:S(2)}, u32[]{:S(2)}) collective-permute-start(bf16[784,128]{1,0:T(8,128)(2,1)S(1)} %collective-permute-done.14.k_across), channel_id=1, source_target_pairs={{8,0},{16,24},{9,1},{17,25},{10,2},{18,26},{11,3},{19,27},{12,4},{... | collective-permute-start | bytes 602120 | tf_op jit(solution)/shard_map/ppermute | solution.py:268
  83.3 3.4 %collective-permute-done.18.v_across = bf16[768,128]{1,0:T(8,128)(2,1)S(1)} collective-permute-done((bf16[768,128]{1,0:T(8,128)(2,1)S(1)}, bf16[768,128]{1,0:T(8,128)(2,1)S(1)}, u32[]{:S(2)}, u32[]{:S(2)}) %collective-permute-start.18) | collective-permute-done | bytes 196640 | tf_op jit(solution)/shard_map/ppermute | solution.py:268
  86.8 1.5 %collective-permute-start.19 = (bf16[768,128]{1,0:T(8,128)(2,1)S(1)}, bf16[768,128]{1,0:T(8,128)(2,1)S(1)}, u32[]{:S(2)}, u32[]{:S(2)}) collective-permute-start(bf16[768,128]{1,0:T(8,128)(2,1)S(1)} %collective-permute-done.18.v_across), channel_id=1, source_target_pairs={{8,0},{16,24},{9,1},{17,25},{10,2},{18,26},{11,3},{19,27},{12,4},{... | collective-permute-start | bytes 589832 | tf_op jit(solution)/shard_map/ppermute | solution.py:268
  88.2 5.1 %attend_own.1 = (f32[8,384,1]{2,1,0:T(8,128)S(1)}, f32[8,384,1]{2,1,0:T(8,128)S(1)}, f32[8,384,128]{2,1,0:T(8,128)S(1)}, bf16[2,192,256]{2,1,0:T(8,128)(2,1)S(1)}) custom-call(s32[1]{0:T(128)} %bitcast.place.info, bf16[384,1024]{1,0:T(8,128)(2,1)} %q_ref.3, s32[12,128]{1,0:T(8,128)S(1)} %bitcast.13, bf16[784,128]{1,0:T(8,128)(2,1)S(1)} %distant.2.k_in, ...), custom_call_target="tpu_custom_call" | custom-call | flops 1207959552 | bytes 18874368 | tf_op jit(solution)/shard_map/attend_own/pallas_call | solution.py:569
  93.3 1.2 %collective-permute-done.19.v_far = bf16[768,128]{1,0:T(8,128)(2,1)S(1)} collective-permute-done((bf16[768,128]{1,0:T(8,128)(2,1)S(1)}, bf16[768,128]{1,0:T(8,128)(2,1)S(1)}, u32[]{:S(2)}, u32[]{:S(2)}) %collective-permute-start.19) | collective-permute-done | bytes 196640 | tf_op jit(solution)/shard_map/ppermute | solution.py:268
  94.5 6.8 %attend_far.1 = (bf16[384,1024]{1,0:T(8,128)(2,1)}, bf16[4,192,256]{2,1,0:T(8,128)(2,1)}) custom-call(s32[1]{0:T(128)} %bitcast.place.info, bf16[384,1024]{1,0:T(8,128)(2,1)} %q_ref.3, s32[12,128]{1,0:T(8,128)S(1)} %bitcast.14, bf16[784,128]{1,0:T(8,128)(2,1)S(1)} %collective-permute-done.14.k_across, bf16[784,128]{1,0:T(8,128)(2,1)S(1)} %collective-permute-done.15.k_far, ...), custom_call_target="tpu_custom_call" | custom-call | flops 1207959552 | bytes 18874368 | tf_op jit(solution)/shard_map/attend_far/pallas_call | solution.py:584
  (30 shorter events, 0.1 us)
Async XLA Ops:
  0.6 15.9 %collective-permute-start.1 = (bf16[2048,128]{1,0:T(8,128)(2,1)}, bf16[2048,128]{1,0:T(8,128)(2,1)S(1)}, u32[]{:S(2)}, u32[]{:S(2)}) collective-permute-start(bf16[2048,128]{1,0:T(8,128)(2,1)} %kw_ref.1), channel_id=1, source_target_pairs={{8,16},{16,8},{9,17},{17,9},{10,18},{18,10},{11,19},{19,11},{12,20... | collective-permute-start | bytes 1572872 | tf_op jit(solution)/shard_map/ppermute | solution.py:268
  4.0 12.5 %collective-permute-start = (bf16[384,512]{1,0:T(8,128)(2,1)S(1)}, bf16[384,512]{1,0:T(8,128)(2,1)S(1)}, u32[]{:S(2)}, u32[]{:S(2)}) collective-permute-start(bf16[384,512]{1,0:T(8,128)(2,1)S(1)} %constant_dynamic-slice_fusion), channel_id=1, source_target_pairs={{0,8},{24,16},{1,9},{25,17},{2,10},{26,18},{3,11},{27,19},{4,12},{... | collective-permute-start | bytes 1179656 | tf_op jit(solution)/shard_map/ppermute | solution.py:268
  5.3 11.2 %copy-start.7 = (bf16[2048,128]{1,0:T(8,128)(2,1)S(1)}, bf16[2048,128]{1,0:T(8,128)(2,1)}, u32[]{:S(2)}) copy-start(bf16[2048,128]{1,0:T(8,128)(2,1)} %kw_ref.1) | copy-start | bytes 1572868
  5.4 11.2 %copy-start.8 = (bf16[2048,128]{1,0:T(8,128)(2,1)S(1)}, bf16[2048,128]{1,0:T(8,128)(2,1)}, u32[]{:S(2)}) copy-start(bf16[2048,128]{1,0:T(8,128)(2,1)} %vw_ref.1) | copy-start | bytes 1572868
  5.4 41.7 %copy-start.9 = (s32[24,1]{0,1:T(1,128)S(1)}, s32[24,1]{0,1:T(1,128)}, u32[]{:S(2)}) copy-start(s32[24,1]{0,1:T(1,128)} %param.15) | copy-start | bytes 292
  16.5 3.6 %copy-start.5 = (bf16[2048,128]{1,0:T(8,128)(2,1)}, bf16[2048,128]{1,0:T(8,128)(2,1)S(1)}, u32[]{:S(2)}) copy-start(bf16[2048,128]{1,0:T(8,128)(2,1)S(1)} %collective-permute-done.1.kw_ref) | copy-start | bytes 1572868
  16.5 15.0 %collective-permute-start.3 = (bf16[2048,128]{1,0:T(8,128)(2,1)S(1)}, bf16[2048,128]{1,0:T(8,128)(2,1)}, u32[]{:S(2)}, u32[]{:S(2)}) collective-permute-start(bf16[2048,128]{1,0:T(8,128)(2,1)S(1)} %copy-done.7), channel_id=1, source_target_pairs={{0,8},{8,0},{16,24},{24,16},{1,9},{9,1},{17,25},{25,17},{2,10},{10... | collective-permute-start | bytes 1572872 | tf_op jit(solution)/shard_map/ppermute | solution.py:268
  16.6 14.9 %collective-permute-start.4 = (bf16[2048,128]{1,0:T(8,128)(2,1)S(1)}, bf16[2048,128]{1,0:T(8,128)(2,1)S(1)}, u32[]{:S(2)}, u32[]{:S(2)}) collective-permute-start(bf16[2048,128]{1,0:T(8,128)(2,1)S(1)} %copy-done.8), channel_id=1, source_target_pairs={{8,16},{16,8},{9,17},{17,9},{10,18},{18,10},{11,19},{19,11},{12,20... | collective-permute-start | bytes 1572872 | tf_op jit(solution)/shard_map/ppermute | solution.py:268
  20.1 24.5 %collective-permute-start.6 = (bf16[2048,128]{1,0:T(8,128)(2,1)S(1)}, bf16[2048,128]{1,0:T(8,128)(2,1)}, u32[]{:S(2)}, u32[]{:S(2)}) collective-permute-start(bf16[2048,128]{1,0:T(8,128)(2,1)S(1)} %copy-done.8), channel_id=1, source_target_pairs={{0,8},{8,0},{16,24},{24,16},{1,9},{9,1},{17,25},{25,17},{2,10},{10... | collective-permute-start | bytes 1572872 | tf_op jit(solution)/shard_map/ppermute | solution.py:268
  20.2 22.5 %collective-permute-start.12 = (bf16[384,512]{1,0:T(8,128)(2,1)S(1)}, bf16[384,512]{1,0:T(8,128)(2,1)S(1)}, u32[]{:S(2)}, u32[]{:S(2)}) collective-permute-start(bf16[384,512]{1,0:T(8,128)(2,1)S(1)} %collective-permute-done.refs_0_), channel_id=1, source_target_pairs={{8,14},{9,15},{10,12},{11,13},{12,10},{13,11},{14,8},{15,9},{16,22... | collective-permute-start | bytes 1179656 | tf_op jit(solution)/shard_map/ppermute | solution.py:272
  31.6 0.8 copy-start.6
  32.4 22.8 %collective-permute-start.5 = (bf16[2048,128]{1,0:T(8,128)(2,1)}, bf16[2048,128]{1,0:T(8,128)(2,1)}, u32[]{:S(2)}, u32[]{:S(2)}) collective-permute-start(bf16[2048,128]{1,0:T(8,128)(2,1)} %collective-permute-done.3.w_ref), channel_id=1, source_target_pairs={{8,16},{16,8},{9,17},{17,9},{10,18},{18,10},{11,19},{19,11},{12,20... | collective-permute-start | bytes 1572872 | tf_op jit(solution)/shard_map/ppermute | solution.py:268
  35.8 15.1 %collective-permute-start.9 = (bf16[384,512]{1,0:T(8,128)(2,1)S(1)}, bf16[384,512]{1,0:T(8,128)(2,1)S(1)}, u32[]{:S(2)}, u32[]{:S(2)}) collective-permute-start(bf16[384,512]{1,0:T(8,128)(2,1)S(1)} %collective-permute-done.refs_0_), channel_id=1, source_target_pairs={{8,10},{9,11},{10,8},{11,9},{12,14},{13,15},{14,12},{15,13},{16,18... | collective-permute-start | bytes 1179656 | tf_op jit(solution)/shard_map/ppermute | solution.py:272
  39.2 14.0 %collective-permute-start.2 = (bf16[384,512]{1,0:T(8,128)(2,1)S(1)}, bf16[384,512]{1,0:T(8,128)(2,1)S(1)}, u32[]{:S(2)}, u32[]{:S(2)}) collective-permute-start(bf16[384,512]{1,0:T(8,128)(2,1)S(1)} %collective-permute-done.refs_0_), channel_id=1, source_target_pairs={{8,12},{9,13},{10,14},{11,15},{12,8},{13,9},{14,10},{15,11},{16,20... | collective-permute-start | bytes 1179656 | tf_op jit(solution)/shard_map/ppermute | solution.py:272
  42.7 14.9 %collective-permute-start.8 = (bf16[384,512]{1,0:T(8,128)(2,1)S(1)}, bf16[384,512]{1,0:T(8,128)(2,1)S(1)}, u32[]{:S(2)}, u32[]{:S(2)}) collective-permute-start(bf16[384,512]{1,0:T(8,128)(2,1)S(1)} %collective-permute-done.refs_0_), channel_id=1, source_target_pairs={{8,9},{9,8},{10,11},{11,10},{12,13},{13,12},{14,15},{15,14},{16,17... | collective-permute-start | bytes 1179656 | tf_op jit(solution)/shard_map/ppermute | solution.py:272
  44.6 17.5 %collective-permute-start.13 = (bf16[384,512]{1,0:T(8,128)(2,1)S(1)}, bf16[384,512]{1,0:T(8,128)(2,1)S(1)}, u32[]{:S(2)}, u32[]{:S(2)}) collective-permute-start(bf16[384,512]{1,0:T(8,128)(2,1)S(1)} %collective-permute-done.12.refs_6_), channel_id=1, source_target_pairs={{8,9},{9,8},{10,11},{11,10},{12,13},{13,12},{14,15},{15,14},{16,17... | collective-permute-start | bytes 1179656 | tf_op jit(solution)/shard_map/ppermute | solution.py:272
  50.2 0.7 copy-start
  50.9 24.2 %collective-permute-start.16 = (bf16[2048,128]{1,0:T(8,128)(2,1)}, bf16[2048,128]{1,0:T(8,128)(2,1)}, u32[]{:S(2)}, u32[]{:S(2)}) collective-permute-start(bf16[2048,128]{1,0:T(8,128)(2,1)} %collective-permute-done.6.w_ref), channel_id=1, source_target_pairs={{8,16},{16,8},{9,17},{17,9},{10,18},{18,10},{11,19},{19,11},{12,20... | collective-permute-start | bytes 1572872 | tf_op jit(solution)/shard_map/ppermute | solution.py:268
  53.3 10.3 %collective-permute-start.10 = (bf16[384,512]{1,0:T(8,128)(2,1)S(1)}, bf16[384,512]{1,0:T(8,128)(2,1)S(1)}, u32[]{:S(2)}, u32[]{:S(2)}) collective-permute-start(bf16[384,512]{1,0:T(8,128)(2,1)S(1)} %collective-permute-done.9.refs_2_), channel_id=1, source_target_pairs={{8,9},{9,8},{10,11},{11,10},{12,13},{13,12},{14,15},{15,14},{16,17... | collective-permute-start | bytes 1179656 | tf_op jit(solution)/shard_map/ppermute | solution.py:272
  55.2 8.3 %collective-permute-start.11 = (bf16[384,512]{1,0:T(8,128)(2,1)S(1)}, bf16[384,512]{1,0:T(8,128)(2,1)S(1)}, u32[]{:S(2)}, u32[]{:S(2)}) collective-permute-start(bf16[384,512]{1,0:T(8,128)(2,1)S(1)} %collective-permute-done.2.refs_4_), channel_id=1, source_target_pairs={{8,9},{9,8},{10,11},{11,10},{12,13},{13,12},{14,15},{15,14},{16,17... | collective-permute-start | bytes 1179656 | tf_op jit(solution)/shard_map/ppermute | solution.py:272
  57.6 9.5 %collective-permute-start.7 = (f32[392,128]{1,0:T(8,128)}, f32[392,128]{1,0:T(8,128)S(1)}, u32[]{:S(2)}, u32[]{:S(2)}) collective-permute-start(f32[392,128]{1,0:T(8,128)} %copy-done), channel_id=1, source_target_pairs={{0,8},{24,16},{1,9},{25,17},{2,10},{26,18},{3,11},{27,19},{4,12},{... | collective-permute-start | bytes 602120 | tf_op jit(solution)/shard_map/ppermute | solution.py:268
  62.1 13.0 %collective-permute-start.17 = (f32[384,128]{1,0:T(8,128)S(1)}, f32[384,128]{1,0:T(8,128)S(1)}, u32[]{:S(2)}, u32[]{:S(2)}) collective-permute-start(f32[384,128]{1,0:T(8,128)S(1)} %partial.3.near_ref), channel_id=1, source_target_pairs={{0,8},{24,16},{1,9},{25,17},{2,10},{26,18},{3,11},{27,19},{4,12},{... | collective-permute-start | bytes 589832 | tf_op jit(solution)/shard_map/ppermute | solution.py:268
  63.5 3.6 %copy-start.1 = (f32[392,128]{1,0:T(8,128)S(1)}, f32[392,128]{1,0:T(8,128)}, u32[]{:S(2)}) copy-start(f32[392,128]{1,0:T(8,128)} %copy-done) | copy-start | bytes 602116
  63.5 3.6 %copy-start.3 = (bf16[128]{0:T(256)(128)(2,1)S(1)}, bf16[128]{0:T(256)(128)(2,1)}, u32[]{:S(2)}) copy-start(bf16[128]{0:T(256)(128)(2,1)} %param.12) | copy-start | bytes 772
  67.2 8.0 %copy-start.4 = (bf16[128]{0:T(256)(128)(2,1)S(1)}, bf16[128]{0:T(256)(128)(2,1)}, u32[]{:S(2)}) copy-start(bf16[128]{0:T(256)(128)(2,1)} %param.13) | copy-start | bytes 772
  70.3 10.4 %collective-permute-start.20 = (bf16[784,128]{1,0:T(8,128)(2,1)S(1)}, bf16[784,128]{1,0:T(8,128)(2,1)S(1)}, u32[]{:S(2)}, u32[]{:S(2)}) collective-permute-start(bf16[784,128]{1,0:T(8,128)(2,1)S(1)} %distant.2.k_in), channel_id=1, source_target_pairs={{8,0},{16,24},{9,1},{17,25},{10,2},{18,26},{11,3},{19,27},{12,4},{... | collective-permute-start | bytes 602120 | tf_op jit(solution)/shard_map/ppermute | solution.py:268
  71.6 10.4 %collective-permute-start.14 = (bf16[784,128]{1,0:T(8,128)(2,1)S(1)}, bf16[784,128]{1,0:T(8,128)(2,1)S(1)}, u32[]{:S(2)}, u32[]{:S(2)}) collective-permute-start(bf16[784,128]{1,0:T(8,128)(2,1)S(1)} %distant.2.k_in), channel_id=1, source_target_pairs={{8,16},{16,8},{9,17},{17,9},{10,18},{18,10},{11,19},{19,11},{12,20... | collective-permute-start | bytes 602120 | tf_op jit(solution)/shard_map/ppermute | solution.py:268
  75.1 13.1 %copy-start.2 = (s32[1536]{0:T(1024)S(1)}, s32[1536]{0:T(1024)}, u32[]{:S(2)}) copy-start(s32[1536]{0:T(1024)} %param.14) | copy-start | bytes 18436
  78.3 8.5 %collective-permute-start.18 = (bf16[768,128]{1,0:T(8,128)(2,1)S(1)}, bf16[768,128]{1,0:T(8,128)(2,1)S(1)}, u32[]{:S(2)}, u32[]{:S(2)}) collective-permute-start(bf16[768,128]{1,0:T(8,128)(2,1)S(1)} %distant.3.v_in), channel_id=1, source_target_pairs={{8,16},{16,8},{9,17},{17,9},{10,18},{18,10},{11,19},{19,11},{12,20... | collective-permute-start | bytes 589832 | tf_op jit(solution)/shard_map/ppermute | solution.py:268
  80.7 7.5 %collective-permute-start.21 = (bf16[768,128]{1,0:T(8,128)(2,1)S(1)}, bf16[768,128]{1,0:T(8,128)(2,1)S(1)}, u32[]{:S(2)}, u32[]{:S(2)}) collective-permute-start(bf16[768,128]{1,0:T(8,128)(2,1)S(1)} %distant.3.v_in), channel_id=1, source_target_pairs={{8,0},{16,24},{9,1},{17,25},{10,2},{18,26},{11,3},{19,27},{12,4},{... | collective-permute-start | bytes 589832 | tf_op jit(solution)/shard_map/ppermute | solution.py:268
  82.0 12.5 %collective-permute-start.15 = (bf16[784,128]{1,0:T(8,128)(2,1)S(1)}, bf16[784,128]{1,0:T(8,128)(2,1)S(1)}, u32[]{:S(2)}, u32[]{:S(2)}) collective-permute-start(bf16[784,128]{1,0:T(8,128)(2,1)S(1)} %collective-permute-done.14.k_across), channel_id=1, source_target_pairs={{8,0},{16,24},{9,1},{17,25},{10,2},{18,26},{11,3},{19,27},{12,4},{... | collective-permute-start | bytes 602120 | tf_op jit(solution)/shard_map/ppermute | solution.py:268
  86.8 7.8 %collective-permute-start.19 = (bf16[768,128]{1,0:T(8,128)(2,1)S(1)}, bf16[768,128]{1,0:T(8,128)(2,1)S(1)}, u32[]{:S(2)}, u32[]{:S(2)}) collective-permute-start(bf16[768,128]{1,0:T(8,128)(2,1)S(1)} %collective-permute-done.18.v_across), channel_id=1, source_target_pairs={{8,0},{16,24},{9,1},{17,25},{10,2},{18,26},{11,3},{19,27},{12,4},{... | collective-permute-start | bytes 589832 | tf_op jit(solution)/shard_map/ppermute | solution.py:268

commit v9 on v7

--- a/solution.py
+++ b/solution.py
@@ -163,40 +163,51 @@
 
 def facing_kernel(place, h_ref, kw_ref, vw_ref, *refs):
     pieces = refs[:PIECES]
-    out_ref, h_buf, w_buf, sem = refs[PIECES:]
-    copy = chunk_copy(h_ref, place[0], h_buf, sem)
-    copy.start()
+    out_ref, h_buf, w_buf, sems = refs[PIECES:]
     span = h_buf.shape[0]
-    w_buf[:, :HD] = kw_ref[...]
-    w_buf[:, HD:] = vw_ref[...]
-    out_ref[span:] = jnp.zeros((span, 2 * HD), jnp.float32)
-    add_pieces(place[2], place[0], pieces, w_buf, out_ref.at[pl.ds(span, span)])
-    copy.wait()
-    out_ref[:span] = jnp.dot(h_buf[...], w_buf[...], preferred_element_type=jnp.float32)
+
+    @pl.when(place[3] == 1)
+    def _():
+        copies = [
+            pltpu.make_async_copy(kw_ref, w_buf.at[:, pl.ds(0, HD)], sems.at[0]),
+            pltpu.make_async_copy(vw_ref, w_buf.at[:, pl.ds(HD, HD)], sems.at[1]),
+            chunk_copy(h_ref, place[0], h_buf, sems.at[2]),
+        ]
+        for copy in copies:
+            copy.start()
+        for copy in copies[:2]:
+            copy.wait()
+        out_ref[span:] = jnp.zeros((span, 2 * HD), jnp.float32)
+        add_pieces(place[2], place[0], pieces, w_buf, out_ref.at[pl.ds(span, span)])
+        copies[2].wait()
+        out_ref[:span] = jnp.dot(h_buf[...], w_buf[...], preferred_element_type=jnp.float32)
 
 
 def distant_kernel(column, place, h_ref, w_ref, near_ref, outer_ref, facing_ref, bias_ref, *refs):
     pieces = refs[:PIECES]
     out_ref, h_buf, acc, sem = refs[PIECES:]
-    copy = chunk_copy(h_ref, place[0], h_buf, sem)
-    copy.start()
     span = h_buf.shape[0]
     part = slice(column * HD, column * HD + HD)
-    own_at = pl.multiple_of(place[1] * span, span)
-    outer_at = pl.multiple_of((1 - place[1]) * span, span)
-    bias = bias_ref[...].astype(jnp.float32)
-    acc[...] = outer_ref[:span] + facing_ref[span:, part] + bias
-    add_pieces(place[2], place[0], pieces, w_ref, acc)
-    out_ref[pl.ds(outer_at, span), :] = acc[...].astype(jnp.bfloat16)
-    own = near_ref[:span] + facing_ref[:span, part] + bias
-    copy.wait()
-    own += jnp.dot(h_buf[...], w_ref[...], preferred_element_type=jnp.float32)
-    out_ref[pl.ds(own_at, span), :] = own.astype(jnp.bfloat16)
-    if column == 0:
-        mine, theirs = near_ref[span:], outer_ref[span:]
-        lower = jnp.where(place[1] == 0, mine, theirs)
-        upper = jnp.where(place[1] == 0, theirs, mine)
-        out_ref[2 * span :] = jnp.concatenate([lower, upper], axis=0).astype(jnp.bfloat16)
+
+    @pl.when(place[3] == 1)
+    def _():
+        copy = chunk_copy(h_ref, place[0], h_buf, sem)
+        copy.start()
+        own_at = pl.multiple_of(place[1] * span, span)
+        outer_at = pl.multiple_of((1 - place[1]) * span, span)
+        bias = bias_ref[...].astype(jnp.float32)
+        acc[...] = outer_ref[:span] + facing_ref[span:, part] + bias
+        add_pieces(place[2], place[0], pieces, w_ref, acc)
+        out_ref[pl.ds(outer_at, span), :] = acc[...].astype(jnp.bfloat16)
+        own = near_ref[:span] + facing_ref[:span, part] + bias
+        copy.wait()
+        own += jnp.dot(h_buf[...], w_ref[...], preferred_element_type=jnp.float32)
+        out_ref[pl.ds(own_at, span), :] = own.astype(jnp.bfloat16)
+        if column == 0:
+            mine, theirs = near_ref[span:], outer_ref[span:]
+            lower = jnp.where(place[1] == 0, mine, theirs)
+            upper = jnp.where(place[1] == 0, theirs, mine)
+            out_ref[2 * span :] = jnp.concatenate([lower, upper], axis=0).astype(jnp.bfloat16)
 
 
 EXTRA = 8
@@ -238,6 +249,7 @@
     near = jnp.bitwise_xor(index, 1)
     distant = jnp.bitwise_xor(facing, 1)
     second = (index < 2).astype(jnp.int32)
+    inner = ((index == 1) | (index == 2)).astype(jnp.int32)
 
     def send(x, pairs):
         return lax.ppermute(x, "pre", pairs)
@@ -274,13 +286,6 @@
     key_swapped, value_facing = tie((key_swapped, value_facing))
     key_distant = send(key_swapped, ACROSS)
     value_distant = send(value_swapped, ACROSS)
-    chips[2], key_distant = tie((chips[2], key_distant))
-    mates = [trade(x, 1) for x in chips]
-    pieces = [x for both_cores in zip(chips, mates) for x in both_cores]
-
-    def place(chunk):
-        return jnp.stack([chunk, second, member])
-
     owners = jnp.broadcast_to(page_owner.T.astype(jnp.float32), (EXTRA, page_owner.shape[0]))
     owners = jnp.pad(owners, ((0, 0), (0, HD - page_owner.shape[0])))
 
@@ -297,6 +302,14 @@
         )
         return part, send(part, INWARD)
 
+    key_part, key_outer = begin(0, key_swapped)
+    chips[2], key_distant, key_outer = tie((chips[2], key_distant, key_outer))
+    mates = [trade(x, 1) for x in chips]
+    pieces = [x for both_cores in zip(chips, mates) for x in both_cores]
+
+    def place(chunk):
+        return jnp.stack([chunk, second, member, inner])
+
     def finish(column, weight, parts, bias):
         return call_project(
             functools.partial(distant_kernel, column),
@@ -309,7 +322,6 @@
             [block, pltpu.VMEM((span, HD), jnp.float32)],
         )
 
-    key_parts = begin(0, key_swapped)
     value_parts = begin(1, value_swapped)
     faced = call_project(
         facing_kernel,
@@ -320,8 +332,10 @@
         2 * HD,
         jnp.float32,
         [block, both],
-    )
-    keys = finish(0, key_distant, key_parts, key_bias)
+        held=3,
+        copies=(3,),
+    )
+    keys = finish(0, key_distant, (key_part, key_outer), key_bias)
     keys_out, keys_across = send(keys, OUTWARD), send(keys, ACROSS)
     values = finish(1, value_distant, value_parts, value_bias)
     values_across = send(values, ACROSS)
@@ -472,6 +486,8 @@
     named,
     laid,
     sems,
+    out_buf,
+    far_cache,
 ):
     copy = pltpu.make_async_copy(q_ref, q_buf, sems.at[0])
     copy.start()
@@ -480,14 +496,27 @@
     inner = (index == 1) | (index == 2)
     held_k[...] = jnp.where(inner, k_across[...], k_far[...])
     held_v[...] = jnp.where(inner, v_across[...], v_far[...])
-    cache_ref[pl.ds(index // 2 * 2, 2)] = own_cache[...]
     owners = read_owners(held_k, span, listed, named, sems.at[1])
+    own_at, far_at = index // 2 * 2, (1 - index // 2) * 2
+    leaving = [pltpu.make_async_copy(own_cache, cache_ref.at[pl.ds(own_at, 2)], sems.at[2])]
+    leaving[0].start()
     copy.wait()
+
+    def leave(g):
+        columns = pl.ds(g * HD, HD)
+        return pltpu.make_async_copy(out_buf.at[:, columns], out_ref.at[:, columns], sems.at[4 + g])
+
+    def place_far():
+        owners.wait()
+        place_pages(index, span, named, held_k, held_v, far_cache, laid)
+        return pltpu.make_async_copy(far_cache, cache_ref.at[pl.ds(far_at, 2)], sems.at[3])
 
     @pl.when(index < 2)
     def _():
         for g in range(heads):
-            out_ref[:, g * HD : (g + 1) * HD] = (mix[g] / total[g]).astype(out_ref.dtype)
+            out_buf[:, g * HD : (g + 1) * HD] = (mix[g] / total[g]).astype(out_buf.dtype)
+            leave(g).start()
+        place_far().start()
 
     @pl.when(index >= 2)
     def _():
@@ -497,13 +526,17 @@
         allowed = columns >= prompt_starts(seg_ref, index * span, span)
 
         def store(g, peak, sums, mixed):
-            out_ref[:, g * HD : (g + 1) * HD] = (mixed / sums).astype(out_ref.dtype)
+            out_buf[:, g * HD : (g + 1) * HD] = (mixed / sums).astype(out_buf.dtype)
+            leave(g).start()
+            if g == heads // 2:
+                place_far().start()
 
         attend(q_buf, heads, keys, values, allowed, lambda g: (top[g], total[g], mix[g]), store)
 
-    owners.wait()
-    far_cache = cache_ref.at[pl.ds((1 - index // 2) * 2, 2)]
-    place_pages(index, span, named, held_k, held_v, far_cache, laid)
+    for g in range(heads):
+        leave(g).wait()
+    leaving[0].wait()
+    pltpu.make_async_copy(far_cache, cache_ref.at[pl.ds(far_at, 2)], sems.at[3]).wait()
 
 
 def attention_of_pairs(queries, segment_ids, keys, values, capacity):
@@ -521,7 +554,7 @@
         pltpu.VMEM((2 * EXTRA, HD), jnp.int32),
         pltpu.SMEM((2 * EXTRA, HD), jnp.int32),
         pltpu.VMEM((2, (capacity + 1) * PAGE, 2 * HD), jnp.bfloat16),
-        pltpu.SemaphoreType.DMA((2,)),
+        pltpu.SemaphoreType.DMA((4 + heads,)),
     ]
     state = pl.pallas_call(
         functools.partial(own_kernel, heads),
@@ -541,12 +574,16 @@
     return pl.pallas_call(
         functools.partial(far_kernel, heads),
         in_specs=[SCALAR, HELD] + [FAST] * 9,
-        out_specs=[FAST] * 2,
+        out_specs=[HELD] * 2,
         out_shape=[
             jax.ShapeDtypeStruct(queries.shape, jnp.bfloat16),
             jax.ShapeDtypeStruct((4, capacity * PAGE, 2 * HD), jnp.bfloat16),
         ],
-        scratch_shapes=scratch,
+        scratch_shapes=scratch
+        + [
+            pltpu.VMEM(queries.shape, jnp.bfloat16),
+            pltpu.VMEM((2, capacity * PAGE, 2 * HD), jnp.bfloat16),
+        ],
         compiler_params=params,
         cost_estimate=cost,
         name="attend_far",

time: 98.4 us -> 94.3 us (0.958)
  waiting for transfers between devices: 29.4 us -> 25 us
  starting transfers between devices: 35.5 us -> 33.2 us
  local copies, waits for them, and re-layouts: 1.86 us -> 3.92 us
    ppermute x7, waiting for transfers between devices: 6.39 us -> 0.51 us  [trade(): lax.ppermute(x, ('dec', 'tp'), [(m, m ^ apart) for m in range(PIECES)])]
    ppermute x15, starting transfers between devices: 29.6 us -> 26.9 us  [send(): return lax.ppermute(x, 'pre', pairs)]
    unnamed x14 -> x22, local copies, waits for them, and re-layouts: 0.82 us -> 2.89 us
    ppermute x15, waiting for transfers between devices: 23 us -> 24.5 us  [send(): return lax.ppermute(x, 'pre', pairs)]
  transfers between devices with their start and end apart: 22 -> 22, of which waited for: 7 -> 8; matrix products, arithmetic and copies ran while one was open for 1% -> 1% of each run, Pallas kernels for 22% -> 24%
where the time goes in v9:
time: 94.3 us; the launch traced here: 92.7 us
  starting transfers between devices  33.2 us (35%)
  Pallas kernels  29.2 us (31%)
  waiting for transfers between devices  25 us (27%)
  local copies, waits for them, and re-layouts  3.92 us (4%)
  between operations  1.15 us (1%)
    ppermute x15, starting transfers between devices, send(): return lax.ppermute(x, 'pre', pairs)  26.9 us
    ppermute x15, waiting for transfers between devices, send(): return lax.ppermute(x, 'pre', pairs)  24.5 us
    pallas_call x6, Pallas kernels, call_project(): pl.pallas_call(kernel, in_specs=[SCALAR] + [HELD] * held + [FAST] * (len(...  17.5 us
    pallas_call x1, Pallas kernels, attention_of_pairs(): pl.pallas_call(functools.partial(far_kernel, heads), in_specs=[SCALAR, HE...  6.62 us
    ppermute x7, starting transfers between devices, trade(): lax.ppermute(x, ('dec', 'tp'), [(m, m ^ apart) for m in range(PIECES)])  6.39 us
    pallas_call x1, Pallas kernels, attention_of_pairs(): pl.pallas_call(functools.partial(own_kernel, heads), in_specs=[SCALAR, HE...  5.06 us
    unnamed x22, local copies, waits for them, and re-layouts  2.89 us
  transfers between devices with their start and end apart: 22, of which 8 were waited for; matrix products, arithmetic and copies ran while one was open for 1% of the time, Pallas kernels for 24%

profile of v9, /device:TPU:16, one launch (start us, length us, event | category | flops | bytes accessed | tf_op | source)
XLA Modules:
  0.0 92.7 jit_solution(10820109867793151446)
XLA Ops:
  0.6 2.4 %collective-permute-start.1 = (bf16[2048,128]{1,0:T(8,128)(2,1)}, bf16[2048,128]{1,0:T(8,128)(2,1)S(1)}, u32[]{:S(2)}, u32[]{:S(2)}) collective-permute-start(bf16[2048,128]{1,0:T(8,128)(2,1)} %kw_ref.1), channel_id=1, source_target_pairs={{8,16},{16,8},{9,17},{17,9},{10,18},{18,10},{11,19},{19,11},{12,20... | collective-permute-start | bytes 1572872 | tf_op jit(solution)/shard_map/ppermute | solution.py:255
  3.0 1.0 %constant_dynamic-slice_fusion = bf16[384,512]{1,0:T(8,128)(2,1)S(1)} fusion(bf16[384,8192]{1,0:T(8,128)(2,1)} %h_ref.11, s32[]{:T(128)S(6)} %select_n.3), kind=kLoop, calls=%fused_computation.3 | loop fusion | bytes 786436 | tf_op jit(solution)/shard_map/dynamic_slice | solution.py:261
  4.0 1.3 %collective-permute-start = (bf16[384,512]{1,0:T(8,128)(2,1)S(1)}, bf16[384,512]{1,0:T(8,128)(2,1)S(1)}, u32[]{:S(2)}, u32[]{:S(2)}) collective-permute-start(bf16[384,512]{1,0:T(8,128)(2,1)S(1)} %constant_dynamic-slice_fusion), channel_id=1, source_target_pairs={{0,8},{24,16},{1,9},{25,17},{2,10},{26,18},{3,11},{27,19},{4,12},{... | collective-permute-start | bytes 1179656 | tf_op jit(solution)/shard_map/ppermute | solution.py:255
  5.3 0.0 copy-start.9
  5.4 0.0 copy-start.10
  5.4 2.3 %near.1.before_ref = f32[384,256]{1,0:T(8,128)S(1)} custom-call(s32[1]{0:T(128)} %bitcast.place.info, bf16[384,8192]{1,0:T(8,128)(2,1)} %h_ref.11, bf16[2048,128]{1,0:T(8,128)(2,1)} %kw_ref.1, bf16[2048,128]{1,0:T(8,128)(2,1)} %vw_ref.1), custom_call_target="tpu_custom_call" | custom-call | tf_op jit(solution)/shard_map/near/pallas_call | solution.py:224
  7.7 8.8 %collective-permute-done.refs_0_ = bf16[384,512]{1,0:T(8,128)(2,1)S(1)} collective-permute-done((bf16[384,512]{1,0:T(8,128)(2,1)S(1)}, bf16[384,512]{1,0:T(8,128)(2,1)S(1)}, u32[]{:S(2)}, u32[]{:S(2)}) %collective-permute-start) | collective-permute-done | bytes 393248 | tf_op jit(solution)/shard_map/ppermute | solution.py:255
  16.5 0.0 collective-permute-done.1.kw_ref
  16.5 0.1 collective-permute-start.3
  16.6 0.7 copy-done.7
  17.3 3.5 %collective-permute-start.4 = (bf16[2048,128]{1,0:T(8,128)(2,1)}, bf16[2048,128]{1,0:T(8,128)(2,1)S(1)}, u32[]{:S(2)}, u32[]{:S(2)}) collective-permute-start(bf16[2048,128]{1,0:T(8,128)(2,1)} %vw_ref.1), channel_id=1, source_target_pairs={{8,16},{16,8},{9,17},{17,9},{10,18},{18,10},{11,19},{19,11},{12,20... | collective-permute-start | bytes 1572872 | tf_op jit(solution)/shard_map/ppermute | solution.py:255
  20.8 2.5 %collective-permute-start.11 = (bf16[384,512]{1,0:T(8,128)(2,1)S(1)}, bf16[384,512]{1,0:T(8,128)(2,1)S(1)}, u32[]{:S(2)}, u32[]{:S(2)}) collective-permute-start(bf16[384,512]{1,0:T(8,128)(2,1)S(1)} %collective-permute-done.refs_0_), channel_id=1, source_target_pairs={{0,6},{1,7},{2,4},{3,5},{4,2},{5,3},{6,0},{7,1},{8,14},{9,15},{10,... | collective-permute-start | bytes 1179656 | tf_op jit(solution)/shard_map/ppermute | solution.py:258
  23.3 8.2 %collective-permute-done.3.w_ref = bf16[2048,128]{1,0:T(8,128)(2,1)} collective-permute-done((bf16[2048,128]{1,0:T(8,128)(2,1)S(1)}, bf16[2048,128]{1,0:T(8,128)(2,1)}, u32[]{:S(2)}, u32[]{:S(2)}) %collective-permute-start.3) | collective-permute-done | bytes 524320 | tf_op jit(solution)/shard_map/ppermute | solution.py:255
  31.6 0.5 collective-permute-done.4.vw_ref
  32.1 0.8 copy-done.8
  32.9 3.3 %collective-permute-start.5 = (bf16[2048,128]{1,0:T(8,128)(2,1)}, bf16[2048,128]{1,0:T(8,128)(2,1)}, u32[]{:S(2)}, u32[]{:S(2)}) collective-permute-start(bf16[2048,128]{1,0:T(8,128)(2,1)} %collective-permute-done.3.w_ref), channel_id=1, source_target_pairs={{8,16},{16,8},{9,17},{17,9},{10,18},{18,10},{11,19},{19,11},{12,20... | collective-permute-start | bytes 1572872 | tf_op jit(solution)/shard_map/ppermute | solution.py:255
  36.1 1.6 %collective-permute-start.8 = (bf16[384,512]{1,0:T(8,128)(2,1)S(1)}, bf16[384,512]{1,0:T(8,128)(2,1)S(1)}, u32[]{:S(2)}, u32[]{:S(2)}) collective-permute-start(bf16[384,512]{1,0:T(8,128)(2,1)S(1)} %collective-permute-done.refs_0_), channel_id=1, source_target_pairs={{0,2},{1,3},{2,0},{3,1},{4,6},{5,7},{6,4},{7,5},{8,10},{9,11},{10,... | collective-permute-start | bytes 1179656 | tf_op jit(solution)/shard_map/ppermute | solution.py:258
  37.7 1.5 %collective-permute-start.2 = (bf16[384,512]{1,0:T(8,128)(2,1)S(1)}, bf16[384,512]{1,0:T(8,128)(2,1)S(1)}, u32[]{:S(2)}, u32[]{:S(2)}) collective-permute-start(bf16[384,512]{1,0:T(8,128)(2,1)S(1)} %collective-permute-done.refs_0_), channel_id=1, source_target_pairs={{0,4},{1,5},{2,6},{3,7},{4,0},{5,1},{6,2},{7,3},{8,12},{9,13},{10,... | collective-permute-start | bytes 1179656 | tf_op jit(solution)/shard_map/ppermute | solution.py:258
  39.2 3.0 %partial.2.near_ref = f32[392,128]{1,0:T(8,128)S(1)} custom-call(s32[1]{0:T(128)} %bitcast.6.place, bf16[384,8192]{1,0:T(8,128)(2,1)} %h_ref.11, bf16[2048,128]{1,0:T(8,128)(2,1)} %collective-permute-done.3.w_ref, f32[384,256]{1,0:T(8,128)S(1)} %near.1.before_ref, f32[8,128]{1,0:T(8,128)S(1)} %pad.7.owner_ref), custom_call_target="tpu_custom_call" | custom-call | tf_op jit(solution)/shard_map/partial/pallas_call | solution.py:224
  42.3 1.3 %collective-permute-start.6 = (f32[392,128]{1,0:T(8,128)S(1)}, f32[392,128]{1,0:T(8,128)S(1)}, u32[]{:S(2)}, u32[]{:S(2)}) collective-permute-start(f32[392,128]{1,0:T(8,128)S(1)} %partial.2.near_ref), channel_id=1, source_target_pairs={{0,8},{24,16},{1,9},{25,17},{2,10},{26,18},{3,11},{27,19},{4,12},{... | collective-permute-start | bytes 602120 | tf_op jit(solution)/shard_map/ppermute | solution.py:255
  43.6 0.0 copy-start
  43.6 0.7 copy-done
  44.3 0.5 collective-permute-done.8.refs_2_
  44.8 2.8 %collective-permute-start.16 = (bf16[2048,128]{1,0:T(8,128)(2,1)}, bf16[2048,128]{1,0:T(8,128)(2,1)}, u32[]{:S(2)}, u32[]{:S(2)}) collective-permute-start(bf16[2048,128]{1,0:T(8,128)(2,1)} %collective-permute-done.15.w_ref), channel_id=1, source_target_pairs={{8,16},{16,8},{9,17},{17,9},{10,18},{18,10},{11,19},{19,11},{12,20... | collective-permute-start | bytes 1572872 | tf_op jit(solution)/shard_map/ppermute | solution.py:255
  47.6 0.3 collective-permute-start.12
  47.9 2.1 %collective-permute-done.6.outer_ref = f32[392,128]{1,0:T(8,128)S(1)} collective-permute-done((f32[392,128]{1,0:T(8,128)S(1)}, f32[392,128]{1,0:T(8,128)S(1)}, u32[]{:S(2)}, u32[]{:S(2)}) %collective-permute-start.6) | collective-permute-done | bytes 200736 | tf_op jit(solution)/shard_map/ppermute | solution.py:255
  49.9 0.7 copy-done.2
  50.6 0.5 collective-permute-start.10
  51.1 0.1 add_add_fusion.place
  51.2 3.0 %partial.3.near_ref = f32[384,128]{1,0:T(8,128)S(1)} custom-call(s32[1]{0:T(128)} %bitcast.6.place, bf16[384,8192]{1,0:T(8,128)(2,1)} %h_ref.11, bf16[2048,128]{1,0:T(8,128)(2,1)} %collective-permute-done.15.w_ref, f32[384,256]{1,0:T(8,128)S(1)} %near.1.before_ref, f32[8,128]{1,0:T(8,128)S(1)} %pad.7.owner_ref), custom_call_target="tpu_custom_call" | custom-call | tf_op jit(solution)/shard_map/partial/pallas_call | solution.py:224
  54.2 1.3 %collective-permute-start.17 = (f32[384,128]{1,0:T(8,128)S(1)}, f32[384,128]{1,0:T(8,128)S(1)}, u32[]{:S(2)}, u32[]{:S(2)}) collective-permute-start(f32[384,128]{1,0:T(8,128)S(1)} %partial.3.near_ref), channel_id=1, source_target_pairs={{0,8},{24,16},{1,9},{25,17},{2,10},{26,18},{3,11},{27,19},{4,12},{... | collective-permute-start | bytes 589832 | tf_op jit(solution)/shard_map/ppermute | solution.py:255
  55.5 0.1 add_add_fusion.1.place
  55.7 3.0 %facing.1.facing_ref = f32[768,256]{1,0:T(8,128)S(1)} custom-call(s32[4]{0:T(128)S(1)} %add_add_fusion.1.place, bf16[384,8192]{1,0:T(8,128)(2,1)} %h_ref.11, bf16[2048,128]{1,0:T(8,128)(2,1)} %copy-done.7, bf16[2048,128]{1,0:T(8,128)(2,1)} %copy-done.8, bf16[384,512]{1,0:T(8,128)(2,1)S(1)} %collective-permute-done.refs_0_, ...), custom_call_target="tpu_custom_call" | custom-call | tf_op jit(solution)/shard_map/facing/pallas_call | solution.py:224
  58.6 0.0 copy-start.6
  58.7 3.1 %distant.2.k_in = bf16[784,128]{1,0:T(8,128)(2,1)S(1)} custom-call(s32[4]{0:T(128)S(1)} %add_add_fusion.place, bf16[384,8192]{1,0:T(8,128)(2,1)} %h_ref.11, bf16[2048,128]{1,0:T(8,128)(2,1)} %collective-permute-done.5.w_ref, f32[392,128]{1,0:T(8,128)S(1)} %copy-done.1, f32[392,128]{1,0:T(8,128)S(1)} %copy-done.3, f32[768,256]{1,0:T(8,128)S(1)} %facing.1.facing_ref, ...), custom_call_target="tpu_custom_call" | custom-call | tf_op jit(solution)/shard_map/distant/pallas_call | solution.py:224
  61.7 1.3 %collective-permute-start.20 = (bf16[784,128]{1,0:T(8,128)(2,1)S(1)}, bf16[784,128]{1,0:T(8,128)(2,1)S(1)}, u32[]{:S(2)}, u32[]{:S(2)}) collective-permute-start(bf16[784,128]{1,0:T(8,128)(2,1)S(1)} %distant.2.k_in), channel_id=1, source_target_pairs={{8,0},{16,24},{9,1},{17,25},{10,2},{18,26},{11,3},{19,27},{12,4},{... | collective-permute-start | bytes 602120 | tf_op jit(solution)/shard_map/ppermute | solution.py:255
  63.0 2.5 %collective-permute-start.13 = (bf16[784,128]{1,0:T(8,128)(2,1)S(1)}, bf16[784,128]{1,0:T(8,128)(2,1)S(1)}, u32[]{:S(2)}, u32[]{:S(2)}) collective-permute-start(bf16[784,128]{1,0:T(8,128)(2,1)S(1)} %distant.2.k_in), channel_id=1, source_target_pairs={{8,16},{16,8},{9,17},{17,9},{10,18},{18,10},{11,19},{19,11},{12,20... | collective-permute-start | bytes 602120 | tf_op jit(solution)/shard_map/ppermute | solution.py:255
  65.6 0.0 copy-start.4
  65.6 3.1 %distant.3.v_in = bf16[768,128]{1,0:T(8,128)(2,1)S(1)} custom-call(s32[4]{0:T(128)S(1)} %add_add_fusion.place, bf16[384,8192]{1,0:T(8,128)(2,1)} %h_ref.11, bf16[2048,128]{1,0:T(8,128)(2,1)} %collective-permute-done.16.w_ref, f32[384,128]{1,0:T(8,128)S(1)} %partial.3.near_ref, f32[384,128]{1,0:T(8,128)S(1)} %collective-permute-done.17.outer_ref, ...), custom_call_target="tpu_custom_call" | custom-call | tf_op jit(solution)/shard_map/distant/pallas_call | solution.py:224
  68.7 3.3 %collective-permute-start.18 = (bf16[768,128]{1,0:T(8,128)(2,1)S(1)}, bf16[768,128]{1,0:T(8,128)(2,1)S(1)}, u32[]{:S(2)}, u32[]{:S(2)}) collective-permute-start(bf16[768,128]{1,0:T(8,128)(2,1)S(1)} %distant.3.v_in), channel_id=1, source_target_pairs={{8,16},{16,8},{9,17},{17,9},{10,18},{18,10},{11,19},{19,11},{12,20... | collective-permute-start | bytes 589832 | tf_op jit(solution)/shard_map/ppermute | solution.py:255
  72.0 1.3 %collective-permute-start.21 = (bf16[768,128]{1,0:T(8,128)(2,1)S(1)}, bf16[768,128]{1,0:T(8,128)(2,1)S(1)}, u32[]{:S(2)}, u32[]{:S(2)}) collective-permute-start(bf16[768,128]{1,0:T(8,128)(2,1)S(1)} %distant.3.v_in), channel_id=1, source_target_pairs={{8,0},{16,24},{9,1},{17,25},{10,2},{18,26},{11,3},{19,27},{12,4},{... | collective-permute-start | bytes 589832 | tf_op jit(solution)/shard_map/ppermute | solution.py:255
  73.3 1.3 %collective-permute-start.14 = (bf16[784,128]{1,0:T(8,128)(2,1)S(1)}, bf16[784,128]{1,0:T(8,128)(2,1)S(1)}, u32[]{:S(2)}, u32[]{:S(2)}) collective-permute-start(bf16[784,128]{1,0:T(8,128)(2,1)S(1)} %collective-permute-done.13.k_across), channel_id=1, source_target_pairs={{8,0},{16,24},{9,1},{17,25},{10,2},{18,26},{11,3},{19,27},{12,4},{... | collective-permute-start | bytes 602120 | tf_op jit(solution)/shard_map/ppermute | solution.py:255
  74.7 2.5 %collective-permute-done.18.v_across = bf16[768,128]{1,0:T(8,128)(2,1)S(1)} collective-permute-done((bf16[768,128]{1,0:T(8,128)(2,1)S(1)}, bf16[768,128]{1,0:T(8,128)(2,1)S(1)}, u32[]{:S(2)}, u32[]{:S(2)}) %collective-permute-start.18) | collective-permute-done | bytes 196640 | tf_op jit(solution)/shard_map/ppermute | solution.py:255
  77.1 1.3 %collective-permute-start.19 = (bf16[768,128]{1,0:T(8,128)(2,1)S(1)}, bf16[768,128]{1,0:T(8,128)(2,1)S(1)}, u32[]{:S(2)}, u32[]{:S(2)}) collective-permute-start(bf16[768,128]{1,0:T(8,128)(2,1)S(1)} %collective-permute-done.18.v_across), channel_id=1, source_target_pairs={{8,0},{16,24},{9,1},{17,25},{10,2},{18,26},{11,3},{19,27},{12,4},{... | collective-permute-start | bytes 589832 | tf_op jit(solution)/shard_map/ppermute | solution.py:255
  78.4 0.2 collective-permute-done.21.v_out
  78.6 5.1 %attend_own.1 = (f32[8,384,1]{2,1,0:T(8,128)S(1)}, f32[8,384,1]{2,1,0:T(8,128)S(1)}, f32[8,384,128]{2,1,0:T(8,128)S(1)}, bf16[2,192,256]{2,1,0:T(8,128)(2,1)S(1)}) custom-call(s32[1]{0:T(128)} %bitcast.place.info, bf16[384,1024]{1,0:T(8,128)(2,1)} %q_ref.3, s32[12,128]{1,0:T(8,128)S(1)} %bitcast.13, bf16[784,128]{1,0:T(8,128)(2,1)S(1)} %distant.2.k_in, ...), custom_call_target="tpu_custom_call" | custom-call | flops 1207959552 | bytes 18874368 | tf_op jit(solution)/shard_map/attend_own/pallas_call | solution.py:559
  83.7 2.2 %collective-permute-done.19.v_far = bf16[768,128]{1,0:T(8,128)(2,1)S(1)} collective-permute-done((bf16[768,128]{1,0:T(8,128)(2,1)S(1)}, bf16[768,128]{1,0:T(8,128)(2,1)S(1)}, u32[]{:S(2)}, u32[]{:S(2)}) %collective-permute-start.19) | collective-permute-done | bytes 196640 | tf_op jit(solution)/shard_map/ppermute | solution.py:255
  85.9 6.6 %attend_far.1 = (bf16[384,1024]{1,0:T(8,128)(2,1)}, bf16[4,192,256]{2,1,0:T(8,128)(2,1)}) custom-call(s32[1]{0:T(128)} %bitcast.place.info, bf16[384,1024]{1,0:T(8,128)(2,1)} %q_ref.3, s32[12,128]{1,0:T(8,128)S(1)} %bitcast.14, bf16[784,128]{1,0:T(8,128)(2,1)S(1)} %collective-permute-done.13.k_across, bf16[784,128]{1,0:T(8,128)(2,1)S(1)} %collective-permute-done.14.k_far, ...), custom_call_target="tpu_custom_call" | custom-call | flops 1207959552 | bytes 18874368 | tf_op jit(solution)/shard_map/attend_far/pallas_call | solution.py:574
  (32 shorter events, 0.1 us)
Async XLA Ops:
  0.6 15.9 %collective-permute-start.1 = (bf16[2048,128]{1,0:T(8,128)(2,1)}, bf16[2048,128]{1,0:T(8,128)(2,1)S(1)}, u32[]{:S(2)}, u32[]{:S(2)}) collective-permute-start(bf16[2048,128]{1,0:T(8,128)(2,1)} %kw_ref.1), channel_id=1, source_target_pairs={{8,16},{16,8},{9,17},{17,9},{10,18},{18,10},{11,19},{19,11},{12,20... | collective-permute-start | bytes 1572872 | tf_op jit(solution)/shard_map/ppermute | solution.py:255
  4.0 12.5 %collective-permute-start = (bf16[384,512]{1,0:T(8,128)(2,1)S(1)}, bf16[384,512]{1,0:T(8,128)(2,1)S(1)}, u32[]{:S(2)}, u32[]{:S(2)}) collective-permute-start(bf16[384,512]{1,0:T(8,128)(2,1)S(1)} %constant_dynamic-slice_fusion), channel_id=1, source_target_pairs={{0,8},{24,16},{1,9},{25,17},{2,10},{26,18},{3,11},{27,19},{4,12},{... | collective-permute-start | bytes 1179656 | tf_op jit(solution)/shard_map/ppermute | solution.py:255
  5.3 11.2 %copy-start.9 = (bf16[2048,128]{1,0:T(8,128)(2,1)S(1)}, bf16[2048,128]{1,0:T(8,128)(2,1)}, u32[]{:S(2)}) copy-start(bf16[2048,128]{1,0:T(8,128)(2,1)} %kw_ref.1) | copy-start | bytes 1572868
  5.4 33.9 %copy-start.10 = (s32[24,1]{0,1:T(1,128)S(1)}, s32[24,1]{0,1:T(1,128)}, u32[]{:S(2)}) copy-start(s32[24,1]{0,1:T(1,128)} %param.15) | copy-start | bytes 292
  16.5 0.8 copy-start.7
  16.5 15.0 %collective-permute-start.3 = (bf16[2048,128]{1,0:T(8,128)(2,1)S(1)}, bf16[2048,128]{1,0:T(8,128)(2,1)}, u32[]{:S(2)}, u32[]{:S(2)}) collective-permute-start(bf16[2048,128]{1,0:T(8,128)(2,1)S(1)} %copy-done.9), channel_id=1, source_target_pairs={{0,8},{8,0},{16,24},{24,16},{1,9},{9,1},{17,25},{25,17},{2,10},{10... | collective-permute-start | bytes 1572872 | tf_op jit(solution)/shard_map/ppermute | solution.py:255
  17.3 14.8 %collective-permute-start.4 = (bf16[2048,128]{1,0:T(8,128)(2,1)}, bf16[2048,128]{1,0:T(8,128)(2,1)S(1)}, u32[]{:S(2)}, u32[]{:S(2)}) collective-permute-start(bf16[2048,128]{1,0:T(8,128)(2,1)} %vw_ref.1), channel_id=1, source_target_pairs={{8,16},{16,8},{9,17},{17,9},{10,18},{18,10},{11,19},{19,11},{12,20... | collective-permute-start | bytes 1572872 | tf_op jit(solution)/shard_map/ppermute | solution.py:255
  20.8 21.5 %collective-permute-start.11 = (bf16[384,512]{1,0:T(8,128)(2,1)S(1)}, bf16[384,512]{1,0:T(8,128)(2,1)S(1)}, u32[]{:S(2)}, u32[]{:S(2)}) collective-permute-start(bf16[384,512]{1,0:T(8,128)(2,1)S(1)} %collective-permute-done.refs_0_), channel_id=1, source_target_pairs={{0,6},{1,7},{2,4},{3,5},{4,2},{5,3},{6,0},{7,1},{8,14},{9,15},{10,... | collective-permute-start | bytes 1179656 | tf_op jit(solution)/shard_map/ppermute | solution.py:258
  23.3 21.5 %collective-permute-start.15 = (bf16[2048,128]{1,0:T(8,128)(2,1)}, bf16[2048,128]{1,0:T(8,128)(2,1)}, u32[]{:S(2)}, u32[]{:S(2)}) collective-permute-start(bf16[2048,128]{1,0:T(8,128)(2,1)} %vw_ref.1), channel_id=1, source_target_pairs={{0,8},{8,0},{16,24},{24,16},{1,9},{9,1},{17,25},{25,17},{2,10},{10... | collective-permute-start | bytes 1572872 | tf_op jit(solution)/shard_map/ppermute | solution.py:255
  32.1 0.8 copy-start.8
  32.9 17.7 %collective-permute-start.5 = (bf16[2048,128]{1,0:T(8,128)(2,1)}, bf16[2048,128]{1,0:T(8,128)(2,1)}, u32[]{:S(2)}, u32[]{:S(2)}) collective-permute-start(bf16[2048,128]{1,0:T(8,128)(2,1)} %collective-permute-done.3.w_ref), channel_id=1, source_target_pairs={{8,16},{16,8},{9,17},{17,9},{10,18},{18,10},{11,19},{19,11},{12,20... | collective-permute-start | bytes 1572872 | tf_op jit(solution)/shard_map/ppermute | solution.py:255
  36.1 8.6 %collective-permute-start.8 = (bf16[384,512]{1,0:T(8,128)(2,1)S(1)}, bf16[384,512]{1,0:T(8,128)(2,1)S(1)}, u32[]{:S(2)}, u32[]{:S(2)}) collective-permute-start(bf16[384,512]{1,0:T(8,128)(2,1)S(1)} %collective-permute-done.refs_0_), channel_id=1, source_target_pairs={{0,2},{1,3},{2,0},{3,1},{4,6},{5,7},{6,4},{7,5},{8,10},{9,11},{10,... | collective-permute-start | bytes 1179656 | tf_op jit(solution)/shard_map/ppermute | solution.py:258
  37.7 9.8 %collective-permute-start.2 = (bf16[384,512]{1,0:T(8,128)(2,1)S(1)}, bf16[384,512]{1,0:T(8,128)(2,1)S(1)}, u32[]{:S(2)}, u32[]{:S(2)}) collective-permute-start(bf16[384,512]{1,0:T(8,128)(2,1)S(1)} %collective-permute-done.refs_0_), channel_id=1, source_target_pairs={{0,4},{1,5},{2,6},{3,7},{4,0},{5,1},{6,2},{7,3},{8,12},{9,13},{10,... | collective-permute-start | bytes 1179656 | tf_op jit(solution)/shard_map/ppermute | solution.py:258
  42.3 7.6 %collective-permute-start.6 = (f32[392,128]{1,0:T(8,128)S(1)}, f32[392,128]{1,0:T(8,128)S(1)}, u32[]{:S(2)}, u32[]{:S(2)}) collective-permute-start(f32[392,128]{1,0:T(8,128)S(1)} %partial.2.near_ref), channel_id=1, source_target_pairs={{0,8},{24,16},{1,9},{25,17},{2,10},{26,18},{3,11},{27,19},{4,12},{... | collective-permute-start | bytes 602120 | tf_op jit(solution)/shard_map/ppermute | solution.py:255
  43.6 0.7 copy-start
  44.8 9.4 %collective-permute-start.7 = (bf16[384,512]{1,0:T(8,128)(2,1)S(1)}, bf16[384,512]{1,0:T(8,128)(2,1)S(1)}, u32[]{:S(2)}, u32[]{:S(2)}) collective-permute-start(bf16[384,512]{1,0:T(8,128)(2,1)S(1)} %collective-permute-done.refs_0_), channel_id=1, source_target_pairs={{0,1},{1,0},{2,3},{3,2},{4,5},{5,4},{6,7},{7,6},{8,9},{9,8},{10,11... | collective-permute-start | bytes 1179656 | tf_op jit(solution)/shard_map/ppermute | solution.py:258
  44.8 20.8 %collective-permute-start.16 = (bf16[2048,128]{1,0:T(8,128)(2,1)}, bf16[2048,128]{1,0:T(8,128)(2,1)}, u32[]{:S(2)}, u32[]{:S(2)}) collective-permute-start(bf16[2048,128]{1,0:T(8,128)(2,1)} %collective-permute-done.15.w_ref), channel_id=1, source_target_pairs={{8,16},{16,8},{9,17},{17,9},{10,18},{18,10},{11,19},{19,11},{12,20... | collective-permute-start | bytes 1572872 | tf_op jit(solution)/shard_map/ppermute | solution.py:255
  47.6 8.1 %collective-permute-start.12 = (bf16[384,512]{1,0:T(8,128)(2,1)S(1)}, bf16[384,512]{1,0:T(8,128)(2,1)S(1)}, u32[]{:S(2)}, u32[]{:S(2)}) collective-permute-start(bf16[384,512]{1,0:T(8,128)(2,1)S(1)} %collective-permute-done.11.refs_6_), channel_id=1, source_target_pairs={{0,1},{1,0},{2,3},{3,2},{4,5},{5,4},{6,7},{7,6},{8,9},{9,8},{10,11... | collective-permute-start | bytes 1179656 | tf_op jit(solution)/shard_map/ppermute | solution.py:258
  49.9 0.7 copy-start.2
  50.6 5.0 %collective-permute-start.9 = (bf16[384,512]{1,0:T(8,128)(2,1)S(1)}, bf16[384,512]{1,0:T(8,128)(2,1)S(1)}, u32[]{:S(2)}, u32[]{:S(2)}) collective-permute-start(bf16[384,512]{1,0:T(8,128)(2,1)S(1)} %collective-permute-done.8.refs_2_), channel_id=1, source_target_pairs={{0,1},{1,0},{2,3},{3,2},{4,5},{5,4},{6,7},{7,6},{8,9},{9,8},{10,11... | collective-permute-start | bytes 1179656 | tf_op jit(solution)/shard_map/ppermute | solution.py:258
  50.6 5.0 %collective-permute-start.10 = (bf16[384,512]{1,0:T(8,128)(2,1)S(1)}, bf16[384,512]{1,0:T(8,128)(2,1)S(1)}, u32[]{:S(2)}, u32[]{:S(2)}) collective-permute-start(bf16[384,512]{1,0:T(8,128)(2,1)S(1)} %collective-permute-done.2.refs_4_), channel_id=1, source_target_pairs={{0,1},{1,0},{2,3},{3,2},{4,5},{5,4},{6,7},{7,6},{8,9},{9,8},{10,11... | collective-permute-start | bytes 1179656 | tf_op jit(solution)/shard_map/ppermute | solution.py:258
  54.2 11.4 %collective-permute-start.17 = (f32[384,128]{1,0:T(8,128)S(1)}, f32[384,128]{1,0:T(8,128)S(1)}, u32[]{:S(2)}, u32[]{:S(2)}) collective-permute-start(f32[384,128]{1,0:T(8,128)S(1)} %partial.3.near_ref), channel_id=1, source_target_pairs={{0,8},{24,16},{1,9},{25,17},{2,10},{26,18},{3,11},{27,19},{4,12},{... | collective-permute-start | bytes 589832 | tf_op jit(solution)/shard_map/ppermute | solution.py:255
  55.6 3.0 %copy-start.1 = (f32[392,128]{1,0:T(8,128)S(1)}, f32[392,128]{1,0:T(8,128)}, u32[]{:S(2)}) copy-start(f32[392,128]{1,0:T(8,128)} %copy-done) | copy-start | bytes 602116
  55.6 3.0 %copy-start.3 = (f32[392,128]{1,0:T(8,128)S(1)}, f32[392,128]{1,0:T(8,128)}, u32[]{:S(2)}) copy-start(f32[392,128]{1,0:T(8,128)} %copy-done.2) | copy-start | bytes 602116
  55.6 3.0 %copy-start.5 = (bf16[128]{0:T(256)(128)(2,1)S(1)}, bf16[128]{0:T(256)(128)(2,1)}, u32[]{:S(2)}) copy-start(bf16[128]{0:T(256)(128)(2,1)} %param.12) | copy-start | bytes 772
  58.6 7.0 %copy-start.6 = (bf16[128]{0:T(256)(128)(2,1)S(1)}, bf16[128]{0:T(256)(128)(2,1)}, u32[]{:S(2)}) copy-start(bf16[128]{0:T(256)(128)(2,1)} %param.13) | copy-start | bytes 772
  61.7 10.3 %collective-permute-start.20 = (bf16[784,128]{1,0:T(8,128)(2,1)S(1)}, bf16[784,128]{1,0:T(8,128)(2,1)S(1)}, u32[]{:S(2)}, u32[]{:S(2)}) collective-permute-start(bf16[784,128]{1,0:T(8,128)(2,1)S(1)} %distant.2.k_in), channel_id=1, source_target_pairs={{8,0},{16,24},{9,1},{17,25},{10,2},{18,26},{11,3},{19,27},{12,4},{... | collective-permute-start | bytes 602120 | tf_op jit(solution)/shard_map/ppermute | solution.py:255
  63.0 10.3 %collective-permute-start.13 = (bf16[784,128]{1,0:T(8,128)(2,1)S(1)}, bf16[784,128]{1,0:T(8,128)(2,1)S(1)}, u32[]{:S(2)}, u32[]{:S(2)}) collective-permute-start(bf16[784,128]{1,0:T(8,128)(2,1)S(1)} %distant.2.k_in), channel_id=1, source_target_pairs={{8,16},{16,8},{9,17},{17,9},{10,18},{18,10},{11,19},{19,11},{12,20... | collective-permute-start | bytes 602120 | tf_op jit(solution)/shard_map/ppermute | solution.py:255
  65.6 13.0 %copy-start.4 = (s32[1536]{0:T(1024)S(1)}, s32[1536]{0:T(1024)}, u32[]{:S(2)}) copy-start(s32[1536]{0:T(1024)} %param.14) | copy-start | bytes 18436
  68.7 8.4 %collective-permute-start.18 = (bf16[768,128]{1,0:T(8,128)(2,1)S(1)}, bf16[768,128]{1,0:T(8,128)(2,1)S(1)}, u32[]{:S(2)}, u32[]{:S(2)}) collective-permute-start(bf16[768,128]{1,0:T(8,128)(2,1)S(1)} %distant.3.v_in), channel_id=1, source_target_pairs={{8,16},{16,8},{9,17},{17,9},{10,18},{18,10},{11,19},{19,11},{12,20... | collective-permute-start | bytes 589832 | tf_op jit(solution)/shard_map/ppermute | solution.py:255
  72.0 6.6 %collective-permute-start.21 = (bf16[768,128]{1,0:T(8,128)(2,1)S(1)}, bf16[768,128]{1,0:T(8,128)(2,1)S(1)}, u32[]{:S(2)}, u32[]{:S(2)}) collective-permute-start(bf16[768,128]{1,0:T(8,128)(2,1)S(1)} %distant.3.v_in), channel_id=1, source_target_pairs={{8,0},{16,24},{9,1},{17,25},{10,2},{18,26},{11,3},{19,27},{12,4},{... | collective-permute-start | bytes 589832 | tf_op jit(solution)/shard_map/ppermute | solution.py:255
  73.3 12.5 %collective-permute-start.14 = (bf16[784,128]{1,0:T(8,128)(2,1)S(1)}, bf16[784,128]{1,0:T(8,128)(2,1)S(1)}, u32[]{:S(2)}, u32[]{:S(2)}) collective-permute-start(bf16[784,128]{1,0:T(8,128)(2,1)S(1)} %collective-permute-done.13.k_across), channel_id=1, source_target_pairs={{8,0},{16,24},{9,1},{17,25},{10,2},{18,26},{11,3},{19,27},{12,4},{... | collective-permute-start | bytes 602120 | tf_op jit(solution)/shard_map/ppermute | solution.py:255
  77.1 8.7 %collective-permute-start.19 = (bf16[768,128]{1,0:T(8,128)(2,1)S(1)}, bf16[768,128]{1,0:T(8,128)(2,1)S(1)}, u32[]{:S(2)}, u32[]{:S(2)}) collective-permute-start(bf16[768,128]{1,0:T(8,128)(2,1)S(1)} %collective-permute-done.18.v_across), channel_id=1, source_target_pairs={{8,0},{16,24},{9,1},{17,25},{10,2},{18,26},{11,3},{19,27},{12,4},{... | collective-permute-start | bytes 589832 | tf_op jit(solution)/shard_map/ppermute | solution.py:255

commit v10 on v9

--- a/solution.py
+++ b/solution.py
@@ -148,16 +148,23 @@
     out_ref[...] = jnp.dot(h_buf[...], w_buf[...], preferred_element_type=jnp.float32)
 
 
-def partial_kernel(column, place, h_ref, w_ref, before_ref, owner_ref, out_ref, h_buf, sem):
-    copy = chunk_copy(h_ref, place[0], h_buf, sem)
-    copy.start()
+def partial_kernel(
+    column, place, h_ref, w_ref, before_ref, owner_ref, out_ref, h_buf, w_buf, sems
+):
+    copies = [
+        pltpu.make_async_copy(w_ref, w_buf, sems.at[0]),
+        chunk_copy(h_ref, place[0], h_buf, sems.at[1]),
+    ]
+    for copy in copies:
+        copy.start()
     span = h_buf.shape[0]
     part = slice(column * HD, column * HD + HD)
     if column == 0:
         out_ref[span:] = owner_ref[...]
-    copy.wait()
+    for copy in copies:
+        copy.wait()
     out_ref[:span] = before_ref[:, part] + jnp.dot(
-        h_buf[...], w_ref[...], preferred_element_type=jnp.float32
+        h_buf[...], w_buf[...], preferred_element_type=jnp.float32
     )
 
 
@@ -185,26 +192,37 @@
 
 def distant_kernel(column, place, h_ref, w_ref, near_ref, outer_ref, facing_ref, bias_ref, *refs):
     pieces = refs[:PIECES]
-    out_ref, h_buf, acc, sem = refs[PIECES:]
+    out_ref, h_buf, w_buf, acc, *parts, sems = refs[PIECES:]
+    near, outer = parts or (near_ref, outer_ref)
     span = h_buf.shape[0]
     part = slice(column * HD, column * HD + HD)
 
     @pl.when(place[3] == 1)
     def _():
-        copy = chunk_copy(h_ref, place[0], h_buf, sem)
-        copy.start()
+        copies = [
+            pltpu.make_async_copy(w_ref, w_buf, sems.at[0]),
+            chunk_copy(h_ref, place[0], h_buf, sems.at[1]),
+        ]
+        if parts:
+            copies.append(pltpu.make_async_copy(outer_ref, outer, sems.at[2]))
+            copies.append(pltpu.make_async_copy(near_ref, near, sems.at[3]))
+        for copy in copies:
+            copy.start()
+        for copy in copies[2:]:
+            copy.wait()
         own_at = pl.multiple_of(place[1] * span, span)
         outer_at = pl.multiple_of((1 - place[1]) * span, span)
         bias = bias_ref[...].astype(jnp.float32)
-        acc[...] = outer_ref[:span] + facing_ref[span:, part] + bias
-        add_pieces(place[2], place[0], pieces, w_ref, acc)
+        acc[...] = outer[:span] + facing_ref[span:, part] + bias
+        copies[0].wait()
+        add_pieces(place[2], place[0], pieces, w_buf, acc)
         out_ref[pl.ds(outer_at, span), :] = acc[...].astype(jnp.bfloat16)
-        own = near_ref[:span] + facing_ref[:span, part] + bias
-        copy.wait()
-        own += jnp.dot(h_buf[...], w_ref[...], preferred_element_type=jnp.float32)
+        own = near[:span] + facing_ref[:span, part] + bias
+        copies[1].wait()
+        own += jnp.dot(h_buf[...], w_buf[...], preferred_element_type=jnp.float32)
         out_ref[pl.ds(own_at, span), :] = own.astype(jnp.bfloat16)
         if column == 0:
-            mine, theirs = near_ref[span:], outer_ref[span:]
+            mine, theirs = near[span:], outer[span:]
             lower = jnp.where(place[1] == 0, mine, theirs)
             upper = jnp.where(place[1] == 0, theirs, mine)
             out_ref[2 * span :] = jnp.concatenate([lower, upper], axis=0).astype(jnp.bfloat16)
@@ -262,6 +280,7 @@
     tie = lax.optimization_barrier
     block = pltpu.VMEM((span, depth), jnp.bfloat16)
     both = pltpu.VMEM((depth, 2 * HD), jnp.bfloat16)
+    single = pltpu.VMEM((depth, HD), jnp.bfloat16)
     key_facing = send(key_weight, ACROSS)
     cut = send(cut, INWARD)
     own_part = call_project(
@@ -298,7 +317,9 @@
             span + (EXTRA if column == 0 else 0),
             HD,
             jnp.float32,
-            [block],
+            [block, single],
+            held=2,
+            copies=(2,),
         )
         return part, send(part, INWARD)
 
@@ -319,7 +340,10 @@
             2 * span + (2 * EXTRA if column == 0 else 0),
             HD,
             jnp.bfloat16,
-            [block, pltpu.VMEM((span, HD), jnp.float32)],
+            [block, single, pltpu.VMEM((span, HD), jnp.float32)]
+            + [pltpu.VMEM(x.shape, jnp.float32) for x in parts if column == 0],
+            held=4 if column == 0 else 2,
+            copies=(4,),
         )
 
     value_parts = begin(1, value_swapped)

time: 94.3 us -> 91.9 us (0.975)
  Pallas kernels: 29.2 us -> 27.6 us
  local copies, waits for them, and re-layouts: 3.92 us -> 2.6 us
    pallas_call x6, Pallas kernels: 17.5 us -> 15.9 us  [call_project(): pl.pallas_call(kernel, in_specs=[SCALAR] + [HELD] * held + [FAST] * (len(...]
    ppermute x7, waiting for transfers between devices: 0.51 us -> 2.04 us  [trade(): lax.ppermute(x, ('dec', 'tp'), [(m, m ^ apart) for m in range(PIECES)])]
    unnamed x22 -> x18, local copies, waits for them, and re-layouts: 2.89 us -> 1.56 us
  transfers between devices with their start and end apart: 22 -> 22, of which waited for: 8 -> 8; matrix products, arithmetic and copies ran while one was open for 1% -> 1% of each run, Pallas kernels for 24% -> 23%
where the time goes in v10:
time: 91.9 us; the launch traced here: 90.4 us
  starting transfers between devices  33.2 us (36%)
  Pallas kernels  27.6 us (30%)
  waiting for transfers between devices  25.6 us (28%)
  local copies, waits for them, and re-layouts  2.6 us (3%)
  between operations  1.13 us (1%)
    ppermute x15, starting transfers between devices, send(): return lax.ppermute(x, 'pre', pairs)  26.8 us
    ppermute x15, waiting for transfers between devices, send(): return lax.ppermute(x, 'pre', pairs)  23.6 us
    pallas_call x6, Pallas kernels, call_project(): pl.pallas_call(kernel, in_specs=[SCALAR] + [HELD] * held + [FAST] * (len(...  15.9 us
    pallas_call x1, Pallas kernels, attention_of_pairs(): pl.pallas_call(functools.partial(far_kernel, heads), in_specs=[SCALAR, HE...  6.61 us
    ppermute x7, starting transfers between devices, trade(): lax.ppermute(x, ('dec', 'tp'), [(m, m ^ apart) for m in range(PIECES)])  6.39 us
    pallas_call x1, Pallas kernels, attention_of_pairs(): pl.pallas_call(functools.partial(own_kernel, heads), in_specs=[SCALAR, HE...  5.06 us
    ppermute x7, waiting for transfers between devices, trade(): lax.ppermute(x, ('dec', 'tp'), [(m, m ^ apart) for m in range(PIECES)])  2.04 us
  transfers between devices with their start and end apart: 22, of which 8 were waited for; matrix products, arithmetic and copies ran while one was open for 1% of the time, Pallas kernels for 23%

profile of v10, /device:TPU:16, one launch (start us, length us, event | category | flops | bytes accessed | tf_op | source)
XLA Modules:
  0.0 90.4 jit_solution(12392782739380860911)
XLA Ops:
  0.6 2.4 %collective-permute-start.1 = (bf16[2048,128]{1,0:T(8,128)(2,1)}, bf16[2048,128]{1,0:T(8,128)(2,1)S(1)}, u32[]{:S(2)}, u32[]{:S(2)}) collective-permute-start(bf16[2048,128]{1,0:T(8,128)(2,1)} %kw_ref.1), channel_id=1, source_target_pairs={{8,16},{16,8},{9,17},{17,9},{10,18},{18,10},{11,19},{19,11},{12,20... | collective-permute-start | bytes 1572872 | tf_op jit(solution)/shard_map/ppermute | solution.py:273
  3.0 1.0 %constant_dynamic-slice_fusion = bf16[384,512]{1,0:T(8,128)(2,1)S(1)} fusion(bf16[384,8192]{1,0:T(8,128)(2,1)} %h_ref.11, s32[]{:T(128)S(6)} %select_n.3), kind=kLoop, calls=%fused_computation.3 | loop fusion | bytes 786436 | tf_op jit(solution)/shard_map/dynamic_slice | solution.py:279
  4.0 1.3 %collective-permute-start = (bf16[384,512]{1,0:T(8,128)(2,1)S(1)}, bf16[384,512]{1,0:T(8,128)(2,1)S(1)}, u32[]{:S(2)}, u32[]{:S(2)}) collective-permute-start(bf16[384,512]{1,0:T(8,128)(2,1)S(1)} %constant_dynamic-slice_fusion), channel_id=1, source_target_pairs={{0,8},{24,16},{1,9},{25,17},{2,10},{26,18},{3,11},{27,19},{4,12},{... | collective-permute-start | bytes 1179656 | tf_op jit(solution)/shard_map/ppermute | solution.py:273
  5.3 0.0 copy-start.6
  5.4 0.0 copy-start.7
  5.4 0.0 copy-start.8
  5.4 2.4 %near.1.before_ref = f32[384,256]{1,0:T(8,128)S(1)} custom-call(s32[1]{0:T(128)} %bitcast.place.info, bf16[384,8192]{1,0:T(8,128)(2,1)} %h_ref.11, bf16[2048,128]{1,0:T(8,128)(2,1)} %kw_ref.1, bf16[2048,128]{1,0:T(8,128)(2,1)} %vw_ref.1), custom_call_target="tpu_custom_call" | custom-call | tf_op jit(solution)/shard_map/near/pallas_call | solution.py:242
  7.7 8.8 %collective-permute-done.refs_0_ = bf16[384,512]{1,0:T(8,128)(2,1)S(1)} collective-permute-done((bf16[384,512]{1,0:T(8,128)(2,1)S(1)}, bf16[384,512]{1,0:T(8,128)(2,1)S(1)}, u32[]{:S(2)}, u32[]{:S(2)}) %collective-permute-start) | collective-permute-done | bytes 393248 | tf_op jit(solution)/shard_map/ppermute | solution.py:273
  16.5 0.0 collective-permute-done.1.kw_ref
  16.5 0.1 collective-permute-start.3
  16.6 0.7 copy-done.4
  17.3 3.5 %collective-permute-start.4 = (bf16[2048,128]{1,0:T(8,128)(2,1)S(1)}, bf16[2048,128]{1,0:T(8,128)(2,1)S(1)}, u32[]{:S(2)}, u32[]{:S(2)}) collective-permute-start(bf16[2048,128]{1,0:T(8,128)(2,1)S(1)} %copy-done.7), channel_id=1, source_target_pairs={{8,16},{16,8},{9,17},{17,9},{10,18},{18,10},{11,19},{19,11},{12,20... | collective-permute-start | bytes 1572872 | tf_op jit(solution)/shard_map/ppermute | solution.py:273
  20.8 2.5 %collective-permute-start.11 = (bf16[384,512]{1,0:T(8,128)(2,1)S(1)}, bf16[384,512]{1,0:T(8,128)(2,1)S(1)}, u32[]{:S(2)}, u32[]{:S(2)}) collective-permute-start(bf16[384,512]{1,0:T(8,128)(2,1)S(1)} %collective-permute-done.refs_0_), channel_id=1, source_target_pairs={{0,6},{1,7},{2,4},{3,5},{4,2},{5,3},{6,0},{7,1},{8,14},{9,15},{10,... | collective-permute-start | bytes 1179656 | tf_op jit(solution)/shard_map/ppermute | solution.py:276
  23.3 8.2 %collective-permute-done.3.w_ref = bf16[2048,128]{1,0:T(8,128)(2,1)} collective-permute-done((bf16[2048,128]{1,0:T(8,128)(2,1)S(1)}, bf16[2048,128]{1,0:T(8,128)(2,1)}, u32[]{:S(2)}, u32[]{:S(2)}) %collective-permute-start.3) | collective-permute-done | bytes 524320 | tf_op jit(solution)/shard_map/ppermute | solution.py:273
  31.6 0.3 collective-permute-done.4.vw_ref
  31.9 0.8 copy-done.5
  32.7 3.3 %collective-permute-start.5 = (bf16[2048,128]{1,0:T(8,128)(2,1)}, bf16[2048,128]{1,0:T(8,128)(2,1)}, u32[]{:S(2)}, u32[]{:S(2)}) collective-permute-start(bf16[2048,128]{1,0:T(8,128)(2,1)} %collective-permute-done.3.w_ref), channel_id=1, source_target_pairs={{8,16},{16,8},{9,17},{17,9},{10,18},{18,10},{11,19},{19,11},{12,20... | collective-permute-start | bytes 1572872 | tf_op jit(solution)/shard_map/ppermute | solution.py:273
  36.0 1.6 %collective-permute-start.8 = (bf16[384,512]{1,0:T(8,128)(2,1)S(1)}, bf16[384,512]{1,0:T(8,128)(2,1)S(1)}, u32[]{:S(2)}, u32[]{:S(2)}) collective-permute-start(bf16[384,512]{1,0:T(8,128)(2,1)S(1)} %collective-permute-done.refs_0_), channel_id=1, source_target_pairs={{0,2},{1,3},{2,0},{3,1},{4,6},{5,7},{6,4},{7,5},{8,10},{9,11},{10,... | collective-permute-start | bytes 1179656 | tf_op jit(solution)/shard_map/ppermute | solution.py:276
  37.5 1.5 %collective-permute-start.2 = (bf16[384,512]{1,0:T(8,128)(2,1)S(1)}, bf16[384,512]{1,0:T(8,128)(2,1)S(1)}, u32[]{:S(2)}, u32[]{:S(2)}) collective-permute-start(bf16[384,512]{1,0:T(8,128)(2,1)S(1)} %collective-permute-done.refs_0_), channel_id=1, source_target_pairs={{0,4},{1,5},{2,6},{3,7},{4,0},{5,1},{6,2},{7,3},{8,12},{9,13},{10,... | collective-permute-start | bytes 1179656 | tf_op jit(solution)/shard_map/ppermute | solution.py:276
  39.1 2.2 %partial.2.near_ref = f32[392,128]{1,0:T(8,128)S(1)} custom-call(s32[1]{0:T(128)} %bitcast.6.place, bf16[384,8192]{1,0:T(8,128)(2,1)} %h_ref.11, bf16[2048,128]{1,0:T(8,128)(2,1)} %collective-permute-done.3.w_ref, f32[384,256]{1,0:T(8,128)S(1)} %near.1.before_ref, f32[8,128]{1,0:T(8,128)S(1)} %pad.7.owner_ref), custom_call_target="tpu_custom_call" | custom-call | tf_op jit(solution)/shard_map/partial/pallas_call | solution.py:242
  41.2 0.0 copy-start
  41.3 1.3 %collective-permute-start.6 = (f32[392,128]{1,0:T(8,128)S(1)}, f32[392,128]{1,0:T(8,128)}, u32[]{:S(2)}, u32[]{:S(2)}) collective-permute-start(f32[392,128]{1,0:T(8,128)S(1)} %partial.2.near_ref), channel_id=1, source_target_pairs={{0,8},{24,16},{1,9},{25,17},{2,10},{26,18},{3,11},{27,19},{4,12},{... | collective-permute-start | bytes 602120 | tf_op jit(solution)/shard_map/ppermute | solution.py:273
  42.6 2.0 %collective-permute-done.8.refs_2_ = bf16[384,512]{1,0:T(8,128)(2,1)S(1)} collective-permute-done((bf16[384,512]{1,0:T(8,128)(2,1)S(1)}, bf16[384,512]{1,0:T(8,128)(2,1)S(1)}, u32[]{:S(2)}, u32[]{:S(2)}) %collective-permute-start.8) | collective-permute-done | bytes 393248 | tf_op jit(solution)/shard_map/ppermute | solution.py:276
  44.6 0.0 collective-permute-start.7
  44.6 2.8 %collective-permute-start.16 = (bf16[2048,128]{1,0:T(8,128)(2,1)}, bf16[2048,128]{1,0:T(8,128)(2,1)}, u32[]{:S(2)}, u32[]{:S(2)}) collective-permute-start(bf16[2048,128]{1,0:T(8,128)(2,1)} %collective-permute-done.15.w_ref), channel_id=1, source_target_pairs={{8,16},{16,8},{9,17},{17,9},{10,18},{18,10},{11,19},{19,11},{12,20... | collective-permute-start | bytes 1572872 | tf_op jit(solution)/shard_map/ppermute | solution.py:273
  47.4 0.3 collective-permute-start.12
  47.7 1.3 %collective-permute-done.6.outer_ref = f32[392,128]{1,0:T(8,128)} collective-permute-done((f32[392,128]{1,0:T(8,128)S(1)}, f32[392,128]{1,0:T(8,128)}, u32[]{:S(2)}, u32[]{:S(2)}) %collective-permute-start.6) | collective-permute-done | bytes 200736 | tf_op jit(solution)/shard_map/ppermute | solution.py:273
  49.0 0.5 collective-permute-start.10
  49.5 0.1 add_add_fusion.place
  49.6 2.2 %partial.3.near_ref = f32[384,128]{1,0:T(8,128)S(1)} custom-call(s32[1]{0:T(128)} %bitcast.6.place, bf16[384,8192]{1,0:T(8,128)(2,1)} %h_ref.11, bf16[2048,128]{1,0:T(8,128)(2,1)} %collective-permute-done.15.w_ref, f32[384,256]{1,0:T(8,128)S(1)} %near.1.before_ref, f32[8,128]{1,0:T(8,128)S(1)} %pad.7.owner_ref), custom_call_target="tpu_custom_call" | custom-call | tf_op jit(solution)/shard_map/partial/pallas_call | solution.py:242
  51.8 1.3 %collective-permute-start.17 = (f32[384,128]{1,0:T(8,128)S(1)}, f32[384,128]{1,0:T(8,128)S(1)}, u32[]{:S(2)}, u32[]{:S(2)}) collective-permute-start(f32[384,128]{1,0:T(8,128)S(1)} %partial.3.near_ref), channel_id=1, source_target_pairs={{0,8},{24,16},{1,9},{25,17},{2,10},{26,18},{3,11},{27,19},{4,12},{... | collective-permute-start | bytes 589832 | tf_op jit(solution)/shard_map/ppermute | solution.py:273
  53.1 0.1 add_add_fusion.1.place
  53.2 3.0 %facing.1.facing_ref = f32[768,256]{1,0:T(8,128)S(1)} custom-call(s32[4]{0:T(128)S(1)} %add_add_fusion.1.place, bf16[384,8192]{1,0:T(8,128)(2,1)} %h_ref.11, bf16[2048,128]{1,0:T(8,128)(2,1)} %copy-done.4, bf16[2048,128]{1,0:T(8,128)(2,1)} %copy-done.5, bf16[384,512]{1,0:T(8,128)(2,1)S(1)} %collective-permute-done.refs_0_, ...), custom_call_target="tpu_custom_call" | custom-call | tf_op jit(solution)/shard_map/facing/pallas_call | solution.py:242
  56.1 0.0 copy-start.3
  56.2 3.4 %distant.2.k_in = bf16[784,128]{1,0:T(8,128)(2,1)S(1)} custom-call(s32[4]{0:T(128)S(1)} %add_add_fusion.place, bf16[384,8192]{1,0:T(8,128)(2,1)} %h_ref.11, bf16[2048,128]{1,0:T(8,128)(2,1)} %collective-permute-done.5.w_ref, f32[392,128]{1,0:T(8,128)} %copy-done, f32[392,128]{1,0:T(8,128)} %collective-permute-done.6.outer_ref, ...), custom_call_target="tpu_custom_call" | custom-call | tf_op jit(solution)/shard_map/distant/pallas_call | solution.py:242
  59.6 1.3 %collective-permute-start.20 = (bf16[784,128]{1,0:T(8,128)(2,1)S(1)}, bf16[784,128]{1,0:T(8,128)(2,1)S(1)}, u32[]{:S(2)}, u32[]{:S(2)}) collective-permute-start(bf16[784,128]{1,0:T(8,128)(2,1)S(1)} %distant.2.k_in), channel_id=1, source_target_pairs={{8,0},{16,24},{9,1},{17,25},{10,2},{18,26},{11,3},{19,27},{12,4},{... | collective-permute-start | bytes 602120 | tf_op jit(solution)/shard_map/ppermute | solution.py:273
  60.9 2.6 %collective-permute-start.13 = (bf16[784,128]{1,0:T(8,128)(2,1)S(1)}, bf16[784,128]{1,0:T(8,128)(2,1)S(1)}, u32[]{:S(2)}, u32[]{:S(2)}) collective-permute-start(bf16[784,128]{1,0:T(8,128)(2,1)S(1)} %distant.2.k_in), channel_id=1, source_target_pairs={{8,16},{16,8},{9,17},{17,9},{10,18},{18,10},{11,19},{19,11},{12,20... | collective-permute-start | bytes 602120 | tf_op jit(solution)/shard_map/ppermute | solution.py:273
  63.5 0.0 copy-start.1
  63.5 2.8 %distant.3.v_in = bf16[768,128]{1,0:T(8,128)(2,1)S(1)} custom-call(s32[4]{0:T(128)S(1)} %add_add_fusion.place, bf16[384,8192]{1,0:T(8,128)(2,1)} %h_ref.11, bf16[2048,128]{1,0:T(8,128)(2,1)} %collective-permute-done.16.w_ref, f32[384,128]{1,0:T(8,128)S(1)} %partial.3.near_ref, f32[384,128]{1,0:T(8,128)S(1)} %collective-permute-done.17.outer_ref, ...), custom_call_target="tpu_custom_call" | custom-call | tf_op jit(solution)/shard_map/distant/pallas_call | solution.py:242
  66.4 3.3 %collective-permute-start.18 = (bf16[768,128]{1,0:T(8,128)(2,1)S(1)}, bf16[768,128]{1,0:T(8,128)(2,1)S(1)}, u32[]{:S(2)}, u32[]{:S(2)}) collective-permute-start(bf16[768,128]{1,0:T(8,128)(2,1)S(1)} %distant.3.v_in), channel_id=1, source_target_pairs={{8,16},{16,8},{9,17},{17,9},{10,18},{18,10},{11,19},{19,11},{12,20... | collective-permute-start | bytes 589832 | tf_op jit(solution)/shard_map/ppermute | solution.py:273
  69.7 1.3 %collective-permute-start.21 = (bf16[768,128]{1,0:T(8,128)(2,1)S(1)}, bf16[768,128]{1,0:T(8,128)(2,1)S(1)}, u32[]{:S(2)}, u32[]{:S(2)}) collective-permute-start(bf16[768,128]{1,0:T(8,128)(2,1)S(1)} %distant.3.v_in), channel_id=1, source_target_pairs={{8,0},{16,24},{9,1},{17,25},{10,2},{18,26},{11,3},{19,27},{12,4},{... | collective-permute-start | bytes 589832 | tf_op jit(solution)/shard_map/ppermute | solution.py:273
  71.0 1.3 %collective-permute-start.14 = (bf16[784,128]{1,0:T(8,128)(2,1)S(1)}, bf16[784,128]{1,0:T(8,128)(2,1)S(1)}, u32[]{:S(2)}, u32[]{:S(2)}) collective-permute-start(bf16[784,128]{1,0:T(8,128)(2,1)S(1)} %collective-permute-done.13.k_across), channel_id=1, source_target_pairs={{8,0},{16,24},{9,1},{17,25},{10,2},{18,26},{11,3},{19,27},{12,4},{... | collective-permute-start | bytes 602120 | tf_op jit(solution)/shard_map/ppermute | solution.py:273
  72.3 2.6 %collective-permute-done.18.v_across = bf16[768,128]{1,0:T(8,128)(2,1)S(1)} collective-permute-done((bf16[768,128]{1,0:T(8,128)(2,1)S(1)}, bf16[768,128]{1,0:T(8,128)(2,1)S(1)}, u32[]{:S(2)}, u32[]{:S(2)}) %collective-permute-start.18) | collective-permute-done | bytes 196640 | tf_op jit(solution)/shard_map/ppermute | solution.py:273
  74.9 1.3 %collective-permute-start.19 = (bf16[768,128]{1,0:T(8,128)(2,1)S(1)}, bf16[768,128]{1,0:T(8,128)(2,1)S(1)}, u32[]{:S(2)}, u32[]{:S(2)}) collective-permute-start(bf16[768,128]{1,0:T(8,128)(2,1)S(1)} %collective-permute-done.18.v_across), channel_id=1, source_target_pairs={{8,0},{16,24},{9,1},{17,25},{10,2},{18,26},{11,3},{19,27},{12,4},{... | collective-permute-start | bytes 589832 | tf_op jit(solution)/shard_map/ppermute | solution.py:273
  76.1 0.1 collective-permute-done.21.v_out
  76.3 5.1 %attend_own.1 = (f32[8,384,1]{2,1,0:T(8,128)S(1)}, f32[8,384,1]{2,1,0:T(8,128)S(1)}, f32[8,384,128]{2,1,0:T(8,128)S(1)}, bf16[2,192,256]{2,1,0:T(8,128)(2,1)S(1)}) custom-call(s32[1]{0:T(128)} %bitcast.place.info, bf16[384,1024]{1,0:T(8,128)(2,1)} %q_ref.3, s32[12,128]{1,0:T(8,128)S(1)} %bitcast.13, bf16[784,128]{1,0:T(8,128)(2,1)S(1)} %distant.2.k_in, ...), custom_call_target="tpu_custom_call" | custom-call | flops 1207959552 | bytes 18874368 | tf_op jit(solution)/shard_map/attend_own/pallas_call | solution.py:583
  81.3 2.3 %collective-permute-done.19.v_far = bf16[768,128]{1,0:T(8,128)(2,1)S(1)} collective-permute-done((bf16[768,128]{1,0:T(8,128)(2,1)S(1)}, bf16[768,128]{1,0:T(8,128)(2,1)S(1)}, u32[]{:S(2)}, u32[]{:S(2)}) %collective-permute-start.19) | collective-permute-done | bytes 196640 | tf_op jit(solution)/shard_map/ppermute | solution.py:273
  83.6 6.6 %attend_far.1 = (bf16[384,1024]{1,0:T(8,128)(2,1)}, bf16[4,192,256]{2,1,0:T(8,128)(2,1)}) custom-call(s32[1]{0:T(128)} %bitcast.place.info, bf16[384,1024]{1,0:T(8,128)(2,1)} %q_ref.3, s32[12,128]{1,0:T(8,128)S(1)} %bitcast.14, bf16[784,128]{1,0:T(8,128)(2,1)S(1)} %collective-permute-done.13.k_across, bf16[784,128]{1,0:T(8,128)(2,1)S(1)} %collective-permute-done.14.k_far, ...), custom_call_target="tpu_custom_call" | custom-call | flops 1207959552 | bytes 18874368 | tf_op jit(solution)/shard_map/attend_far/pallas_call | solution.py:598
  (28 shorter events, 0.1 us)
Async XLA Ops:
  0.6 15.9 %collective-permute-start.1 = (bf16[2048,128]{1,0:T(8,128)(2,1)}, bf16[2048,128]{1,0:T(8,128)(2,1)S(1)}, u32[]{:S(2)}, u32[]{:S(2)}) collective-permute-start(bf16[2048,128]{1,0:T(8,128)(2,1)} %kw_ref.1), channel_id=1, source_target_pairs={{8,16},{16,8},{9,17},{17,9},{10,18},{18,10},{11,19},{19,11},{12,20... | collective-permute-start | bytes 1572872 | tf_op jit(solution)/shard_map/ppermute | solution.py:273
  4.0 12.5 %collective-permute-start = (bf16[384,512]{1,0:T(8,128)(2,1)S(1)}, bf16[384,512]{1,0:T(8,128)(2,1)S(1)}, u32[]{:S(2)}, u32[]{:S(2)}) collective-permute-start(bf16[384,512]{1,0:T(8,128)(2,1)S(1)} %constant_dynamic-slice_fusion), channel_id=1, source_target_pairs={{0,8},{24,16},{1,9},{25,17},{2,10},{26,18},{3,11},{27,19},{4,12},{... | collective-permute-start | bytes 1179656 | tf_op jit(solution)/shard_map/ppermute | solution.py:273
  5.3 11.2 %copy-start.6 = (bf16[2048,128]{1,0:T(8,128)(2,1)S(1)}, bf16[2048,128]{1,0:T(8,128)(2,1)}, u32[]{:S(2)}) copy-start(bf16[2048,128]{1,0:T(8,128)(2,1)} %kw_ref.1) | copy-start | bytes 1572868
  5.4 12.0 %copy-start.7 = (bf16[2048,128]{1,0:T(8,128)(2,1)S(1)}, bf16[2048,128]{1,0:T(8,128)(2,1)}, u32[]{:S(2)}) copy-start(bf16[2048,128]{1,0:T(8,128)(2,1)} %vw_ref.1) | copy-start | bytes 1572868
  5.4 33.7 %copy-start.8 = (s32[24,1]{0,1:T(1,128)S(1)}, s32[24,1]{0,1:T(1,128)}, u32[]{:S(2)}) copy-start(s32[24,1]{0,1:T(1,128)} %param.15) | copy-start | bytes 292
  16.5 0.8 copy-start.4
  16.5 15.0 %collective-permute-start.3 = (bf16[2048,128]{1,0:T(8,128)(2,1)S(1)}, bf16[2048,128]{1,0:T(8,128)(2,1)}, u32[]{:S(2)}, u32[]{:S(2)}) collective-permute-start(bf16[2048,128]{1,0:T(8,128)(2,1)S(1)} %copy-done.6), channel_id=1, source_target_pairs={{0,8},{8,0},{16,24},{24,16},{1,9},{9,1},{17,25},{25,17},{2,10},{10... | collective-permute-start | bytes 1572872 | tf_op jit(solution)/shard_map/ppermute | solution.py:273
  17.3 14.6 %collective-permute-start.4 = (bf16[2048,128]{1,0:T(8,128)(2,1)S(1)}, bf16[2048,128]{1,0:T(8,128)(2,1)S(1)}, u32[]{:S(2)}, u32[]{:S(2)}) collective-permute-start(bf16[2048,128]{1,0:T(8,128)(2,1)S(1)} %copy-done.7), channel_id=1, source_target_pairs={{8,16},{16,8},{9,17},{17,9},{10,18},{18,10},{11,19},{19,11},{12,20... | collective-permute-start | bytes 1572872 | tf_op jit(solution)/shard_map/ppermute | solution.py:273
  20.8 20.5 %collective-permute-start.11 = (bf16[384,512]{1,0:T(8,128)(2,1)S(1)}, bf16[384,512]{1,0:T(8,128)(2,1)S(1)}, u32[]{:S(2)}, u32[]{:S(2)}) collective-permute-start(bf16[384,512]{1,0:T(8,128)(2,1)S(1)} %collective-permute-done.refs_0_), channel_id=1, source_target_pairs={{0,6},{1,7},{2,4},{3,5},{4,2},{5,3},{6,0},{7,1},{8,14},{9,15},{10,... | collective-permute-start | bytes 1179656 | tf_op jit(solution)/shard_map/ppermute | solution.py:276
  23.3 21.3 %collective-permute-start.15 = (bf16[2048,128]{1,0:T(8,128)(2,1)S(1)}, bf16[2048,128]{1,0:T(8,128)(2,1)}, u32[]{:S(2)}, u32[]{:S(2)}) collective-permute-start(bf16[2048,128]{1,0:T(8,128)(2,1)S(1)} %copy-done.7), channel_id=1, source_target_pairs={{0,8},{8,0},{16,24},{24,16},{1,9},{9,1},{17,25},{25,17},{2,10},{10... | collective-permute-start | bytes 1572872 | tf_op jit(solution)/shard_map/ppermute | solution.py:273
  31.9 0.8 copy-start.5
  32.7 16.3 %collective-permute-start.5 = (bf16[2048,128]{1,0:T(8,128)(2,1)}, bf16[2048,128]{1,0:T(8,128)(2,1)}, u32[]{:S(2)}, u32[]{:S(2)}) collective-permute-start(bf16[2048,128]{1,0:T(8,128)(2,1)} %collective-permute-done.3.w_ref), channel_id=1, source_target_pairs={{8,16},{16,8},{9,17},{17,9},{10,18},{18,10},{11,19},{19,11},{12,20... | collective-permute-start | bytes 1572872 | tf_op jit(solution)/shard_map/ppermute | solution.py:273
  36.0 8.6 %collective-permute-start.8 = (bf16[384,512]{1,0:T(8,128)(2,1)S(1)}, bf16[384,512]{1,0:T(8,128)(2,1)S(1)}, u32[]{:S(2)}, u32[]{:S(2)}) collective-permute-start(bf16[384,512]{1,0:T(8,128)(2,1)S(1)} %collective-permute-done.refs_0_), channel_id=1, source_target_pairs={{0,2},{1,3},{2,0},{3,1},{4,6},{5,7},{6,4},{7,5},{8,10},{9,11},{10,... | collective-permute-start | bytes 1179656 | tf_op jit(solution)/shard_map/ppermute | solution.py:276
  37.5 9.8 %collective-permute-start.2 = (bf16[384,512]{1,0:T(8,128)(2,1)S(1)}, bf16[384,512]{1,0:T(8,128)(2,1)S(1)}, u32[]{:S(2)}, u32[]{:S(2)}) collective-permute-start(bf16[384,512]{1,0:T(8,128)(2,1)S(1)} %collective-permute-done.refs_0_), channel_id=1, source_target_pairs={{0,4},{1,5},{2,6},{3,7},{4,0},{5,1},{6,2},{7,3},{8,12},{9,13},{10,... | collective-permute-start | bytes 1179656 | tf_op jit(solution)/shard_map/ppermute | solution.py:276
  41.2 7.7 %copy-start = (f32[392,128]{1,0:T(8,128)}, f32[392,128]{1,0:T(8,128)S(1)}, u32[]{:S(2)}) copy-start(f32[392,128]{1,0:T(8,128)S(1)} %partial.2.near_ref) | copy-start | bytes 602116
  41.3 7.7 %collective-permute-start.6 = (f32[392,128]{1,0:T(8,128)S(1)}, f32[392,128]{1,0:T(8,128)}, u32[]{:S(2)}, u32[]{:S(2)}) collective-permute-start(f32[392,128]{1,0:T(8,128)S(1)} %partial.2.near_ref), channel_id=1, source_target_pairs={{0,8},{24,16},{1,9},{25,17},{2,10},{26,18},{3,11},{27,19},{4,12},{... | collective-permute-start | bytes 602120 | tf_op jit(solution)/shard_map/ppermute | solution.py:273
  44.6 7.2 %collective-permute-start.7 = (bf16[384,512]{1,0:T(8,128)(2,1)S(1)}, bf16[384,512]{1,0:T(8,128)(2,1)S(1)}, u32[]{:S(2)}, u32[]{:S(2)}) collective-permute-start(bf16[384,512]{1,0:T(8,128)(2,1)S(1)} %collective-permute-done.refs_0_), channel_id=1, source_target_pairs={{0,1},{1,0},{2,3},{3,2},{4,5},{5,4},{6,7},{7,6},{8,9},{9,8},{10,11... | collective-permute-start | bytes 1179656 | tf_op jit(solution)/shard_map/ppermute | solution.py:276
  44.6 18.9 %collective-permute-start.16 = (bf16[2048,128]{1,0:T(8,128)(2,1)}, bf16[2048,128]{1,0:T(8,128)(2,1)}, u32[]{:S(2)}, u32[]{:S(2)}) collective-permute-start(bf16[2048,128]{1,0:T(8,128)(2,1)} %collective-permute-done.15.w_ref), channel_id=1, source_target_pairs={{8,16},{16,8},{9,17},{17,9},{10,18},{18,10},{11,19},{19,11},{12,20... | collective-permute-start | bytes 1572872 | tf_op jit(solution)/shard_map/ppermute | solution.py:273
  47.4 5.8 %collective-permute-start.12 = (bf16[384,512]{1,0:T(8,128)(2,1)S(1)}, bf16[384,512]{1,0:T(8,128)(2,1)S(1)}, u32[]{:S(2)}, u32[]{:S(2)}) collective-permute-start(bf16[384,512]{1,0:T(8,128)(2,1)S(1)} %collective-permute-done.11.refs_6_), channel_id=1, source_target_pairs={{0,1},{1,0},{2,3},{3,2},{4,5},{5,4},{6,7},{7,6},{8,9},{9,8},{10,11... | collective-permute-start | bytes 1179656 | tf_op jit(solution)/shard_map/ppermute | solution.py:276
  49.0 4.2 %collective-permute-start.9 = (bf16[384,512]{1,0:T(8,128)(2,1)S(1)}, bf16[384,512]{1,0:T(8,128)(2,1)S(1)}, u32[]{:S(2)}, u32[]{:S(2)}) collective-permute-start(bf16[384,512]{1,0:T(8,128)(2,1)S(1)} %collective-permute-done.8.refs_2_), channel_id=1, source_target_pairs={{0,1},{1,0},{2,3},{3,2},{4,5},{5,4},{6,7},{7,6},{8,9},{9,8},{10,11... | collective-permute-start | bytes 1179656 | tf_op jit(solution)/shard_map/ppermute | solution.py:276
  49.0 4.2 %collective-permute-start.10 = (bf16[384,512]{1,0:T(8,128)(2,1)S(1)}, bf16[384,512]{1,0:T(8,128)(2,1)S(1)}, u32[]{:S(2)}, u32[]{:S(2)}) collective-permute-start(bf16[384,512]{1,0:T(8,128)(2,1)S(1)} %collective-permute-done.2.refs_4_), channel_id=1, source_target_pairs={{0,1},{1,0},{2,3},{3,2},{4,5},{5,4},{6,7},{7,6},{8,9},{9,8},{10,11... | collective-permute-start | bytes 1179656 | tf_op jit(solution)/shard_map/ppermute | solution.py:276
  51.8 11.7 %collective-permute-start.17 = (f32[384,128]{1,0:T(8,128)S(1)}, f32[384,128]{1,0:T(8,128)S(1)}, u32[]{:S(2)}, u32[]{:S(2)}) collective-permute-start(f32[384,128]{1,0:T(8,128)S(1)} %partial.3.near_ref), channel_id=1, source_target_pairs={{0,8},{24,16},{1,9},{25,17},{2,10},{26,18},{3,11},{27,19},{4,12},{... | collective-permute-start | bytes 589832 | tf_op jit(solution)/shard_map/ppermute | solution.py:273
  53.1 3.0 %copy-start.2 = (bf16[128]{0:T(256)(128)(2,1)S(1)}, bf16[128]{0:T(256)(128)(2,1)}, u32[]{:S(2)}) copy-start(bf16[128]{0:T(256)(128)(2,1)} %param.12) | copy-start | bytes 772
  56.1 7.4 %copy-start.3 = (bf16[128]{0:T(256)(128)(2,1)S(1)}, bf16[128]{0:T(256)(128)(2,1)}, u32[]{:S(2)}) copy-start(bf16[128]{0:T(256)(128)(2,1)} %param.13) | copy-start | bytes 772
  59.6 10.0 %collective-permute-start.20 = (bf16[784,128]{1,0:T(8,128)(2,1)S(1)}, bf16[784,128]{1,0:T(8,128)(2,1)S(1)}, u32[]{:S(2)}, u32[]{:S(2)}) collective-permute-start(bf16[784,128]{1,0:T(8,128)(2,1)S(1)} %distant.2.k_in), channel_id=1, source_target_pairs={{8,0},{16,24},{9,1},{17,25},{10,2},{18,26},{11,3},{19,27},{12,4},{... | collective-permute-start | bytes 602120 | tf_op jit(solution)/shard_map/ppermute | solution.py:273
  60.9 10.1 %collective-permute-start.13 = (bf16[784,128]{1,0:T(8,128)(2,1)S(1)}, bf16[784,128]{1,0:T(8,128)(2,1)S(1)}, u32[]{:S(2)}, u32[]{:S(2)}) collective-permute-start(bf16[784,128]{1,0:T(8,128)(2,1)S(1)} %distant.2.k_in), channel_id=1, source_target_pairs={{8,16},{16,8},{9,17},{17,9},{10,18},{18,10},{11,19},{19,11},{12,20... | collective-permute-start | bytes 602120 | tf_op jit(solution)/shard_map/ppermute | solution.py:273
  63.5 12.7 %copy-start.1 = (s32[1536]{0:T(1024)S(1)}, s32[1536]{0:T(1024)}, u32[]{:S(2)}) copy-start(s32[1536]{0:T(1024)} %param.14) | copy-start | bytes 18436
  66.4 8.5 %collective-permute-start.18 = (bf16[768,128]{1,0:T(8,128)(2,1)S(1)}, bf16[768,128]{1,0:T(8,128)(2,1)S(1)}, u32[]{:S(2)}, u32[]{:S(2)}) collective-permute-start(bf16[768,128]{1,0:T(8,128)(2,1)S(1)} %distant.3.v_in), channel_id=1, source_target_pairs={{8,16},{16,8},{9,17},{17,9},{10,18},{18,10},{11,19},{19,11},{12,20... | collective-permute-start | bytes 589832 | tf_op jit(solution)/shard_map/ppermute | solution.py:273
  69.7 6.6 %collective-permute-start.21 = (bf16[768,128]{1,0:T(8,128)(2,1)S(1)}, bf16[768,128]{1,0:T(8,128)(2,1)S(1)}, u32[]{:S(2)}, u32[]{:S(2)}) collective-permute-start(bf16[768,128]{1,0:T(8,128)(2,1)S(1)} %distant.3.v_in), channel_id=1, source_target_pairs={{8,0},{16,24},{9,1},{17,25},{10,2},{18,26},{11,3},{19,27},{12,4},{... | collective-permute-start | bytes 589832 | tf_op jit(solution)/shard_map/ppermute | solution.py:273
  71.0 12.6 %collective-permute-start.14 = (bf16[784,128]{1,0:T(8,128)(2,1)S(1)}, bf16[784,128]{1,0:T(8,128)(2,1)S(1)}, u32[]{:S(2)}, u32[]{:S(2)}) collective-permute-start(bf16[784,128]{1,0:T(8,128)(2,1)S(1)} %collective-permute-done.13.k_across), channel_id=1, source_target_pairs={{8,0},{16,24},{9,1},{17,25},{10,2},{18,26},{11,3},{19,27},{12,4},{... | collective-permute-start | bytes 602120 | tf_op jit(solution)/shard_map/ppermute | solution.py:273
  74.9 8.7 %collective-permute-start.19 = (bf16[768,128]{1,0:T(8,128)(2,1)S(1)}, bf16[768,128]{1,0:T(8,128)(2,1)S(1)}, u32[]{:S(2)}, u32[]{:S(2)}) collective-permute-start(bf16[768,128]{1,0:T(8,128)(2,1)S(1)} %collective-permute-done.18.v_across), channel_id=1, source_target_pairs={{8,0},{16,24},{9,1},{17,25},{10,2},{18,26},{11,3},{19,27},{12,4},{... | collective-permute-start | bytes 589832 | tf_op jit(solution)/shard_map/ppermute | solution.py:273

commit v11 on v10

--- a/solution.py
+++ b/solution.py
@@ -254,6 +254,7 @@
 INWARD = [(0, 1), (3, 2)]
 ACROSS = [(1, 2), (2, 1)]
 OUTWARD = [(1, 0), (2, 3)]
+LEAP = [(1, 3), (2, 0)]
 SWAP = [(0, 1), (1, 0), (2, 3), (3, 2)]
 
 
@@ -360,12 +361,13 @@
         copies=(3,),
     )
     keys = finish(0, key_distant, (key_part, key_outer), key_bias)
-    keys_out, keys_across = send(keys, OUTWARD), send(keys, ACROSS)
+    keys_far, keys_out, keys_across = send(keys, LEAP), send(keys, OUTWARD), send(keys, ACROSS)
     values = finish(1, value_distant, value_parts, value_bias)
     values_across = send(values, ACROSS)
     keys_out, values_after = tie((keys_out, values))
     values_out = send(values_after, OUTWARD)
-    keys_far, values_far = send(keys_across, OUTWARD), send(values_across, OUTWARD)
+    values_across, keys_far = tie((values_across, keys_far))
+    values_far = send(values_across, OUTWARD)
     return (
         (keys, keys_out, keys_across, keys_far),
         (values, values_out, values_across, values_far),

time: 91.9 us -> 92.3 us (level)
  starting transfers between devices: 33.2 us -> 35.6 us
  waiting for transfers between devices: 25.6 us -> 23.5 us
    ppermute x15, starting transfers between devices: 26.8 us -> 29.2 us  [send(): return lax.ppermute(x, 'pre', pairs)]
    ppermute x15, waiting for transfers between devices: 23.6 us -> 21.4 us  [send(): return lax.ppermute(x, 'pre', pairs)]
  transfers between devices with their start and end apart: 22 -> 22, of which waited for: 8 -> 7; matrix products, arithmetic and copies ran while one was open for 1% -> 1% of each run, Pallas kernels for 23% -> 23%
where the time goes in v11:
time: 92.3 us; the launch traced here: 90.8 us
  starting transfers between devices  35.6 us (39%)
  Pallas kernels  27.8 us (30%)
  waiting for transfers between devices  23.5 us (25%)
  local copies, waits for them, and re-layouts  2.6 us (3%)
  between operations  1.15 us (1%)
    ppermute x15, starting transfers between devices, send(): return lax.ppermute(x, 'pre', pairs)  29.2 us
    ppermute x15, waiting for transfers between devices, send(): return lax.ppermute(x, 'pre', pairs)  21.4 us
    pallas_call x6, Pallas kernels, call_project(): pl.pallas_call(kernel, in_specs=[SCALAR] + [HELD] * held + [FAST] * (len(...  15.9 us
    pallas_call x1, Pallas kernels, attention_of_pairs(): pl.pallas_call(functools.partial(far_kernel, heads), in_specs=[SCALAR, HE...  6.8 us
    ppermute x7, starting transfers between devices, trade(): lax.ppermute(x, ('dec', 'tp'), [(m, m ^ apart) for m in range(PIECES)])  6.39 us
    pallas_call x1, Pallas kernels, attention_of_pairs(): pl.pallas_call(functools.partial(own_kernel, heads), in_specs=[SCALAR, HE...  5.05 us
    ppermute x7, waiting for transfers between devices, trade(): lax.ppermute(x, ('dec', 'tp'), [(m, m ^ apart) for m in range(PIECES)])  2.04 us
  transfers between devices with their start and end apart: 22, of which 7 were waited for; matrix products, arithmetic and copies ran while one was open for 1% of the time, Pallas kernels for 23%

profile of v11, /device:TPU:16, one launch (start us, length us, event | category | flops | bytes accessed | tf_op | source)
XLA Modules:
  0.0 90.8 jit_solution(12763164530707891699)
XLA Ops:
  0.6 2.4 %collective-permute-start.1 = (bf16[2048,128]{1,0:T(8,128)(2,1)}, bf16[2048,128]{1,0:T(8,128)(2,1)S(1)}, u32[]{:S(2)}, u32[]{:S(2)}) collective-permute-start(bf16[2048,128]{1,0:T(8,128)(2,1)} %kw_ref.1), channel_id=1, source_target_pairs={{8,16},{16,8},{9,17},{17,9},{10,18},{18,10},{11,19},{19,11},{12,20... | collective-permute-start | bytes 1572872 | tf_op jit(solution)/shard_map/ppermute | solution.py:274
  3.0 1.0 %constant_dynamic-slice_fusion = bf16[384,512]{1,0:T(8,128)(2,1)S(1)} fusion(bf16[384,8192]{1,0:T(8,128)(2,1)} %h_ref.11, s32[]{:T(128)S(6)} %select_n.3), kind=kLoop, calls=%fused_computation.3 | loop fusion | bytes 786436 | tf_op jit(solution)/shard_map/dynamic_slice | solution.py:280
  4.0 1.3 %collective-permute-start = (bf16[384,512]{1,0:T(8,128)(2,1)S(1)}, bf16[384,512]{1,0:T(8,128)(2,1)S(1)}, u32[]{:S(2)}, u32[]{:S(2)}) collective-permute-start(bf16[384,512]{1,0:T(8,128)(2,1)S(1)} %constant_dynamic-slice_fusion), channel_id=1, source_target_pairs={{0,8},{24,16},{1,9},{25,17},{2,10},{26,18},{3,11},{27,19},{4,12},{... | collective-permute-start | bytes 1179656 | tf_op jit(solution)/shard_map/ppermute | solution.py:274
  5.3 0.0 copy-start.6
  5.4 0.0 copy-start.7
  5.4 0.0 copy-start.8
  5.4 2.4 %near.1.before_ref = f32[384,256]{1,0:T(8,128)S(1)} custom-call(s32[1]{0:T(128)} %bitcast.place.info, bf16[384,8192]{1,0:T(8,128)(2,1)} %h_ref.11, bf16[2048,128]{1,0:T(8,128)(2,1)} %kw_ref.1, bf16[2048,128]{1,0:T(8,128)(2,1)} %vw_ref.1), custom_call_target="tpu_custom_call" | custom-call | tf_op jit(solution)/shard_map/near/pallas_call | solution.py:242
  7.7 8.8 %collective-permute-done.refs_0_ = bf16[384,512]{1,0:T(8,128)(2,1)S(1)} collective-permute-done((bf16[384,512]{1,0:T(8,128)(2,1)S(1)}, bf16[384,512]{1,0:T(8,128)(2,1)S(1)}, u32[]{:S(2)}, u32[]{:S(2)}) %collective-permute-start) | collective-permute-done | bytes 393248 | tf_op jit(solution)/shard_map/ppermute | solution.py:274
  16.5 0.0 collective-permute-done.1.kw_ref
  16.5 0.1 collective-permute-start.3
  16.6 0.7 copy-done.4
  17.3 3.5 %collective-permute-start.4 = (bf16[2048,128]{1,0:T(8,128)(2,1)S(1)}, bf16[2048,128]{1,0:T(8,128)(2,1)S(1)}, u32[]{:S(2)}, u32[]{:S(2)}) collective-permute-start(bf16[2048,128]{1,0:T(8,128)(2,1)S(1)} %copy-done.7), channel_id=1, source_target_pairs={{8,16},{16,8},{9,17},{17,9},{10,18},{18,10},{11,19},{19,11},{12,20... | collective-permute-start | bytes 1572872 | tf_op jit(solution)/shard_map/ppermute | solution.py:274
  20.8 2.5 %collective-permute-start.11 = (bf16[384,512]{1,0:T(8,128)(2,1)S(1)}, bf16[384,512]{1,0:T(8,128)(2,1)S(1)}, u32[]{:S(2)}, u32[]{:S(2)}) collective-permute-start(bf16[384,512]{1,0:T(8,128)(2,1)S(1)} %collective-permute-done.refs_0_), channel_id=1, source_target_pairs={{0,6},{1,7},{2,4},{3,5},{4,2},{5,3},{6,0},{7,1},{8,14},{9,15},{10,... | collective-permute-start | bytes 1179656 | tf_op jit(solution)/shard_map/ppermute | solution.py:277
  23.3 8.2 %collective-permute-done.3.w_ref = bf16[2048,128]{1,0:T(8,128)(2,1)} collective-permute-done((bf16[2048,128]{1,0:T(8,128)(2,1)S(1)}, bf16[2048,128]{1,0:T(8,128)(2,1)}, u32[]{:S(2)}, u32[]{:S(2)}) %collective-permute-start.3) | collective-permute-done | bytes 524320 | tf_op jit(solution)/shard_map/ppermute | solution.py:274
  31.6 0.3 collective-permute-done.4.vw_ref
  31.9 0.8 copy-done.5
  32.7 3.3 %collective-permute-start.5 = (bf16[2048,128]{1,0:T(8,128)(2,1)}, bf16[2048,128]{1,0:T(8,128)(2,1)}, u32[]{:S(2)}, u32[]{:S(2)}) collective-permute-start(bf16[2048,128]{1,0:T(8,128)(2,1)} %collective-permute-done.3.w_ref), channel_id=1, source_target_pairs={{8,16},{16,8},{9,17},{17,9},{10,18},{18,10},{11,19},{19,11},{12,20... | collective-permute-start | bytes 1572872 | tf_op jit(solution)/shard_map/ppermute | solution.py:274
  36.0 1.6 %collective-permute-start.8 = (bf16[384,512]{1,0:T(8,128)(2,1)S(1)}, bf16[384,512]{1,0:T(8,128)(2,1)S(1)}, u32[]{:S(2)}, u32[]{:S(2)}) collective-permute-start(bf16[384,512]{1,0:T(8,128)(2,1)S(1)} %collective-permute-done.refs_0_), channel_id=1, source_target_pairs={{0,2},{1,3},{2,0},{3,1},{4,6},{5,7},{6,4},{7,5},{8,10},{9,11},{10,... | collective-permute-start | bytes 1179656 | tf_op jit(solution)/shard_map/ppermute | solution.py:277
  37.5 1.5 %collective-permute-start.2 = (bf16[384,512]{1,0:T(8,128)(2,1)S(1)}, bf16[384,512]{1,0:T(8,128)(2,1)S(1)}, u32[]{:S(2)}, u32[]{:S(2)}) collective-permute-start(bf16[384,512]{1,0:T(8,128)(2,1)S(1)} %collective-permute-done.refs_0_), channel_id=1, source_target_pairs={{0,4},{1,5},{2,6},{3,7},{4,0},{5,1},{6,2},{7,3},{8,12},{9,13},{10,... | collective-permute-start | bytes 1179656 | tf_op jit(solution)/shard_map/ppermute | solution.py:277
  39.1 2.2 %partial.2.near_ref = f32[392,128]{1,0:T(8,128)S(1)} custom-call(s32[1]{0:T(128)} %bitcast.6.place, bf16[384,8192]{1,0:T(8,128)(2,1)} %h_ref.11, bf16[2048,128]{1,0:T(8,128)(2,1)} %collective-permute-done.3.w_ref, f32[384,256]{1,0:T(8,128)S(1)} %near.1.before_ref, f32[8,128]{1,0:T(8,128)S(1)} %pad.7.owner_ref), custom_call_target="tpu_custom_call" | custom-call | tf_op jit(solution)/shard_map/partial/pallas_call | solution.py:242
  41.2 0.0 copy-start
  41.3 1.3 %collective-permute-start.6 = (f32[392,128]{1,0:T(8,128)S(1)}, f32[392,128]{1,0:T(8,128)}, u32[]{:S(2)}, u32[]{:S(2)}) collective-permute-start(f32[392,128]{1,0:T(8,128)S(1)} %partial.2.near_ref), channel_id=1, source_target_pairs={{0,8},{24,16},{1,9},{25,17},{2,10},{26,18},{3,11},{27,19},{4,12},{... | collective-permute-start | bytes 602120 | tf_op jit(solution)/shard_map/ppermute | solution.py:274
  42.6 2.0 %collective-permute-done.8.refs_2_ = bf16[384,512]{1,0:T(8,128)(2,1)S(1)} collective-permute-done((bf16[384,512]{1,0:T(8,128)(2,1)S(1)}, bf16[384,512]{1,0:T(8,128)(2,1)S(1)}, u32[]{:S(2)}, u32[]{:S(2)}) %collective-permute-start.8) | collective-permute-done | bytes 393248 | tf_op jit(solution)/shard_map/ppermute | solution.py:277
  44.6 2.8 %collective-permute-start.15 = (bf16[2048,128]{1,0:T(8,128)(2,1)}, bf16[2048,128]{1,0:T(8,128)(2,1)}, u32[]{:S(2)}, u32[]{:S(2)}) collective-permute-start(bf16[2048,128]{1,0:T(8,128)(2,1)} %collective-permute-done.14.w_ref), channel_id=1, source_target_pairs={{8,16},{16,8},{9,17},{17,9},{10,18},{18,10},{11,19},{19,11},{12,20... | collective-permute-start | bytes 1572872 | tf_op jit(solution)/shard_map/ppermute | solution.py:274
  47.4 0.0 collective-permute-done.2.refs_4_
  47.4 0.3 collective-permute-start.12
  47.7 1.3 %collective-permute-done.6.outer_ref = f32[392,128]{1,0:T(8,128)} collective-permute-done((f32[392,128]{1,0:T(8,128)S(1)}, f32[392,128]{1,0:T(8,128)}, u32[]{:S(2)}, u32[]{:S(2)}) %collective-permute-start.6) | collective-permute-done | bytes 200736 | tf_op jit(solution)/shard_map/ppermute | solution.py:274
  49.0 0.0 collective-permute-start.9
  49.0 0.5 collective-permute-start.10
  49.5 0.1 add_add_fusion.place
  49.6 2.2 %partial.3.near_ref = f32[384,128]{1,0:T(8,128)S(1)} custom-call(s32[1]{0:T(128)} %bitcast.6.place, bf16[384,8192]{1,0:T(8,128)(2,1)} %h_ref.11, bf16[2048,128]{1,0:T(8,128)(2,1)} %collective-permute-done.14.w_ref, f32[384,256]{1,0:T(8,128)S(1)} %near.1.before_ref, f32[8,128]{1,0:T(8,128)S(1)} %pad.7.owner_ref), custom_call_target="tpu_custom_call" | custom-call | tf_op jit(solution)/shard_map/partial/pallas_call | solution.py:242
  51.8 1.3 %collective-permute-start.16 = (f32[384,128]{1,0:T(8,128)S(1)}, f32[384,128]{1,0:T(8,128)S(1)}, u32[]{:S(2)}, u32[]{:S(2)}) collective-permute-start(f32[384,128]{1,0:T(8,128)S(1)} %partial.3.near_ref), channel_id=1, source_target_pairs={{0,8},{24,16},{1,9},{25,17},{2,10},{26,18},{3,11},{27,19},{4,12},{... | collective-permute-start | bytes 589832 | tf_op jit(solution)/shard_map/ppermute | solution.py:274
  53.1 0.1 add_add_fusion.1.place
  53.2 3.0 %facing.1.facing_ref = f32[768,256]{1,0:T(8,128)S(1)} custom-call(s32[4]{0:T(128)S(1)} %add_add_fusion.1.place, bf16[384,8192]{1,0:T(8,128)(2,1)} %h_ref.11, bf16[2048,128]{1,0:T(8,128)(2,1)} %copy-done.4, bf16[2048,128]{1,0:T(8,128)(2,1)} %copy-done.5, bf16[384,512]{1,0:T(8,128)(2,1)S(1)} %collective-permute-done.refs_0_, ...), custom_call_target="tpu_custom_call" | custom-call | tf_op jit(solution)/shard_map/facing/pallas_call | solution.py:242
  56.1 0.0 copy-start.3
  56.2 3.4 %distant.2.k_in = bf16[784,128]{1,0:T(8,128)(2,1)S(1)} custom-call(s32[4]{0:T(128)S(1)} %add_add_fusion.place, bf16[384,8192]{1,0:T(8,128)(2,1)} %h_ref.11, bf16[2048,128]{1,0:T(8,128)(2,1)} %collective-permute-done.5.w_ref, f32[392,128]{1,0:T(8,128)} %copy-done, f32[392,128]{1,0:T(8,128)} %collective-permute-done.6.outer_ref, ...), custom_call_target="tpu_custom_call" | custom-call | tf_op jit(solution)/shard_map/distant/pallas_call | solution.py:242
  59.6 1.3 %collective-permute-start.20 = (bf16[784,128]{1,0:T(8,128)(2,1)S(1)}, bf16[784,128]{1,0:T(8,128)(2,1)S(1)}, u32[]{:S(2)}, u32[]{:S(2)}) collective-permute-start(bf16[784,128]{1,0:T(8,128)(2,1)S(1)} %distant.2.k_in), channel_id=1, source_target_pairs={{8,0},{16,24},{9,1},{17,25},{10,2},{18,26},{11,3},{19,27},{12,4},{... | collective-permute-start | bytes 602120 | tf_op jit(solution)/shard_map/ppermute | solution.py:274
  60.9 1.3 %collective-permute-start.18 = (bf16[784,128]{1,0:T(8,128)(2,1)S(1)}, bf16[784,128]{1,0:T(8,128)(2,1)S(1)}, u32[]{:S(2)}, u32[]{:S(2)}) collective-permute-start(bf16[784,128]{1,0:T(8,128)(2,1)S(1)} %distant.2.k_in), channel_id=1, source_target_pairs={{8,24},{16,0},{9,25},{17,1},{10,26},{18,2},{11,27},{19,3},{12,28},... | collective-permute-start | bytes 602120 | tf_op jit(solution)/shard_map/ppermute | solution.py:274
  62.3 0.0 copy-start.1
  62.3 2.8 %distant.3.v_in = bf16[768,128]{1,0:T(8,128)(2,1)S(1)} custom-call(s32[4]{0:T(128)S(1)} %add_add_fusion.place, bf16[384,8192]{1,0:T(8,128)(2,1)} %h_ref.11, bf16[2048,128]{1,0:T(8,128)(2,1)} %collective-permute-done.15.w_ref, f32[384,128]{1,0:T(8,128)S(1)} %partial.3.near_ref, f32[384,128]{1,0:T(8,128)S(1)} %collective-permute-done.16.outer_ref, ...), custom_call_target="tpu_custom_call" | custom-call | tf_op jit(solution)/shard_map/distant/pallas_call | solution.py:242
  65.1 2.6 %collective-permute-start.17 = (bf16[768,128]{1,0:T(8,128)(2,1)S(1)}, bf16[768,128]{1,0:T(8,128)(2,1)S(1)}, u32[]{:S(2)}, u32[]{:S(2)}) collective-permute-start(bf16[768,128]{1,0:T(8,128)(2,1)S(1)} %distant.3.v_in), channel_id=1, source_target_pairs={{8,16},{16,8},{9,17},{17,9},{10,18},{18,10},{11,19},{19,11},{12,20... | collective-permute-start | bytes 589832 | tf_op jit(solution)/shard_map/ppermute | solution.py:274
  67.7 2.3 %collective-permute-done.20.k_out = bf16[784,128]{1,0:T(8,128)(2,1)S(1)} collective-permute-done((bf16[784,128]{1,0:T(8,128)(2,1)S(1)}, bf16[784,128]{1,0:T(8,128)(2,1)S(1)}, u32[]{:S(2)}, u32[]{:S(2)}) %collective-permute-start.20) | collective-permute-done | bytes 200736 | tf_op jit(solution)/shard_map/ppermute | solution.py:274
  70.0 4.4 %collective-permute-start.21 = (bf16[768,128]{1,0:T(8,128)(2,1)S(1)}, bf16[768,128]{1,0:T(8,128)(2,1)S(1)}, u32[]{:S(2)}, u32[]{:S(2)}) collective-permute-start(bf16[768,128]{1,0:T(8,128)(2,1)S(1)} %distant.3.v_in), channel_id=1, source_target_pairs={{8,0},{16,24},{9,1},{17,25},{10,2},{18,26},{11,3},{19,27},{12,4},{... | collective-permute-start | bytes 589832 | tf_op jit(solution)/shard_map/ppermute | solution.py:274
  74.4 2.6 %collective-permute-start.13 = (bf16[784,128]{1,0:T(8,128)(2,1)S(1)}, bf16[784,128]{1,0:T(8,128)(2,1)S(1)}, u32[]{:S(2)}, u32[]{:S(2)}) collective-permute-start(bf16[784,128]{1,0:T(8,128)(2,1)S(1)} %distant.2.k_in), channel_id=1, source_target_pairs={{8,16},{16,8},{9,17},{17,9},{10,18},{18,10},{11,19},{19,11},{12,20... | collective-permute-start | bytes 602120 | tf_op jit(solution)/shard_map/ppermute | solution.py:274
  76.9 1.3 %collective-permute-start.19 = (bf16[768,128]{1,0:T(8,128)(2,1)S(1)}, bf16[768,128]{1,0:T(8,128)(2,1)S(1)}, u32[]{:S(2)}, u32[]{:S(2)}) collective-permute-start(bf16[768,128]{1,0:T(8,128)(2,1)S(1)} %collective-permute-done.17.v_across), channel_id=1, source_target_pairs={{8,0},{16,24},{9,1},{17,25},{10,2},{18,26},{11,3},{19,27},{12,4},{... | collective-permute-start | bytes 589832 | tf_op jit(solution)/shard_map/ppermute | solution.py:274
  78.2 0.5 collective-permute-done.21.v_out
  78.7 5.1 %attend_own.1 = (f32[8,384,1]{2,1,0:T(8,128)S(1)}, f32[8,384,1]{2,1,0:T(8,128)S(1)}, f32[8,384,128]{2,1,0:T(8,128)S(1)}, bf16[2,192,256]{2,1,0:T(8,128)(2,1)S(1)}) custom-call(s32[1]{0:T(128)} %bitcast.place.info, bf16[384,1024]{1,0:T(8,128)(2,1)} %q_ref.3, s32[12,128]{1,0:T(8,128)S(1)} %bitcast.13, bf16[784,128]{1,0:T(8,128)(2,1)S(1)} %distant.2.k_in, ...), custom_call_target="tpu_custom_call" | custom-call | flops 1207959552 | bytes 18874368 | tf_op jit(solution)/shard_map/attend_own/pallas_call | solution.py:585
  83.8 6.8 %attend_far.1 = (bf16[384,1024]{1,0:T(8,128)(2,1)}, bf16[4,192,256]{2,1,0:T(8,128)(2,1)}) custom-call(s32[1]{0:T(128)} %bitcast.place.info, bf16[384,1024]{1,0:T(8,128)(2,1)} %q_ref.3, s32[12,128]{1,0:T(8,128)S(1)} %bitcast.14, bf16[784,128]{1,0:T(8,128)(2,1)S(1)} %collective-permute-done.13.k_across, bf16[784,128]{1,0:T(8,128)(2,1)S(1)} %collective-permute-done.18.k_far, ...), custom_call_target="tpu_custom_call" | custom-call | flops 1207959552 | bytes 18874368 | tf_op jit(solution)/shard_map/attend_far/pallas_call | solution.py:600
  (28 shorter events, 0.1 us)
Async XLA Ops:
  0.6 15.9 %collective-permute-start.1 = (bf16[2048,128]{1,0:T(8,128)(2,1)}, bf16[2048,128]{1,0:T(8,128)(2,1)S(1)}, u32[]{:S(2)}, u32[]{:S(2)}) collective-permute-start(bf16[2048,128]{1,0:T(8,128)(2,1)} %kw_ref.1), channel_id=1, source_target_pairs={{8,16},{16,8},{9,17},{17,9},{10,18},{18,10},{11,19},{19,11},{12,20... | collective-permute-start | bytes 1572872 | tf_op jit(solution)/shard_map/ppermute | solution.py:274
  4.0 12.5 %collective-permute-start = (bf16[384,512]{1,0:T(8,128)(2,1)S(1)}, bf16[384,512]{1,0:T(8,128)(2,1)S(1)}, u32[]{:S(2)}, u32[]{:S(2)}) collective-permute-start(bf16[384,512]{1,0:T(8,128)(2,1)S(1)} %constant_dynamic-slice_fusion), channel_id=1, source_target_pairs={{0,8},{24,16},{1,9},{25,17},{2,10},{26,18},{3,11},{27,19},{4,12},{... | collective-permute-start | bytes 1179656 | tf_op jit(solution)/shard_map/ppermute | solution.py:274
  5.3 11.2 %copy-start.6 = (bf16[2048,128]{1,0:T(8,128)(2,1)S(1)}, bf16[2048,128]{1,0:T(8,128)(2,1)}, u32[]{:S(2)}) copy-start(bf16[2048,128]{1,0:T(8,128)(2,1)} %kw_ref.1) | copy-start | bytes 1572868
  5.4 12.0 %copy-start.7 = (bf16[2048,128]{1,0:T(8,128)(2,1)S(1)}, bf16[2048,128]{1,0:T(8,128)(2,1)}, u32[]{:S(2)}) copy-start(bf16[2048,128]{1,0:T(8,128)(2,1)} %vw_ref.1) | copy-start | bytes 1572868
  5.4 33.7 %copy-start.8 = (s32[24,1]{0,1:T(1,128)S(1)}, s32[24,1]{0,1:T(1,128)}, u32[]{:S(2)}) copy-start(s32[24,1]{0,1:T(1,128)} %param.15) | copy-start | bytes 292
  16.5 0.8 copy-start.4
  16.5 15.0 %collective-permute-start.3 = (bf16[2048,128]{1,0:T(8,128)(2,1)S(1)}, bf16[2048,128]{1,0:T(8,128)(2,1)}, u32[]{:S(2)}, u32[]{:S(2)}) collective-permute-start(bf16[2048,128]{1,0:T(8,128)(2,1)S(1)} %copy-done.6), channel_id=1, source_target_pairs={{0,8},{8,0},{16,24},{24,16},{1,9},{9,1},{17,25},{25,17},{2,10},{10... | collective-permute-start | bytes 1572872 | tf_op jit(solution)/shard_map/ppermute | solution.py:274
  17.3 14.6 %collective-permute-start.4 = (bf16[2048,128]{1,0:T(8,128)(2,1)S(1)}, bf16[2048,128]{1,0:T(8,128)(2,1)S(1)}, u32[]{:S(2)}, u32[]{:S(2)}) collective-permute-start(bf16[2048,128]{1,0:T(8,128)(2,1)S(1)} %copy-done.7), channel_id=1, source_target_pairs={{8,16},{16,8},{9,17},{17,9},{10,18},{18,10},{11,19},{19,11},{12,20... | collective-permute-start | bytes 1572872 | tf_op jit(solution)/shard_map/ppermute | solution.py:274
  20.8 20.5 %collective-permute-start.11 = (bf16[384,512]{1,0:T(8,128)(2,1)S(1)}, bf16[384,512]{1,0:T(8,128)(2,1)S(1)}, u32[]{:S(2)}, u32[]{:S(2)}) collective-permute-start(bf16[384,512]{1,0:T(8,128)(2,1)S(1)} %collective-permute-done.refs_0_), channel_id=1, source_target_pairs={{0,6},{1,7},{2,4},{3,5},{4,2},{5,3},{6,0},{7,1},{8,14},{9,15},{10,... | collective-permute-start | bytes 1179656 | tf_op jit(solution)/shard_map/ppermute | solution.py:277
  23.3 21.3 %collective-permute-start.14 = (bf16[2048,128]{1,0:T(8,128)(2,1)S(1)}, bf16[2048,128]{1,0:T(8,128)(2,1)}, u32[]{:S(2)}, u32[]{:S(2)}) collective-permute-start(bf16[2048,128]{1,0:T(8,128)(2,1)S(1)} %copy-done.7), channel_id=1, source_target_pairs={{0,8},{8,0},{16,24},{24,16},{1,9},{9,1},{17,25},{25,17},{2,10},{10... | collective-permute-start | bytes 1572872 | tf_op jit(solution)/shard_map/ppermute | solution.py:274
  31.9 0.8 copy-start.5
  32.7 16.3 %collective-permute-start.5 = (bf16[2048,128]{1,0:T(8,128)(2,1)}, bf16[2048,128]{1,0:T(8,128)(2,1)}, u32[]{:S(2)}, u32[]{:S(2)}) collective-permute-start(bf16[2048,128]{1,0:T(8,128)(2,1)} %collective-permute-done.3.w_ref), channel_id=1, source_target_pairs={{8,16},{16,8},{9,17},{17,9},{10,18},{18,10},{11,19},{19,11},{12,20... | collective-permute-start | bytes 1572872 | tf_op jit(solution)/shard_map/ppermute | solution.py:274
  36.0 8.6 %collective-permute-start.8 = (bf16[384,512]{1,0:T(8,128)(2,1)S(1)}, bf16[384,512]{1,0:T(8,128)(2,1)S(1)}, u32[]{:S(2)}, u32[]{:S(2)}) collective-permute-start(bf16[384,512]{1,0:T(8,128)(2,1)S(1)} %collective-permute-done.refs_0_), channel_id=1, source_target_pairs={{0,2},{1,3},{2,0},{3,1},{4,6},{5,7},{6,4},{7,5},{8,10},{9,11},{10,... | collective-permute-start | bytes 1179656 | tf_op jit(solution)/shard_map/ppermute | solution.py:277
  37.5 9.8 %collective-permute-start.2 = (bf16[384,512]{1,0:T(8,128)(2,1)S(1)}, bf16[384,512]{1,0:T(8,128)(2,1)S(1)}, u32[]{:S(2)}, u32[]{:S(2)}) collective-permute-start(bf16[384,512]{1,0:T(8,128)(2,1)S(1)} %collective-permute-done.refs_0_), channel_id=1, source_target_pairs={{0,4},{1,5},{2,6},{3,7},{4,0},{5,1},{6,2},{7,3},{8,12},{9,13},{10,... | collective-permute-start | bytes 1179656 | tf_op jit(solution)/shard_map/ppermute | solution.py:277
  41.2 7.7 %copy-start = (f32[392,128]{1,0:T(8,128)}, f32[392,128]{1,0:T(8,128)S(1)}, u32[]{:S(2)}) copy-start(f32[392,128]{1,0:T(8,128)S(1)} %partial.2.near_ref) | copy-start | bytes 602116
  41.3 7.7 %collective-permute-start.6 = (f32[392,128]{1,0:T(8,128)S(1)}, f32[392,128]{1,0:T(8,128)}, u32[]{:S(2)}, u32[]{:S(2)}) collective-permute-start(f32[392,128]{1,0:T(8,128)S(1)} %partial.2.near_ref), channel_id=1, source_target_pairs={{0,8},{24,16},{1,9},{25,17},{2,10},{26,18},{3,11},{27,19},{4,12},{... | collective-permute-start | bytes 602120 | tf_op jit(solution)/shard_map/ppermute | solution.py:274
  44.6 7.2 %collective-permute-start.7 = (bf16[384,512]{1,0:T(8,128)(2,1)S(1)}, bf16[384,512]{1,0:T(8,128)(2,1)S(1)}, u32[]{:S(2)}, u32[]{:S(2)}) collective-permute-start(bf16[384,512]{1,0:T(8,128)(2,1)S(1)} %collective-permute-done.refs_0_), channel_id=1, source_target_pairs={{0,1},{1,0},{2,3},{3,2},{4,5},{5,4},{6,7},{7,6},{8,9},{9,8},{10,11... | collective-permute-start | bytes 1179656 | tf_op jit(solution)/shard_map/ppermute | solution.py:277
  44.6 17.6 %collective-permute-start.15 = (bf16[2048,128]{1,0:T(8,128)(2,1)}, bf16[2048,128]{1,0:T(8,128)(2,1)}, u32[]{:S(2)}, u32[]{:S(2)}) collective-permute-start(bf16[2048,128]{1,0:T(8,128)(2,1)} %collective-permute-done.14.w_ref), channel_id=1, source_target_pairs={{8,16},{16,8},{9,17},{17,9},{10,18},{18,10},{11,19},{19,11},{12,20... | collective-permute-start | bytes 1572872 | tf_op jit(solution)/shard_map/ppermute | solution.py:274
  47.4 5.8 %collective-permute-start.12 = (bf16[384,512]{1,0:T(8,128)(2,1)S(1)}, bf16[384,512]{1,0:T(8,128)(2,1)S(1)}, u32[]{:S(2)}, u32[]{:S(2)}) collective-permute-start(bf16[384,512]{1,0:T(8,128)(2,1)S(1)} %collective-permute-done.11.refs_6_), channel_id=1, source_target_pairs={{0,1},{1,0},{2,3},{3,2},{4,5},{5,4},{6,7},{7,6},{8,9},{9,8},{10,11... | collective-permute-start | bytes 1179656 | tf_op jit(solution)/shard_map/ppermute | solution.py:277
  49.0 4.2 %collective-permute-start.9 = (bf16[384,512]{1,0:T(8,128)(2,1)S(1)}, bf16[384,512]{1,0:T(8,128)(2,1)S(1)}, u32[]{:S(2)}, u32[]{:S(2)}) collective-permute-start(bf16[384,512]{1,0:T(8,128)(2,1)S(1)} %collective-permute-done.8.refs_2_), channel_id=1, source_target_pairs={{0,1},{1,0},{2,3},{3,2},{4,5},{5,4},{6,7},{7,6},{8,9},{9,8},{10,11... | collective-permute-start | bytes 1179656 | tf_op jit(solution)/shard_map/ppermute | solution.py:277
  49.0 4.2 %collective-permute-start.10 = (bf16[384,512]{1,0:T(8,128)(2,1)S(1)}, bf16[384,512]{1,0:T(8,128)(2,1)S(1)}, u32[]{:S(2)}, u32[]{:S(2)}) collective-permute-start(bf16[384,512]{1,0:T(8,128)(2,1)S(1)} %collective-permute-done.2.refs_4_), channel_id=1, source_target_pairs={{0,1},{1,0},{2,3},{3,2},{4,5},{5,4},{6,7},{7,6},{8,9},{9,8},{10,11... | collective-permute-start | bytes 1179656 | tf_op jit(solution)/shard_map/ppermute | solution.py:277
  51.8 10.5 %collective-permute-start.16 = (f32[384,128]{1,0:T(8,128)S(1)}, f32[384,128]{1,0:T(8,128)S(1)}, u32[]{:S(2)}, u32[]{:S(2)}) collective-permute-start(f32[384,128]{1,0:T(8,128)S(1)} %partial.3.near_ref), channel_id=1, source_target_pairs={{0,8},{24,16},{1,9},{25,17},{2,10},{26,18},{3,11},{27,19},{4,12},{... | collective-permute-start | bytes 589832 | tf_op jit(solution)/shard_map/ppermute | solution.py:274
  53.1 3.0 %copy-start.2 = (bf16[128]{0:T(256)(128)(2,1)S(1)}, bf16[128]{0:T(256)(128)(2,1)}, u32[]{:S(2)}) copy-start(bf16[128]{0:T(256)(128)(2,1)} %param.12) | copy-start | bytes 772
  56.1 6.1 %copy-start.3 = (bf16[128]{0:T(256)(128)(2,1)S(1)}, bf16[128]{0:T(256)(128)(2,1)}, u32[]{:S(2)}) copy-start(bf16[128]{0:T(256)(128)(2,1)} %param.13) | copy-start | bytes 772
  59.6 10.3 %collective-permute-start.20 = (bf16[784,128]{1,0:T(8,128)(2,1)S(1)}, bf16[784,128]{1,0:T(8,128)(2,1)S(1)}, u32[]{:S(2)}, u32[]{:S(2)}) collective-permute-start(bf16[784,128]{1,0:T(8,128)(2,1)S(1)} %distant.2.k_in), channel_id=1, source_target_pairs={{8,0},{16,24},{9,1},{17,25},{10,2},{18,26},{11,3},{19,27},{12,4},{... | collective-permute-start | bytes 602120 | tf_op jit(solution)/shard_map/ppermute | solution.py:274
  60.9 16.0 %collective-permute-start.18 = (bf16[784,128]{1,0:T(8,128)(2,1)S(1)}, bf16[784,128]{1,0:T(8,128)(2,1)S(1)}, u32[]{:S(2)}, u32[]{:S(2)}) collective-permute-start(bf16[784,128]{1,0:T(8,128)(2,1)S(1)} %distant.2.k_in), channel_id=1, source_target_pairs={{8,24},{16,0},{9,25},{17,1},{10,26},{18,2},{11,27},{19,3},{12,28},... | collective-permute-start | bytes 602120 | tf_op jit(solution)/shard_map/ppermute | solution.py:274
  62.3 16.5 %copy-start.1 = (s32[1536]{0:T(1024)S(1)}, s32[1536]{0:T(1024)}, u32[]{:S(2)}) copy-start(s32[1536]{0:T(1024)} %param.14) | copy-start | bytes 18436
  65.1 11.8 %collective-permute-start.17 = (bf16[768,128]{1,0:T(8,128)(2,1)S(1)}, bf16[768,128]{1,0:T(8,128)(2,1)S(1)}, u32[]{:S(2)}, u32[]{:S(2)}) collective-permute-start(bf16[768,128]{1,0:T(8,128)(2,1)S(1)} %distant.3.v_in), channel_id=1, source_target_pairs={{8,16},{16,8},{9,17},{17,9},{10,18},{18,10},{11,19},{19,11},{12,20... | collective-permute-start | bytes 589832 | tf_op jit(solution)/shard_map/ppermute | solution.py:274
  70.0 8.8 %collective-permute-start.21 = (bf16[768,128]{1,0:T(8,128)(2,1)S(1)}, bf16[768,128]{1,0:T(8,128)(2,1)S(1)}, u32[]{:S(2)}, u32[]{:S(2)}) collective-permute-start(bf16[768,128]{1,0:T(8,128)(2,1)S(1)} %distant.3.v_in), channel_id=1, source_target_pairs={{8,0},{16,24},{9,1},{17,25},{10,2},{18,26},{11,3},{19,27},{12,4},{... | collective-permute-start | bytes 589832 | tf_op jit(solution)/shard_map/ppermute | solution.py:274
  74.4 9.5 %collective-permute-start.13 = (bf16[784,128]{1,0:T(8,128)(2,1)S(1)}, bf16[784,128]{1,0:T(8,128)(2,1)S(1)}, u32[]{:S(2)}, u32[]{:S(2)}) collective-permute-start(bf16[784,128]{1,0:T(8,128)(2,1)S(1)} %distant.2.k_in), channel_id=1, source_target_pairs={{8,16},{16,8},{9,17},{17,9},{10,18},{18,10},{11,19},{19,11},{12,20... | collective-permute-start | bytes 602120 | tf_op jit(solution)/shard_map/ppermute | solution.py:274
  76.9 6.9 %collective-permute-start.19 = (bf16[768,128]{1,0:T(8,128)(2,1)S(1)}, bf16[768,128]{1,0:T(8,128)(2,1)S(1)}, u32[]{:S(2)}, u32[]{:S(2)}) collective-permute-start(bf16[768,128]{1,0:T(8,128)(2,1)S(1)} %collective-permute-done.17.v_across), channel_id=1, source_target_pairs={{8,0},{16,24},{9,1},{17,25},{10,2},{18,26},{11,3},{19,27},{12,4},{... | collective-permute-start | bytes 589832 | tf_op jit(solution)/shard_map/ppermute | solution.py:274

commit v12 on v11

--- a/solution.py
+++ b/solution.py
@@ -364,9 +364,8 @@
     keys_far, keys_out, keys_across = send(keys, LEAP), send(keys, OUTWARD), send(keys, ACROSS)
     values = finish(1, value_distant, value_parts, value_bias)
     values_across = send(values, ACROSS)
-    keys_out, values_after = tie((keys_out, values))
-    values_out = send(values_after, OUTWARD)
-    values_across, keys_far = tie((values_across, keys_far))
+    values_out = send(values, OUTWARD)
+    values_across, keys_far, keys_out = tie((values_across, keys_far, keys_out))
     values_far = send(values_across, OUTWARD)
     return (
         (keys, keys_out, keys_across, keys_far),

time: 92.3 us -> 88.4 us (0.958)
  starting transfers between devices: 35.6 us -> 32 us
    ppermute x15, starting transfers between devices: 29.2 us -> 26.8 us  [send(): return lax.ppermute(x, 'pre', pairs)]
    ppermute x7, waiting for transfers between devices: 2.04 us -> 3.71 us  [trade(): lax.ppermute(x, ('dec', 'tp'), [(m, m ^ apart) for m in range(PIECES)])]
    ppermute x7, starting transfers between devices: 6.39 us -> 5.21 us  [trade(): lax.ppermute(x, ('dec', 'tp'), [(m, m ^ apart) for m in range(PIECES)])]
    ppermute x15, waiting for transfers between devices: 21.4 us -> 20.3 us  [send(): return lax.ppermute(x, 'pre', pairs)]
  transfers between devices with their start and end apart: 22 -> 22, of which waited for: 7 -> 6; matrix products, arithmetic and copies ran while one was open for 1% -> 1% of each run, Pallas kernels for 23% -> 24%
where the time goes in v12:
time: 88.4 us; the launch traced here: 87.7 us
  starting transfers between devices  32 us (36%)
  Pallas kernels  27.8 us (31%)
  waiting for transfers between devices  24 us (27%)
  local copies, waits for them, and re-layouts  2.6 us (3%)
  between operations  1.16 us (1%)
    ppermute x15, starting transfers between devices, send(): return lax.ppermute(x, 'pre', pairs)  26.8 us
    ppermute x15, waiting for transfers between devices, send(): return lax.ppermute(x, 'pre', pairs)  20.3 us
    pallas_call x6, Pallas kernels, call_project(): pl.pallas_call(kernel, in_specs=[SCALAR] + [HELD] * held + [FAST] * (len(...  15.9 us
    pallas_call x1, Pallas kernels, attention_of_pairs(): pl.pallas_call(functools.partial(far_kernel, heads), in_specs=[SCALAR, HE...  6.79 us
    ppermute x7, starting transfers between devices, trade(): lax.ppermute(x, ('dec', 'tp'), [(m, m ^ apart) for m in range(PIECES)])  5.21 us
    pallas_call x1, Pallas kernels, attention_of_pairs(): pl.pallas_call(functools.partial(own_kernel, heads), in_specs=[SCALAR, HE...  5.06 us
    ppermute x7, waiting for transfers between devices, trade(): lax.ppermute(x, ('dec', 'tp'), [(m, m ^ apart) for m in range(PIECES)])  3.71 us
  transfers between devices with their start and end apart: 22, of which 6 were waited for; matrix products, arithmetic and copies ran while one was open for 1% of the time, Pallas kernels for 24%

profile of v12, /device:TPU:16, one launch (start us, length us, event | category | flops | bytes accessed | tf_op | source)
XLA Modules:
  0.0 87.7 jit_solution(8069337448521532719)
XLA Ops:
  0.6 2.4 %collective-permute-start.1 = (bf16[2048,128]{1,0:T(8,128)(2,1)}, bf16[2048,128]{1,0:T(8,128)(2,1)S(1)}, u32[]{:S(2)}, u32[]{:S(2)}) collective-permute-start(bf16[2048,128]{1,0:T(8,128)(2,1)} %kw_ref.1), channel_id=1, source_target_pairs={{8,16},{16,8},{9,17},{17,9},{10,18},{18,10},{11,19},{19,11},{12,20... | collective-permute-start | bytes 1572872 | tf_op jit(solution)/shard_map/ppermute | solution.py:274
  3.0 1.0 %constant_dynamic-slice_fusion = bf16[384,512]{1,0:T(8,128)(2,1)S(1)} fusion(bf16[384,8192]{1,0:T(8,128)(2,1)} %h_ref.11, s32[]{:T(128)S(6)} %select_n.3), kind=kLoop, calls=%fused_computation.3 | loop fusion | bytes 786436 | tf_op jit(solution)/shard_map/dynamic_slice | solution.py:280
  4.0 1.3 %collective-permute-start = (bf16[384,512]{1,0:T(8,128)(2,1)S(1)}, bf16[384,512]{1,0:T(8,128)(2,1)S(1)}, u32[]{:S(2)}, u32[]{:S(2)}) collective-permute-start(bf16[384,512]{1,0:T(8,128)(2,1)S(1)} %constant_dynamic-slice_fusion), channel_id=1, source_target_pairs={{0,8},{24,16},{1,9},{25,17},{2,10},{26,18},{3,11},{27,19},{4,12},{... | collective-permute-start | bytes 1179656 | tf_op jit(solution)/shard_map/ppermute | solution.py:274
  5.3 0.0 copy-start.6
  5.4 0.0 copy-start.7
  5.4 0.0 copy-start.8
  5.4 2.4 %near.1.before_ref = f32[384,256]{1,0:T(8,128)S(1)} custom-call(s32[1]{0:T(128)} %bitcast.place.info, bf16[384,8192]{1,0:T(8,128)(2,1)} %h_ref.11, bf16[2048,128]{1,0:T(8,128)(2,1)} %kw_ref.1, bf16[2048,128]{1,0:T(8,128)(2,1)} %vw_ref.1), custom_call_target="tpu_custom_call" | custom-call | tf_op jit(solution)/shard_map/near/pallas_call | solution.py:242
  7.7 8.8 %collective-permute-done.refs_0_ = bf16[384,512]{1,0:T(8,128)(2,1)S(1)} collective-permute-done((bf16[384,512]{1,0:T(8,128)(2,1)S(1)}, bf16[384,512]{1,0:T(8,128)(2,1)S(1)}, u32[]{:S(2)}, u32[]{:S(2)}) %collective-permute-start) | collective-permute-done | bytes 393248 | tf_op jit(solution)/shard_map/ppermute | solution.py:274
  16.5 0.0 collective-permute-done.1.kw_ref
  16.5 0.1 collective-permute-start.3
  16.6 0.7 copy-done.4
  17.3 3.5 %collective-permute-start.4 = (bf16[2048,128]{1,0:T(8,128)(2,1)S(1)}, bf16[2048,128]{1,0:T(8,128)(2,1)S(1)}, u32[]{:S(2)}, u32[]{:S(2)}) collective-permute-start(bf16[2048,128]{1,0:T(8,128)(2,1)S(1)} %copy-done.7), channel_id=1, source_target_pairs={{8,16},{16,8},{9,17},{17,9},{10,18},{18,10},{11,19},{19,11},{12,20... | collective-permute-start | bytes 1572872 | tf_op jit(solution)/shard_map/ppermute | solution.py:274
  20.8 2.5 %collective-permute-start.11 = (bf16[384,512]{1,0:T(8,128)(2,1)S(1)}, bf16[384,512]{1,0:T(8,128)(2,1)S(1)}, u32[]{:S(2)}, u32[]{:S(2)}) collective-permute-start(bf16[384,512]{1,0:T(8,128)(2,1)S(1)} %collective-permute-done.refs_0_), channel_id=1, source_target_pairs={{0,6},{1,7},{2,4},{3,5},{4,2},{5,3},{6,0},{7,1},{8,14},{9,15},{10,... | collective-permute-start | bytes 1179656 | tf_op jit(solution)/shard_map/ppermute | solution.py:277
  23.3 0.5 collective-permute-start.8
  23.8 7.7 %collective-permute-done.3.w_ref = bf16[2048,128]{1,0:T(8,128)(2,1)} collective-permute-done((bf16[2048,128]{1,0:T(8,128)(2,1)S(1)}, bf16[2048,128]{1,0:T(8,128)(2,1)}, u32[]{:S(2)}, u32[]{:S(2)}) %collective-permute-start.3) | collective-permute-done | bytes 524320 | tf_op jit(solution)/shard_map/ppermute | solution.py:274
  31.6 0.3 collective-permute-done.4.vw_ref
  31.9 0.8 copy-done.5
  32.7 3.3 %collective-permute-start.5 = (bf16[2048,128]{1,0:T(8,128)(2,1)}, bf16[2048,128]{1,0:T(8,128)(2,1)}, u32[]{:S(2)}, u32[]{:S(2)}) collective-permute-start(bf16[2048,128]{1,0:T(8,128)(2,1)} %collective-permute-done.3.w_ref), channel_id=1, source_target_pairs={{8,16},{16,8},{9,17},{17,9},{10,18},{18,10},{11,19},{19,11},{12,20... | collective-permute-start | bytes 1572872 | tf_op jit(solution)/shard_map/ppermute | solution.py:274
  36.0 0.1 collective-permute-start.7
  36.0 1.6 %collective-permute-start.2 = (bf16[384,512]{1,0:T(8,128)(2,1)S(1)}, bf16[384,512]{1,0:T(8,128)(2,1)S(1)}, u32[]{:S(2)}, u32[]{:S(2)}) collective-permute-start(bf16[384,512]{1,0:T(8,128)(2,1)S(1)} %collective-permute-done.refs_0_), channel_id=1, source_target_pairs={{0,4},{1,5},{2,6},{3,7},{4,0},{5,1},{6,2},{7,3},{8,12},{9,13},{10,... | collective-permute-start | bytes 1179656 | tf_op jit(solution)/shard_map/ppermute | solution.py:277
  37.7 2.2 %partial.2.near_ref = f32[392,128]{1,0:T(8,128)S(1)} custom-call(s32[1]{0:T(128)} %bitcast.6.place, bf16[384,8192]{1,0:T(8,128)(2,1)} %h_ref.11, bf16[2048,128]{1,0:T(8,128)(2,1)} %collective-permute-done.3.w_ref, f32[384,256]{1,0:T(8,128)S(1)} %near.1.before_ref, f32[8,128]{1,0:T(8,128)S(1)} %pad.7.owner_ref), custom_call_target="tpu_custom_call" | custom-call | tf_op jit(solution)/shard_map/partial/pallas_call | solution.py:242
  39.8 0.0 copy-start
  39.9 0.0 collective-permute-done.8.refs_2_
  39.9 1.3 %collective-permute-start.6 = (f32[392,128]{1,0:T(8,128)S(1)}, f32[392,128]{1,0:T(8,128)}, u32[]{:S(2)}, u32[]{:S(2)}) collective-permute-start(f32[392,128]{1,0:T(8,128)S(1)} %partial.2.near_ref), channel_id=1, source_target_pairs={{0,8},{24,16},{1,9},{25,17},{2,10},{26,18},{3,11},{27,19},{4,12},{... | collective-permute-start | bytes 602120 | tf_op jit(solution)/shard_map/ppermute | solution.py:274
  41.2 2.7 %collective-permute-start.15 = (bf16[2048,128]{1,0:T(8,128)(2,1)}, bf16[2048,128]{1,0:T(8,128)(2,1)}, u32[]{:S(2)}, u32[]{:S(2)}) collective-permute-start(bf16[2048,128]{1,0:T(8,128)(2,1)} %collective-permute-done.14.w_ref), channel_id=1, source_target_pairs={{8,16},{16,8},{9,17},{17,9},{10,18},{18,10},{11,19},{19,11},{12,20... | collective-permute-start | bytes 1572872 | tf_op jit(solution)/shard_map/ppermute | solution.py:274
  43.9 3.7 %collective-permute-done.2.refs_4_ = bf16[384,512]{1,0:T(8,128)(2,1)S(1)} collective-permute-done((bf16[384,512]{1,0:T(8,128)(2,1)S(1)}, bf16[384,512]{1,0:T(8,128)(2,1)S(1)}, u32[]{:S(2)}, u32[]{:S(2)}) %collective-permute-start.2) | collective-permute-done | bytes 393248 | tf_op jit(solution)/shard_map/ppermute | solution.py:277
  47.6 0.0 collective-permute-start.12
  47.6 1.3 %collective-permute-done.6.outer_ref = f32[392,128]{1,0:T(8,128)} collective-permute-done((f32[392,128]{1,0:T(8,128)S(1)}, f32[392,128]{1,0:T(8,128)}, u32[]{:S(2)}, u32[]{:S(2)}) %collective-permute-start.6) | collective-permute-done | bytes 200736 | tf_op jit(solution)/shard_map/ppermute | solution.py:274
  48.9 0.0 collective-permute-start.9
  48.9 0.5 collective-permute-start.10
  49.4 2.2 %partial.3.near_ref = f32[384,128]{1,0:T(8,128)S(1)} custom-call(s32[1]{0:T(128)} %bitcast.6.place, bf16[384,8192]{1,0:T(8,128)(2,1)} %h_ref.11, bf16[2048,128]{1,0:T(8,128)(2,1)} %collective-permute-done.14.w_ref, f32[384,256]{1,0:T(8,128)S(1)} %near.1.before_ref, f32[8,128]{1,0:T(8,128)S(1)} %pad.7.owner_ref), custom_call_target="tpu_custom_call" | custom-call | tf_op jit(solution)/shard_map/partial/pallas_call | solution.py:242
  51.6 1.3 %collective-permute-start.16 = (f32[384,128]{1,0:T(8,128)S(1)}, f32[384,128]{1,0:T(8,128)S(1)}, u32[]{:S(2)}, u32[]{:S(2)}) collective-permute-start(f32[384,128]{1,0:T(8,128)S(1)} %partial.3.near_ref), channel_id=1, source_target_pairs={{0,8},{24,16},{1,9},{25,17},{2,10},{26,18},{3,11},{27,19},{4,12},{... | collective-permute-start | bytes 589832 | tf_op jit(solution)/shard_map/ppermute | solution.py:274
  52.9 0.1 add_add_fusion.place
  53.0 0.1 add_add_fusion.1.place
  53.1 3.0 %facing.1.facing_ref = f32[768,256]{1,0:T(8,128)S(1)} custom-call(s32[4]{0:T(128)S(1)} %add_add_fusion.1.place, bf16[384,8192]{1,0:T(8,128)(2,1)} %h_ref.11, bf16[2048,128]{1,0:T(8,128)(2,1)} %copy-done.4, bf16[2048,128]{1,0:T(8,128)(2,1)} %copy-done.5, bf16[384,512]{1,0:T(8,128)(2,1)S(1)} %collective-permute-done.refs_0_, ...), custom_call_target="tpu_custom_call" | custom-call | tf_op jit(solution)/shard_map/facing/pallas_call | solution.py:242
  56.1 0.0 copy-start.3
  56.1 3.5 %distant.2.k_in = bf16[784,128]{1,0:T(8,128)(2,1)S(1)} custom-call(s32[4]{0:T(128)S(1)} %add_add_fusion.place, bf16[384,8192]{1,0:T(8,128)(2,1)} %h_ref.11, bf16[2048,128]{1,0:T(8,128)(2,1)} %collective-permute-done.5.w_ref, f32[392,128]{1,0:T(8,128)} %copy-done, f32[392,128]{1,0:T(8,128)} %collective-permute-done.6.outer_ref, ...), custom_call_target="tpu_custom_call" | custom-call | tf_op jit(solution)/shard_map/distant/pallas_call | solution.py:242
  59.6 1.3 %collective-permute-start.19 = (bf16[784,128]{1,0:T(8,128)(2,1)S(1)}, bf16[784,128]{1,0:T(8,128)(2,1)S(1)}, u32[]{:S(2)}, u32[]{:S(2)}) collective-permute-start(bf16[784,128]{1,0:T(8,128)(2,1)S(1)} %distant.2.k_in), channel_id=1, source_target_pairs={{8,0},{16,24},{9,1},{17,25},{10,2},{18,26},{11,3},{19,27},{12,4},{... | collective-permute-start | bytes 602120 | tf_op jit(solution)/shard_map/ppermute | solution.py:274
  60.9 1.3 %collective-permute-start.18 = (bf16[784,128]{1,0:T(8,128)(2,1)S(1)}, bf16[784,128]{1,0:T(8,128)(2,1)S(1)}, u32[]{:S(2)}, u32[]{:S(2)}) collective-permute-start(bf16[784,128]{1,0:T(8,128)(2,1)S(1)} %distant.2.k_in), channel_id=1, source_target_pairs={{8,24},{16,0},{9,25},{17,1},{10,26},{18,2},{11,27},{19,3},{12,28},... | collective-permute-start | bytes 602120 | tf_op jit(solution)/shard_map/ppermute | solution.py:274
  62.2 0.0 copy-start.1
  62.2 2.8 %distant.3.v_in = bf16[768,128]{1,0:T(8,128)(2,1)S(1)} custom-call(s32[4]{0:T(128)S(1)} %add_add_fusion.place, bf16[384,8192]{1,0:T(8,128)(2,1)} %h_ref.11, bf16[2048,128]{1,0:T(8,128)(2,1)} %collective-permute-done.15.w_ref, f32[384,128]{1,0:T(8,128)S(1)} %partial.3.near_ref, f32[384,128]{1,0:T(8,128)S(1)} %collective-permute-done.16.outer_ref, ...), custom_call_target="tpu_custom_call" | custom-call | tf_op jit(solution)/shard_map/distant/pallas_call | solution.py:242
  65.1 2.6 %collective-permute-start.17 = (bf16[768,128]{1,0:T(8,128)(2,1)S(1)}, bf16[768,128]{1,0:T(8,128)(2,1)S(1)}, u32[]{:S(2)}, u32[]{:S(2)}) collective-permute-start(bf16[768,128]{1,0:T(8,128)(2,1)S(1)} %distant.3.v_in), channel_id=1, source_target_pairs={{8,16},{16,8},{9,17},{17,9},{10,18},{18,10},{11,19},{19,11},{12,20... | collective-permute-start | bytes 589832 | tf_op jit(solution)/shard_map/ppermute | solution.py:274
  67.6 1.3 %collective-permute-start.21 = (bf16[768,128]{1,0:T(8,128)(2,1)S(1)}, bf16[768,128]{1,0:T(8,128)(2,1)S(1)}, u32[]{:S(2)}, u32[]{:S(2)}) collective-permute-start(bf16[768,128]{1,0:T(8,128)(2,1)S(1)} %distant.3.v_in), channel_id=1, source_target_pairs={{8,0},{16,24},{9,1},{17,25},{10,2},{18,26},{11,3},{19,27},{12,4},{... | collective-permute-start | bytes 589832 | tf_op jit(solution)/shard_map/ppermute | solution.py:274
  68.9 3.3 %collective-permute-start.13 = (bf16[784,128]{1,0:T(8,128)(2,1)S(1)}, bf16[784,128]{1,0:T(8,128)(2,1)S(1)}, u32[]{:S(2)}, u32[]{:S(2)}) collective-permute-start(bf16[784,128]{1,0:T(8,128)(2,1)S(1)} %distant.2.k_in), channel_id=1, source_target_pairs={{8,16},{16,8},{9,17},{17,9},{10,18},{18,10},{11,19},{19,11},{12,20... | collective-permute-start | bytes 602120 | tf_op jit(solution)/shard_map/ppermute | solution.py:274
  72.2 2.2 %collective-permute-done.17.v_across = bf16[768,128]{1,0:T(8,128)(2,1)S(1)} collective-permute-done((bf16[768,128]{1,0:T(8,128)(2,1)S(1)}, bf16[768,128]{1,0:T(8,128)(2,1)S(1)}, u32[]{:S(2)}, u32[]{:S(2)}) %collective-permute-start.17) | collective-permute-done | bytes 196640 | tf_op jit(solution)/shard_map/ppermute | solution.py:274
  74.4 1.3 %collective-permute-start.20 = (bf16[768,128]{1,0:T(8,128)(2,1)S(1)}, bf16[768,128]{1,0:T(8,128)(2,1)S(1)}, u32[]{:S(2)}, u32[]{:S(2)}) collective-permute-start(bf16[768,128]{1,0:T(8,128)(2,1)S(1)} %collective-permute-done.17.v_across), channel_id=1, source_target_pairs={{8,0},{16,24},{9,1},{17,25},{10,2},{18,26},{11,3},{19,27},{12,4},{... | collective-permute-start | bytes 589832 | tf_op jit(solution)/shard_map/ppermute | solution.py:274
  75.7 5.1 %attend_own.1 = (f32[8,384,1]{2,1,0:T(8,128)S(1)}, f32[8,384,1]{2,1,0:T(8,128)S(1)}, f32[8,384,128]{2,1,0:T(8,128)S(1)}, bf16[2,192,256]{2,1,0:T(8,128)(2,1)S(1)}) custom-call(s32[1]{0:T(128)} %bitcast.place.info, bf16[384,1024]{1,0:T(8,128)(2,1)} %q_ref.3, s32[12,128]{1,0:T(8,128)S(1)} %bitcast.13, bf16[784,128]{1,0:T(8,128)(2,1)S(1)} %distant.2.k_in, ...), custom_call_target="tpu_custom_call" | custom-call | flops 1207959552 | bytes 18874368 | tf_op jit(solution)/shard_map/attend_own/pallas_call | solution.py:584
  80.8 6.8 %attend_far.1 = (bf16[384,1024]{1,0:T(8,128)(2,1)}, bf16[4,192,256]{2,1,0:T(8,128)(2,1)}) custom-call(s32[1]{0:T(128)} %bitcast.place.info, bf16[384,1024]{1,0:T(8,128)(2,1)} %q_ref.3, s32[12,128]{1,0:T(8,128)S(1)} %bitcast.14, bf16[784,128]{1,0:T(8,128)(2,1)S(1)} %collective-permute-done.13.k_across, bf16[784,128]{1,0:T(8,128)(2,1)S(1)} %collective-permute-done.18.k_far, ...), custom_call_target="tpu_custom_call" | custom-call | flops 1207959552 | bytes 18874368 | tf_op jit(solution)/shard_map/attend_far/pallas_call | solution.py:599
  (28 shorter events, 0.1 us)
Async XLA Ops:
  0.6 15.9 %collective-permute-start.1 = (bf16[2048,128]{1,0:T(8,128)(2,1)}, bf16[2048,128]{1,0:T(8,128)(2,1)S(1)}, u32[]{:S(2)}, u32[]{:S(2)}) collective-permute-start(bf16[2048,128]{1,0:T(8,128)(2,1)} %kw_ref.1), channel_id=1, source_target_pairs={{8,16},{16,8},{9,17},{17,9},{10,18},{18,10},{11,19},{19,11},{12,20... | collective-permute-start | bytes 1572872 | tf_op jit(solution)/shard_map/ppermute | solution.py:274
  4.0 12.5 %collective-permute-start = (bf16[384,512]{1,0:T(8,128)(2,1)S(1)}, bf16[384,512]{1,0:T(8,128)(2,1)S(1)}, u32[]{:S(2)}, u32[]{:S(2)}) collective-permute-start(bf16[384,512]{1,0:T(8,128)(2,1)S(1)} %constant_dynamic-slice_fusion), channel_id=1, source_target_pairs={{0,8},{24,16},{1,9},{25,17},{2,10},{26,18},{3,11},{27,19},{4,12},{... | collective-permute-start | bytes 1179656 | tf_op jit(solution)/shard_map/ppermute | solution.py:274
  5.3 11.2 %copy-start.6 = (bf16[2048,128]{1,0:T(8,128)(2,1)S(1)}, bf16[2048,128]{1,0:T(8,128)(2,1)}, u32[]{:S(2)}) copy-start(bf16[2048,128]{1,0:T(8,128)(2,1)} %kw_ref.1) | copy-start | bytes 1572868
  5.4 12.0 %copy-start.7 = (bf16[2048,128]{1,0:T(8,128)(2,1)S(1)}, bf16[2048,128]{1,0:T(8,128)(2,1)}, u32[]{:S(2)}) copy-start(bf16[2048,128]{1,0:T(8,128)(2,1)} %vw_ref.1) | copy-start | bytes 1572868
  5.4 32.3 %copy-start.8 = (s32[24,1]{0,1:T(1,128)S(1)}, s32[24,1]{0,1:T(1,128)}, u32[]{:S(2)}) copy-start(s32[24,1]{0,1:T(1,128)} %param.15) | copy-start | bytes 292
  16.5 0.8 copy-start.4
  16.5 15.0 %collective-permute-start.3 = (bf16[2048,128]{1,0:T(8,128)(2,1)S(1)}, bf16[2048,128]{1,0:T(8,128)(2,1)}, u32[]{:S(2)}, u32[]{:S(2)}) collective-permute-start(bf16[2048,128]{1,0:T(8,128)(2,1)S(1)} %copy-done.6), channel_id=1, source_target_pairs={{0,8},{8,0},{16,24},{24,16},{1,9},{9,1},{17,25},{25,17},{2,10},{10... | collective-permute-start | bytes 1572872 | tf_op jit(solution)/shard_map/ppermute | solution.py:274
  17.3 14.6 %collective-permute-start.4 = (bf16[2048,128]{1,0:T(8,128)(2,1)S(1)}, bf16[2048,128]{1,0:T(8,128)(2,1)S(1)}, u32[]{:S(2)}, u32[]{:S(2)}) collective-permute-start(bf16[2048,128]{1,0:T(8,128)(2,1)S(1)} %copy-done.7), channel_id=1, source_target_pairs={{8,16},{16,8},{9,17},{17,9},{10,18},{18,10},{11,19},{19,11},{12,20... | collective-permute-start | bytes 1572872 | tf_op jit(solution)/shard_map/ppermute | solution.py:274
  20.8 15.2 %collective-permute-start.11 = (bf16[384,512]{1,0:T(8,128)(2,1)S(1)}, bf16[384,512]{1,0:T(8,128)(2,1)S(1)}, u32[]{:S(2)}, u32[]{:S(2)}) collective-permute-start(bf16[384,512]{1,0:T(8,128)(2,1)S(1)} %collective-permute-done.refs_0_), channel_id=1, source_target_pairs={{0,6},{1,7},{2,4},{3,5},{4,2},{5,3},{6,0},{7,1},{8,14},{9,15},{10,... | collective-permute-start | bytes 1179656 | tf_op jit(solution)/shard_map/ppermute | solution.py:277
  23.3 17.9 %collective-permute-start.14 = (bf16[2048,128]{1,0:T(8,128)(2,1)S(1)}, bf16[2048,128]{1,0:T(8,128)(2,1)}, u32[]{:S(2)}, u32[]{:S(2)}) collective-permute-start(bf16[2048,128]{1,0:T(8,128)(2,1)S(1)} %copy-done.7), channel_id=1, source_target_pairs={{0,8},{8,0},{16,24},{24,16},{1,9},{9,1},{17,25},{25,17},{2,10},{10... | collective-permute-start | bytes 1572872 | tf_op jit(solution)/shard_map/ppermute | solution.py:274
  23.3 16.5 %collective-permute-start.8 = (bf16[384,512]{1,0:T(8,128)(2,1)S(1)}, bf16[384,512]{1,0:T(8,128)(2,1)S(1)}, u32[]{:S(2)}, u32[]{:S(2)}) collective-permute-start(bf16[384,512]{1,0:T(8,128)(2,1)S(1)} %collective-permute-done.refs_0_), channel_id=1, source_target_pairs={{0,2},{1,3},{2,0},{3,1},{4,6},{5,7},{6,4},{7,5},{8,10},{9,11},{10,... | collective-permute-start | bytes 1179656 | tf_op jit(solution)/shard_map/ppermute | solution.py:277
  31.9 0.8 copy-start.5
  32.7 16.2 %collective-permute-start.5 = (bf16[2048,128]{1,0:T(8,128)(2,1)}, bf16[2048,128]{1,0:T(8,128)(2,1)}, u32[]{:S(2)}, u32[]{:S(2)}) collective-permute-start(bf16[2048,128]{1,0:T(8,128)(2,1)} %collective-permute-done.3.w_ref), channel_id=1, source_target_pairs={{8,16},{16,8},{9,17},{17,9},{10,18},{18,10},{11,19},{19,11},{12,20... | collective-permute-start | bytes 1572872 | tf_op jit(solution)/shard_map/ppermute | solution.py:274
  36.0 15.7 %collective-permute-start.7 = (bf16[384,512]{1,0:T(8,128)(2,1)S(1)}, bf16[384,512]{1,0:T(8,128)(2,1)S(1)}, u32[]{:S(2)}, u32[]{:S(2)}) collective-permute-start(bf16[384,512]{1,0:T(8,128)(2,1)S(1)} %collective-permute-done.refs_0_), channel_id=1, source_target_pairs={{0,1},{1,0},{2,3},{3,2},{4,5},{5,4},{6,7},{7,6},{8,9},{9,8},{10,11... | collective-permute-start | bytes 1179656 | tf_op jit(solution)/shard_map/ppermute | solution.py:277
  36.0 11.5 %collective-permute-start.2 = (bf16[384,512]{1,0:T(8,128)(2,1)S(1)}, bf16[384,512]{1,0:T(8,128)(2,1)S(1)}, u32[]{:S(2)}, u32[]{:S(2)}) collective-permute-start(bf16[384,512]{1,0:T(8,128)(2,1)S(1)} %collective-permute-done.refs_0_), channel_id=1, source_target_pairs={{0,4},{1,5},{2,6},{3,7},{4,0},{5,1},{6,2},{7,3},{8,12},{9,13},{10,... | collective-permute-start | bytes 1179656 | tf_op jit(solution)/shard_map/ppermute | solution.py:277
  39.8 9.1 %copy-start = (f32[392,128]{1,0:T(8,128)}, f32[392,128]{1,0:T(8,128)S(1)}, u32[]{:S(2)}) copy-start(f32[392,128]{1,0:T(8,128)S(1)} %partial.2.near_ref) | copy-start | bytes 602116
  39.9 9.1 %collective-permute-start.6 = (f32[392,128]{1,0:T(8,128)S(1)}, f32[392,128]{1,0:T(8,128)}, u32[]{:S(2)}, u32[]{:S(2)}) collective-permute-start(f32[392,128]{1,0:T(8,128)S(1)} %partial.2.near_ref), channel_id=1, source_target_pairs={{0,8},{24,16},{1,9},{25,17},{2,10},{26,18},{3,11},{27,19},{4,12},{... | collective-permute-start | bytes 602120 | tf_op jit(solution)/shard_map/ppermute | solution.py:274
  41.2 21.0 %collective-permute-start.15 = (bf16[2048,128]{1,0:T(8,128)(2,1)}, bf16[2048,128]{1,0:T(8,128)(2,1)}, u32[]{:S(2)}, u32[]{:S(2)}) collective-permute-start(bf16[2048,128]{1,0:T(8,128)(2,1)} %collective-permute-done.14.w_ref), channel_id=1, source_target_pairs={{8,16},{16,8},{9,17},{17,9},{10,18},{18,10},{11,19},{19,11},{12,20... | collective-permute-start | bytes 1572872 | tf_op jit(solution)/shard_map/ppermute | solution.py:274
  47.6 5.5 %collective-permute-start.12 = (bf16[384,512]{1,0:T(8,128)(2,1)S(1)}, bf16[384,512]{1,0:T(8,128)(2,1)S(1)}, u32[]{:S(2)}, u32[]{:S(2)}) collective-permute-start(bf16[384,512]{1,0:T(8,128)(2,1)S(1)} %collective-permute-done.11.refs_6_), channel_id=1, source_target_pairs={{0,1},{1,0},{2,3},{3,2},{4,5},{5,4},{6,7},{7,6},{8,9},{9,8},{10,11... | collective-permute-start | bytes 1179656 | tf_op jit(solution)/shard_map/ppermute | solution.py:277
  48.9 4.2 %collective-permute-start.9 = (bf16[384,512]{1,0:T(8,128)(2,1)S(1)}, bf16[384,512]{1,0:T(8,128)(2,1)S(1)}, u32[]{:S(2)}, u32[]{:S(2)}) collective-permute-start(bf16[384,512]{1,0:T(8,128)(2,1)S(1)} %collective-permute-done.8.refs_2_), channel_id=1, source_target_pairs={{0,1},{1,0},{2,3},{3,2},{4,5},{5,4},{6,7},{7,6},{8,9},{9,8},{10,11... | collective-permute-start | bytes 1179656 | tf_op jit(solution)/shard_map/ppermute | solution.py:277
  48.9 4.2 %collective-permute-start.10 = (bf16[384,512]{1,0:T(8,128)(2,1)S(1)}, bf16[384,512]{1,0:T(8,128)(2,1)S(1)}, u32[]{:S(2)}, u32[]{:S(2)}) collective-permute-start(bf16[384,512]{1,0:T(8,128)(2,1)S(1)} %collective-permute-done.2.refs_4_), channel_id=1, source_target_pairs={{0,1},{1,0},{2,3},{3,2},{4,5},{5,4},{6,7},{7,6},{8,9},{9,8},{10,11... | collective-permute-start | bytes 1179656 | tf_op jit(solution)/shard_map/ppermute | solution.py:277
  51.6 10.5 %collective-permute-start.16 = (f32[384,128]{1,0:T(8,128)S(1)}, f32[384,128]{1,0:T(8,128)S(1)}, u32[]{:S(2)}, u32[]{:S(2)}) collective-permute-start(f32[384,128]{1,0:T(8,128)S(1)} %partial.3.near_ref), channel_id=1, source_target_pairs={{0,8},{24,16},{1,9},{25,17},{2,10},{26,18},{3,11},{27,19},{4,12},{... | collective-permute-start | bytes 589832 | tf_op jit(solution)/shard_map/ppermute | solution.py:274
  53.1 3.0 %copy-start.2 = (bf16[128]{0:T(256)(128)(2,1)S(1)}, bf16[128]{0:T(256)(128)(2,1)}, u32[]{:S(2)}) copy-start(bf16[128]{0:T(256)(128)(2,1)} %param.12) | copy-start | bytes 772
  56.1 6.1 %copy-start.3 = (bf16[128]{0:T(256)(128)(2,1)S(1)}, bf16[128]{0:T(256)(128)(2,1)}, u32[]{:S(2)}) copy-start(bf16[128]{0:T(256)(128)(2,1)} %param.13) | copy-start | bytes 772
  59.6 14.8 %collective-permute-start.19 = (bf16[784,128]{1,0:T(8,128)(2,1)S(1)}, bf16[784,128]{1,0:T(8,128)(2,1)S(1)}, u32[]{:S(2)}, u32[]{:S(2)}) collective-permute-start(bf16[784,128]{1,0:T(8,128)(2,1)S(1)} %distant.2.k_in), channel_id=1, source_target_pairs={{8,0},{16,24},{9,1},{17,25},{10,2},{18,26},{11,3},{19,27},{12,4},{... | collective-permute-start | bytes 602120 | tf_op jit(solution)/shard_map/ppermute | solution.py:274
  60.9 13.5 %collective-permute-start.18 = (bf16[784,128]{1,0:T(8,128)(2,1)S(1)}, bf16[784,128]{1,0:T(8,128)(2,1)S(1)}, u32[]{:S(2)}, u32[]{:S(2)}) collective-permute-start(bf16[784,128]{1,0:T(8,128)(2,1)S(1)} %distant.2.k_in), channel_id=1, source_target_pairs={{8,24},{16,0},{9,25},{17,1},{10,26},{18,2},{11,27},{19,3},{12,28},... | collective-permute-start | bytes 602120 | tf_op jit(solution)/shard_map/ppermute | solution.py:274
  62.2 13.5 %copy-start.1 = (s32[1536]{0:T(1024)S(1)}, s32[1536]{0:T(1024)}, u32[]{:S(2)}) copy-start(s32[1536]{0:T(1024)} %param.14) | copy-start | bytes 18436
  65.1 9.3 %collective-permute-start.17 = (bf16[768,128]{1,0:T(8,128)(2,1)S(1)}, bf16[768,128]{1,0:T(8,128)(2,1)S(1)}, u32[]{:S(2)}, u32[]{:S(2)}) collective-permute-start(bf16[768,128]{1,0:T(8,128)(2,1)S(1)} %distant.3.v_in), channel_id=1, source_target_pairs={{8,16},{16,8},{9,17},{17,9},{10,18},{18,10},{11,19},{19,11},{12,20... | collective-permute-start | bytes 589832 | tf_op jit(solution)/shard_map/ppermute | solution.py:274
  67.6 8.1 %collective-permute-start.21 = (bf16[768,128]{1,0:T(8,128)(2,1)S(1)}, bf16[768,128]{1,0:T(8,128)(2,1)S(1)}, u32[]{:S(2)}, u32[]{:S(2)}) collective-permute-start(bf16[768,128]{1,0:T(8,128)(2,1)S(1)} %distant.3.v_in), channel_id=1, source_target_pairs={{8,0},{16,24},{9,1},{17,25},{10,2},{18,26},{11,3},{19,27},{12,4},{... | collective-permute-start | bytes 589832 | tf_op jit(solution)/shard_map/ppermute | solution.py:274
  68.9 11.8 %collective-permute-start.13 = (bf16[784,128]{1,0:T(8,128)(2,1)S(1)}, bf16[784,128]{1,0:T(8,128)(2,1)S(1)}, u32[]{:S(2)}, u32[]{:S(2)}) collective-permute-start(bf16[784,128]{1,0:T(8,128)(2,1)S(1)} %distant.2.k_in), channel_id=1, source_target_pairs={{8,16},{16,8},{9,17},{17,9},{10,18},{18,10},{11,19},{19,11},{12,20... | collective-permute-start | bytes 602120 | tf_op jit(solution)/shard_map/ppermute | solution.py:274
  74.4 6.4 %collective-permute-start.20 = (bf16[768,128]{1,0:T(8,128)(2,1)S(1)}, bf16[768,128]{1,0:T(8,128)(2,1)S(1)}, u32[]{:S(2)}, u32[]{:S(2)}) collective-permute-start(bf16[768,128]{1,0:T(8,128)(2,1)S(1)} %collective-permute-done.17.v_across), channel_id=1, source_target_pairs={{8,0},{16,24},{9,1},{17,25},{10,2},{18,26},{11,3},{19,27},{12,4},{... | collective-permute-start | bytes 589832 | tf_op jit(solution)/shard_map/ppermute | solution.py:274

commit v13 on v12

--- a/solution.py
+++ b/solution.py
@@ -483,10 +483,11 @@
         top[g] = peak
         total[g] = sums[:, :1]
         mix[g] = mixed
+        if g == heads // 2:
+            owners.wait()
+            place_pages(index, span, named, held_k, held_v, cache_ref, laid)
 
     attend(q_buf, heads, keys, values, allowed, None, store)
-    owners.wait()
-    place_pages(index, span, named, held_k, held_v, cache_ref, laid)
 
 
 def far_kernel(

time: 88.4 us -> 88.8 us (level)
  no operation moved by 1% of the time
where the time goes in v13:
time: 88.8 us; the launch traced here: 88.2 us
  starting transfers between devices  32.2 us (36%)
  Pallas kernels  28 us (32%)
  waiting for transfers between devices  24 us (27%)
  local copies, waits for them, and re-layouts  2.6 us (3%)
  between operations  1.16 us (1%)
    ppermute x15, starting transfers between devices, send(): return lax.ppermute(x, 'pre', pairs)  27 us
    ppermute x15, waiting for transfers between devices, send(): return lax.ppermute(x, 'pre', pairs)  20.3 us
    pallas_call x6, Pallas kernels, call_project(): pl.pallas_call(kernel, in_specs=[SCALAR] + [HELD] * held + [FAST] * (len(...  15.9 us
    pallas_call x1, Pallas kernels, attention_of_pairs(): pl.pallas_call(functools.partial(far_kernel, heads), in_specs=[SCALAR, HE...  6.79 us
    pallas_call x1, Pallas kernels, attention_of_pairs(): pl.pallas_call(functools.partial(own_kernel, heads), in_specs=[SCALAR, HE...  5.31 us
    ppermute x7, starting transfers between devices, trade(): lax.ppermute(x, ('dec', 'tp'), [(m, m ^ apart) for m in range(PIECES)])  5.21 us
    ppermute x7, waiting for transfers between devices, trade(): lax.ppermute(x, ('dec', 'tp'), [(m, m ^ apart) for m in range(PIECES)])  3.71 us
  transfers between devices with their start and end apart: 22, of which 6 were waited for; matrix products, arithmetic and copies ran while one was open for 1% of the time, Pallas kernels for 24%

profile of v13, /device:TPU:16, one launch (start us, length us, event | category | flops | bytes accessed | tf_op | source)
XLA Modules:
  0.0 88.2 jit_solution(14727088526512437859)
XLA Ops:
  0.6 2.4 %collective-permute-start.1 = (bf16[2048,128]{1,0:T(8,128)(2,1)}, bf16[2048,128]{1,0:T(8,128)(2,1)S(1)}, u32[]{:S(2)}, u32[]{:S(2)}) collective-permute-start(bf16[2048,128]{1,0:T(8,128)(2,1)} %kw_ref.1), channel_id=1, source_target_pairs={{8,16},{16,8},{9,17},{17,9},{10,18},{18,10},{11,19},{19,11},{12,20... | collective-permute-start | bytes 1572872 | tf_op jit(solution)/shard_map/ppermute | solution.py:274
  3.0 1.0 %constant_dynamic-slice_fusion = bf16[384,512]{1,0:T(8,128)(2,1)S(1)} fusion(bf16[384,8192]{1,0:T(8,128)(2,1)} %h_ref.11, s32[]{:T(128)S(6)} %select_n.3), kind=kLoop, calls=%fused_computation.3 | loop fusion | bytes 786436 | tf_op jit(solution)/shard_map/dynamic_slice | solution.py:280
  4.0 1.3 %collective-permute-start = (bf16[384,512]{1,0:T(8,128)(2,1)S(1)}, bf16[384,512]{1,0:T(8,128)(2,1)S(1)}, u32[]{:S(2)}, u32[]{:S(2)}) collective-permute-start(bf16[384,512]{1,0:T(8,128)(2,1)S(1)} %constant_dynamic-slice_fusion), channel_id=1, source_target_pairs={{0,8},{24,16},{1,9},{25,17},{2,10},{26,18},{3,11},{27,19},{4,12},{... | collective-permute-start | bytes 1179656 | tf_op jit(solution)/shard_map/ppermute | solution.py:274
  5.3 0.0 copy-start.6
  5.4 0.0 copy-start.7
  5.4 0.0 copy-start.8
  5.4 2.4 %near.1.before_ref = f32[384,256]{1,0:T(8,128)S(1)} custom-call(s32[1]{0:T(128)} %bitcast.place.info, bf16[384,8192]{1,0:T(8,128)(2,1)} %h_ref.11, bf16[2048,128]{1,0:T(8,128)(2,1)} %kw_ref.1, bf16[2048,128]{1,0:T(8,128)(2,1)} %vw_ref.1), custom_call_target="tpu_custom_call" | custom-call | tf_op jit(solution)/shard_map/near/pallas_call | solution.py:242
  7.7 8.8 %collective-permute-done.refs_0_ = bf16[384,512]{1,0:T(8,128)(2,1)S(1)} collective-permute-done((bf16[384,512]{1,0:T(8,128)(2,1)S(1)}, bf16[384,512]{1,0:T(8,128)(2,1)S(1)}, u32[]{:S(2)}, u32[]{:S(2)}) %collective-permute-start) | collective-permute-done | bytes 393248 | tf_op jit(solution)/shard_map/ppermute | solution.py:274
  16.5 0.0 collective-permute-done.1.kw_ref
  16.5 0.1 collective-permute-start.3
  16.6 0.7 copy-done.4
  17.3 3.5 %collective-permute-start.4 = (bf16[2048,128]{1,0:T(8,128)(2,1)S(1)}, bf16[2048,128]{1,0:T(8,128)(2,1)S(1)}, u32[]{:S(2)}, u32[]{:S(2)}) collective-permute-start(bf16[2048,128]{1,0:T(8,128)(2,1)S(1)} %copy-done.7), channel_id=1, source_target_pairs={{8,16},{16,8},{9,17},{17,9},{10,18},{18,10},{11,19},{19,11},{12,20... | collective-permute-start | bytes 1572872 | tf_op jit(solution)/shard_map/ppermute | solution.py:274
  20.8 2.5 %collective-permute-start.11 = (bf16[384,512]{1,0:T(8,128)(2,1)S(1)}, bf16[384,512]{1,0:T(8,128)(2,1)S(1)}, u32[]{:S(2)}, u32[]{:S(2)}) collective-permute-start(bf16[384,512]{1,0:T(8,128)(2,1)S(1)} %collective-permute-done.refs_0_), channel_id=1, source_target_pairs={{0,6},{1,7},{2,4},{3,5},{4,2},{5,3},{6,0},{7,1},{8,14},{9,15},{10,... | collective-permute-start | bytes 1179656 | tf_op jit(solution)/shard_map/ppermute | solution.py:277
  23.3 0.5 collective-permute-start.8
  23.8 7.7 %collective-permute-done.3.w_ref = bf16[2048,128]{1,0:T(8,128)(2,1)} collective-permute-done((bf16[2048,128]{1,0:T(8,128)(2,1)S(1)}, bf16[2048,128]{1,0:T(8,128)(2,1)}, u32[]{:S(2)}, u32[]{:S(2)}) %collective-permute-start.3) | collective-permute-done | bytes 524320 | tf_op jit(solution)/shard_map/ppermute | solution.py:274
  31.6 0.3 collective-permute-done.4.vw_ref
  31.9 0.8 copy-done.5
  32.7 3.3 %collective-permute-start.5 = (bf16[2048,128]{1,0:T(8,128)(2,1)}, bf16[2048,128]{1,0:T(8,128)(2,1)}, u32[]{:S(2)}, u32[]{:S(2)}) collective-permute-start(bf16[2048,128]{1,0:T(8,128)(2,1)} %collective-permute-done.3.w_ref), channel_id=1, source_target_pairs={{8,16},{16,8},{9,17},{17,9},{10,18},{18,10},{11,19},{19,11},{12,20... | collective-permute-start | bytes 1572872 | tf_op jit(solution)/shard_map/ppermute | solution.py:274
  36.0 0.1 collective-permute-start.7
  36.0 1.6 %collective-permute-start.2 = (bf16[384,512]{1,0:T(8,128)(2,1)S(1)}, bf16[384,512]{1,0:T(8,128)(2,1)S(1)}, u32[]{:S(2)}, u32[]{:S(2)}) collective-permute-start(bf16[384,512]{1,0:T(8,128)(2,1)S(1)} %collective-permute-done.refs_0_), channel_id=1, source_target_pairs={{0,4},{1,5},{2,6},{3,7},{4,0},{5,1},{6,2},{7,3},{8,12},{9,13},{10,... | collective-permute-start | bytes 1179656 | tf_op jit(solution)/shard_map/ppermute | solution.py:277
  37.7 2.2 %partial.2.near_ref = f32[392,128]{1,0:T(8,128)S(1)} custom-call(s32[1]{0:T(128)} %bitcast.6.place, bf16[384,8192]{1,0:T(8,128)(2,1)} %h_ref.11, bf16[2048,128]{1,0:T(8,128)(2,1)} %collective-permute-done.3.w_ref, f32[384,256]{1,0:T(8,128)S(1)} %near.1.before_ref, f32[8,128]{1,0:T(8,128)S(1)} %pad.7.owner_ref), custom_call_target="tpu_custom_call" | custom-call | tf_op jit(solution)/shard_map/partial/pallas_call | solution.py:242
  39.8 0.0 copy-start
  39.9 0.0 collective-permute-done.8.refs_2_
  39.9 1.3 %collective-permute-start.6 = (f32[392,128]{1,0:T(8,128)S(1)}, f32[392,128]{1,0:T(8,128)}, u32[]{:S(2)}, u32[]{:S(2)}) collective-permute-start(f32[392,128]{1,0:T(8,128)S(1)} %partial.2.near_ref), channel_id=1, source_target_pairs={{0,8},{24,16},{1,9},{25,17},{2,10},{26,18},{3,11},{27,19},{4,12},{... | collective-permute-start | bytes 602120 | tf_op jit(solution)/shard_map/ppermute | solution.py:274
  41.2 2.7 %collective-permute-start.15 = (bf16[2048,128]{1,0:T(8,128)(2,1)}, bf16[2048,128]{1,0:T(8,128)(2,1)}, u32[]{:S(2)}, u32[]{:S(2)}) collective-permute-start(bf16[2048,128]{1,0:T(8,128)(2,1)} %collective-permute-done.14.w_ref), channel_id=1, source_target_pairs={{8,16},{16,8},{9,17},{17,9},{10,18},{18,10},{11,19},{19,11},{12,20... | collective-permute-start | bytes 1572872 | tf_op jit(solution)/shard_map/ppermute | solution.py:274
  43.9 3.7 %collective-permute-done.2.refs_4_ = bf16[384,512]{1,0:T(8,128)(2,1)S(1)} collective-permute-done((bf16[384,512]{1,0:T(8,128)(2,1)S(1)}, bf16[384,512]{1,0:T(8,128)(2,1)S(1)}, u32[]{:S(2)}, u32[]{:S(2)}) %collective-permute-start.2) | collective-permute-done | bytes 393248 | tf_op jit(solution)/shard_map/ppermute | solution.py:277
  47.6 0.0 collective-permute-start.12
  47.6 1.3 %collective-permute-done.6.outer_ref = f32[392,128]{1,0:T(8,128)} collective-permute-done((f32[392,128]{1,0:T(8,128)S(1)}, f32[392,128]{1,0:T(8,128)}, u32[]{:S(2)}, u32[]{:S(2)}) %collective-permute-start.6) | collective-permute-done | bytes 200736 | tf_op jit(solution)/shard_map/ppermute | solution.py:274
  48.9 0.0 collective-permute-start.9
  48.9 0.5 collective-permute-start.10
  49.4 2.2 %partial.3.near_ref = f32[384,128]{1,0:T(8,128)S(1)} custom-call(s32[1]{0:T(128)} %bitcast.6.place, bf16[384,8192]{1,0:T(8,128)(2,1)} %h_ref.11, bf16[2048,128]{1,0:T(8,128)(2,1)} %collective-permute-done.14.w_ref, f32[384,256]{1,0:T(8,128)S(1)} %near.1.before_ref, f32[8,128]{1,0:T(8,128)S(1)} %pad.7.owner_ref), custom_call_target="tpu_custom_call" | custom-call | tf_op jit(solution)/shard_map/partial/pallas_call | solution.py:242
  51.6 1.3 %collective-permute-start.16 = (f32[384,128]{1,0:T(8,128)S(1)}, f32[384,128]{1,0:T(8,128)S(1)}, u32[]{:S(2)}, u32[]{:S(2)}) collective-permute-start(f32[384,128]{1,0:T(8,128)S(1)} %partial.3.near_ref), channel_id=1, source_target_pairs={{0,8},{24,16},{1,9},{25,17},{2,10},{26,18},{3,11},{27,19},{4,12},{... | collective-permute-start | bytes 589832 | tf_op jit(solution)/shard_map/ppermute | solution.py:274
  52.9 0.1 add_add_fusion.place
  53.0 0.1 add_add_fusion.1.place
  53.1 3.0 %facing.1.facing_ref = f32[768,256]{1,0:T(8,128)S(1)} custom-call(s32[4]{0:T(128)S(1)} %add_add_fusion.1.place, bf16[384,8192]{1,0:T(8,128)(2,1)} %h_ref.11, bf16[2048,128]{1,0:T(8,128)(2,1)} %copy-done.4, bf16[2048,128]{1,0:T(8,128)(2,1)} %copy-done.5, bf16[384,512]{1,0:T(8,128)(2,1)S(1)} %collective-permute-done.refs_0_, ...), custom_call_target="tpu_custom_call" | custom-call | tf_op jit(solution)/shard_map/facing/pallas_call | solution.py:242
  56.1 0.0 copy-start.3
  56.1 3.5 %distant.2.k_in = bf16[784,128]{1,0:T(8,128)(2,1)S(1)} custom-call(s32[4]{0:T(128)S(1)} %add_add_fusion.place, bf16[384,8192]{1,0:T(8,128)(2,1)} %h_ref.11, bf16[2048,128]{1,0:T(8,128)(2,1)} %collective-permute-done.5.w_ref, f32[392,128]{1,0:T(8,128)} %copy-done, f32[392,128]{1,0:T(8,128)} %collective-permute-done.6.outer_ref, ...), custom_call_target="tpu_custom_call" | custom-call | tf_op jit(solution)/shard_map/distant/pallas_call | solution.py:242
  59.6 1.3 %collective-permute-start.19 = (bf16[784,128]{1,0:T(8,128)(2,1)S(1)}, bf16[784,128]{1,0:T(8,128)(2,1)S(1)}, u32[]{:S(2)}, u32[]{:S(2)}) collective-permute-start(bf16[784,128]{1,0:T(8,128)(2,1)S(1)} %distant.2.k_in), channel_id=1, source_target_pairs={{8,0},{16,24},{9,1},{17,25},{10,2},{18,26},{11,3},{19,27},{12,4},{... | collective-permute-start | bytes 602120 | tf_op jit(solution)/shard_map/ppermute | solution.py:274
  60.9 1.3 %collective-permute-start.18 = (bf16[784,128]{1,0:T(8,128)(2,1)S(1)}, bf16[784,128]{1,0:T(8,128)(2,1)S(1)}, u32[]{:S(2)}, u32[]{:S(2)}) collective-permute-start(bf16[784,128]{1,0:T(8,128)(2,1)S(1)} %distant.2.k_in), channel_id=1, source_target_pairs={{8,24},{16,0},{9,25},{17,1},{10,26},{18,2},{11,27},{19,3},{12,28},... | collective-permute-start | bytes 602120 | tf_op jit(solution)/shard_map/ppermute | solution.py:274
  62.2 0.0 copy-start.1
  62.2 2.8 %distant.3.v_in = bf16[768,128]{1,0:T(8,128)(2,1)S(1)} custom-call(s32[4]{0:T(128)S(1)} %add_add_fusion.place, bf16[384,8192]{1,0:T(8,128)(2,1)} %h_ref.11, bf16[2048,128]{1,0:T(8,128)(2,1)} %collective-permute-done.15.w_ref, f32[384,128]{1,0:T(8,128)S(1)} %partial.3.near_ref, f32[384,128]{1,0:T(8,128)S(1)} %collective-permute-done.16.outer_ref, ...), custom_call_target="tpu_custom_call" | custom-call | tf_op jit(solution)/shard_map/distant/pallas_call | solution.py:242
  65.1 2.6 %collective-permute-start.17 = (bf16[768,128]{1,0:T(8,128)(2,1)S(1)}, bf16[768,128]{1,0:T(8,128)(2,1)S(1)}, u32[]{:S(2)}, u32[]{:S(2)}) collective-permute-start(bf16[768,128]{1,0:T(8,128)(2,1)S(1)} %distant.3.v_in), channel_id=1, source_target_pairs={{8,16},{16,8},{9,17},{17,9},{10,18},{18,10},{11,19},{19,11},{12,20... | collective-permute-start | bytes 589832 | tf_op jit(solution)/shard_map/ppermute | solution.py:274
  67.6 1.3 %collective-permute-start.21 = (bf16[768,128]{1,0:T(8,128)(2,1)S(1)}, bf16[768,128]{1,0:T(8,128)(2,1)S(1)}, u32[]{:S(2)}, u32[]{:S(2)}) collective-permute-start(bf16[768,128]{1,0:T(8,128)(2,1)S(1)} %distant.3.v_in), channel_id=1, source_target_pairs={{8,0},{16,24},{9,1},{17,25},{10,2},{18,26},{11,3},{19,27},{12,4},{... | collective-permute-start | bytes 589832 | tf_op jit(solution)/shard_map/ppermute | solution.py:274
  68.9 3.3 %collective-permute-start.13 = (bf16[784,128]{1,0:T(8,128)(2,1)S(1)}, bf16[784,128]{1,0:T(8,128)(2,1)S(1)}, u32[]{:S(2)}, u32[]{:S(2)}) collective-permute-start(bf16[784,128]{1,0:T(8,128)(2,1)S(1)} %distant.2.k_in), channel_id=1, source_target_pairs={{8,16},{16,8},{9,17},{17,9},{10,18},{18,10},{11,19},{19,11},{12,20... | collective-permute-start | bytes 602120 | tf_op jit(solution)/shard_map/ppermute | solution.py:274
  72.2 2.2 %collective-permute-done.17.v_across = bf16[768,128]{1,0:T(8,128)(2,1)S(1)} collective-permute-done((bf16[768,128]{1,0:T(8,128)(2,1)S(1)}, bf16[768,128]{1,0:T(8,128)(2,1)S(1)}, u32[]{:S(2)}, u32[]{:S(2)}) %collective-permute-start.17) | collective-permute-done | bytes 196640 | tf_op jit(solution)/shard_map/ppermute | solution.py:274
  74.4 1.5 %collective-permute-start.20 = (bf16[768,128]{1,0:T(8,128)(2,1)S(1)}, bf16[768,128]{1,0:T(8,128)(2,1)S(1)}, u32[]{:S(2)}, u32[]{:S(2)}) collective-permute-start(bf16[768,128]{1,0:T(8,128)(2,1)S(1)} %collective-permute-done.17.v_across), channel_id=1, source_target_pairs={{8,0},{16,24},{9,1},{17,25},{10,2},{18,26},{11,3},{19,27},{12,4},{... | collective-permute-start | bytes 589832 | tf_op jit(solution)/shard_map/ppermute | solution.py:274
  75.9 5.3 %attend_own.1 = (f32[8,384,1]{2,1,0:T(8,128)S(1)}, f32[8,384,1]{2,1,0:T(8,128)S(1)}, f32[8,384,128]{2,1,0:T(8,128)S(1)}, bf16[2,192,256]{2,1,0:T(8,128)(2,1)S(1)}) custom-call(s32[1]{0:T(128)} %bitcast.place.info, bf16[384,1024]{1,0:T(8,128)(2,1)} %q_ref.3, s32[12,128]{1,0:T(8,128)S(1)} %bitcast.13, bf16[784,128]{1,0:T(8,128)(2,1)S(1)} %distant.2.k_in, ...), custom_call_target="tpu_custom_call" | custom-call | flops 1207959552 | bytes 18874368 | tf_op jit(solution)/shard_map/attend_own/pallas_call | solution.py:585
  81.2 6.8 %attend_far.1 = (bf16[384,1024]{1,0:T(8,128)(2,1)}, bf16[4,192,256]{2,1,0:T(8,128)(2,1)}) custom-call(s32[1]{0:T(128)} %bitcast.place.info, bf16[384,1024]{1,0:T(8,128)(2,1)} %q_ref.3, s32[12,128]{1,0:T(8,128)S(1)} %bitcast.14, bf16[784,128]{1,0:T(8,128)(2,1)S(1)} %collective-permute-done.13.k_across, bf16[784,128]{1,0:T(8,128)(2,1)S(1)} %collective-permute-done.18.k_far, ...), custom_call_target="tpu_custom_call" | custom-call | flops 1207959552 | bytes 18874368 | tf_op jit(solution)/shard_map/attend_far/pallas_call | solution.py:600
  (28 shorter events, 0.1 us)
Async XLA Ops:
  0.6 15.9 %collective-permute-start.1 = (bf16[2048,128]{1,0:T(8,128)(2,1)}, bf16[2048,128]{1,0:T(8,128)(2,1)S(1)}, u32[]{:S(2)}, u32[]{:S(2)}) collective-permute-start(bf16[2048,128]{1,0:T(8,128)(2,1)} %kw_ref.1), channel_id=1, source_target_pairs={{8,16},{16,8},{9,17},{17,9},{10,18},{18,10},{11,19},{19,11},{12,20... | collective-permute-start | bytes 1572872 | tf_op jit(solution)/shard_map/ppermute | solution.py:274
  4.0 12.5 %collective-permute-start = (bf16[384,512]{1,0:T(8,128)(2,1)S(1)}, bf16[384,512]{1,0:T(8,128)(2,1)S(1)}, u32[]{:S(2)}, u32[]{:S(2)}) collective-permute-start(bf16[384,512]{1,0:T(8,128)(2,1)S(1)} %constant_dynamic-slice_fusion), channel_id=1, source_target_pairs={{0,8},{24,16},{1,9},{25,17},{2,10},{26,18},{3,11},{27,19},{4,12},{... | collective-permute-start | bytes 1179656 | tf_op jit(solution)/shard_map/ppermute | solution.py:274
  5.3 11.2 %copy-start.6 = (bf16[2048,128]{1,0:T(8,128)(2,1)S(1)}, bf16[2048,128]{1,0:T(8,128)(2,1)}, u32[]{:S(2)}) copy-start(bf16[2048,128]{1,0:T(8,128)(2,1)} %kw_ref.1) | copy-start | bytes 1572868
  5.4 12.0 %copy-start.7 = (bf16[2048,128]{1,0:T(8,128)(2,1)S(1)}, bf16[2048,128]{1,0:T(8,128)(2,1)}, u32[]{:S(2)}) copy-start(bf16[2048,128]{1,0:T(8,128)(2,1)} %vw_ref.1) | copy-start | bytes 1572868
  5.4 32.3 %copy-start.8 = (s32[24,1]{0,1:T(1,128)S(1)}, s32[24,1]{0,1:T(1,128)}, u32[]{:S(2)}) copy-start(s32[24,1]{0,1:T(1,128)} %param.15) | copy-start | bytes 292
  16.5 0.8 copy-start.4
  16.5 15.0 %collective-permute-start.3 = (bf16[2048,128]{1,0:T(8,128)(2,1)S(1)}, bf16[2048,128]{1,0:T(8,128)(2,1)}, u32[]{:S(2)}, u32[]{:S(2)}) collective-permute-start(bf16[2048,128]{1,0:T(8,128)(2,1)S(1)} %copy-done.6), channel_id=1, source_target_pairs={{0,8},{8,0},{16,24},{24,16},{1,9},{9,1},{17,25},{25,17},{2,10},{10... | collective-permute-start | bytes 1572872 | tf_op jit(solution)/shard_map/ppermute | solution.py:274
  17.3 14.6 %collective-permute-start.4 = (bf16[2048,128]{1,0:T(8,128)(2,1)S(1)}, bf16[2048,128]{1,0:T(8,128)(2,1)S(1)}, u32[]{:S(2)}, u32[]{:S(2)}) collective-permute-start(bf16[2048,128]{1,0:T(8,128)(2,1)S(1)} %copy-done.7), channel_id=1, source_target_pairs={{8,16},{16,8},{9,17},{17,9},{10,18},{18,10},{11,19},{19,11},{12,20... | collective-permute-start | bytes 1572872 | tf_op jit(solution)/shard_map/ppermute | solution.py:274
  20.8 15.2 %collective-permute-start.11 = (bf16[384,512]{1,0:T(8,128)(2,1)S(1)}, bf16[384,512]{1,0:T(8,128)(2,1)S(1)}, u32[]{:S(2)}, u32[]{:S(2)}) collective-permute-start(bf16[384,512]{1,0:T(8,128)(2,1)S(1)} %collective-permute-done.refs_0_), channel_id=1, source_target_pairs={{0,6},{1,7},{2,4},{3,5},{4,2},{5,3},{6,0},{7,1},{8,14},{9,15},{10,... | collective-permute-start | bytes 1179656 | tf_op jit(solution)/shard_map/ppermute | solution.py:277
  23.3 17.9 %collective-permute-start.14 = (bf16[2048,128]{1,0:T(8,128)(2,1)S(1)}, bf16[2048,128]{1,0:T(8,128)(2,1)}, u32[]{:S(2)}, u32[]{:S(2)}) collective-permute-start(bf16[2048,128]{1,0:T(8,128)(2,1)S(1)} %copy-done.7), channel_id=1, source_target_pairs={{0,8},{8,0},{16,24},{24,16},{1,9},{9,1},{17,25},{25,17},{2,10},{10... | collective-permute-start | bytes 1572872 | tf_op jit(solution)/shard_map/ppermute | solution.py:274
  23.3 16.5 %collective-permute-start.8 = (bf16[384,512]{1,0:T(8,128)(2,1)S(1)}, bf16[384,512]{1,0:T(8,128)(2,1)S(1)}, u32[]{:S(2)}, u32[]{:S(2)}) collective-permute-start(bf16[384,512]{1,0:T(8,128)(2,1)S(1)} %collective-permute-done.refs_0_), channel_id=1, source_target_pairs={{0,2},{1,3},{2,0},{3,1},{4,6},{5,7},{6,4},{7,5},{8,10},{9,11},{10,... | collective-permute-start | bytes 1179656 | tf_op jit(solution)/shard_map/ppermute | solution.py:277
  31.9 0.8 copy-start.5
  32.7 16.2 %collective-permute-start.5 = (bf16[2048,128]{1,0:T(8,128)(2,1)}, bf16[2048,128]{1,0:T(8,128)(2,1)}, u32[]{:S(2)}, u32[]{:S(2)}) collective-permute-start(bf16[2048,128]{1,0:T(8,128)(2,1)} %collective-permute-done.3.w_ref), channel_id=1, source_target_pairs={{8,16},{16,8},{9,17},{17,9},{10,18},{18,10},{11,19},{19,11},{12,20... | collective-permute-start | bytes 1572872 | tf_op jit(solution)/shard_map/ppermute | solution.py:274
  36.0 15.7 %collective-permute-start.7 = (bf16[384,512]{1,0:T(8,128)(2,1)S(1)}, bf16[384,512]{1,0:T(8,128)(2,1)S(1)}, u32[]{:S(2)}, u32[]{:S(2)}) collective-permute-start(bf16[384,512]{1,0:T(8,128)(2,1)S(1)} %collective-permute-done.refs_0_), channel_id=1, source_target_pairs={{0,1},{1,0},{2,3},{3,2},{4,5},{5,4},{6,7},{7,6},{8,9},{9,8},{10,11... | collective-permute-start | bytes 1179656 | tf_op jit(solution)/shard_map/ppermute | solution.py:277
  36.0 11.5 %collective-permute-start.2 = (bf16[384,512]{1,0:T(8,128)(2,1)S(1)}, bf16[384,512]{1,0:T(8,128)(2,1)S(1)}, u32[]{:S(2)}, u32[]{:S(2)}) collective-permute-start(bf16[384,512]{1,0:T(8,128)(2,1)S(1)} %collective-permute-done.refs_0_), channel_id=1, source_target_pairs={{0,4},{1,5},{2,6},{3,7},{4,0},{5,1},{6,2},{7,3},{8,12},{9,13},{10,... | collective-permute-start | bytes 1179656 | tf_op jit(solution)/shard_map/ppermute | solution.py:277
  39.8 9.1 %copy-start = (f32[392,128]{1,0:T(8,128)}, f32[392,128]{1,0:T(8,128)S(1)}, u32[]{:S(2)}) copy-start(f32[392,128]{1,0:T(8,128)S(1)} %partial.2.near_ref) | copy-start | bytes 602116
  39.9 9.1 %collective-permute-start.6 = (f32[392,128]{1,0:T(8,128)S(1)}, f32[392,128]{1,0:T(8,128)}, u32[]{:S(2)}, u32[]{:S(2)}) collective-permute-start(f32[392,128]{1,0:T(8,128)S(1)} %partial.2.near_ref), channel_id=1, source_target_pairs={{0,8},{24,16},{1,9},{25,17},{2,10},{26,18},{3,11},{27,19},{4,12},{... | collective-permute-start | bytes 602120 | tf_op jit(solution)/shard_map/ppermute | solution.py:274
  41.2 21.0 %collective-permute-start.15 = (bf16[2048,128]{1,0:T(8,128)(2,1)}, bf16[2048,128]{1,0:T(8,128)(2,1)}, u32[]{:S(2)}, u32[]{:S(2)}) collective-permute-start(bf16[2048,128]{1,0:T(8,128)(2,1)} %collective-permute-done.14.w_ref), channel_id=1, source_target_pairs={{8,16},{16,8},{9,17},{17,9},{10,18},{18,10},{11,19},{19,11},{12,20... | collective-permute-start | bytes 1572872 | tf_op jit(solution)/shard_map/ppermute | solution.py:274
  47.6 5.5 %collective-permute-start.12 = (bf16[384,512]{1,0:T(8,128)(2,1)S(1)}, bf16[384,512]{1,0:T(8,128)(2,1)S(1)}, u32[]{:S(2)}, u32[]{:S(2)}) collective-permute-start(bf16[384,512]{1,0:T(8,128)(2,1)S(1)} %collective-permute-done.11.refs_6_), channel_id=1, source_target_pairs={{0,1},{1,0},{2,3},{3,2},{4,5},{5,4},{6,7},{7,6},{8,9},{9,8},{10,11... | collective-permute-start | bytes 1179656 | tf_op jit(solution)/shard_map/ppermute | solution.py:277
  48.9 4.2 %collective-permute-start.9 = (bf16[384,512]{1,0:T(8,128)(2,1)S(1)}, bf16[384,512]{1,0:T(8,128)(2,1)S(1)}, u32[]{:S(2)}, u32[]{:S(2)}) collective-permute-start(bf16[384,512]{1,0:T(8,128)(2,1)S(1)} %collective-permute-done.8.refs_2_), channel_id=1, source_target_pairs={{0,1},{1,0},{2,3},{3,2},{4,5},{5,4},{6,7},{7,6},{8,9},{9,8},{10,11... | collective-permute-start | bytes 1179656 | tf_op jit(solution)/shard_map/ppermute | solution.py:277
  48.9 4.2 %collective-permute-start.10 = (bf16[384,512]{1,0:T(8,128)(2,1)S(1)}, bf16[384,512]{1,0:T(8,128)(2,1)S(1)}, u32[]{:S(2)}, u32[]{:S(2)}) collective-permute-start(bf16[384,512]{1,0:T(8,128)(2,1)S(1)} %collective-permute-done.2.refs_4_), channel_id=1, source_target_pairs={{0,1},{1,0},{2,3},{3,2},{4,5},{5,4},{6,7},{7,6},{8,9},{9,8},{10,11... | collective-permute-start | bytes 1179656 | tf_op jit(solution)/shard_map/ppermute | solution.py:277
  51.6 10.5 %collective-permute-start.16 = (f32[384,128]{1,0:T(8,128)S(1)}, f32[384,128]{1,0:T(8,128)S(1)}, u32[]{:S(2)}, u32[]{:S(2)}) collective-permute-start(f32[384,128]{1,0:T(8,128)S(1)} %partial.3.near_ref), channel_id=1, source_target_pairs={{0,8},{24,16},{1,9},{25,17},{2,10},{26,18},{3,11},{27,19},{4,12},{... | collective-permute-start | bytes 589832 | tf_op jit(solution)/shard_map/ppermute | solution.py:274
  53.1 3.0 %copy-start.2 = (bf16[128]{0:T(256)(128)(2,1)S(1)}, bf16[128]{0:T(256)(128)(2,1)}, u32[]{:S(2)}) copy-start(bf16[128]{0:T(256)(128)(2,1)} %param.12) | copy-start | bytes 772
  56.1 6.1 %copy-start.3 = (bf16[128]{0:T(256)(128)(2,1)S(1)}, bf16[128]{0:T(256)(128)(2,1)}, u32[]{:S(2)}) copy-start(bf16[128]{0:T(256)(128)(2,1)} %param.13) | copy-start | bytes 772
  59.6 14.8 %collective-permute-start.19 = (bf16[784,128]{1,0:T(8,128)(2,1)S(1)}, bf16[784,128]{1,0:T(8,128)(2,1)S(1)}, u32[]{:S(2)}, u32[]{:S(2)}) collective-permute-start(bf16[784,128]{1,0:T(8,128)(2,1)S(1)} %distant.2.k_in), channel_id=1, source_target_pairs={{8,0},{16,24},{9,1},{17,25},{10,2},{18,26},{11,3},{19,27},{12,4},{... | collective-permute-start | bytes 602120 | tf_op jit(solution)/shard_map/ppermute | solution.py:274
  60.9 13.5 %collective-permute-start.18 = (bf16[784,128]{1,0:T(8,128)(2,1)S(1)}, bf16[784,128]{1,0:T(8,128)(2,1)S(1)}, u32[]{:S(2)}, u32[]{:S(2)}) collective-permute-start(bf16[784,128]{1,0:T(8,128)(2,1)S(1)} %distant.2.k_in), channel_id=1, source_target_pairs={{8,24},{16,0},{9,25},{17,1},{10,26},{18,2},{11,27},{19,3},{12,28},... | collective-permute-start | bytes 602120 | tf_op jit(solution)/shard_map/ppermute | solution.py:274
  62.2 13.7 %copy-start.1 = (s32[1536]{0:T(1024)S(1)}, s32[1536]{0:T(1024)}, u32[]{:S(2)}) copy-start(s32[1536]{0:T(1024)} %param.14) | copy-start | bytes 18436
  65.1 9.3 %collective-permute-start.17 = (bf16[768,128]{1,0:T(8,128)(2,1)S(1)}, bf16[768,128]{1,0:T(8,128)(2,1)S(1)}, u32[]{:S(2)}, u32[]{:S(2)}) collective-permute-start(bf16[768,128]{1,0:T(8,128)(2,1)S(1)} %distant.3.v_in), channel_id=1, source_target_pairs={{8,16},{16,8},{9,17},{17,9},{10,18},{18,10},{11,19},{19,11},{12,20... | collective-permute-start | bytes 589832 | tf_op jit(solution)/shard_map/ppermute | solution.py:274
  67.6 8.2 %collective-permute-start.21 = (bf16[768,128]{1,0:T(8,128)(2,1)S(1)}, bf16[768,128]{1,0:T(8,128)(2,1)S(1)}, u32[]{:S(2)}, u32[]{:S(2)}) collective-permute-start(bf16[768,128]{1,0:T(8,128)(2,1)S(1)} %distant.3.v_in), channel_id=1, source_target_pairs={{8,0},{16,24},{9,1},{17,25},{10,2},{18,26},{11,3},{19,27},{12,4},{... | collective-permute-start | bytes 589832 | tf_op jit(solution)/shard_map/ppermute | solution.py:274
  68.9 12.3 %collective-permute-start.13 = (bf16[784,128]{1,0:T(8,128)(2,1)S(1)}, bf16[784,128]{1,0:T(8,128)(2,1)S(1)}, u32[]{:S(2)}, u32[]{:S(2)}) collective-permute-start(bf16[784,128]{1,0:T(8,128)(2,1)S(1)} %distant.2.k_in), channel_id=1, source_target_pairs={{8,16},{16,8},{9,17},{17,9},{10,18},{18,10},{11,19},{19,11},{12,20... | collective-permute-start | bytes 602120 | tf_op jit(solution)/shard_map/ppermute | solution.py:274
  74.4 6.8 %collective-permute-start.20 = (bf16[768,128]{1,0:T(8,128)(2,1)S(1)}, bf16[768,128]{1,0:T(8,128)(2,1)S(1)}, u32[]{:S(2)}, u32[]{:S(2)}) collective-permute-start(bf16[768,128]{1,0:T(8,128)(2,1)S(1)} %collective-permute-done.17.v_across), channel_id=1, source_target_pairs={{8,0},{16,24},{9,1},{17,25},{10,2},{18,26},{11,3},{19,27},{12,4},{... | collective-permute-start | bytes 589832 | tf_op jit(solution)/shard_map/ppermute | solution.py:274
